TPU v7x, 32 devices: a whole 2x2x4 slice. The times are simulated.
32 devices in a mesh: dp: 8 (over y, x, core), mp: 4 (over z).
Axes of the slice: x: 2, y: 2, z: 4, core: 2. Of those that a mesh axis runs over, the one named last changes fastest.
Arguments:
- samples: bfloat16 [64, 55, 128], P('dp'), may hold values from -6 to 6
- targets: bfloat16 [64, 53, 128], P('dp'), may hold values from -6 to 6
- counts: int32 [8], P('dp'), may hold values from 1 to 7, as said below
- weight_in: float32 [55, 2048], P(None, ('mp', 'dp')), may hold values from -0.875 to 0.875
- weight_mid: float32 [2048, 2048], P('mp', 'dp'), may hold values from -0.125 to 0.125
- weight_top: float32 [2048, 2048], P('dp', 'mp'), may hold values from -0.125 to 0.125
- weight_out: float32 [2048, 53], P(('mp', 'dp')), may hold values from -0.125 to 0.125
- moment_in: float32 [55, 2048], P(None, ('mp', 'dp')), may hold values from -0.15625 to 0.15625
- moment_mid: float32 [2048, 2048], P('mp', 'dp'), may hold values from -0.15625 to 0.15625
- moment_top: float32 [2048, 2048], P('dp', 'mp'), may hold values from -0.15625 to 0.15625
- moment_out: float32 [2048, 53], P(('mp', 'dp')), may hold values from -0.15625 to 0.15625
Outputs:
- new_in: float32 [55, 2048], P(None, ('mp', 'dp'))
- new_mid: float32 [2048, 2048], P('mp', 'dp')
- new_top: float32 [2048, 2048], P('dp', 'mp')
- new_out: float32 [2048, 53], P(('mp', 'dp'))
- mom_in: float32 [55, 2048], P(None, ('mp', 'dp'))
- mom_mid: float32 [2048, 2048], P('mp', 'dp')
- mom_top: float32 [2048, 2048], P('dp', 'mp')
- mom_out: float32 [2048, 53], P(('mp', 'dp'))
Inputs may be any that keep to these rules, and one draw needn't show every extreme that they name: Partition p and partition (p + 4) mod 8 form a matched pair whose counts sum to at most 8; some partition has 7.
All inputs are finite; a program needn't handle non-finite values.
Results may differ from a plain program's by a relative error of at most 0.011.
Values may be sent and summed in bfloat16 or wider, within the bound.
No kernel may reach another device: no remote copies, remote signals or barrier semaphores. Data moves between devices by JAX's collectives and lax.ppermute only.
A program may use at most 64 MiB of HBM per device.

v0:
```python
import math

import jax
import jax.numpy as jnp
from jax import lax
from jax.sharding import PartitionSpec as P

momentum_decay = 0.9
learn_rate = 0.05


def from_partner(block, axis, stride):
    count = lax.axis_size(axis)
    route = []
    for low in range(count):
        high = low | 1 << stride
        if high != low and high < count:
            route += [(low, high), (high, low)]
    return lax.ppermute(block, axis, route)


def gelu_act(value):
    return 0.5 * value * (1.0 + jax.scipy.special.erf(value / math.sqrt(2.0)))


def gelu_slope(value):
    return 0.5 * (1.0 + jax.scipy.special.erf(value / math.sqrt(2.0))) + value * jnp.exp(
        -0.5 * value * value
    ) / math.sqrt(2.0 * math.pi)


def columns_sum(term):
    return lax.psum(term.astype(jnp.bfloat16), "mp").astype(jnp.float32)


def on_device(
    samples,
    targets,
    counts,
    weight_in,
    weight_mid,
    weight_top,
    weight_out,
    moment_in,
    moment_mid,
    moment_top,
    moment_out,
):
    all_counts = lax.all_gather(counts, "dp", axis=0, tiled=True)
    total = jnp.sum(all_counts).astype(jnp.float32) * samples.shape[2]
    myself = lax.axis_index("dp")
    slots = samples.shape[0]
    half_slots = slots // 2
    mine = all_counts[myself]
    peers = lax.axis_size("dp")
    top_bit = peers.bit_length() - 2
    partner = (myself + peers // 2) % peers
    theirs = all_counts[partner]
    own_valid = jnp.minimum(mine, half_slots)
    extra = jnp.maximum(theirs - half_slots, 0)
    recv_x, recv_y = from_partner((samples[half_slots:], targets[half_slots:]), "dp", top_bit)
    zero_int = jnp.zeros((), jnp.int32)
    inputs = lax.dynamic_update_slice(
        jnp.concatenate([samples[:half_slots], jnp.zeros_like(recv_x)], 0),
        recv_x,
        (own_valid, zero_int, zero_int),
    )[:half_slots]
    wanted = lax.dynamic_update_slice(
        jnp.concatenate([targets[:half_slots], jnp.zeros_like(recv_y)], 0),
        recv_y,
        (own_valid, zero_int, zero_int),
    )[:half_slots]
    live = (jnp.arange(half_slots, dtype=jnp.int32) < own_valid + extra).astype(jnp.float32)
    first, second, third, fourth = (
        lax.all_gather(weight_in.astype(jnp.bfloat16), "dp", axis=1, tiled=True),
        lax.all_gather(weight_mid.astype(jnp.bfloat16), "dp", axis=1, tiled=True),
        lax.all_gather(weight_top.astype(jnp.bfloat16), "dp", axis=0, tiled=True),
        lax.all_gather(weight_out.astype(jnp.bfloat16), "dp", axis=0, tiled=True),
    )
    f32 = jnp.float32
    pre_one = jnp.einsum("bir,ih->brh", inputs, first, preferred_element_type=f32)
    act_one = gelu_act(pre_one).astype(jnp.bfloat16)
    pre_two = columns_sum(jnp.einsum("brk,kh->brh", act_one, second, preferred_element_type=f32))
    act_two = gelu_act(pre_two).astype(jnp.bfloat16)
    pre_three = jnp.einsum("brh,hk->brk", act_two, third, preferred_element_type=f32)
    act_three = gelu_act(pre_three).astype(jnp.bfloat16)
    predicted = columns_sum(
        jnp.einsum("brk,ko->bor", act_three, fourth, preferred_element_type=f32)
    )
    grad_pred = (2.0 / total * (predicted - wanted.astype(f32)) * live[:, None, None]).astype(
        jnp.bfloat16
    )
    grad_four = jnp.einsum("brk,bor->ko", act_three, grad_pred, preferred_element_type=f32)
    delta_three = (
        jnp.einsum("bor,ko->brk", grad_pred, fourth, preferred_element_type=f32)
        * gelu_slope(pre_three)
    ).astype(jnp.bfloat16)
    grad_three = jnp.einsum("brh,brk->hk", act_two, delta_three, preferred_element_type=f32)
    delta_two = (
        columns_sum(jnp.einsum("brk,hk->brh", delta_three, third, preferred_element_type=f32))
        * gelu_slope(pre_two)
    ).astype(jnp.bfloat16)
    grad_two = jnp.einsum("brk,brh->kh", act_one, delta_two, preferred_element_type=f32)
    delta_one = (
        jnp.einsum("brh,kh->brk", delta_two, second, preferred_element_type=f32)
        * gelu_slope(pre_one)
    ).astype(jnp.bfloat16)
    grad_one = jnp.einsum("bir,brk->ik", inputs, delta_one, preferred_element_type=f32)
    sum_one, sum_two, sum_three, sum_four = (
        lax.psum_scatter(
            grad_one.astype(jnp.bfloat16), "dp", scatter_dimension=1, tiled=True
        ).astype(jnp.float32),
        lax.psum_scatter(
            grad_two.astype(jnp.bfloat16), "dp", scatter_dimension=1, tiled=True
        ).astype(jnp.float32),
        lax.psum_scatter(
            grad_three.astype(jnp.bfloat16), "dp", scatter_dimension=0, tiled=True
        ).astype(jnp.float32),
        lax.psum_scatter(
            grad_four.astype(jnp.bfloat16), "dp", scatter_dimension=0, tiled=True
        ).astype(jnp.float32),
    )
    mom_in = momentum_decay * moment_in + sum_one
    mom_mid = momentum_decay * moment_mid + sum_two
    mom_top = momentum_decay * moment_top + sum_three
    mom_out = momentum_decay * moment_out + sum_four
    return (
        weight_in - learn_rate * mom_in,
        weight_mid - learn_rate * mom_mid,
        weight_top - learn_rate * mom_top,
        weight_out - learn_rate * mom_out,
        mom_in,
        mom_mid,
        mom_top,
        mom_out,
    )


def solution(mesh):
    in_specs = (
        P("dp", None, None),
        P("dp", None, None),
        P("dp"),
        P(None, ("mp", "dp")),
        P("mp", "dp"),
        P("dp", "mp"),
        P(("mp", "dp"), None),
        P(None, ("mp", "dp")),
        P("mp", "dp"),
        P("dp", "mp"),
        P(("mp", "dp"), None),
    )
    out_specs = (
        P(None, ("mp", "dp")),
        P("mp", "dp"),
        P("dp", "mp"),
        P(("mp", "dp"), None),
        P(None, ("mp", "dp")),
        P("mp", "dp"),
        P("dp", "mp"),
        P(("mp", "dp"), None),
    )
    return jax.shard_map(
        on_device, mesh=mesh, in_specs=in_specs, out_specs=out_specs, check_vma=False
    )
```

profile of v0, /device:TPU:0, one launch (start us, length us, event | category | flops | bytes accessed | tf_op | source)
XLA Modules:
  0.0 447.7 jit_solution(7801918861911822031)
XLA Ops:
  7.2 1.8 convert_element_type.94
  9.1 0.9 slice.20
  10.0 3.0 collective-permute-start
  13.7 1.2 dynamic-slice
  15.7 1.0 broadcast_select_fusion.1
  17.5 7.0 %all-reduce = s32[8]{0:T(128)S(1)} all-reduce(s32[8]{0:T(128)S(1)} %dynamic-update-slice), channel_id=1, replica_groups=mesh['dp'=8,'mp'=4] {'dp'}, use_global_device_ids=true, to_apply=%add | all-reduce | flops 8 | bytes 64
  25.7 9.3 %all-gather = bf16[8,64,55]{1,2,0:T(8,128)(2,1)S(1)} all-gather(bf16[1,64,55]{1,2,0:T(8,128)(2,1)S(1)} %convert_bitcast_fusion.1), channel_id=1, replica_groups=mesh['dp'=8,'mp'=4] {'dp'}, dimensions={0}, use_global_device_ids=true | all-gather | bytes 63360 | tf_op jit(solution)/shard_map/all_gather | solution.py:75
  35.5 6.0 %all-gather.5.cloned.1.call-done = bf16[512,2048]{1,0:T(8,128)(2,1)} async-done(((bf16[512,256]{1,0:T(8,128)(2,1)}), bf16[512,2048]{1,0:T(8,128)(2,1)}) %all-gather.5.cloned.1.call-update) | async-done | bytes 2097168 | tf_op jit(solution)/shard_map/all_gather | solution.py:76
  41.6 4.2 convolution_convert_fusion.1
  45.8 0.9 copy-done.2
  47.7 1.1 collective-permute-start.1
  50.2 8.7 %all-gather.1 = bf16[8,64,53]{1,2,0:T(8,128)(2,1)S(1)} all-gather(bf16[1,64,53]{1,2,0:T(8,128)(2,1)S(1)} %convert_bitcast_fusion), channel_id=1, replica_groups=mesh['dp'=8,'mp'=4] {'dp'}, dimensions={0}, use_global_device_ids=true | all-gather | bytes 61056 | tf_op jit(solution)/shard_map/all_gather | solution.py:78
  59.8 72.7 %all-reduce.4.cloned.1.call-done = bf16[4,128,2048]{2,1,0:T(8,128)(2,1)} async-done(((bf16[4,128,2048]{2,1,0:T(8,128)(2,1)}), bf16[4,128,2048]{2,1,0:T(8,128)(2,1)}) %all-reduce.4.cloned.1.call-update) | async-done | bytes 2097168 | tf_op jit(solution)/shard_map/psum | solution.py:33
  132.5 3.6 fusion.3
  136.1 25.9 %all-gather.7.cloned.1.call-done = bf16[2048,512]{1,0:T(8,128)(2,1)} async-done(((bf16[256,512]{1,0:T(8,128)(2,1)}), bf16[2048,512]{1,0:T(8,128)(2,1)}) %all-gather.7.cloned.1.call-update) | async-done | bytes 2097168 | tf_op jit(solution)/shard_map/all_gather | solution.py:77
  162.0 5.2 %multiply_convert_fusion = (bf16[4,128,512]{2,1,0:T(8,128)(2,1)S(1)}, f32[4,128,512]{2,1,0:T(8,128)}) fusion(bf16[2048,512]{1,0:T(8,128)(2,1)} %all-gather.7.cloned.1.call-done, f32[4,128,2048]{2,1,0:T(8,128)} %fusion.3, bf16[4,128,2048]{2,1,0:T(8,128)(2,1)S(1)} %copy-done), kind=kOutput, calls=%fused_computation.44 | convolution fusion | flops 1079246848 | bytes 9961472 | tf_op jit(solution)/shard_map/brh,hk->brk/dot_general | solution.py:85
  167.4 19.7 %psum.22 = bf16[4,53,128]{2,1,0:T(8,128)(2,1)S(1)} all-reduce(bf16[4,53,128]{2,1,0:T(8,128)(2,1)S(1)} %fusion.18), channel_id=1, replica_groups=mesh['dp'=8,'mp'=4] {'mp'}, use_global_device_ids=true, to_apply=%region_2.3 | all-reduce | flops 27136 | bytes 108544 | tf_op jit(solution)/shard_map/psum | solution.py:33
  187.1 2.0 fusion.15
  189.9 2.7 convolution_convert_fusion
  193.8 82.8 %all-reduce.6.cloned.1.call-done = bf16[4,128,2048]{2,1,0:T(8,128)(2,1)} async-done(((bf16[4,128,2048]{2,1,0:T(8,128)(2,1)}), bf16[4,128,2048]{2,1,0:T(8,128)(2,1)}) %all-reduce.6.cloned.1.call-update) | async-done | bytes 2097168 | tf_op jit(solution)/shard_map/psum | solution.py:33
  276.6 4.3 fusion.8
  280.8 4.2 fusion.17
  285.9 4.9 %bitcast_convert_fusion = bf16[2048,512]{1,0:T(8,128)(2,1)} fusion(bf16[4,128,512]{2,1,0:T(8,128)(2,1)S(1)} %copy-done.7, f32[4,128,2048]{2,1,0:T(8,128)} %fusion.3, bf16[4,128,2048]{2,1,0:T(8,128)(2,1)S(1)} %copy-done), kind=kOutput, calls=%fused_computation.14 | convolution fusion | flops 1078984704 | bytes 8912896 | tf_op jit(solution)/shard_map/brh,brk->hk/dot_general | solution.py:98
  290.8 1.5 copy-done.1
  292.3 3.9 bitcast_convert_fusion.1
  296.3 16.0 %reduce-scatter.15.cloned.1.call-done = bf16[64,53]{1,0:T(8,128)(2,1)} async-done(((bf16[512,53]{1,0:T(8,128)(2,1)}), bf16[64,53]{1,0:T(8,128)(2,1)}) %reduce-scatter.15.cloned.1.call-update) | async-done | bytes 6800
  312.3 0.8 copy.40
  313.8 35.7 %reduce-scatter.13.cloned.1.call-done = bf16[64,55]{1,0:T(8,128)(2,1)} async-done(((bf16[512,55]{1,0:T(8,128)(2,1)}), bf16[64,55]{1,0:T(8,128)(2,1)}) %reduce-scatter.13.cloned.1.call-update) | async-done | bytes 7056
  350.9 43.1 %reduce-scatter.11.cloned.1.call-done = bf16[256,512]{1,0:T(8,128)(2,1)} async-done(((bf16[2048,512]{1,0:T(8,128)(2,1)}), bf16[256,512]{1,0:T(8,128)(2,1)}) %reduce-scatter.11.cloned.1.call-update) | async-done | bytes 262160 | tf_op jit(solution)/shard_map/reduce_scatter | solution.py:116
  394.0 2.1 multiply_subtract_fusion
  396.0 42.8 %reduce-scatter.9.cloned.1.call-done = bf16[512,256]{1,0:T(8,128)(2,1)} async-done(((bf16[512,2048]{1,0:T(8,128)(2,1)}), bf16[512,256]{1,0:T(8,128)(2,1)}) %reduce-scatter.9.cloned.1.call-update) | async-done | bytes 262160 | tf_op jit(solution)/shard_map/reduce_scatter | solution.py:113
  438.9 2.0 multiply_subtract_fusion.1
  (76 shorter events, 9.7 us)
Async XLA Ops:
  7.2 34.4 %all-gather.5.cloned.1.call-start = ((), (), s32[]{:S(2)}) async-start(), calls=%async_computation.4 | async-start | bytes 2359296 | tf_op jit(solution)/shard_map/all_gather | solution.py:76
  9.0 123.4 %all-reduce.4.cloned.1.call-start = ((), (), s32[]{:S(2)}) async-start(), calls=%async_computation.5 | async-start | bytes 4194304 | tf_op jit(solution)/shard_map/psum | solution.py:33
  10.0 25.2 %collective-permute-start = (bf16[4,55,128]{2,1,0:T(8,128)(2,1)S(1)}, bf16[4,55,128]{2,1,0:T(8,128)(2,1)S(1)}, u32[]{:S(2)}, u32[]{:S(2)}) collective-permute-start(bf16[4,55,128]{2,1,0:T(8,128)(2,1)S(1)} %copy.43), channel_id=1, source_target_pairs={{0,16},{16,0},{4,20},{20,4},{8,24},{24,8},{12,28},{28,12},{1,17},{... | collective-permute-start | bytes 168968 | tf_op jit(solution)/shard_map/ppermute | solution.py:19
  35.5 10.2 %copy-start.5 = (f32[4,128,512]{2,1,0:T(8,128)}, f32[4,128,512]{2,1,0:T(8,128)S(1)}, u32[]{:S(2)}) copy-start(f32[4,128,512]{2,1,0:T(8,128)S(1)} %fusion.40) | copy-start | bytes 3145732
  45.7 1.0 copy-start.2
  45.7 1.9 copy-start.10
  45.7 3.7 copy-start.11
  45.8 3.7 copy-start.16
  45.8 116.2 %all-gather.7.cloned.1.call-start = ((), (), s32[]{:S(2)}) async-start(), calls=%async_computation.6 | async-start | bytes 2359296 | tf_op jit(solution)/shard_map/all_gather | solution.py:77
  47.5 229.0 %all-reduce.6.cloned.1.call-start = ((), (), s32[]{:S(2)}) async-start(), calls=%async_computation.7 | async-start | bytes 4194304 | tf_op jit(solution)/shard_map/psum | solution.py:33
  47.7 12.1 %collective-permute-start.1 = (bf16[4,53,128]{2,1,0:T(8,128)(2,1)S(1)}, bf16[4,53,128]{2,1,0:T(8,128)(2,1)S(1)}, u32[]{:S(2)}, u32[]{:S(2)}) collective-permute-start(bf16[4,53,128]{2,1,0:T(8,128)(2,1)S(1)} %copy.44), channel_id=1, source_target_pairs={{0,16},{16,0},{4,20},{20,4},{8,24},{24,8},{12,28},{28,12},{1,17},{... | collective-permute-start | bytes 162824 | tf_op jit(solution)/shard_map/ppermute | solution.py:19
  132.4 29.5 %copy-start = (bf16[4,128,2048]{2,1,0:T(8,128)(2,1)S(1)}, bf16[4,128,2048]{2,1,0:T(8,128)(2,1)}, u32[]{:S(2)}) copy-start(bf16[4,128,2048]{2,1,0:T(8,128)(2,1)} %all-reduce.4.cloned.1.call-done) | copy-start | bytes 6291460
  187.1 2.8 copy-start.4
  189.1 0.8 copy-start.6
  192.6 119.7 %reduce-scatter.15.cloned.1.call-start = ((), (), s32[]{:S(2)}) async-start(), calls=%async_computation.11 | async-start | bytes 147456
  193.7 155.7 %reduce-scatter.13.cloned.1.call-start = ((), (), s32[]{:S(2)}) async-start(), calls=%async_computation.10 | async-start | bytes 147456
  280.8 5.0 %copy-start.7 = (bf16[4,128,512]{2,1,0:T(8,128)(2,1)S(1)}, bf16[4,128,512]{2,1,0:T(8,128)(2,1)}, u32[]{:S(2)}) copy-start(bf16[4,128,512]{2,1,0:T(8,128)(2,1)} %copy-done.6) | copy-start | bytes 1572868
  285.8 108.2 %reduce-scatter.11.cloned.1.call-start = ((), (), s32[]{:S(2)}) async-start(), calls=%async_computation.9 | async-start | bytes 2359296 | tf_op jit(solution)/shard_map/reduce_scatter | solution.py:116
  290.7 1.6 copy-start.1
  290.8 148.1 %reduce-scatter.9.cloned.1.call-start = ((), (), s32[]{:S(2)}) async-start(), calls=%async_computation.8 | async-start | bytes 2359296 | tf_op jit(solution)/shard_map/reduce_scatter | solution.py:113
  296.2 16.9 %copy-start.12 = (f32[64,53]{0,1:T(8,128)S(1)}, f32[64,53]{0,1:T(8,128)}, u32[]{:S(2)}) copy-start(f32[64,53]{0,1:T(8,128)} %param.17) | copy-start | bytes 40708
  296.2 16.9 %copy-start.14 = (f32[64,53]{0,1:T(8,128)S(1)}, f32[64,53]{0,1:T(8,128)}, u32[]{:S(2)}) copy-start(f32[64,53]{0,1:T(8,128)} %param.21) | copy-start | bytes 40708
  296.2 54.0 %copy-start.13 = (f32[55,64]{1,0:T(8,128)S(1)}, f32[55,64]{1,0:T(8,128)}, u32[]{:S(2)}) copy-start(f32[55,64]{1,0:T(8,128)} %param.14) | copy-start | bytes 42244
  296.2 54.0 %copy-start.15 = (f32[55,64]{1,0:T(8,128)S(1)}, f32[55,64]{1,0:T(8,128)}, u32[]{:S(2)}) copy-start(f32[55,64]{1,0:T(8,128)} %param.18) | copy-start | bytes 42244
  296.2 97.7 %copy-start.8 = (f32[256,512]{1,0:T(8,128)S(1)}, f32[256,512]{1,0:T(8,128)}, u32[]{:S(2)}) copy-start(f32[256,512]{1,0:T(8,128)} %param.20) | copy-start | bytes 1572868
  296.2 142.6 %copy-start.3 = (f32[512,256]{1,0:T(8,128)S(1)}, f32[512,256]{1,0:T(8,128)}, u32[]{:S(2)}) copy-start(f32[512,256]{1,0:T(8,128)} %param.15) | copy-start | bytes 1572868
  296.2 142.6 %copy-start.9 = (f32[512,256]{1,0:T(8,128)S(1)}, f32[512,256]{1,0:T(8,128)}, u32[]{:S(2)}) copy-start(f32[512,256]{1,0:T(8,128)} %param.19) | copy-start | bytes 1572868
Sparse Core Ops, SparseCore 0:
  10.5 31.0 all-gather.4
  45.9 86.4 all-reduce.3
  135.1 26.8 all-gather.6
  192.7 83.7 all-reduce.5
  280.0 32.2 reduce-scatter.14
  316.0 33.3 reduce-scatter.12
  352.7 41.2 reduce-scatter.10
  397.6 41.2 reduce-scatter.8
where the time goes:
time: 448 us
  waiting for transfers between devices  325 us (73%)
  blocking collectives  44.7 us (10%)
  matrix products  27.8 us (6%)
  other arithmetic  18.2 us (4%)
  between operations  17.1 us (4%)
  local copies, waits for them, and re-layouts  10.4 us (2%)
    psum x2, waiting for transfers between devices, columns_sum(): return lax.psum(term.astype(jnp.bfloat16), 'mp').astype(jnp.float32)  155 us
    unnamed x10, waiting for transfers between devices  51.8 us
    reduce_scatter x1, waiting for transfers between devices, on_device(): lax.psum_scatter(grad_three.astype(jnp.bfloat16), 'dp', scatter_dimension...  43.1 us
    reduce_scatter x1, waiting for transfers between devices, on_device(): lax.psum_scatter(grad_two.astype(jnp.bfloat16), 'dp', scatter_dimension=1...  42.8 us
    all_gather x1, waiting for transfers between devices, on_device(): lax.all_gather(weight_top.astype(jnp.bfloat16), 'dp', axis=0, tiled=True)  25.9 us
    psum x1, blocking collectives, columns_sum(): return lax.psum(term.astype(jnp.bfloat16), 'mp').astype(jnp.float32)  19.7 us
    all_gather x1, blocking collectives, on_device(): lax.all_gather(weight_in.astype(jnp.bfloat16), 'dp', axis=1, tiled=True)  9.31 us
  transfers between devices with their start and end apart: 10, of which 8 were waited for; matrix products, arithmetic and copies ran while one was open for 8% of the time, Pallas kernels for 0%

commit v1 on v0

v1 whole, which is shorter than its diff:
```python
import math

import jax
import jax.numpy as jnp
from jax import lax
from jax.sharding import PartitionSpec as P

momentum_decay = 0.9
learn_rate = 0.05
bf16 = jnp.bfloat16
f32 = jnp.float32


def swap(value, axis, step):
    count = lax.axis_size(axis)
    return lax.ppermute(value, axis, [(at, at ^ step) for at in range(count)])


def gelu_act(value):
    return 0.5 * value * (1.0 + jax.scipy.special.erf(value / math.sqrt(2.0)))


def gelu_slope(value):
    return 0.5 * (1.0 + jax.scipy.special.erf(value / math.sqrt(2.0))) + value * jnp.exp(
        -0.5 * value * value
    ) / math.sqrt(2.0 * math.pi)


def dot(left, right, contract):
    return lax.dot_general(left, right, (contract, ((), ())), preferred_element_type=f32)


def fit(value, lanes):
    return jnp.pad(value, ((0, 0), (0, lanes - value.shape[1])))


def on_device(
    samples,
    targets,
    counts,
    weight_in,
    weight_mid,
    weight_top,
    weight_out,
    moment_in,
    moment_mid,
    moment_top,
    moment_out,
):
    slots, n_in, block = samples.shape
    n_out = targets.shape[1]
    n_dp, n_mp = lax.axis_size("dp"), lax.axis_size("mp")
    dp_at, mp_at = lax.axis_index("dp"), lax.axis_index("mp")
    half = n_dp // 2
    per = slots // n_mp
    rows = per * block // 2
    wide = weight_in.shape[1]
    lanes = max(rows, 2 * wide)
    high = dp_at >= half
    planes = range(n_mp)

    n_small = n_in + 1
    piece = jnp.concatenate(
        [
            jnp.pad(weight_in.astype(bf16), ((0, n_small - n_in), (0, 0))),
            jnp.pad(weight_out.astype(bf16).T, ((0, n_small - n_out), (0, 0))),
        ],
        1,
    )
    pieces = [piece] + [swap(piece, "mp", k) for k in planes[1:]]
    mid = weight_mid.astype(bf16)
    top = weight_top.astype(bf16)
    second = [mid] + [swap(mid, "mp", k) for k in planes[1:]]

    own = []
    for j in range(per):
        at = per * mp_at + j
        slot = jnp.where(high, slots - 1 - at, at)
        keep = slot < counts[0]
        x = lax.dynamic_index_in_dim(samples, slot, 0, False)
        y = lax.dynamic_index_in_dim(targets, slot, 0, False)
        number = jnp.broadcast_to(counts[0].astype(bf16), (1, block))
        lit = jnp.broadcast_to(keep.astype(bf16), (1, block))
        x = jnp.where(keep, x, jnp.zeros_like(x))
        y = jnp.where(keep, y, jnp.zeros_like(y))
        own.append(jnp.concatenate([x, number, y, lit], 0))
    mine = jnp.concatenate(own, 1)
    n_rows = mine.shape[0]
    mine = mine.reshape(n_rows, 2, rows)
    mine = jnp.concatenate([mine[:, 0], mine[:, 1]], 0)
    n_piece = n_mp * n_small
    sent = jnp.concatenate([fit(mine, lanes)] + [fit(p, lanes) for p in pieces], 0)
    got = swap(sent, "dp", half)
    pair = sent[: 2 * n_rows, :rows] + got[: 2 * n_rows, :rows]
    first_half, second_half = pair[:n_rows], pair[n_rows:]
    at_home = jnp.where(high, second_half, first_half)
    away = jnp.where(high, first_half, second_half)
    wanted = at_home[n_small : n_small + n_out]
    live = at_home[n_small + n_out :].astype(f32)

    def both(bit, held, other):
        return [jnp.where(bit, other, held), jnp.where(bit, held, other)]

    held_x = {0: at_home[:n_small], half: away[:n_small]}
    held_p = both(high, sent[2 * n_rows :, : 2 * wide], got[2 * n_rows :, : 2 * wide])
    step = 1
    while step < half:
        keys = list(held_x)
        sent = jnp.concatenate(
            [fit(held_x[k], lanes) for k in keys] + [fit(p, lanes) for p in held_p], 0
        )
        got = swap(sent, "dp", step)
        got_x = got[: len(keys) * n_small, :rows]
        for i, k in enumerate(keys):
            held_x[k | step] = got_x[i * n_small : (i + 1) * n_small]
        got_p = got[len(keys) * n_small :, : 2 * wide]
        bit = (dp_at & step) != 0
        others = [got_p[i * n_piece : (i + 1) * n_piece] for i in range(len(held_p))]
        pairs = [both(bit, a, b) for a, b in zip(held_p, others)]
        held_p = [p[0] for p in pairs] + [p[1] for p in pairs]
        step *= 2
    order = []
    for at in range(n_dp):
        low = at & (half - 1)
        order.append(low * 2 + (at >= half))
    first, fourth = [], []
    for k in planes:
        cut = [held_p[o][k * n_small : (k + 1) * n_small] for o in order]
        first.append(jnp.concatenate([c[:n_in, :wide] for c in cut], 1))
        fourth.append(jnp.concatenate([c[:n_out, wide:] for c in cut], 1))
    fourth = jnp.concatenate(fourth, 1)

    blocks = [k for k in range(n_dp) if k % 2 == 0] + [k for k in range(n_dp) if k % 2 == 1]
    inputs = jnp.concatenate([held_x[k][:n_in] for k in blocks], 1)
    pair_counts = jnp.concatenate([held_x[k][n_in:, :1] for k in range(half)], 0)
    total = jnp.sum(pair_counts.astype(f32)) * block

    pre_one = [dot(inputs, b, ((0,), (0,))) for b in first]
    act_one = [gelu_act(a).astype(bf16) for a in pre_one]
    pre_two = sum(dot(a, b, ((1,), (0,))) for a, b in zip(act_one, second))
    act_two = gelu_act(pre_two).astype(bf16)
    third = [top] + [swap(top, "mp", k) for k in planes[1:]]
    third = jnp.concatenate(third, 1)

    kept = half * rows
    away_sum = dot(act_two[kept:], third, ((1,), (0,))).astype(bf16)
    home_sum = dot(act_two[:kept], third, ((1,), (0,)))
    core_sum = home_sum + swap(away_sum, "dp", 1).astype(f32)
    pre_three = core_sum[:rows]
    core_sum = core_sum.astype(bf16)
    for i in range(1, half):
        pre_three = pre_three + swap(core_sum[i * rows : (i + 1) * rows], "dp", 2 * i).astype(f32)
    act_three = gelu_act(pre_three).astype(bf16)
    predicted = dot(fourth, act_three, ((1,), (1,)))
    grad_pred = (2.0 / total * (predicted - wanted.astype(f32)) * live).astype(bf16)
    grad_four = dot(grad_pred, act_three, ((1,), (0,)))
    delta_three = (dot(grad_pred, fourth, ((0,), (0,))) * gelu_slope(pre_three)).astype(bf16)
    deltas = [delta_three] + [swap(delta_three, "dp", 2 * i) for i in range(1, half)]
    deltas = jnp.concatenate(deltas, 0)
    deltas = jnp.concatenate([deltas, swap(deltas, "dp", 1)], 0)

    n_top = top.shape[1]
    sum_two = dot(deltas, third, ((1,), (1,)))
    delta_two = (sum_two * gelu_slope(pre_two)).astype(bf16)
    grad_three = dot(act_two, deltas, ((0,), (0,)))
    sum_three = grad_three[:, :n_top]
    for k in planes[1:]:
        sent = grad_three[:, k * n_top : (k + 1) * n_top].astype(bf16)
        sum_three = sum_three + swap(sent, "mp", k).astype(f32)
    sum_mid = None
    small = None
    for k in planes:
        grad_two = dot(act_one[k], delta_two, ((0,), (0,)))
        delta_one = (dot(delta_two, second[k], ((1,), (1,))) * gelu_slope(pre_one[k])).astype(bf16)
        grad_one = dot(inputs, delta_one, ((1,), (0,)))
        both_small = jnp.concatenate([grad_one, grad_four[:, k * n_top : (k + 1) * n_top]], 0)
        if k == 0:
            sum_mid, small = grad_two, both_small
        else:
            sum_mid = sum_mid + swap(grad_two.astype(bf16), "mp", k).astype(f32)
            small = small + swap(both_small.astype(bf16), "mp", k).astype(f32)
    small = small.astype(bf16).reshape(n_in + n_out, n_dp, wide).transpose(1, 0, 2)
    small = jnp.sum(lax.all_to_all(small, "dp", 0, 0, tiled=True).astype(f32), 0)

    mom_in = momentum_decay * moment_in + small[:n_in]
    mom_mid = momentum_decay * moment_mid + sum_mid
    mom_top = momentum_decay * moment_top + sum_three
    mom_out = momentum_decay * moment_out + small[n_in:].T
    return (
        weight_in - learn_rate * mom_in,
        weight_mid - learn_rate * mom_mid,
        weight_top - learn_rate * mom_top,
        weight_out - learn_rate * mom_out,
        mom_in,
        mom_mid,
        mom_top,
        mom_out,
    )


def solution(mesh):
    in_specs = (
        P("dp", None, None),
        P("dp", None, None),
        P("dp"),
        P(None, ("mp", "dp")),
        P("mp", "dp"),
        P("dp", "mp"),
        P(("mp", "dp"), None),
        P(None, ("mp", "dp")),
        P("mp", "dp"),
        P("dp", "mp"),
        P(("mp", "dp"), None),
    )
    out_specs = (
        P(None, ("mp", "dp")),
        P("mp", "dp"),
        P("dp", "mp"),
        P(("mp", "dp"), None),
        P(None, ("mp", "dp")),
        P("mp", "dp"),
        P("dp", "mp"),
        P(("mp", "dp"), None),
    )
    return jax.shard_map(
        on_device, mesh=mesh, in_specs=in_specs, out_specs=out_specs, check_vma=False
    )
```

time: 448 us -> 234 us (0.52)
  waiting for transfers between devices: 325 us -> 92.2 us
  blocking collectives: 44.7 us -> 0 us
  starting transfers between devices: 4.47 us -> 38 us
  local copies, waits for them, and re-layouts: 10.4 us -> 34.4 us
  matrix products: 27.8 us -> 49.6 us
  between operations: 17.1 us -> 2.79 us
    psum x2 -> x0, waiting for transfers between devices: 155 us -> none  [columns_sum(): return lax.psum(term.astype(jnp.bfloat16), 'mp').astype(jnp.float32)]
    ppermute x2 -> x29, waiting for transfers between devices: 0.01 us -> 89.9 us  [swap(): return lax.ppermute(value, axis, [(at, at ^ step) for at in range(count)])]
    reduce_scatter x2 -> x0, waiting for transfers between devices: 85.9 us -> none  [the longest x1 43.1 us: on_device(): lax.psum_scatter(grad_three.astype(jnp.bfloat16), 'dp', scatter_dimension...]
    unnamed x10 -> x0, waiting for transfers between devices: 51.8 us -> none
    all_gather x2 -> x0, waiting for transfers between devices: 31.9 us -> none  [the longest x1 25.9 us: on_device(): lax.all_gather(weight_top.astype(jnp.bfloat16), 'dp', axis=0, tiled=True)]
    ppermute x2 -> x29, starting transfers between devices: 4.14 us -> 34.6 us  [swap(): return lax.ppermute(value, axis, [(at, at ^ step) for at in range(count)])]
    dot_general x10 -> x23, matrix products: 27.8 us -> 49.6 us  [dot(): lax.dot_general(left, right, (contract, ((), ())), preferred_element_type...]
    psum x1 -> x0, blocking collectives: 19.7 us -> none  [columns_sum(): return lax.psum(term.astype(jnp.bfloat16), 'mp').astype(jnp.float32)]
  transfers between devices with their start and end apart: 10 -> 30, of which waited for: 8 -> 15; matrix products, arithmetic and copies ran while one was open for 8% -> 26% of each run, Pallas kernels for 0% -> 0%
where the time goes in v1:
time: 234 us; the launch traced here: 232 us
  waiting for transfers between devices  92.2 us (39%)
  matrix products  49.6 us (21%)
  starting transfers between devices  38 us (16%)
  local copies, waits for them, and re-layouts  34.4 us (15%)
  other arithmetic  15.5 us (7%)
  between operations  2.79 us (1%)
    ppermute x29, waiting for transfers between devices, swap(): return lax.ppermute(value, axis, [(at, at ^ step) for at in range(count)])  89.9 us
    dot_general x23, matrix products, dot(): lax.dot_general(left, right, (contract, ((), ())), preferred_element_type...  49.6 us
    ppermute x29, starting transfers between devices, swap(): return lax.ppermute(value, axis, [(at, at ^ step) for at in range(count)])  34.6 us
    unnamed x127, local copies, waits for them, and re-layouts  10.6 us
    slice x8, local copies, waits for them, and re-layouts, on_device(): fourth.append(jnp.concatenate([c[:n_out, wide:] for c in cut], 1))  7.15 us
  transfers between devices with their start and end apart: 30, of which 15 were waited for; matrix products, arithmetic and copies ran while one was open for 26% of the time, Pallas kernels for 0%

profile of v1, /device:TPU:0, one launch (start us, length us, event | category | flops | bytes accessed | tf_op | source)
XLA Modules:
  0.0 232.5 jit_solution(8157433089419018235)
XLA Ops:
  2.4 3.0 %collective-permute-start = (bf16[56,128]{1,0:T(8,128)(2,1)S(1)}, bf16[56,128]{1,0:T(8,128)(2,1)S(1)}, u32[]{:S(2)}, u32[]{:S(2)}) collective-permute-start(bf16[56,128]{1,0:T(8,128)(2,1)S(1)} %pad_maximum_fusion.7), channel_id=1, source_target_pairs={{0,1},{1,0},{2,3},{3,2},{4,5},{5,4},{6,7},{7,6},{8,9},{9,8},{10,11... | collective-permute-start | bytes 43016 | tf_op jit(solution)/shard_map/ppermute | solution.py:16
  5.4 2.6 %collective-permute-start.1 = (bf16[56,128]{1,0:T(8,128)(2,1)S(1)}, bf16[56,128]{1,0:T(8,128)(2,1)S(1)}, u32[]{:S(2)}, u32[]{:S(2)}) collective-permute-start(bf16[56,128]{1,0:T(8,128)(2,1)S(1)} %pad_maximum_fusion.7), channel_id=1, source_target_pairs={{0,2},{1,3},{2,0},{3,1},{4,6},{5,7},{6,4},{7,5},{8,10},{9,11},{10,... | collective-permute-start | bytes 43016 | tf_op jit(solution)/shard_map/ppermute | solution.py:16
  11.0 2.4 %collective-permute-done.2 = bf16[56,128]{1,0:T(8,128)(2,1)S(1)} collective-permute-done((bf16[56,128]{1,0:T(8,128)(2,1)S(1)}, bf16[56,128]{1,0:T(8,128)(2,1)S(1)}, u32[]{:S(2)}, u32[]{:S(2)}) %collective-permute-start.2) | collective-permute-done | bytes 14368 | tf_op jit(solution)/shard_map/ppermute | solution.py:16
  15.9 3.3 %collective-permute-done.3 = bf16[444,128]{1,0:T(8,128)(2,1)S(1)} collective-permute-done((bf16[444,128]{1,0:T(8,128)(2,1)S(1)}, bf16[444,128]{1,0:T(8,128)(2,1)S(1)}, u32[]{:S(2)}, u32[]{:S(2)}) %collective-permute-start.3) | collective-permute-done | bytes 113696 | tf_op jit(solution)/shard_map/ppermute | solution.py:16
  24.0 3.0 %collective-permute-start.7 = (bf16[512,256]{1,0:T(8,128)(2,1)S(1)}, bf16[512,256]{1,0:T(8,128)(2,1)}, u32[]{:S(2)}, u32[]{:S(2)}) collective-permute-start(bf16[512,256]{1,0:T(8,128)(2,1)S(1)} %convert_element_type.153), channel_id=1, source_target_pairs={{0,2},{1,3},{2,0},{3,1},{4,6},{5,7},{6,4},{7,5},{8,10},{9,11},{10,... | collective-permute-start | bytes 786440 | tf_op jit(solution)/shard_map/ppermute | solution.py:16
  31.6 2.3 multiply_convert_fusion
  38.4 3.0 %collective-permute-done.6 = bf16[512,256]{1,0:T(8,128)(2,1)} collective-permute-done((bf16[512,256]{1,0:T(8,128)(2,1)S(1)}, bf16[512,256]{1,0:T(8,128)(2,1)}, u32[]{:S(2)}, u32[]{:S(2)}) %collective-permute-start.6) | collective-permute-done | bytes 262176 | tf_op jit(solution)/shard_map/ppermute | solution.py:16
  46.1 12.1 %collective-permute-done.7 = bf16[512,256]{1,0:T(8,128)(2,1)} collective-permute-done((bf16[512,256]{1,0:T(8,128)(2,1)S(1)}, bf16[512,256]{1,0:T(8,128)(2,1)}, u32[]{:S(2)}, u32[]{:S(2)}) %collective-permute-start.7) | collective-permute-done | bytes 262176 | tf_op jit(solution)/shard_map/ppermute | solution.py:16
  58.1 2.4 %multiply_convert_fusion.5 = (bf16[1024,256]{1,0:T(8,128)(2,1)S(1)}, f32[1024,256]{1,0:T(8,128)}) fusion(f32[1024,256]{1,0:T(8,128)S(1)} %fusion.114, f32[1024,256]{1,0:T(8,128)S(1)} %convolution_add_fusion.1, bf16[1024,512]{1,0:T(8,128)(2,1)S(1)} %get-tuple-element.141, bf16[512,256]{1,0:T(8,128)(2,1)} %collective-permute-done.7), kind=kOutput, calls=%fused_computation.84 | convolution fusion | flops 270270464 | bytes 4980736 | tf_op jit(solution)/shard_map/dot_general | solution.py:30
  60.5 7.7 %collective-permute-done.10 = bf16[256,512]{1,0:T(8,128)(2,1)} collective-permute-done((bf16[256,512]{1,0:T(8,128)(2,1)S(1)}, bf16[256,512]{1,0:T(8,128)(2,1)}, u32[]{:S(2)}, u32[]{:S(2)}) %collective-permute-start.10) | collective-permute-done | bytes 262176 | tf_op jit(solution)/shard_map/ppermute | solution.py:16
  75.7 3.8 %fusion.110 = (bf16[512,2048]{1,0:T(8,128)(2,1)S(1)}, f32[512,2048]{1,0:T(8,128)}) fusion(bf16[512,2048]{1,0:T(8,128)(2,1)S(1)} %collective-permute-done.12, bf16[256,512]{1,0:T(8,128)(2,1)} %collective-permute-done.11, bf16[256,512]{1,0:T(8,128)(2,1)} %collective-permute-done.10, bf16[256,512]{1,0:T(8,128)(2,1)S(1)} %collective-permute-done.9, ...), kind=kOutput, calls=%fused_computation.206 | convolution fusion | flops 544210944 | bytes 9699328 | tf_op jit(solution)/shard_map/dot_general | solution.py:30
  85.5 3.2 %convert_reduce_fusion.1 = f32[]{:T(128)} fusion(bf16[1,1]{1,0:T(2,128)(2,1)} %get-tuple-element.47, bf16[1,1]{1,0:T(2,128)(2,1)} %get-tuple-element.46, bf16[1,1]{1,0:T(2,128)(2,1)} %slice.594, bf16[1,1]{1,0:T(2,128)(2,1)} %slice.593), kind=kLoop, calls=%fused_computation.164 | loop fusion | flops 35 | bytes 12 | tf_op jit(solution)/shard_map/reduce_sum | solution.py:136
  94.2 2.4 %collective-permute-done.15 = bf16[128,2048]{1,0:T(8,128)(2,1)S(1)} collective-permute-done((bf16[128,2048]{1,0:T(8,128)(2,1)}, bf16[128,2048]{1,0:T(8,128)(2,1)S(1)}, u32[]{:S(2)}, u32[]{:S(2)}) %collective-permute-start.15) | collective-permute-done | bytes 524320 | tf_op jit(solution)/shard_map/ppermute | solution.py:16
  96.6 10.9 %collective-permute-done.14 = bf16[128,2048]{1,0:T(8,128)(2,1)} collective-permute-done((bf16[128,2048]{1,0:T(8,128)(2,1)}, bf16[128,2048]{1,0:T(8,128)(2,1)}, u32[]{:S(2)}, u32[]{:S(2)}) %collective-permute-start.14) | collective-permute-done | bytes 524320 | tf_op jit(solution)/shard_map/ppermute | solution.py:16
  110.1 3.1 %constant_dynamic-update-slice_fusion.19 = (bf16[1024,2048]{1,0:T(8,128)(2,1)}, bf16[128,2048]{1,0:T(8,128)(2,1)S(1)}) fusion(bf16[128,2048]{1,0:T(8,128)(2,1)S(1)} %copy-done.26, bf16[128,2048]{1,0:T(8,128)(2,1)} %collective-permute-done.14, bf16[128,2048]{1,0:T(8,128)(2,1)} %collective-permute-done.13, f32[512,2048]{1,0:T(8,128)} %get-tuple-element.146, ...), kind=kOutput, calls=%fused_computation.144 | convolution fusion | flops 31981568 | bytes 3900672 | tf_op jit(solution)/shard_map/dot_general | solution.py:30
  116.7 11.3 %collective-permute-done.16 = bf16[128,2048]{1,0:T(8,128)(2,1)S(1)} collective-permute-done((bf16[128,2048]{1,0:T(8,128)(2,1)S(1)}, bf16[128,2048]{1,0:T(8,128)(2,1)S(1)}, u32[]{:S(2)}, u32[]{:S(2)}) %collective-permute-start.16) | collective-permute-done | bytes 524320 | tf_op jit(solution)/shard_map/ppermute | solution.py:16
  128.0 10.5 %collective-permute-done.17 = bf16[128,2048]{1,0:T(8,128)(2,1)S(1)} collective-permute-done((bf16[128,2048]{1,0:T(8,128)(2,1)S(1)}, bf16[128,2048]{1,0:T(8,128)(2,1)S(1)}, u32[]{:S(2)}, u32[]{:S(2)}) %collective-permute-start.17) | collective-permute-done | bytes 524320 | tf_op jit(solution)/shard_map/ppermute | solution.py:16
  150.2 3.4 %constant_dynamic-update-slice_fusion.15 = bf16[1024,2048]{1,0:T(8,128)(2,1)} fusion(bf16[1024,2048]{1,0:T(8,128)(2,1)} %constant_dynamic-update-slice_fusion.16, bf16[512,2048]{1,0:T(8,128)(2,1)} %collective-permute-done.19), kind=kLoop, calls=%fused_computation.140 | loop fusion | bytes 4194304 | tf_op jit(solution)/shard_map/concatenate | solution.py:160
  153.6 3.8 %fusion.26 = bf16[1024,256]{1,0:T(8,128)(2,1)S(1)} fusion(bf16[1024,2048]{1,0:T(8,128)(2,1)} %constant_dynamic-update-slice_fusion.15, f32[1024,256]{1,0:T(8,128)S(1)} %copy-done.17, bf16[256,512]{1,0:T(8,128)(2,1)} %collective-permute-done.11, bf16[256,512]{1,0:T(8,128)(2,1)} %collective-permute-done.10, bf16[256,512]{1,0:T(8,128)(2,1)S(1)} %copy-done.44, ...), kind=kOutput, calls=%fused_computation.47 | convolution fusion | flops 1080557568 | bytes 6815744 | tf_op jit(solution)/shard_map/dot_general | solution.py:30
  160.0 3.0 %fusion.112 = (bf16[256,2048]{1,0:T(8,128)(2,1)}, f32[256,2048]{1,0:T(8,128)}) fusion(bf16[1024,256]{1,0:T(8,128)(2,1)S(1)} %get-tuple-element.143, bf16[1024,2048]{1,0:T(8,128)(2,1)S(1)} %copy-done.4), kind=kOutput, calls=%fused_computation.208 | convolution fusion | flops 1074266112 | bytes 7864320 | tf_op jit(solution)/shard_map/dot_general | solution.py:30
  163.0 3.6 %fusion.30 = f32[55,512]{1,0:T(8,128)} fusion(bf16[55,1024]{1,0:T(8,128)(2,1)S(1)} %constant_dynamic-update-slice_fusion.7, f32[1024,512]{1,0:T(8,128)} %get-tuple-element.138, bf16[1024,256]{1,0:T(8,128)(2,1)} %copy-done.22, bf16[512,256]{1,0:T(8,128)(2,1)S(1)} %convert_element_type.153), kind=kOutput, calls=%fused_computation.51 | convolution fusion | flops 331350016 | bytes 3108864 | tf_op jit(solution)/shard_map/dot_general | solution.py:30
  169.5 2.3 collective-permute-start.22
  171.8 3.0 %fusion.32 = bf16[55,512]{1,0:T(8,128)(2,1)S(1)} fusion(bf16[55,1024]{1,0:T(8,128)(2,1)S(1)} %constant_dynamic-update-slice_fusion.7, f32[1024,512]{1,0:T(8,128)} %get-tuple-element.142, bf16[1024,256]{1,0:T(8,128)(2,1)} %copy-done.22, bf16[512,256]{1,0:T(8,128)(2,1)} %collective-permute-done.7), kind=kOutput, calls=%fused_computation.56 | convolution fusion | flops 331378176 | bytes 3052544 | tf_op jit(solution)/shard_map/dot_general | solution.py:30
  175.5 2.9 %fusion.31 = bf16[55,512]{1,0:T(8,128)(2,1)S(1)} fusion(bf16[55,1024]{1,0:T(8,128)(2,1)S(1)} %constant_dynamic-update-slice_fusion.7, f32[1024,512]{1,0:T(8,128)} %get-tuple-element.140, bf16[1024,256]{1,0:T(8,128)(2,1)S(1)} %copy-done.23, bf16[512,256]{1,0:T(8,128)(2,1)} %collective-permute-done.6), kind=kOutput, calls=%fused_computation.55 | convolution fusion | flops 331378176 | bytes 3052544 | tf_op jit(solution)/shard_map/dot_general | solution.py:30
  182.9 2.3 collective-permute-start.25
  189.1 3.4 %all-to-all-start = ((bf16[8,108,64]{1,2,0:T(8,128)(2,1)}), bf16[8,108,64]{1,2,0:T(8,128)(2,1)S(1)}, u32[]{:S(2)}, u32[]{:S(2)}) async-start(bf16[8,108,64]{1,2,0:T(8,128)(2,1)} %bitcast.10), calls=%async_computation | async-start | bytes 262144 | tf_op jit(solution)/shard_map/all_to_all | solution.py:183
  193.4 2.3 collective-permute-start.28
  195.7 2.3 all-to-all-done
  204.0 16.1 %collective-permute-done.24 = bf16[512,256]{1,0:T(8,128)(2,1)} collective-permute-done((bf16[512,256]{1,0:T(8,128)(2,1)}, bf16[512,256]{1,0:T(8,128)(2,1)}, u32[]{:S(2)}, u32[]{:S(2)}) %collective-permute-start.24) | collective-permute-done | bytes 262176 | tf_op jit(solution)/shard_map/ppermute | solution.py:16
  220.1 2.7 %multiply_subtract_fusion.1 = (f32[512,256]{1,0:T(8,128)}, f32[512,256]{1,0:T(8,128)}) fusion(f32[512,256]{1,0:T(8,128)S(1)} %copy-done.7, bf16[512,256]{1,0:T(8,128)(2,1)S(1)} %collective-permute-done.25, bf16[512,256]{1,0:T(8,128)(2,1)} %collective-permute-done.24, bf16[512,256]{1,0:T(8,128)(2,1)} %collective-permute-done.23, ...), kind=kOutput, calls=%fused_computation.95 | convolution fusion | flops 269746176 | bytes 4456448 | tf_op jit(solution)/shard_map/dot_general | solution.py:30
  222.8 7.4 %collective-permute-done.27 = bf16[256,512]{1,0:T(8,128)(2,1)S(1)} collective-permute-done((bf16[256,512]{1,0:T(8,128)(2,1)}, bf16[256,512]{1,0:T(8,128)(2,1)S(1)}, u32[]{:S(2)}, u32[]{:S(2)}) %collective-permute-start.27) | collective-permute-done | bytes 262176 | tf_op jit(solution)/shard_map/ppermute | solution.py:16
  230.2 2.3 multiply_subtract_fusion
  (250 shorter events, 82.1 us)
Async XLA Ops:
  2.4 8.7 %collective-permute-start = (bf16[56,128]{1,0:T(8,128)(2,1)S(1)}, bf16[56,128]{1,0:T(8,128)(2,1)S(1)}, u32[]{:S(2)}, u32[]{:S(2)}) collective-permute-start(bf16[56,128]{1,0:T(8,128)(2,1)S(1)} %pad_maximum_fusion.7), channel_id=1, source_target_pairs={{0,1},{1,0},{2,3},{3,2},{4,5},{5,4},{6,7},{7,6},{8,9},{9,8},{10,11... | collective-permute-start | bytes 43016 | tf_op jit(solution)/shard_map/ppermute | solution.py:16
  5.4 5.7 %collective-permute-start.1 = (bf16[56,128]{1,0:T(8,128)(2,1)S(1)}, bf16[56,128]{1,0:T(8,128)(2,1)S(1)}, u32[]{:S(2)}, u32[]{:S(2)}) collective-permute-start(bf16[56,128]{1,0:T(8,128)(2,1)S(1)} %pad_maximum_fusion.7), channel_id=1, source_target_pairs={{0,2},{1,3},{2,0},{3,1},{4,6},{5,7},{6,4},{7,5},{8,10},{9,11},{10,... | collective-permute-start | bytes 43016 | tf_op jit(solution)/shard_map/ppermute | solution.py:16
  8.0 5.5 %collective-permute-start.2 = (bf16[56,128]{1,0:T(8,128)(2,1)S(1)}, bf16[56,128]{1,0:T(8,128)(2,1)S(1)}, u32[]{:S(2)}, u32[]{:S(2)}) collective-permute-start(bf16[56,128]{1,0:T(8,128)(2,1)S(1)} %pad_maximum_fusion.7), channel_id=1, source_target_pairs={{0,3},{1,2},{2,1},{3,0},{4,7},{5,6},{6,5},{7,4},{8,11},{9,10},{10,... | collective-permute-start | bytes 43016 | tf_op jit(solution)/shard_map/ppermute | solution.py:16
  14.3 4.9 %collective-permute-start.3 = (bf16[444,128]{1,0:T(8,128)(2,1)S(1)}, bf16[444,128]{1,0:T(8,128)(2,1)S(1)}, u32[]{:S(2)}, u32[]{:S(2)}) collective-permute-start(bf16[444,128]{1,0:T(8,128)(2,1)S(1)} %concatenate.88), channel_id=1, source_target_pairs={{0,16},{4,20},{8,24},{12,28},{16,0},{20,4},{24,8},{28,12},{1,17},{... | collective-permute-start | bytes 341000 | tf_op jit(solution)/shard_map/ppermute | solution.py:16
  19.4 1.4 collective-permute-start.4
  21.0 8.9 %collective-permute-start.5 = (bf16[1120,128]{1,0:T(8,128)(2,1)S(1)}, bf16[1120,128]{1,0:T(8,128)(2,1)S(1)}, u32[]{:S(2)}, u32[]{:S(2)}) collective-permute-start(bf16[1120,128]{1,0:T(8,128)(2,1)S(1)} %get-tuple-element.24), channel_id=1, source_target_pairs={{0,8},{4,12},{8,0},{12,4},{16,24},{20,28},{24,16},{28,20},{1,9},{5... | collective-permute-start | bytes 860168 | tf_op jit(solution)/shard_map/ppermute | solution.py:16
  22.6 22.1 %collective-permute-start.8 = (bf16[512,256]{1,0:T(8,128)(2,1)S(1)}, bf16[512,256]{1,0:T(8,128)(2,1)}, u32[]{:S(2)}, u32[]{:S(2)}) collective-permute-start(bf16[512,256]{1,0:T(8,128)(2,1)S(1)} %convert_element_type.153), channel_id=1, source_target_pairs={{0,3},{1,2},{2,1},{3,0},{4,7},{5,6},{6,5},{7,4},{8,11},{9,10},{10,... | collective-permute-start | bytes 786440 | tf_op jit(solution)/shard_map/ppermute | solution.py:16
  24.0 17.4 %collective-permute-start.6 = (bf16[512,256]{1,0:T(8,128)(2,1)S(1)}, bf16[512,256]{1,0:T(8,128)(2,1)}, u32[]{:S(2)}, u32[]{:S(2)}) collective-permute-start(bf16[512,256]{1,0:T(8,128)(2,1)S(1)} %convert_element_type.153), channel_id=1, source_target_pairs={{0,1},{1,0},{2,3},{3,2},{4,5},{5,4},{6,7},{7,6},{8,9},{9,8},{10,11... | collective-permute-start | bytes 786440 | tf_op jit(solution)/shard_map/ppermute | solution.py:16
  24.0 34.1 %collective-permute-start.7 = (bf16[512,256]{1,0:T(8,128)(2,1)S(1)}, bf16[512,256]{1,0:T(8,128)(2,1)}, u32[]{:S(2)}, u32[]{:S(2)}) collective-permute-start(bf16[512,256]{1,0:T(8,128)(2,1)S(1)} %convert_element_type.153), channel_id=1, source_target_pairs={{0,2},{1,3},{2,0},{3,1},{4,6},{5,7},{6,4},{7,5},{8,10},{9,11},{10,... | collective-permute-start | bytes 786440 | tf_op jit(solution)/shard_map/ppermute | solution.py:16
  27.1 48.7 %copy-start.18 = (bf16[256,512]{1,0:T(8,128)(2,1)}, bf16[256,512]{1,0:T(8,128)(2,1)S(1)}, u32[]{:S(2)}) copy-start(bf16[256,512]{1,0:T(8,128)(2,1)S(1)} %convert_element_type.158) | copy-start | bytes 786436
  27.1 33.5 %collective-permute-start.11 = (bf16[256,512]{1,0:T(8,128)(2,1)S(1)}, bf16[256,512]{1,0:T(8,128)(2,1)}, u32[]{:S(2)}, u32[]{:S(2)}) collective-permute-start(bf16[256,512]{1,0:T(8,128)(2,1)S(1)} %convert_element_type.158), channel_id=1, source_target_pairs={{0,3},{1,2},{2,1},{3,0},{4,7},{5,6},{6,5},{7,4},{8,11},{9,10},{10,... | collective-permute-start | bytes 786440 | tf_op jit(solution)/shard_map/ppermute | solution.py:16
  29.9 38.3 %collective-permute-start.10 = (bf16[256,512]{1,0:T(8,128)(2,1)S(1)}, bf16[256,512]{1,0:T(8,128)(2,1)}, u32[]{:S(2)}, u32[]{:S(2)}) collective-permute-start(bf16[256,512]{1,0:T(8,128)(2,1)S(1)} %convert_element_type.158), channel_id=1, source_target_pairs={{0,2},{1,3},{2,0},{3,1},{4,6},{5,7},{6,4},{7,5},{8,10},{9,11},{10,... | collective-permute-start | bytes 786440 | tf_op jit(solution)/shard_map/ppermute | solution.py:16
  41.4 26.9 %collective-permute-start.9 = (bf16[256,512]{1,0:T(8,128)(2,1)S(1)}, bf16[256,512]{1,0:T(8,128)(2,1)S(1)}, u32[]{:S(2)}, u32[]{:S(2)}) collective-permute-start(bf16[256,512]{1,0:T(8,128)(2,1)S(1)} %convert_element_type.158), channel_id=1, source_target_pairs={{0,1},{1,0},{2,3},{3,2},{4,5},{5,4},{6,7},{7,6},{8,9},{9,8},{10,11... | collective-permute-start | bytes 786440 | tf_op jit(solution)/shard_map/ppermute | solution.py:16
  70.2 5.5 %collective-permute-start.12 = (bf16[512,2048]{1,0:T(8,128)(2,1)S(1)}, bf16[512,2048]{1,0:T(8,128)(2,1)S(1)}, u32[]{:S(2)}, u32[]{:S(2)}) collective-permute-start(bf16[512,2048]{1,0:T(8,128)(2,1)S(1)} %convolution_convert_fusion), channel_id=1, source_target_pairs={{0,4},{4,0},{8,12},{12,8},{16,20},{20,16},{24,28},{28,24},{1,5},{5... | collective-permute-start | bytes 6291464 | tf_op jit(solution)/shard_map/ppermute | solution.py:16
  80.7 15.9 %collective-permute-start.15 = (bf16[128,2048]{1,0:T(8,128)(2,1)}, bf16[128,2048]{1,0:T(8,128)(2,1)S(1)}, u32[]{:S(2)}, u32[]{:S(2)}) collective-permute-start(bf16[128,2048]{1,0:T(8,128)(2,1)} %get-tuple-element.33), channel_id=1, source_target_pairs={{0,24},{4,28},{8,16},{12,20},{16,8},{20,12},{24,0},{28,4},{1,25},{... | collective-permute-start | bytes 1572872 | tf_op jit(solution)/shard_map/ppermute | solution.py:16
  82.2 25.3 %collective-permute-start.14 = (bf16[128,2048]{1,0:T(8,128)(2,1)}, bf16[128,2048]{1,0:T(8,128)(2,1)}, u32[]{:S(2)}, u32[]{:S(2)}) collective-permute-start(bf16[128,2048]{1,0:T(8,128)(2,1)} %get-tuple-element.34), channel_id=1, source_target_pairs={{0,16},{4,20},{8,24},{12,28},{16,0},{20,4},{24,8},{28,12},{1,17},{... | collective-permute-start | bytes 1572872 | tf_op jit(solution)/shard_map/ppermute | solution.py:16
  82.7 24.9 %collective-permute-start.13 = (bf16[128,2048]{1,0:T(8,128)(2,1)}, bf16[128,2048]{1,0:T(8,128)(2,1)}, u32[]{:S(2)}, u32[]{:S(2)}) collective-permute-start(bf16[128,2048]{1,0:T(8,128)(2,1)} %get-tuple-element.32), channel_id=1, source_target_pairs={{0,8},{4,12},{8,0},{12,4},{16,24},{20,28},{24,16},{28,20},{1,9},{5... | collective-permute-start | bytes 1572872 | tf_op jit(solution)/shard_map/ppermute | solution.py:16
  113.2 14.8 %collective-permute-start.16 = (bf16[128,2048]{1,0:T(8,128)(2,1)S(1)}, bf16[128,2048]{1,0:T(8,128)(2,1)S(1)}, u32[]{:S(2)}, u32[]{:S(2)}) collective-permute-start(bf16[128,2048]{1,0:T(8,128)(2,1)S(1)} %get-tuple-element.148), channel_id=1, source_target_pairs={{0,8},{4,12},{8,0},{12,4},{16,24},{20,28},{24,16},{28,20},{1,9},{5... | collective-permute-start | bytes 1572872 | tf_op jit(solution)/shard_map/ppermute | solution.py:16
  113.8 24.7 %collective-permute-start.17 = (bf16[128,2048]{1,0:T(8,128)(2,1)S(1)}, bf16[128,2048]{1,0:T(8,128)(2,1)S(1)}, u32[]{:S(2)}, u32[]{:S(2)}) collective-permute-start(bf16[128,2048]{1,0:T(8,128)(2,1)S(1)} %get-tuple-element.148), channel_id=1, source_target_pairs={{0,16},{4,20},{8,24},{12,28},{16,0},{20,4},{24,8},{28,12},{1,17},{... | collective-permute-start | bytes 1572872 | tf_op jit(solution)/shard_map/ppermute | solution.py:16
  115.2 23.3 %collective-permute-start.18 = (bf16[128,2048]{1,0:T(8,128)(2,1)S(1)}, bf16[128,2048]{1,0:T(8,128)(2,1)S(1)}, u32[]{:S(2)}, u32[]{:S(2)}) collective-permute-start(bf16[128,2048]{1,0:T(8,128)(2,1)S(1)} %get-tuple-element.148), channel_id=1, source_target_pairs={{0,24},{4,28},{8,16},{12,20},{16,8},{20,12},{24,0},{28,4},{1,25},{... | collective-permute-start | bytes 1572872 | tf_op jit(solution)/shard_map/ppermute | solution.py:16
  140.2 10.0 %collective-permute-start.19 = (bf16[512,2048]{1,0:T(8,128)(2,1)}, bf16[512,2048]{1,0:T(8,128)(2,1)}, u32[]{:S(2)}, u32[]{:S(2)}) collective-permute-start(bf16[512,2048]{1,0:T(8,128)(2,1)} %pad_maximum_fusion), channel_id=1, source_target_pairs={{0,4},{4,0},{8,12},{12,8},{16,20},{20,16},{24,28},{28,24},{1,5},{5... | collective-permute-start | bytes 6291464 | tf_op jit(solution)/shard_map/ppermute | solution.py:16
  169.5 15.6 %collective-permute-start.22 = (bf16[108,512]{1,0:T(8,128)(2,1)}, bf16[108,512]{1,0:T(8,128)(2,1)}, u32[]{:S(2)}, u32[]{:S(2)}) collective-permute-start(bf16[108,512]{1,0:T(8,128)(2,1)} %pad_maximum_fusion.5), channel_id=1, source_target_pairs={{0,3},{1,2},{2,1},{3,0},{4,7},{5,6},{6,5},{7,4},{8,11},{9,10},{10,... | collective-permute-start | bytes 331784 | tf_op jit(solution)/shard_map/ppermute | solution.py:16
  175.5 11.7 %collective-permute-start.21 = (bf16[108,512]{1,0:T(8,128)(2,1)}, bf16[108,512]{1,0:T(8,128)(2,1)}, u32[]{:S(2)}, u32[]{:S(2)}) collective-permute-start(bf16[108,512]{1,0:T(8,128)(2,1)} %pad_maximum_fusion.4), channel_id=1, source_target_pairs={{0,2},{1,3},{2,0},{3,1},{4,6},{5,7},{6,4},{7,5},{8,10},{9,11},{10,... | collective-permute-start | bytes 331784 | tf_op jit(solution)/shard_map/ppermute | solution.py:16
  178.5 8.8 %collective-permute-start.20 = (bf16[108,512]{1,0:T(8,128)(2,1)S(1)}, bf16[108,512]{1,0:T(8,128)(2,1)S(1)}, u32[]{:S(2)}, u32[]{:S(2)}) collective-permute-start(bf16[108,512]{1,0:T(8,128)(2,1)S(1)} %pad_maximum_fusion.3), channel_id=1, source_target_pairs={{0,1},{1,0},{2,3},{3,2},{4,5},{5,4},{6,7},{7,6},{8,9},{9,8},{10,11... | collective-permute-start | bytes 331784 | tf_op jit(solution)/shard_map/ppermute | solution.py:16
  182.9 37.2 %copy-start.21 = (f32[512,256]{1,0:T(8,128)S(1)}, f32[512,256]{1,0:T(8,128)}, u32[]{:S(2)}) copy-start(f32[512,256]{1,0:T(8,128)} %param.19) | copy-start | bytes 1572868
  182.9 19.5 %collective-permute-start.25 = (bf16[512,256]{1,0:T(8,128)(2,1)}, bf16[512,256]{1,0:T(8,128)(2,1)S(1)}, u32[]{:S(2)}, u32[]{:S(2)}) collective-permute-start(bf16[512,256]{1,0:T(8,128)(2,1)} %convolution_convert_fusion.1), channel_id=1, source_target_pairs={{0,3},{1,2},{2,1},{3,0},{4,7},{5,6},{6,5},{7,4},{8,11},{9,10},{10,... | collective-permute-start | bytes 786440 | tf_op jit(solution)/shard_map/ppermute | solution.py:16
  185.2 34.9 %collective-permute-start.24 = (bf16[512,256]{1,0:T(8,128)(2,1)}, bf16[512,256]{1,0:T(8,128)(2,1)}, u32[]{:S(2)}, u32[]{:S(2)}) collective-permute-start(bf16[512,256]{1,0:T(8,128)(2,1)} %convolution_convert_fusion.2), channel_id=1, source_target_pairs={{0,2},{1,3},{2,0},{3,1},{4,6},{5,7},{6,4},{7,5},{8,10},{9,11},{10,... | collective-permute-start | bytes 786440 | tf_op jit(solution)/shard_map/ppermute | solution.py:16
  185.2 34.9 %collective-permute-start.23 = (bf16[512,256]{1,0:T(8,128)(2,1)}, bf16[512,256]{1,0:T(8,128)(2,1)}, u32[]{:S(2)}, u32[]{:S(2)}) collective-permute-start(bf16[512,256]{1,0:T(8,128)(2,1)} %convolution_convert_fusion.3), channel_id=1, source_target_pairs={{0,1},{1,0},{2,3},{3,2},{4,5},{5,4},{6,7},{7,6},{8,9},{9,8},{10,11... | collective-permute-start | bytes 786440 | tf_op jit(solution)/shard_map/ppermute | solution.py:16
  189.1 8.8 %all-to-all-start = ((bf16[8,108,64]{1,2,0:T(8,128)(2,1)}), bf16[8,108,64]{1,2,0:T(8,128)(2,1)S(1)}, u32[]{:S(2)}, u32[]{:S(2)}) async-start(bf16[8,108,64]{1,2,0:T(8,128)(2,1)} %bitcast.10), calls=%async_computation | async-start | bytes 262144 | tf_op jit(solution)/shard_map/all_to_all | solution.py:183
  193.4 29.4 %collective-permute-start.28 = (bf16[256,512]{1,0:T(8,128)(2,1)}, bf16[256,512]{1,0:T(8,128)(2,1)S(1)}, u32[]{:S(2)}, u32[]{:S(2)}) collective-permute-start(bf16[256,512]{1,0:T(8,128)(2,1)} %get-tuple-element.36), channel_id=1, source_target_pairs={{0,3},{1,2},{2,1},{3,0},{4,7},{5,6},{6,5},{7,4},{8,11},{9,10},{10,... | collective-permute-start | bytes 786440 | tf_op jit(solution)/shard_map/ppermute | solution.py:16
  195.7 34.5 %collective-permute-start.27 = (bf16[256,512]{1,0:T(8,128)(2,1)}, bf16[256,512]{1,0:T(8,128)(2,1)S(1)}, u32[]{:S(2)}, u32[]{:S(2)}) collective-permute-start(bf16[256,512]{1,0:T(8,128)(2,1)} %get-tuple-element.37), channel_id=1, source_target_pairs={{0,2},{1,3},{2,0},{3,1},{4,6},{5,7},{6,4},{7,5},{8,10},{9,11},{10,... | collective-permute-start | bytes 786440 | tf_op jit(solution)/shard_map/ppermute | solution.py:16
  202.4 27.8 %collective-permute-start.26 = (bf16[256,512]{1,0:T(8,128)(2,1)}, bf16[256,512]{1,0:T(8,128)(2,1)S(1)}, u32[]{:S(2)}, u32[]{:S(2)}) collective-permute-start(bf16[256,512]{1,0:T(8,128)(2,1)} %get-tuple-element.35), channel_id=1, source_target_pairs={{0,1},{1,0},{2,3},{3,2},{4,5},{5,4},{6,7},{7,6},{8,9},{9,8},{10,11... | collective-permute-start | bytes 786440 | tf_op jit(solution)/shard_map/ppermute | solution.py:16
  (51 other events, 378.2 us)

commit v2 on v0

v2 whole, which is shorter than its diff:
```python
import functools
import math

import jax
import jax.numpy as jnp
from jax import lax
from jax.experimental import pallas as pl
from jax.experimental.pallas import tpu as pltpu
from jax.sharding import PartitionSpec as P

momentum_decay = 0.9
learn_rate = 0.05
bf16 = jnp.bfloat16
f32 = jnp.float32
VMEM_BYTES = 24 << 20


def swap(value, axis, step):
    count = lax.axis_size(axis)
    return lax.ppermute(value, axis, [(at, at ^ step) for at in range(count)])


def parent(k):
    return k & (k - 1)


def low_bit(k):
    return k & -k


def up_to(value, unit):
    return -(-value // unit) * unit


def gelu_act(value):
    return 0.5 * value * (1.0 + lax.erf(value * math.sqrt(0.5)))


def gelu_slope(value):
    return 0.5 * (1.0 + lax.erf(value * math.sqrt(0.5))) + value * jnp.exp(
        -0.5 * value * value
    ) * (1.0 / math.sqrt(2.0 * math.pi))


def dot(left, right, at_left, at_right):
    dims = (((at_left,), (at_right,)), ((), ()))
    return lax.dot_general(left, right, dims, preferred_element_type=f32)


def shaped(dims, kind):
    return jax.ShapeDtypeStruct(dims, kind)


def on_core(body, outs, args, name, flops=0, scratch=(), scalars=()):
    at = pl.BlockSpec(memory_space=pltpu.VMEM)
    return pl.pallas_call(
        body,
        out_shape=outs,
        in_specs=[pl.BlockSpec(memory_space=pltpu.SMEM)] * len(scalars) + [at] * len(args),
        out_specs=jax.tree.map(lambda _: at, outs),
        scratch_shapes=list(scratch),
        compiler_params=pltpu.CompilerParams(vmem_limit_bytes=VMEM_BYTES),
        cost_estimate=pl.CostEstimate(flops=flops, bytes_accessed=0, transcendentals=0),
        name=name,
    )(*scalars, *args)


def pack_small(w_in, w_out, out, *, tall):
    n_in, wide = w_in.shape
    n_out = w_out.shape[0]
    left = jnp.concatenate([w_in[...], jnp.zeros((tall - n_in, wide), f32)], 0)
    right = jnp.concatenate([w_out[...], jnp.zeros((tall - n_out, wide), f32)], 0)
    parts = [left, right]
    spare = out.shape[1] - 2 * wide
    if spare:
        parts.append(jnp.zeros((tall, spare), f32))
    out[...] = jnp.concatenate(parts, 1).astype(bf16)


def pack_rows(count, samples, targets, *refs, tall, rows, per):
    pieces, out = refs[:-1], refs[-1]
    slots, n_in, block = samples.shape
    n_out = targets.shape[1]
    half = lax.axis_size("dp") // 2
    high = lax.axis_index("dp") >= half
    mine = []
    for j in range(per):
        at = per * lax.axis_index("mp") + j
        slot = jnp.where(high, slots - 1 - at, at)
        keep = slot < count[0]
        x = samples[slot].astype(f32)
        y = targets[slot].astype(f32)
        x = jnp.where(keep, x, jnp.zeros_like(x))
        y = jnp.where(keep, y, jnp.zeros_like(y))
        number = jnp.full((1, block), count[0].astype(f32))
        lit = jnp.where(keep, jnp.ones((1, block), f32), jnp.zeros((1, block), f32))
        parts = [x, number]
        if tall > n_in + 1:
            parts.append(jnp.zeros((tall - n_in - 1, block), f32))
        parts += [y, lit]
        if tall > n_out + 1:
            parts.append(jnp.zeros((tall - n_out - 1, block), f32))
        mine.append(jnp.concatenate(parts, 0).astype(bf16))
    if per > 1:
        mine = jnp.concatenate(mine, 1)
    else:
        mine = mine[0]
    spare = out.shape[1] - rows
    for t in range(2):
        half_rows = mine[:, t * rows : (t + 1) * rows]
        if spare:
            half_rows = jnp.concatenate([half_rows, jnp.zeros((2 * tall, spare), bf16)], 1)
        out[2 * tall * t : 2 * tall * (t + 1)] = half_rows
    for i, piece in enumerate(pieces):
        out[4 * tall + i * tall : 4 * tall + (i + 1) * tall] = piece[...]


def in_order(bit, own, got, out, base):
    span = own.shape[0]
    out[base : base + span] = jnp.where(bit, got, own)
    out[base + span : base + 2 * span] = jnp.where(bit, own, got)


def first_step(own, got, out, wanted, *, tall):
    half = lax.axis_size("dp") // 2
    high = lax.axis_index("dp") >= half
    front = own[: 2 * tall] + got[: 2 * tall]
    back = own[2 * tall : 4 * tall] + got[2 * tall : 4 * tall]
    home = jnp.where(high, back, front)
    away = jnp.where(high, front, back)
    out[:tall] = home[:tall]
    out[tall : 2 * tall] = away[:tall]
    wanted[...] = home[tall:, : wanted.shape[1]]
    in_order(high, own[4 * tall :], got[4 * tall :], out, 2 * tall)


def next_step(own, got, out, *, step, span):
    bit = (lax.axis_index("dp") & step) != 0
    out[:span] = own[:span]
    out[span : 2 * span] = got[:span]
    in_order(bit, own[span:], got[span:], out, 2 * span)


def place_small(own, got, inputs, first, fourth, *, step, span, tall, rows, wide, order):
    n_dp, n_mp = lax.axis_size("dp"), lax.axis_size("mp")
    bit = (lax.axis_index("dp") & step) != 0
    count = span // tall
    for place, at in enumerate(order):
        source = own if at < count else got
        row = (at % count) * tall
        inputs[:, place * rows : (place + 1) * rows] = source[row : row + tall, :rows]
    own_p, got_p = own[span:], got[span:]
    low_p = jnp.where(bit, got_p, own_p).reshape(-1, tall, own.shape[1])
    high_p = jnp.where(bit, own_p, got_p).reshape(-1, tall, own.shape[1])
    half = n_dp // 2
    n_low = half // 2 * 2
    for k in range(n_mp):
        ones, fours = [], []
        for at in range(n_dp):
            low = at & (half - 1)
            where = low * 2 + (at >= half)
            if where < n_low:
                piece = low_p[where * n_mp + k]
            else:
                piece = high_p[(where - n_low) * n_mp + k]
            ones.append(piece[:, :wide])
            fours.append(piece[:, wide : 2 * wide])
        hidden = n_dp * wide
        first[:, k * hidden : (k + 1) * hidden] = jnp.concatenate(ones, 1)
        fourth[:, k * hidden : (k + 1) * hidden] = jnp.concatenate(fours, 1)


def one_forward(inputs, first, out, *, tile):
    n_rows = inputs.shape[1]
    cut = min(256, n_rows)

    def step(i, _):
        at = pl.ds(pl.multiple_of(i * tile, tile), tile)
        weights = first[:, at].T
        for c in range(0, n_rows, cut):
            pre = dot(weights, inputs[:, c : c + cut], 1, 0)
            out[at, c : c + cut] = gelu_act(pre).astype(bf16)
        return 0

    lax.fori_loop(0, first.shape[1] // tile, step, 0)


def one_slope(inputs, first, out, *, tile):
    n_rows = inputs.shape[1]
    cut = min(256, n_rows)

    def step(i, _):
        at = pl.ds(pl.multiple_of(i * tile, tile), tile)
        weights = first[:, at].T
        for c in range(0, n_rows, cut):
            pre = dot(weights, inputs[:, c : c + cut], 1, 0)
            out[at, c : c + cut] = gelu_slope(pre).astype(bf16)
        return 0

    lax.fori_loop(0, first.shape[1] // tile, step, 0)


def two_forward(act_one, *refs):
    seconds, (act, act_t, slope) = refs[:-3], refs[-3:]
    n_rows = act_one.shape[1]
    cut = min(256, n_rows)
    span = seconds[0].shape[0]
    turned = [s[...].T for s in seconds]
    for c in range(0, n_rows, cut):
        at = slice(c, c + cut)
        pre = dot(turned[0], act_one[:span, at], 1, 0)
        for k in range(1, len(seconds)):
            pre = pre + dot(turned[k], act_one[k * span : (k + 1) * span, at], 1, 0)
        value = gelu_act(pre)
        act_t[:, at] = value.astype(bf16)
        act[at] = value.T.astype(bf16)
        slope[:, at] = gelu_slope(pre)


def three_away(act, *refs, kept):
    thirds, out = refs[:-1], refs[-1]
    span = thirds[0].shape[1]
    for k, third in enumerate(thirds):
        out[:, k * span : (k + 1) * span] = dot(act[kept:], third[...], 1, 0).astype(bf16)


def three_home(act, got, *refs, kept, rows):
    half = kept // rows
    thirds, own, sends = refs[:-half], refs[-half], refs[len(refs) - half + 1 :]
    span = thirds[0].shape[1]
    for k, third in enumerate(thirds):
        at = slice(k * span, (k + 1) * span)
        total = dot(act[:kept], third[...], 1, 0) + got[:, at].astype(f32)
        own[:, at] = total[:rows]
        for i, send in enumerate(sends):
            send[:, at] = total[(i + 1) * rows : (i + 2) * rows].astype(bf16)


def error_step(inputs, wanted, fourth, *refs, groups, half, per, n_in, n_out):
    terms = refs[: groups * half]
    act, pre = refs[-2:]
    deltas, grad_four = refs[groups * half : groups * half + groups], refs[-3]
    width = pre.shape[1] // groups
    for g in range(groups):
        at = slice(g * width, (g + 1) * width)
        own, others = terms[g * half], terms[g * half + 1 : (g + 1) * half]
        total = own[...]
        for other in others:
            total = total + other[...].astype(f32)
        pre[:, at] = total
        act[:, at] = gelu_act(total).astype(bf16)
    predicted = dot(fourth[...], act[...], 1, 1)
    number = jnp.sum(inputs[n_in : n_in + 1, :].astype(f32), axis=1, keepdims=True) / per
    live = wanted[n_out : n_out + 1, :].astype(f32)
    error = (2.0 / number * (predicted - wanted[...].astype(f32)) * live).astype(bf16)
    row = lax.broadcasted_iota(jnp.int32, error.shape, 0)
    error = jnp.where(row < n_out, error, jnp.zeros_like(error))
    grad_four[...] = dot(error, act[...], 1, 0)
    turned = error.astype(f32).T.astype(bf16)
    for g in range(groups):
        at = slice(g * width, (g + 1) * width)
        delta = dot(turned, fourth[:, at], 1, 0) * gelu_slope(pre[:, at])
        deltas[g][...] = delta.astype(bf16)


def three_back(act_t, *refs, n_blocks, ks, carried):
    blocks = refs[:n_blocks]
    thirds = refs[n_blocks : n_blocks + len(ks)]
    refs = refs[n_blocks + len(ks) :]
    before = refs[0] if carried else None
    refs = refs[carried:]
    sum_two, grads, whole = refs[0], refs[1 : 1 + len(ks)], refs[-1]
    rows = blocks[0].shape[0]
    span = thirds[0].shape[1]
    for i, block in enumerate(blocks):
        whole[i * rows : (i + 1) * rows] = block[...]
    for i in range(len(ks)):
        at = slice(i * span, (i + 1) * span)
        grads[i][...] = dot(act_t[...], whole[:, at], 1, 0).astype(grads[i].dtype)
    total = before[...] if carried else None
    for i, third in enumerate(thirds):
        term = dot(third[...], whole[:, i * span : (i + 1) * span], 1, 1)
        total = term if total is None else total + term
    sum_two[...] = total


def two_back(sum_two, slope, act_one, delta, *grads):
    value = (sum_two[...] * slope[...]).astype(bf16)
    delta[...] = value
    span = act_one.shape[0] // len(grads)
    for k, grad in enumerate(grads):
        grad[...] = dot(act_one[k * span : (k + 1) * span], value, 1, 1).astype(grad.dtype)


def one_back(inputs, delta, slope, grad_four, *refs, n_mp):
    seconds, outs = refs[:n_mp], refs[n_mp:]
    tall = inputs.shape[0]
    span = seconds[0].shape[0]
    for k in range(n_mp):
        value = dot(seconds[k][...], delta[...], 1, 0)
        value = (value * slope[k * span : (k + 1) * span].astype(f32)).astype(bf16)
        outs[k][:tall] = dot(inputs[...], value, 1, 1).astype(outs[k].dtype)
        outs[k][tall:] = grad_four[:, k * span : (k + 1) * span].astype(outs[k].dtype)


def add_up(own, got, out):
    out[...] = (own[...].astype(f32) + got[...].astype(f32)).astype(out.dtype)


def spread_small(own, *refs):
    gots, out = refs[:-1], refs[-1]
    total = own[...].astype(f32)
    for got in gots:
        total = total + got[...].astype(f32)
    wide = out.shape[2]
    for d in range(out.shape[0]):
        out[d] = total[:, d * wide : (d + 1) * wide].astype(bf16)


def update_small(got, w_in, w_out, m_in, m_out, nw_in, nw_out, nm_in, nm_out):
    tall = got.shape[1] // 2
    total = jnp.sum(got[...].astype(f32), axis=0)
    n_in, n_out = w_in.shape[0], w_out.shape[0]
    mom = momentum_decay * m_in[...] + total[:n_in]
    nm_in[...] = mom
    nw_in[...] = w_in[...] - learn_rate * mom
    mom = momentum_decay * m_out[...] + total[tall : tall + n_out]
    nm_out[...] = mom
    nw_out[...] = w_out[...] - learn_rate * mom


def update_big(weight, moment, own, *refs):
    gots, (new_weight, new_moment) = refs[:-2], refs[-2:]
    total = own[...]
    for got in gots:
        total = total + got[...].astype(f32)
    mom = momentum_decay * moment[...] + total
    new_moment[...] = mom
    new_weight[...] = weight[...] - learn_rate * mom


def gathered(own, n_mp):
    held = {0: own}
    tops = [k for k in range(1, n_mp) if parent(k) == 0][::-1]
    rest = [k for k in range(1, n_mp) if parent(k) != 0]
    for k in tops + sorted(rest, key=lambda k: -low_bit(k)):
        held[k] = swap(held[parent(k)], "mp", low_bit(k))
    return held


def summed(held, n_mp, shape):
    gots = []
    for k in sorted(range(1, n_mp), key=lambda k: (low_bit(k), -k)):
        got = swap(held[k], "mp", low_bit(k))
        to = parent(k)
        if to:
            held[to] = on_core(add_up, shaped(shape, bf16), [held[to], got], "add_up")
        else:
            gots.append(got)
    return gots


def on_device(
    samples,
    targets,
    counts,
    weight_in,
    weight_mid,
    weight_top,
    weight_out,
    moment_in,
    moment_mid,
    moment_top,
    moment_out,
):
    slots, n_in, block = samples.shape
    n_out = targets.shape[1]
    n_dp, n_mp = lax.axis_size("dp"), lax.axis_size("mp")
    half = n_dp // 2
    per = slots // n_mp
    rows = per * block // 2
    n_rows = n_dp * rows
    wide = weight_in.shape[1]
    lanes = max(rows, 2 * wide)
    tall = up_to(max(n_in, n_out) + 1, 16)
    hidden = wide * n_dp
    width = hidden * n_mp
    n_mid, n_top = weight_mid.shape[1], weight_top.shape[1]
    planes = range(n_mp)
    part = functools.partial

    second = gathered(weight_mid.astype(bf16), n_mp)
    piece = on_core(
        part(pack_small, tall=tall), shaped((tall, lanes), bf16), [weight_in, weight_out.T], "pack_small"
    )
    pieces = [piece] + [swap(piece, "mp", k) for k in planes[1:]]
    third = gathered(weight_top.astype(bf16), n_mp)

    own = on_core(
        part(pack_rows, tall=tall, rows=rows, per=per),
        shaped(((4 + n_mp) * tall, lanes), bf16),
        [samples, targets, *pieces],
        "pack_rows",
        scalars=[counts],
    )
    got = swap(own, "dp", half)
    n_piece = n_mp * tall
    own, wanted = on_core(
        part(first_step, tall=tall),
        [shaped((2 * tall + 2 * n_piece, lanes), bf16), shaped((tall, rows), bf16)],
        [own, got],
        "first_step",
    )
    span, keys, step = 2 * tall, [0, half], 1
    while step * 2 < half:
        got = swap(own, "dp", step)
        own = on_core(
            part(next_step, step=step, span=span),
            shaped((2 * own.shape[0], lanes), bf16),
            [own, got],
            "next_step",
        )
        keys = keys + [k | step for k in keys]
        span, step = 2 * span, 2 * step
    got = swap(own, "dp", step)
    keys = keys + [k | step for k in keys]
    order = [keys.index(k) for k in list(range(0, n_dp, 2)) + list(range(1, n_dp, 2))]
    inputs, first, fourth = on_core(
        part(place_small, step=step, span=span, tall=tall, rows=rows, wide=wide, order=order),
        [shaped((tall, n_rows), bf16), shaped((tall, width), bf16), shaped((tall, width), bf16)],
        [own, got],
        "place_small",
    )

    act_one = on_core(
        part(one_forward, tile=128), shaped((width, n_rows), bf16), [inputs, first], "one_forward"
    )
    act_two, act_two_t, slope_two = on_core(
        two_forward,
        [shaped((n_rows, n_mid), bf16), shaped((n_mid, n_rows), bf16), shaped((n_mid, n_rows), f32)],
        [act_one] + [second[k] for k in planes],
        "two_forward",
    )
    groups = [list(planes[: n_mp // 2]), list(planes[n_mp // 2 :])]
    kept = half * rows
    terms = []
    for ks in groups:
        cols = len(ks) * n_top
        weights = [third[k] for k in ks]
        away = on_core(
            part(three_away, kept=kept), shaped((kept, cols), bf16), [act_two, *weights], "three_away"
        )
        own, *sends = on_core(
            part(three_home, kept=kept, rows=rows),
            [shaped((rows, cols), f32)] + [shaped((rows, cols), bf16)] * (half - 1),
            [act_two, swap(away, "dp", 1), *weights],
            "three_home",
        )
        terms += [own] + [swap(send, "dp", 2 * (i + 1)) for i, send in enumerate(sends)]
    slope_one = on_core(
        part(one_slope, tile=128), shaped((width, n_rows), bf16), [inputs, first], "one_slope",
        flops=12_000_000_000,
    )
    *deltas, grad_four = on_core(
        part(error_step, groups=len(groups), half=half, per=per, n_in=n_in, n_out=n_out),
        [shaped((rows, len(ks) * n_top), bf16) for ks in groups] + [shaped((tall, width), f32)],
        [inputs, wanted, fourth, *terms],
        "error_step",
        scratch=[pltpu.VMEM((rows, width), bf16), pltpu.VMEM((rows, width), f32)],
    )

    sum_two = None
    grad_three = {}
    gots_three = None
    for g in reversed(range(len(groups))):
        ks = groups[g]
        home = [deltas[g]] + [swap(deltas[g], "dp", 2 * i) for i in range(1, half)]
        away = [swap(value, "dp", 1) for value in home]
        carried = sum_two is not None
        sum_two, *grads = on_core(
            part(three_back, n_blocks=n_dp, ks=ks, carried=carried),
            [shaped((n_mid, n_rows), f32)]
            + [shaped((n_mid, n_top), bf16 if k else f32) for k in ks],
            [act_two_t, *home, *away] + [third[k] for k in ks] + ([sum_two] if carried else []),
            "three_back",
            scratch=[pltpu.VMEM((n_rows, len(ks) * n_top), bf16)],
        )
        grad_three.update(zip(ks, grads))
    gots_three = summed(grad_three, n_mp, (n_mid, n_top))
    grad_two = {}
    delta_two, *grads = on_core(
        two_back,
        [shaped((n_mid, n_rows), bf16)] + [shaped((hidden, n_mid), bf16 if k else f32) for k in planes],
        [sum_two, slope_two, act_one],
        "two_back",
    )
    grad_two = dict(zip(planes, grads))
    gots_two = summed(grad_two, n_mp, (hidden, n_mid))
    small = on_core(
        part(one_back, n_mp=n_mp),
        [shaped((2 * tall, hidden), bf16 if k else f32) for k in planes],
        [inputs, delta_two, slope_one, grad_four] + [second[k] for k in planes],
        "one_back",
    )
    small = on_core(
        spread_small,
        shaped((n_dp, 2 * tall, wide), bf16),
        [small[0]] + [swap(small[k], "mp", k) for k in planes[1:]],
        "spread_small",
    )
    small = lax.all_to_all(small, "dp", 0, 0, tiled=True)

    like = lambda value: shaped(value.shape, f32)
    flat = (weight_in, weight_out.T, moment_in, moment_out.T)
    new_in, new_out, mom_in, mom_out = on_core(
        update_small, [like(value) for value in flat], [small, *flat], "update_small"
    )
    new_top, mom_top = on_core(
        update_big, [like(weight_top)] * 2, [weight_top, moment_top, grad_three[0], *gots_three], "update_top"
    )
    new_mid, mom_mid = on_core(
        update_big, [like(weight_mid)] * 2, [weight_mid, moment_mid, grad_two[0], *gots_two], "update_mid"
    )
    return (new_in, new_mid, new_top, new_out.T, mom_in, mom_mid, mom_top, mom_out.T)


def solution(mesh):
    in_specs = (
        P("dp", None, None),
        P("dp", None, None),
        P("dp"),
        P(None, ("mp", "dp")),
        P("mp", "dp"),
        P("dp", "mp"),
        P(("mp", "dp"), None),
        P(None, ("mp", "dp")),
        P("mp", "dp"),
        P("dp", "mp"),
        P(("mp", "dp"), None),
    )
    out_specs = (
        P(None, ("mp", "dp")),
        P("mp", "dp"),
        P("dp", "mp"),
        P(("mp", "dp"), None),
        P(None, ("mp", "dp")),
        P("mp", "dp"),
        P("dp", "mp"),
        P(("mp", "dp"), None),
    )
    return jax.shard_map(
        on_device, mesh=mesh, in_specs=in_specs, out_specs=out_specs, check_vma=False
    )
```

time: 448 us -> 181 us (0.40)
  waiting for transfers between devices: 325 us -> 94.8 us
  blocking collectives: 44.7 us -> 9.51 us
  starting transfers between devices: 4.47 us -> 36 us
  Pallas kernels: 0 us -> 28.9 us
  matrix products: 27.8 us -> 0 us
  other arithmetic: 18.2 us -> 2.14 us
  between operations: 17.1 us -> 1.68 us
  local copies, waits for them, and re-layouts: 10.4 us -> 5.24 us
    psum x2 -> x0, waiting for transfers between devices: 155 us -> none  [columns_sum(): return lax.psum(term.astype(jnp.bfloat16), 'mp').astype(jnp.float32)]
    ppermute x2 -> x43, waiting for transfers between devices: 0.01 us -> 94.8 us  [swap(): return lax.ppermute(value, axis, [(at, at ^ step) for at in range(count)])]
    reduce_scatter x2 -> x0, waiting for transfers between devices: 85.9 us -> none  [the longest x1 43.1 us: on_device(): lax.psum_scatter(grad_three.astype(jnp.bfloat16), 'dp', scatter_dimension...]
    unnamed x10 -> x0, waiting for transfers between devices: 51.8 us -> none
    all_gather x2 -> x0, waiting for transfers between devices: 31.9 us -> none  [the longest x1 25.9 us: on_device(): lax.all_gather(weight_top.astype(jnp.bfloat16), 'dp', axis=0, tiled=True)]
    ppermute x2 -> x43, starting transfers between devices: 4.14 us -> 36 us  [swap(): return lax.ppermute(value, axis, [(at, at ^ step) for at in range(count)])]
    pallas_call x0 -> x23, Pallas kernels: none -> 28.9 us  [on_core(): pl.pallas_call(body, out_shape=outs, in_specs=[pl.BlockSpec(memory_space=...]
    dot_general x10 -> x0, matrix products: 27.8 us -> none  [the longest x1 5.19 us: on_device(): jnp.einsum('brh,hk->brk', act_two, third, preferred_element_type=f32)]
  transfers between devices with their start and end apart: 10 -> 43, of which waited for: 8 -> 18; matrix products, arithmetic and copies ran while one was open for 8% -> 3% of each run, Pallas kernels for 0% -> 14%
where the time goes in v2:
time: 181 us; the launch traced here: 178 us
  waiting for transfers between devices  94.8 us (52%)
  starting transfers between devices  36 us (20%)
  Pallas kernels  28.9 us (16%)
  blocking collectives  9.51 us (5%)
  local copies, waits for them, and re-layouts  5.24 us (3%)
  other arithmetic  2.14 us (1%)
    ppermute x43, waiting for transfers between devices, swap(): return lax.ppermute(value, axis, [(at, at ^ step) for at in range(count)])  94.8 us
    ppermute x43, starting transfers between devices, swap(): return lax.ppermute(value, axis, [(at, at ^ step) for at in range(count)])  36 us
    pallas_call x23, Pallas kernels, on_core(): pl.pallas_call(body, out_shape=outs, in_specs=[pl.BlockSpec(memory_space=...  28.9 us
    all_to_all x1, blocking collectives, on_device(): small = lax.all_to_all(small, 'dp', 0, 0, tiled=True)  9.51 us
  transfers between devices with their start and end apart: 43, of which 18 were waited for; matrix products, arithmetic and copies ran while one was open for 3% of the time, Pallas kernels for 14%

profile of v2, /device:TPU:0, one launch (start us, length us, event | category | flops | bytes accessed | tf_op | source)
XLA Modules:
  0.0 178.2 jit_solution(7027336670746113676)
XLA Ops:
  2.2 3.0 %collective-permute-start = (bf16[64,128]{1,0:T(8,128)(2,1)S(1)}, bf16[64,128]{1,0:T(8,128)(2,1)S(1)}, u32[]{:S(2)}, u32[]{:S(2)}) collective-permute-start(bf16[64,128]{1,0:T(8,128)(2,1)S(1)} %pack_small.1.refs_0_), channel_id=1, source_target_pairs={{0,1},{1,0},{2,3},{3,2},{4,5},{5,4},{6,7},{7,6},{8,9},{9,8},{10,11... | collective-permute-start | bytes 49160 | tf_op jit(solution)/shard_map/ppermute | solution.py:20
  5.2 2.6 %collective-permute-start.1 = (bf16[64,128]{1,0:T(8,128)(2,1)S(1)}, bf16[64,128]{1,0:T(8,128)(2,1)S(1)}, u32[]{:S(2)}, u32[]{:S(2)}) collective-permute-start(bf16[64,128]{1,0:T(8,128)(2,1)S(1)} %pack_small.1.refs_0_), channel_id=1, source_target_pairs={{0,2},{1,3},{2,0},{3,1},{4,6},{5,7},{6,4},{7,5},{8,10},{9,11},{10,... | collective-permute-start | bytes 49160 | tf_op jit(solution)/shard_map/ppermute | solution.py:20
  10.3 3.0 %collective-permute-done.2.refs_3_ = bf16[64,128]{1,0:T(8,128)(2,1)S(1)} collective-permute-done((bf16[64,128]{1,0:T(8,128)(2,1)S(1)}, bf16[64,128]{1,0:T(8,128)(2,1)S(1)}, u32[]{:S(2)}, u32[]{:S(2)}) %collective-permute-start.2) | collective-permute-done | bytes 16416 | tf_op jit(solution)/shard_map/ppermute | solution.py:20
  13.4 1.6 collective-permute-start.3
  17.2 3.0 %collective-permute-start.14 = (bf16[256,512]{1,0:T(8,128)(2,1)S(1)}, bf16[256,512]{1,0:T(8,128)(2,1)S(1)}, u32[]{:S(2)}, u32[]{:S(2)}) collective-permute-start(bf16[256,512]{1,0:T(8,128)(2,1)S(1)} %convert_element_type.7.refs_0_.refs_8_), channel_id=1, source_target_pairs={{0,2},{1,3},{2,0},{3,1},{4,6},{5,7},{6,4},{7,5},{8,10},{9,11},{10,... | collective-permute-start | bytes 786440 | tf_op jit(solution)/shard_map/ppermute | solution.py:20
  23.3 10.2 %collective-permute-done.7.refs_2_ = bf16[512,256]{1,0:T(8,128)(2,1)S(1)} collective-permute-done((bf16[512,256]{1,0:T(8,128)(2,1)S(1)}, bf16[512,256]{1,0:T(8,128)(2,1)S(1)}, u32[]{:S(2)}, u32[]{:S(2)}) %collective-permute-start.7) | collective-permute-done | bytes 262176 | tf_op jit(solution)/shard_map/ppermute | solution.py:20
  33.5 5.5 %collective-permute-done.14.refs_0_.refs_8_ = bf16[256,512]{1,0:T(8,128)(2,1)S(1)} collective-permute-done((bf16[256,512]{1,0:T(8,128)(2,1)S(1)}, bf16[256,512]{1,0:T(8,128)(2,1)S(1)}, u32[]{:S(2)}, u32[]{:S(2)}) %collective-permute-start.14) | collective-permute-done | bytes 262176 | tf_op jit(solution)/shard_map/ppermute | solution.py:20
  39.1 2.0 %collective-permute-start.9 = (bf16[256,512]{1,0:T(8,128)(2,1)S(1)}, bf16[256,512]{1,0:T(8,128)(2,1)S(1)}, u32[]{:S(2)}, u32[]{:S(2)}) collective-permute-start(bf16[256,512]{1,0:T(8,128)(2,1)S(1)} %convert_element_type.7.refs_0_.refs_8_), channel_id=1, source_target_pairs={{0,1},{1,0},{2,3},{3,2},{4,5},{5,4},{6,7},{7,6},{8,9},{9,8},{10,11... | collective-permute-start | bytes 786440 | tf_op jit(solution)/shard_map/ppermute | solution.py:20
  41.3 4.7 %one_forward.1.act_one = bf16[2048,1024]{1,0:T(8,128)(2,1)S(1)} custom-call(bf16[64,1024]{1,0:T(8,128)(2,1)S(1)} %get-tuple-element.51.inputs, bf16[64,2048]{1,0:T(8,128)(2,1)S(1)} %get-tuple-element.52.first), custom_call_target="tpu_custom_call" | custom-call | tf_op jit(solution)/shard_map/one_forward/pallas_call | solution.py:56
  46.0 2.7 %collective-permute-done.8.refs_3_ = bf16[512,256]{1,0:T(8,128)(2,1)S(1)} collective-permute-done((bf16[512,256]{1,0:T(8,128)(2,1)S(1)}, bf16[512,256]{1,0:T(8,128)(2,1)S(1)}, u32[]{:S(2)}, u32[]{:S(2)}) %collective-permute-start.8) | collective-permute-done | bytes 262176 | tf_op jit(solution)/shard_map/ppermute | solution.py:20
  48.7 1.7 two_forward.1
  50.4 3.9 %collective-permute-done.15.refs_1_.refs_9_ = bf16[256,512]{1,0:T(8,128)(2,1)S(1)} collective-permute-done((bf16[256,512]{1,0:T(8,128)(2,1)S(1)}, bf16[256,512]{1,0:T(8,128)(2,1)S(1)}, u32[]{:S(2)}, u32[]{:S(2)}) %collective-permute-start.15) | collective-permute-done | bytes 262176 | tf_op jit(solution)/shard_map/ppermute | solution.py:20
  54.8 4.5 %collective-permute-done.9.refs_1_.refs_9_ = bf16[256,512]{1,0:T(8,128)(2,1)S(1)} collective-permute-done((bf16[256,512]{1,0:T(8,128)(2,1)S(1)}, bf16[256,512]{1,0:T(8,128)(2,1)S(1)}, u32[]{:S(2)}, u32[]{:S(2)}) %collective-permute-start.9) | collective-permute-done | bytes 262176 | tf_op jit(solution)/shard_map/ppermute | solution.py:20
  61.4 2.4 %collective-permute-start.19 = (bf16[128,1024]{1,0:T(8,128)(2,1)S(1)}, bf16[128,1024]{1,0:T(8,128)(2,1)S(1)}, u32[]{:S(2)}, u32[]{:S(2)}) collective-permute-start(bf16[128,1024]{1,0:T(8,128)(2,1)S(1)} %get-tuple-element.64), channel_id=1, source_target_pairs={{0,24},{4,28},{8,16},{12,20},{16,8},{20,12},{24,0},{28,4},{1,25},{... | collective-permute-start | bytes 786440 | tf_op jit(solution)/shard_map/ppermute | solution.py:20
  65.4 4.1 %collective-permute-done.17.refs_5_ = bf16[128,1024]{1,0:T(8,128)(2,1)S(1)} collective-permute-done((bf16[128,1024]{1,0:T(8,128)(2,1)S(1)}, bf16[128,1024]{1,0:T(8,128)(2,1)S(1)}, u32[]{:S(2)}, u32[]{:S(2)}) %collective-permute-start.17) | collective-permute-done | bytes 262176 | tf_op jit(solution)/shard_map/ppermute | solution.py:20
  70.0 5.7 %collective-permute-done.18.refs_6_ = bf16[128,1024]{1,0:T(8,128)(2,1)S(1)} collective-permute-done((bf16[128,1024]{1,0:T(8,128)(2,1)S(1)}, bf16[128,1024]{1,0:T(8,128)(2,1)S(1)}, u32[]{:S(2)}, u32[]{:S(2)}) %collective-permute-start.18) | collective-permute-done | bytes 262176 | tf_op jit(solution)/shard_map/ppermute | solution.py:20
  75.7 5.1 %collective-permute-done.11.refs_1_ = bf16[128,1024]{1,0:T(8,128)(2,1)S(1)} collective-permute-done((bf16[128,1024]{1,0:T(8,128)(2,1)S(1)}, bf16[128,1024]{1,0:T(8,128)(2,1)S(1)}, u32[]{:S(2)}, u32[]{:S(2)}) %collective-permute-start.11) | collective-permute-done | bytes 262176 | tf_op jit(solution)/shard_map/ppermute | solution.py:20
  80.8 5.4 %collective-permute-done.12.refs_2_ = bf16[128,1024]{1,0:T(8,128)(2,1)S(1)} collective-permute-done((bf16[128,1024]{1,0:T(8,128)(2,1)S(1)}, bf16[128,1024]{1,0:T(8,128)(2,1)S(1)}, u32[]{:S(2)}, u32[]{:S(2)}) %collective-permute-start.12) | collective-permute-done | bytes 262176 | tf_op jit(solution)/shard_map/ppermute | solution.py:20
  92.3 4.3 %collective-permute-done.27.refs_1_ = bf16[128,1024]{1,0:T(8,128)(2,1)S(1)} collective-permute-done((bf16[128,1024]{1,0:T(8,128)(2,1)S(1)}, bf16[128,1024]{1,0:T(8,128)(2,1)S(1)}, u32[]{:S(2)}, u32[]{:S(2)}) %collective-permute-start.27) | collective-permute-done | bytes 262176 | tf_op jit(solution)/shard_map/ppermute | solution.py:20
  97.8 4.1 %collective-permute-done.28.refs_2_ = bf16[128,1024]{1,0:T(8,128)(2,1)S(1)} collective-permute-done((bf16[128,1024]{1,0:T(8,128)(2,1)S(1)}, bf16[128,1024]{1,0:T(8,128)(2,1)S(1)}, u32[]{:S(2)}, u32[]{:S(2)}) %collective-permute-start.28) | collective-permute-done | bytes 262176 | tf_op jit(solution)/shard_map/ppermute | solution.py:20
  101.9 1.9 %collective-permute-start.22 = (bf16[128,1024]{1,0:T(8,128)(2,1)S(1)}, bf16[128,1024]{1,0:T(8,128)(2,1)S(1)}, u32[]{:S(2)}, u32[]{:S(2)}) collective-permute-start(bf16[128,1024]{1,0:T(8,128)(2,1)S(1)} %get-tuple-element.65.refs_0_), channel_id=1, source_target_pairs={{0,24},{4,28},{8,16},{12,20},{16,8},{20,12},{24,0},{28,4},{1,25},{... | collective-permute-start | bytes 786440 | tf_op jit(solution)/shard_map/ppermute | solution.py:20
  104.3 3.5 %collective-permute-done.20.refs_1_ = bf16[128,1024]{1,0:T(8,128)(2,1)S(1)} collective-permute-done((bf16[128,1024]{1,0:T(8,128)(2,1)S(1)}, bf16[128,1024]{1,0:T(8,128)(2,1)S(1)}, u32[]{:S(2)}, u32[]{:S(2)}) %collective-permute-start.20) | collective-permute-done | bytes 262176 | tf_op jit(solution)/shard_map/ppermute | solution.py:20
  107.9 5.1 %collective-permute-done.21.refs_2_ = bf16[128,1024]{1,0:T(8,128)(2,1)S(1)} collective-permute-done((bf16[128,1024]{1,0:T(8,128)(2,1)S(1)}, bf16[128,1024]{1,0:T(8,128)(2,1)S(1)}, u32[]{:S(2)}, u32[]{:S(2)}) %collective-permute-start.21) | collective-permute-done | bytes 262176 | tf_op jit(solution)/shard_map/ppermute | solution.py:20
  118.5 1.8 collective-permute-start.38
  120.3 6.3 %one_slope.1.slope = bf16[2048,1024]{1,0:T(8,128)(2,1)S(1)} custom-call(bf16[64,1024]{1,0:T(8,128)(2,1)S(1)} %get-tuple-element.51.inputs, bf16[64,2048]{1,0:T(8,128)(2,1)S(1)} %get-tuple-element.52.first), custom_call_target="tpu_custom_call" | custom-call | flops 12000000000 | tf_op jit(solution)/shard_map/one_slope/pallas_call | solution.py:56
  126.6 2.4 %one_back.1 = (f32[128,512]{1,0:T(8,128)S(1)}, bf16[128,512]{1,0:T(8,128)(2,1)S(1)}, bf16[128,512]{1,0:T(8,128)(2,1)S(1)}, bf16[128,512]{1,0:T(8,128)(2,1)S(1)}) custom-call(bf16[64,1024]{1,0:T(8,128)(2,1)S(1)} %get-tuple-element.51.inputs, bf16[256,1024]{1,0:T(8,128)(2,1)S(1)} %get-tuple-element.70.delta, bf16[2048,1024]{1,0:T(8,128)(2,1)S(1)} %one_slope.1.slope, ...), custom_call_target="tpu_custom_call" | custom-call | tf_op jit(solution)/shard_map/one_back/pallas_call | solution.py:56
  131.9 2.9 %collective-permute-start.42 = (bf16[256,512]{1,0:T(8,128)(2,1)}, bf16[256,512]{1,0:T(8,128)(2,1)}, u32[]{:S(2)}, u32[]{:S(2)}) collective-permute-start(bf16[256,512]{1,0:T(8,128)(2,1)} %add_up.3), channel_id=1, source_target_pairs={{0,2},{1,3},{2,0},{3,1},{4,6},{5,7},{6,4},{7,5},{8,10},{9,11},{10,... | collective-permute-start | bytes 786440 | tf_op jit(solution)/shard_map/ppermute | solution.py:20
  135.9 4.7 %collective-permute-done.34.refs_0_ = bf16[128,512]{1,0:T(8,128)(2,1)S(1)} collective-permute-done((bf16[128,512]{1,0:T(8,128)(2,1)S(1)}, bf16[128,512]{1,0:T(8,128)(2,1)S(1)}, u32[]{:S(2)}, u32[]{:S(2)}) %collective-permute-start.34) | collective-permute-done | bytes 131104 | tf_op jit(solution)/shard_map/ppermute | solution.py:20
  140.6 21.1 %collective-permute-done.36.refs_2_ = bf16[128,512]{1,0:T(8,128)(2,1)S(1)} collective-permute-done((bf16[128,512]{1,0:T(8,128)(2,1)S(1)}, bf16[128,512]{1,0:T(8,128)(2,1)S(1)}, u32[]{:S(2)}, u32[]{:S(2)}) %collective-permute-start.36) | collective-permute-done | bytes 131104 | tf_op jit(solution)/shard_map/ppermute | solution.py:20
  162.7 9.5 %all_to_all.5 = bf16[8,128,64]{1,2,0:T(8,128)(2,1)} all-to-all(bf16[8,128,64]{1,2,0:T(8,128)(2,1)} %copy.23), channel_id=1, replica_groups=mesh['dp'=8,'mp'=4] {'dp'}, dimensions={0} | all-to-all | bytes 262144 | tf_op jit(solution)/shard_map/all_to_all | solution.py:511
  174.0 2.1 %update_top.1 = (f32[256,512]{1,0:T(8,128)}, f32[256,512]{1,0:T(8,128)}) custom-call(f32[256,512]{1,0:T(8,128)S(1)} %copy-done, f32[256,512]{1,0:T(8,128)S(1)} %copy-done.2, f32[256,512]{1,0:T(8,128)S(1)} %get-tuple-element.82.own, bf16[256,512]{1,0:T(8,128)(2,1)} %collective-permute-done.40.refs_0_, bf16[256,512]{1,0:T(8,128)(2,1)} %collective-permute-done.42.refs_1_), custom_call_target="tpu_custom_call" | custom-call | tf_op jit(solution)/shard_map/update_top/pallas_call | solution.py:56
  176.1 2.1 %update_mid.1 = (f32[512,256]{1,0:T(8,128)}, f32[512,256]{1,0:T(8,128)}) custom-call(f32[512,256]{1,0:T(8,128)S(1)} %copy-done.1, f32[512,256]{1,0:T(8,128)S(1)} %copy-done.3, f32[512,256]{1,0:T(8,128)S(1)} %get-tuple-element.77.own, bf16[512,256]{1,0:T(8,128)(2,1)} %collective-permute-done.37.refs_0_, bf16[512,256]{1,0:T(8,128)(2,1)} %collective-permute-done.39.refs_1_), custom_call_target="tpu_custom_call" | custom-call | tf_op jit(solution)/shard_map/update_mid/pallas_call | solution.py:56
  (104 shorter events, 33.6 us)
Async XLA Ops:
  2.2 8.1 %collective-permute-start = (bf16[64,128]{1,0:T(8,128)(2,1)S(1)}, bf16[64,128]{1,0:T(8,128)(2,1)S(1)}, u32[]{:S(2)}, u32[]{:S(2)}) collective-permute-start(bf16[64,128]{1,0:T(8,128)(2,1)S(1)} %pack_small.1.refs_0_), channel_id=1, source_target_pairs={{0,1},{1,0},{2,3},{3,2},{4,5},{5,4},{6,7},{7,6},{8,9},{9,8},{10,11... | collective-permute-start | bytes 49160 | tf_op jit(solution)/shard_map/ppermute | solution.py:20
  16.0 17.5 %collective-permute-start.7 = (bf16[512,256]{1,0:T(8,128)(2,1)S(1)}, bf16[512,256]{1,0:T(8,128)(2,1)S(1)}, u32[]{:S(2)}, u32[]{:S(2)}) collective-permute-start(bf16[512,256]{1,0:T(8,128)(2,1)S(1)} %convert_element_type.6.refs_0_), channel_id=1, source_target_pairs={{0,2},{1,3},{2,0},{3,1},{4,6},{5,7},{6,4},{7,5},{8,10},{9,11},{10,... | collective-permute-start | bytes 786440 | tf_op jit(solution)/shard_map/ppermute | solution.py:20
  17.2 21.9 %collective-permute-start.14 = (bf16[256,512]{1,0:T(8,128)(2,1)S(1)}, bf16[256,512]{1,0:T(8,128)(2,1)S(1)}, u32[]{:S(2)}, u32[]{:S(2)}) collective-permute-start(bf16[256,512]{1,0:T(8,128)(2,1)S(1)} %convert_element_type.7.refs_0_.refs_8_), channel_id=1, source_target_pairs={{0,2},{1,3},{2,0},{3,1},{4,6},{5,7},{6,4},{7,5},{8,10},{9,11},{10,... | collective-permute-start | bytes 786440 | tf_op jit(solution)/shard_map/ppermute | solution.py:20
  21.7 19.4 %collective-permute-start.5 = (bf16[1280,128]{1,0:T(8,128)(2,1)S(1)}, bf16[1280,128]{1,0:T(8,128)(2,1)S(1)}, u32[]{:S(2)}, u32[]{:S(2)}) collective-permute-start(bf16[1280,128]{1,0:T(8,128)(2,1)S(1)} %next_step.1.own), channel_id=1, source_target_pairs={{0,8},{4,12},{8,0},{12,4},{16,24},{20,28},{24,16},{28,20},{1,9},{5... | collective-permute-start | bytes 983048 | tf_op jit(solution)/shard_map/ppermute | solution.py:20
  23.3 22.7 %collective-permute-start.6 = (bf16[512,256]{1,0:T(8,128)(2,1)S(1)}, bf16[512,256]{1,0:T(8,128)(2,1)S(1)}, u32[]{:S(2)}, u32[]{:S(2)}) collective-permute-start(bf16[512,256]{1,0:T(8,128)(2,1)S(1)} %convert_element_type.6.refs_0_), channel_id=1, source_target_pairs={{0,1},{1,0},{2,3},{3,2},{4,5},{5,4},{6,7},{7,6},{8,9},{9,8},{10,11... | collective-permute-start | bytes 786440 | tf_op jit(solution)/shard_map/ppermute | solution.py:20
  33.5 15.2 %collective-permute-start.8 = (bf16[512,256]{1,0:T(8,128)(2,1)S(1)}, bf16[512,256]{1,0:T(8,128)(2,1)S(1)}, u32[]{:S(2)}, u32[]{:S(2)}) collective-permute-start(bf16[512,256]{1,0:T(8,128)(2,1)S(1)} %collective-permute-done.7.refs_2_), channel_id=1, source_target_pairs={{0,1},{1,0},{2,3},{3,2},{4,5},{5,4},{6,7},{7,6},{8,9},{9,8},{10,11... | collective-permute-start | bytes 786440 | tf_op jit(solution)/shard_map/ppermute | solution.py:20
  39.1 15.2 %collective-permute-start.15 = (bf16[256,512]{1,0:T(8,128)(2,1)S(1)}, bf16[256,512]{1,0:T(8,128)(2,1)S(1)}, u32[]{:S(2)}, u32[]{:S(2)}) collective-permute-start(bf16[256,512]{1,0:T(8,128)(2,1)S(1)} %collective-permute-done.14.refs_0_.refs_8_), channel_id=1, source_target_pairs={{0,1},{1,0},{2,3},{3,2},{4,5},{5,4},{6,7},{7,6},{8,9},{9,8},{10,11... | collective-permute-start | bytes 786440 | tf_op jit(solution)/shard_map/ppermute | solution.py:20
  39.1 20.3 %collective-permute-start.9 = (bf16[256,512]{1,0:T(8,128)(2,1)S(1)}, bf16[256,512]{1,0:T(8,128)(2,1)S(1)}, u32[]{:S(2)}, u32[]{:S(2)}) collective-permute-start(bf16[256,512]{1,0:T(8,128)(2,1)S(1)} %convert_element_type.7.refs_0_.refs_8_), channel_id=1, source_target_pairs={{0,1},{1,0},{2,3},{3,2},{4,5},{5,4},{6,7},{7,6},{8,9},{9,8},{10,11... | collective-permute-start | bytes 786440 | tf_op jit(solution)/shard_map/ppermute | solution.py:20
  60.3 9.2 %collective-permute-start.17 = (bf16[128,1024]{1,0:T(8,128)(2,1)S(1)}, bf16[128,1024]{1,0:T(8,128)(2,1)S(1)}, u32[]{:S(2)}, u32[]{:S(2)}) collective-permute-start(bf16[128,1024]{1,0:T(8,128)(2,1)S(1)} %get-tuple-element.62), channel_id=1, source_target_pairs={{0,8},{4,12},{8,0},{12,4},{16,24},{20,28},{24,16},{28,20},{1,9},{5... | collective-permute-start | bytes 786440 | tf_op jit(solution)/shard_map/ppermute | solution.py:20
  60.9 14.8 %collective-permute-start.18 = (bf16[128,1024]{1,0:T(8,128)(2,1)S(1)}, bf16[128,1024]{1,0:T(8,128)(2,1)S(1)}, u32[]{:S(2)}, u32[]{:S(2)}) collective-permute-start(bf16[128,1024]{1,0:T(8,128)(2,1)S(1)} %get-tuple-element.63), channel_id=1, source_target_pairs={{0,16},{4,20},{8,24},{12,28},{16,0},{20,4},{24,8},{28,12},{1,17},{... | collective-permute-start | bytes 786440 | tf_op jit(solution)/shard_map/ppermute | solution.py:20
  61.4 14.3 %collective-permute-start.19 = (bf16[128,1024]{1,0:T(8,128)(2,1)S(1)}, bf16[128,1024]{1,0:T(8,128)(2,1)S(1)}, u32[]{:S(2)}, u32[]{:S(2)}) collective-permute-start(bf16[128,1024]{1,0:T(8,128)(2,1)S(1)} %get-tuple-element.64), channel_id=1, source_target_pairs={{0,24},{4,28},{8,16},{12,20},{16,8},{20,12},{24,0},{28,4},{1,25},{... | collective-permute-start | bytes 786440 | tf_op jit(solution)/shard_map/ppermute | solution.py:20
  64.3 16.4 %collective-permute-start.11 = (bf16[128,1024]{1,0:T(8,128)(2,1)S(1)}, bf16[128,1024]{1,0:T(8,128)(2,1)S(1)}, u32[]{:S(2)}, u32[]{:S(2)}) collective-permute-start(bf16[128,1024]{1,0:T(8,128)(2,1)S(1)} %get-tuple-element.58), channel_id=1, source_target_pairs={{0,8},{4,12},{8,0},{12,4},{16,24},{20,28},{24,16},{28,20},{1,9},{5... | collective-permute-start | bytes 786440 | tf_op jit(solution)/shard_map/ppermute | solution.py:20
  64.9 21.3 %collective-permute-start.12 = (bf16[128,1024]{1,0:T(8,128)(2,1)S(1)}, bf16[128,1024]{1,0:T(8,128)(2,1)S(1)}, u32[]{:S(2)}, u32[]{:S(2)}) collective-permute-start(bf16[128,1024]{1,0:T(8,128)(2,1)S(1)} %get-tuple-element.59), channel_id=1, source_target_pairs={{0,16},{4,20},{8,24},{12,28},{16,0},{20,4},{24,8},{28,12},{1,17},{... | collective-permute-start | bytes 786440 | tf_op jit(solution)/shard_map/ppermute | solution.py:20
  69.5 16.7 %collective-permute-start.13 = (bf16[128,1024]{1,0:T(8,128)(2,1)S(1)}, bf16[128,1024]{1,0:T(8,128)(2,1)S(1)}, u32[]{:S(2)}, u32[]{:S(2)}) collective-permute-start(bf16[128,1024]{1,0:T(8,128)(2,1)S(1)} %get-tuple-element.60), channel_id=1, source_target_pairs={{0,24},{4,28},{8,16},{12,20},{16,8},{20,12},{24,0},{28,4},{1,25},{... | collective-permute-start | bytes 786440 | tf_op jit(solution)/shard_map/ppermute | solution.py:20
  87.3 9.3 %collective-permute-start.27 = (bf16[128,1024]{1,0:T(8,128)(2,1)S(1)}, bf16[128,1024]{1,0:T(8,128)(2,1)S(1)}, u32[]{:S(2)}, u32[]{:S(2)}) collective-permute-start(bf16[128,1024]{1,0:T(8,128)(2,1)S(1)} %get-tuple-element.66.refs_0_), channel_id=1, source_target_pairs={{0,8},{4,12},{8,0},{12,4},{16,24},{20,28},{24,16},{28,20},{1,9},{5... | collective-permute-start | bytes 786440 | tf_op jit(solution)/shard_map/ppermute | solution.py:20
  88.8 13.1 %collective-permute-start.28 = (bf16[128,1024]{1,0:T(8,128)(2,1)S(1)}, bf16[128,1024]{1,0:T(8,128)(2,1)S(1)}, u32[]{:S(2)}, u32[]{:S(2)}) collective-permute-start(bf16[128,1024]{1,0:T(8,128)(2,1)S(1)} %get-tuple-element.66.refs_0_), channel_id=1, source_target_pairs={{0,16},{4,20},{8,24},{12,28},{16,0},{20,4},{24,8},{28,12},{1,17},{... | collective-permute-start | bytes 786440 | tf_op jit(solution)/shard_map/ppermute | solution.py:20
  89.3 14.5 %collective-permute-start.29 = (bf16[128,1024]{1,0:T(8,128)(2,1)S(1)}, bf16[128,1024]{1,0:T(8,128)(2,1)S(1)}, u32[]{:S(2)}, u32[]{:S(2)}) collective-permute-start(bf16[128,1024]{1,0:T(8,128)(2,1)S(1)} %get-tuple-element.66.refs_0_), channel_id=1, source_target_pairs={{0,24},{4,28},{8,16},{12,20},{16,8},{20,12},{24,0},{28,4},{1,25},{... | collective-permute-start | bytes 786440 | tf_op jit(solution)/shard_map/ppermute | solution.py:20
  90.8 13.0 %collective-permute-start.30 = (bf16[128,1024]{1,0:T(8,128)(2,1)S(1)}, bf16[128,1024]{1,0:T(8,128)(2,1)S(1)}, u32[]{:S(2)}, u32[]{:S(2)}) collective-permute-start(bf16[128,1024]{1,0:T(8,128)(2,1)S(1)} %get-tuple-element.66.refs_0_), channel_id=1, source_target_pairs={{0,4},{4,0},{8,12},{12,8},{16,20},{20,16},{24,28},{28,24},{1,5},{5... | collective-permute-start | bytes 786440 | tf_op jit(solution)/shard_map/ppermute | solution.py:20
  90.8 17.0 %collective-permute-start.20 = (bf16[128,1024]{1,0:T(8,128)(2,1)S(1)}, bf16[128,1024]{1,0:T(8,128)(2,1)S(1)}, u32[]{:S(2)}, u32[]{:S(2)}) collective-permute-start(bf16[128,1024]{1,0:T(8,128)(2,1)S(1)} %get-tuple-element.65.refs_0_), channel_id=1, source_target_pairs={{0,8},{4,12},{8,0},{12,4},{16,24},{20,28},{24,16},{28,20},{1,9},{5... | collective-permute-start | bytes 786440 | tf_op jit(solution)/shard_map/ppermute | solution.py:20
  96.6 16.4 %collective-permute-start.21 = (bf16[128,1024]{1,0:T(8,128)(2,1)S(1)}, bf16[128,1024]{1,0:T(8,128)(2,1)S(1)}, u32[]{:S(2)}, u32[]{:S(2)}) collective-permute-start(bf16[128,1024]{1,0:T(8,128)(2,1)S(1)} %get-tuple-element.65.refs_0_), channel_id=1, source_target_pairs={{0,16},{4,20},{8,24},{12,28},{16,0},{20,4},{24,8},{28,12},{1,17},{... | collective-permute-start | bytes 786440 | tf_op jit(solution)/shard_map/ppermute | solution.py:20
  101.9 11.1 %collective-permute-start.22 = (bf16[128,1024]{1,0:T(8,128)(2,1)S(1)}, bf16[128,1024]{1,0:T(8,128)(2,1)S(1)}, u32[]{:S(2)}, u32[]{:S(2)}) collective-permute-start(bf16[128,1024]{1,0:T(8,128)(2,1)S(1)} %get-tuple-element.65.refs_0_), channel_id=1, source_target_pairs={{0,24},{4,28},{8,16},{12,20},{16,8},{20,12},{24,0},{28,4},{1,25},{... | collective-permute-start | bytes 786440 | tf_op jit(solution)/shard_map/ppermute | solution.py:20
  103.8 9.7 %collective-permute-start.31 = (bf16[128,1024]{1,0:T(8,128)(2,1)S(1)}, bf16[128,1024]{1,0:T(8,128)(2,1)S(1)}, u32[]{:S(2)}, u32[]{:S(2)}) collective-permute-start(bf16[128,1024]{1,0:T(8,128)(2,1)S(1)} %collective-permute-done.27.refs_1_), channel_id=1, source_target_pairs={{0,4},{4,0},{8,12},{12,8},{16,20},{20,16},{24,28},{28,24},{1,5},{5... | collective-permute-start | bytes 786440 | tf_op jit(solution)/shard_map/ppermute | solution.py:20
  103.8 9.8 %collective-permute-start.32 = (bf16[128,1024]{1,0:T(8,128)(2,1)S(1)}, bf16[128,1024]{1,0:T(8,128)(2,1)S(1)}, u32[]{:S(2)}, u32[]{:S(2)}) collective-permute-start(bf16[128,1024]{1,0:T(8,128)(2,1)S(1)} %collective-permute-done.28.refs_2_), channel_id=1, source_target_pairs={{0,4},{4,0},{8,12},{12,8},{16,20},{20,16},{24,28},{28,24},{1,5},{5... | collective-permute-start | bytes 786440 | tf_op jit(solution)/shard_map/ppermute | solution.py:20
  115.3 15.8 %collective-permute-start.41 = (bf16[256,512]{1,0:T(8,128)(2,1)S(1)}, bf16[256,512]{1,0:T(8,128)(2,1)S(1)}, u32[]{:S(2)}, u32[]{:S(2)}) collective-permute-start(bf16[256,512]{1,0:T(8,128)(2,1)S(1)} %get-tuple-element.85), channel_id=1, source_target_pairs={{0,1},{1,0},{2,3},{3,2},{4,5},{5,4},{6,7},{7,6},{8,9},{9,8},{10,11... | collective-permute-start | bytes 786440 | tf_op jit(solution)/shard_map/ppermute | solution.py:20
  118.5 16.3 %collective-permute-start.38 = (bf16[512,256]{1,0:T(8,128)(2,1)S(1)}, bf16[512,256]{1,0:T(8,128)(2,1)S(1)}, u32[]{:S(2)}, u32[]{:S(2)}) collective-permute-start(bf16[512,256]{1,0:T(8,128)(2,1)S(1)} %get-tuple-element.80), channel_id=1, source_target_pairs={{0,1},{1,0},{2,3},{3,2},{4,5},{5,4},{6,7},{7,6},{8,9},{9,8},{10,11... | collective-permute-start | bytes 786440 | tf_op jit(solution)/shard_map/ppermute | solution.py:20
  129.0 11.6 %collective-permute-start.34 = (bf16[128,512]{1,0:T(8,128)(2,1)S(1)}, bf16[128,512]{1,0:T(8,128)(2,1)S(1)}, u32[]{:S(2)}, u32[]{:S(2)}) collective-permute-start(bf16[128,512]{1,0:T(8,128)(2,1)S(1)} %get-tuple-element.73), channel_id=1, source_target_pairs={{0,1},{1,0},{2,3},{3,2},{4,5},{5,4},{6,7},{7,6},{8,9},{9,8},{10,11... | collective-permute-start | bytes 393224 | tf_op jit(solution)/shard_map/ppermute | solution.py:20
  129.4 11.2 %collective-permute-start.35 = (bf16[128,512]{1,0:T(8,128)(2,1)S(1)}, bf16[128,512]{1,0:T(8,128)(2,1)S(1)}, u32[]{:S(2)}, u32[]{:S(2)}) collective-permute-start(bf16[128,512]{1,0:T(8,128)(2,1)S(1)} %get-tuple-element.74), channel_id=1, source_target_pairs={{0,2},{1,3},{2,0},{3,1},{4,6},{5,7},{6,4},{7,5},{8,10},{9,11},{10,... | collective-permute-start | bytes 393224 | tf_op jit(solution)/shard_map/ppermute | solution.py:20
  130.5 43.5 %collective-permute-start.40 = (bf16[256,512]{1,0:T(8,128)(2,1)}, bf16[256,512]{1,0:T(8,128)(2,1)}, u32[]{:S(2)}, u32[]{:S(2)}) collective-permute-start(bf16[256,512]{1,0:T(8,128)(2,1)} %get-tuple-element.83), channel_id=1, source_target_pairs={{0,1},{1,0},{2,3},{3,2},{4,5},{5,4},{6,7},{7,6},{8,9},{9,8},{10,11... | collective-permute-start | bytes 786440 | tf_op jit(solution)/shard_map/ppermute | solution.py:20
  131.9 42.1 %collective-permute-start.42 = (bf16[256,512]{1,0:T(8,128)(2,1)}, bf16[256,512]{1,0:T(8,128)(2,1)}, u32[]{:S(2)}, u32[]{:S(2)}) collective-permute-start(bf16[256,512]{1,0:T(8,128)(2,1)} %add_up.3), channel_id=1, source_target_pairs={{0,2},{1,3},{2,0},{3,1},{4,6},{5,7},{6,4},{7,5},{8,10},{9,11},{10,... | collective-permute-start | bytes 786440 | tf_op jit(solution)/shard_map/ppermute | solution.py:20
  134.8 41.3 %collective-permute-start.37 = (bf16[512,256]{1,0:T(8,128)(2,1)}, bf16[512,256]{1,0:T(8,128)(2,1)}, u32[]{:S(2)}, u32[]{:S(2)}) collective-permute-start(bf16[512,256]{1,0:T(8,128)(2,1)} %get-tuple-element.78), channel_id=1, source_target_pairs={{0,1},{1,0},{2,3},{3,2},{4,5},{5,4},{6,7},{7,6},{8,9},{9,8},{10,11... | collective-permute-start | bytes 786440 | tf_op jit(solution)/shard_map/ppermute | solution.py:20
  140.6 35.5 %collective-permute-start.39 = (bf16[512,256]{1,0:T(8,128)(2,1)}, bf16[512,256]{1,0:T(8,128)(2,1)}, u32[]{:S(2)}, u32[]{:S(2)}) collective-permute-start(bf16[512,256]{1,0:T(8,128)(2,1)} %add_up.2), channel_id=1, source_target_pairs={{0,2},{1,3},{2,0},{3,1},{4,6},{5,7},{6,4},{7,5},{8,10},{9,11},{10,... | collective-permute-start | bytes 786440 | tf_op jit(solution)/shard_map/ppermute | solution.py:20
  140.6 21.1 %collective-permute-start.36 = (bf16[128,512]{1,0:T(8,128)(2,1)S(1)}, bf16[128,512]{1,0:T(8,128)(2,1)S(1)}, u32[]{:S(2)}, u32[]{:S(2)}) collective-permute-start(bf16[128,512]{1,0:T(8,128)(2,1)S(1)} %get-tuple-element.75), channel_id=1, source_target_pairs={{0,3},{1,2},{2,1},{3,0},{4,7},{5,6},{6,5},{7,4},{8,11},{9,10},{10,... | collective-permute-start | bytes 393224 | tf_op jit(solution)/shard_map/ppermute | solution.py:20
  (21 other events, 420.2 us)

commit v3 on v2

v3 whole, which is shorter than its diff:
```python
import functools
import math

import jax
import jax.numpy as jnp
from jax import lax
from jax.experimental import pallas as pl
from jax.experimental.pallas import tpu as pltpu
from jax.sharding import PartitionSpec as P

momentum_decay = 0.9
learn_rate = 0.05
bf16 = jnp.bfloat16
f32 = jnp.float32
VMEM_BYTES = 24 << 20
LONG = 100_000_000_000


def swap(value, axis, step):
    count = lax.axis_size(axis)
    return lax.ppermute(value, axis, [(at, at ^ step) for at in range(count)])


def parent(k):
    return k & (k - 1)


def low_bit(k):
    return k & -k


def up_to(value, unit):
    return -(-value // unit) * unit


def gelu_act(value):
    return 0.5 * value * (1.0 + lax.erf(value * math.sqrt(0.5)))


def gelu_slope(value):
    return 0.5 * (1.0 + lax.erf(value * math.sqrt(0.5))) + value * jnp.exp(
        -0.5 * value * value
    ) * (1.0 / math.sqrt(2.0 * math.pi))


def dot(left, right, at_left, at_right):
    dims = (((at_left,), (at_right,)), ((), ()))
    return lax.dot_general(left, right, dims, preferred_element_type=f32)


def shaped(dims, kind):
    return jax.ShapeDtypeStruct(dims, kind)


def on_core(body, outs, args, name, flops=0, scratch=(), scalars=()):
    at = pl.BlockSpec(memory_space=pltpu.VMEM)
    return pl.pallas_call(
        body,
        out_shape=outs,
        in_specs=[pl.BlockSpec(memory_space=pltpu.SMEM)] * len(scalars) + [at] * len(args),
        out_specs=jax.tree.map(lambda _: at, outs),
        scratch_shapes=list(scratch),
        compiler_params=pltpu.CompilerParams(vmem_limit_bytes=VMEM_BYTES),
        cost_estimate=pl.CostEstimate(flops=flops, bytes_accessed=0, transcendentals=0),
        name=name,
    )(*scalars, *args)


def pack_small(w_in, w_out, out, *, tall):
    n_in, wide = w_in.shape
    n_out = w_out.shape[0]
    left = jnp.concatenate([w_in[...], jnp.zeros((tall - n_in, wide), f32)], 0)
    right = jnp.concatenate([w_out[...], jnp.zeros((tall - n_out, wide), f32)], 0)
    parts = [left, right]
    spare = out.shape[1] - 2 * wide
    if spare:
        parts.append(jnp.zeros((tall, spare), f32))
    out[...] = jnp.concatenate(parts, 1).astype(bf16)


def pick_rows(count, samples, targets, out, wanted, *, tall, rows, per):
    slots, n_in, block = samples.shape
    n_out = targets.shape[1]
    half = lax.axis_size("dp") // 2
    high = lax.axis_index("dp") >= half
    xs, ys = [], []
    for j in range(per):
        at = per * lax.axis_index("mp") + j
        slot = jnp.where(high, slots - 1 - at, at)
        keep = slot < count[0]
        for source, last, all_of in (
            (samples, jnp.full((1, block), count[0].astype(f32)), xs),
            (targets, jnp.full((1, block), keep.astype(f32)), ys),
        ):
            value = source[slot].astype(f32)
            parts = [jnp.where(keep, value, jnp.zeros_like(value)), last]
            spare = tall - value.shape[0] - 1
            if spare:
                parts.append(jnp.zeros((spare, block), f32))
            all_of.append(jnp.concatenate(parts, 0).astype(bf16))
    x = jnp.concatenate(xs, 1) if per > 1 else xs[0]
    y = jnp.concatenate(ys, 1) if per > 1 else ys[0]
    spare = out.shape[1] - rows
    for t in range(2):
        at = slice(t * rows, (t + 1) * rows)
        half_x = x[:, at]
        if spare:
            half_x = jnp.concatenate([half_x, jnp.zeros((tall, spare), bf16)], 1)
        out[tall * t : tall * (t + 1)] = half_x
        wanted[t] = y[:, at]


def pack_all(*refs):
    out, at = refs[-1], 0
    for part in refs[:-1]:
        out[at : at + part.shape[0]] = part[...]
        at += part.shape[0]


def place_small(held, inputs, first, fourth, *, tall, rows, wide, places):
    n_dp, n_mp = lax.axis_size("dp"), lax.axis_size("mp")
    half = n_dp // 2
    blocks = list(range(0, n_dp, 2)) + list(range(1, n_dp, 2))
    for place, k in enumerate(blocks):
        at = lax.axis_index("dp") ^ k
        high = at >= half
        pair = jnp.where(high, at - half, at)
        both = held[pair, : 2 * tall] + held[pair + half, : 2 * tall]
        value = jnp.where(high, both[tall:], both[:tall])
        inputs[:, place * rows : (place + 1) * rows] = value[:, :rows]
    hidden = n_dp * wide
    for k in range(n_mp):
        row = slice((2 + k) * tall, (3 + k) * tall)
        pieces = [held[d, row] for d in range(n_dp)]
        at = slice(k * hidden, (k + 1) * hidden)
        first[:, at] = jnp.concatenate([piece[:, :wide] for piece in pieces], 1)
        at = slice(places.index(k) * hidden, (places.index(k) + 1) * hidden)
        fourth[:, at] = jnp.concatenate([piece[:, wide : 2 * wide] for piece in pieces], 1)


def one_forward(inputs, first, out, *, tile):
    n_rows = inputs.shape[1]
    cut = min(256, n_rows)

    def step(i, _):
        at = pl.ds(pl.multiple_of(i * tile, tile), tile)
        weights = first[:, at].T
        for c in range(0, n_rows, cut):
            pre = dot(weights, inputs[:, c : c + cut], 1, 0)
            out[at, c : c + cut] = gelu_act(pre).astype(bf16)
        return 0

    lax.fori_loop(0, first.shape[1] // tile, step, 0)


def one_slope(inputs, first, out, *, tile):
    n_rows = inputs.shape[1]
    cut = min(256, n_rows)

    def step(i, _):
        at = pl.ds(pl.multiple_of(i * tile, tile), tile)
        weights = first[:, at].T
        for c in range(0, n_rows, cut):
            pre = dot(weights, inputs[:, c : c + cut], 1, 0)
            out[at, c : c + cut] = gelu_slope(pre).astype(bf16)
        return 0

    lax.fori_loop(0, first.shape[1] // tile, step, 0)


def two_forward(act_one, *refs):
    seconds, (act, act_t, slope) = refs[:-3], refs[-3:]
    n_rows = act_one.shape[1]
    cut = min(256, n_rows)
    span = seconds[0].shape[0]
    turned = [s[...].T for s in seconds]
    for c in range(0, n_rows, cut):
        at = slice(c, c + cut)
        pre = dot(turned[0], act_one[:span, at], 1, 0)
        for k in range(1, len(seconds)):
            pre = pre + dot(turned[k], act_one[k * span : (k + 1) * span, at], 1, 0)
        value = gelu_act(pre)
        act_t[:, at] = value.astype(bf16)
        act[at] = value.T.astype(bf16)
        slope[:, at] = gelu_slope(pre)


def three_away(act, *refs, kept):
    thirds, out = refs[:-1], refs[-1]
    span = thirds[0].shape[1]
    for k, third in enumerate(thirds):
        out[:, k * span : (k + 1) * span] = dot(act[kept:], third[...], 1, 0).astype(bf16)


def three_home(act, got, *refs, kept, rows):
    half = kept // rows
    thirds, own, sends = refs[:-half], refs[-half], refs[len(refs) - half + 1 :]
    span = thirds[0].shape[1]
    for k, third in enumerate(thirds):
        at = slice(k * span, (k + 1) * span)
        total = dot(act[:kept], third[...], 1, 0) + got[:, at].astype(f32)
        own[:, at] = total[:rows]
        for i, send in enumerate(sends):
            send[:, at] = total[(i + 1) * rows : (i + 2) * rows].astype(bf16)


def error_step(inputs, wanted, wanted_too, fourth, *refs, groups, half, per, n_in, n_out):
    terms = refs[: groups * half]
    act, pre = refs[-2:]
    deltas, grad_four = refs[groups * half : groups * half + groups], refs[-3]
    width = pre.shape[1] // groups
    for g in range(groups):
        at = slice(g * width, (g + 1) * width)
        own, others = terms[g * half], terms[g * half + 1 : (g + 1) * half]
        total = own[...]
        for other in others:
            total = total + other[...].astype(f32)
        pre[:, at] = total
        act[:, at] = gelu_act(total).astype(bf16)
    predicted = dot(fourth[...], act[...], 1, 1)
    number = jnp.sum(inputs[n_in : n_in + 1, :].astype(f32), axis=1, keepdims=True) / per
    mine = jnp.where(lax.axis_index("dp") >= half, 1, 0)
    wanted = wanted[mine] + wanted_too[mine]
    live = wanted[n_out : n_out + 1, :].astype(f32)
    error = (2.0 / number * (predicted - wanted.astype(f32)) * live).astype(bf16)
    row = lax.broadcasted_iota(jnp.int32, error.shape, 0)
    error = jnp.where(row < n_out, error, jnp.zeros_like(error))
    grad_four[...] = dot(error, act[...], 1, 0)
    turned = error.astype(f32).T.astype(bf16)
    for g in range(groups):
        at = slice(g * width, (g + 1) * width)
        delta = dot(turned, fourth[:, at], 1, 0) * gelu_slope(pre[:, at])
        deltas[g][: delta.shape[0]] = delta.astype(bf16)


def join(*refs):
    rows = refs[-1].shape[0] // (len(refs) - 1)
    for i, part in enumerate(refs[:-1]):
        refs[-1][i * rows : (i + 1) * rows] = part[:rows]


def three_back(act_t, home, away, *refs, ks, carried):
    thirds = refs[: len(ks)]
    refs = refs[len(ks) :]
    before = refs[0] if carried else None
    refs = refs[carried:]
    sum_two, grads, whole = refs[0], refs[1 : 1 + len(ks)], refs[-1]
    rows = home.shape[0]
    span = thirds[0].shape[1]
    whole[:rows] = home[...]
    whole[rows:] = away[...]
    for i in range(len(ks)):
        at = slice(i * span, (i + 1) * span)
        grads[i][...] = dot(act_t[...], whole[:, at], 1, 0).astype(grads[i].dtype)
    total = before[...] if carried else None
    for i, third in enumerate(thirds):
        term = dot(third[...], whole[:, i * span : (i + 1) * span], 1, 1)
        total = term if total is None else total + term
    sum_two[...] = total


def two_back(sum_two, slope, act_one, delta, *grads):
    value = (sum_two[...] * slope[...]).astype(bf16)
    delta[...] = value
    span = act_one.shape[0] // len(grads)
    for k, grad in enumerate(grads):
        grad[...] = dot(act_one[k * span : (k + 1) * span], value, 1, 1).astype(grad.dtype)


def split_dp(parts, step, keep, send):
    bit = (lax.axis_index("dp") & step) != 0
    for i in range(len(parts) // 2):
        even, odd = parts[2 * i], parts[2 * i + 1]
        keep[i] = jnp.where(bit, odd, even)
        send[i] = jnp.where(bit, even, odd).astype(bf16)


def one_back(inputs, delta, slope, grad_four, *refs, n_mp, n_dp, places):
    seconds, (keep, send) = refs[:n_mp], refs[n_mp:]
    span = seconds[0].shape[0]
    wide = span // n_dp
    whole = []
    for k in range(n_mp):
        value = dot(seconds[k][...], delta[...], 1, 0)
        value = (value * slope[k * span : (k + 1) * span].astype(f32)).astype(bf16)
        grad_one = dot(inputs[...], value, 1, 1)
        at = places.index(k) * span
        whole.append(jnp.concatenate([grad_one, grad_four[:, at : at + span]], 0))
    parts = [
        jnp.concatenate([value[:, d * wide : (d + 1) * wide] for value in whole], 1)
        for d in range(n_dp)
    ]
    split_dp(parts, 1, keep, send)


def halve(own, got, keep, send, *, step):
    split_dp([own[i] + got[i].astype(f32) for i in range(own.shape[0])], step, keep, send)


def last_half(own, got, keep, send):
    total = own[0] + got[0].astype(f32)
    wide = keep.shape[1]
    keep[...] = total[:, :wide]
    send[...] = total[:, wide:].astype(bf16)


def last_half_mp(own, got, keep, send):
    total = own[...] + got[...].astype(f32)
    wide = keep.shape[1]
    keep[...] = total[:, :wide]
    send[...] = total[:, wide:].astype(bf16)


def add_up(own, got, out):
    out[...] = (own[...].astype(f32) + got[...].astype(f32)).astype(out.dtype)


def update_small(own, *refs):
    gots, (w_in, w_out, m_in, m_out), outs = refs[:-8], refs[-8:-4], refs[-4:]
    nw_in, nw_out, nm_in, nm_out = outs
    tall = own.shape[0] // 2
    total = own[...]
    for got in gots:
        total = total + got[...].astype(f32)
    n_in, n_out = w_in.shape[0], w_out.shape[0]
    mom = momentum_decay * m_in[...] + total[:n_in]
    nm_in[...] = mom
    nw_in[...] = w_in[...] - learn_rate * mom
    mom = momentum_decay * m_out[...] + total[tall : tall + n_out]
    nm_out[...] = mom
    nw_out[...] = w_out[...] - learn_rate * mom


def update_big(weight, moment, own, *refs):
    gots, (new_weight, new_moment) = refs[:-2], refs[-2:]
    total = own[...]
    for got in gots:
        total = total + got[...].astype(f32)
    mom = momentum_decay * moment[...] + total
    new_moment[...] = mom
    new_weight[...] = weight[...] - learn_rate * mom


def after(first, *values):
    return lax.optimization_barrier((first, *values))[1:]


def gathered(own, n_mp):
    held = {0: own}
    for k in [k for k in range(1, n_mp) if parent(k) == 0][::-1]:
        held[k] = swap(own, "mp", k)
    return held


def passed_on(held, n_mp, ready):
    for k in sorted((k for k in range(1, n_mp) if parent(k)), key=lambda k: -low_bit(k)):
        held[k] = swap(after(ready, held[parent(k)])[0], "mp", low_bit(k))


def summed(held, ks, sent):
    gots = []
    for k in sorted((k for k in ks if k), key=lambda k: (low_bit(k), -k)):
        got = sent[k] if k in sent else swap(held[k], "mp", low_bit(k))
        to = parent(k)
        if to:
            held[to] = on_core(add_up, shaped(got.shape, bf16), [held[to], got], "add_up")
        else:
            gots.append(got)
    return gots


def on_device(
    samples,
    targets,
    counts,
    weight_in,
    weight_mid,
    weight_top,
    weight_out,
    moment_in,
    moment_mid,
    moment_top,
    moment_out,
):
    slots, n_in, block = samples.shape
    n_out = targets.shape[1]
    n_dp, n_mp = lax.axis_size("dp"), lax.axis_size("mp")
    half = n_dp // 2
    per = slots // n_mp
    rows = per * block // 2
    n_rows = n_dp * rows
    wide = weight_in.shape[1]
    lanes = max(rows, 2 * wide)
    tall = up_to(max(n_in, n_out) + 1, 16)
    hidden = wide * n_dp
    width = hidden * n_mp
    n_mid, n_top = weight_mid.shape[1], weight_top.shape[1]
    planes = range(n_mp)
    groups = [list(planes[::2]), list(planes[1::2])]
    places = [k for ks in groups for k in ks]
    part = functools.partial

    piece = on_core(
        part(pack_small, tall=tall), shaped((tall, lanes), bf16), [weight_in, weight_out.T], "pack_small"
    )
    second = gathered(weight_mid.astype(bf16), n_mp)
    picked, wanted = on_core(
        part(pick_rows, tall=tall, rows=rows, per=per),
        [shaped((2 * tall, lanes), bf16), shaped((2, tall, rows), bf16)],
        [samples, targets],
        "pick_rows",
        scalars=[counts],
    )
    pieces = [piece] + [swap(piece, "mp", k) for k in planes[1:]]
    top = after((picked, pieces), weight_top.astype(bf16))[0]
    third = gathered(top, n_mp)
    passed_on(second, n_mp, (picked, pieces))

    early = [second[k] for k in planes if k and not parent(k)]
    packed = on_core(
        pack_all,
        shaped(((2 + n_mp) * tall, lanes), bf16),
        [picked, *after(early, *pieces)],
        "pack_all",
    )
    wanted = [wanted, swap(wanted, "dp", half)]
    held = lax.all_gather(packed, "dp")
    inputs, first, fourth = on_core(
        part(place_small, tall=tall, rows=rows, wide=wide, places=places),
        [shaped((tall, n_rows), bf16), shaped((tall, width), bf16), shaped((tall, width), bf16)],
        [held],
        "place_small",
    )

    act_one = on_core(
        part(one_forward, tile=128), shaped((width, n_rows), bf16), [inputs, first], "one_forward"
    )
    act_two, act_two_t, slope_two = on_core(
        two_forward,
        [shaped((n_rows, n_mid), bf16), shaped((n_mid, n_rows), bf16), shaped((n_mid, n_rows), f32)],
        [act_one] + [second[k] for k in planes],
        "two_forward",
    )
    passed_on(third, n_mp, act_one)
    kept = half * rows
    terms = []
    ahead = [third[k] for k in planes if k and not parent(k)]
    for ks in groups:
        cols = len(ks) * n_top
        weights = after(ahead, *[third[k] for k in ks])
        away = on_core(
            part(three_away, kept=kept), shaped((kept, cols), bf16), [act_two, *weights], "three_away"
        )
        own, *sends = on_core(
            part(three_home, kept=kept, rows=rows),
            [shaped((rows, cols), f32)] + [shaped((rows, cols), bf16)] * (half - 1),
            [act_two, swap(away, "dp", 1), *weights],
            "three_home",
        )
        ahead = [swap(send, "dp", 2 * (i + 1)) for i, send in enumerate(sends)]
        terms += [own, *ahead]
    slope_one = on_core(
        part(one_slope, tile=128), shaped((width, n_rows), bf16), [inputs, first], "one_slope",
        flops=12_000_000_000,
    )
    *deltas, grad_four = on_core(
        part(error_step, groups=len(groups), half=half, per=per, n_in=n_in, n_out=n_out),
        [shaped((rows + 16 * (g == 0), len(ks) * n_top), bf16) for g, ks in enumerate(groups)] + [shaped((tall, width), f32)],
        [inputs, *wanted, fourth, *after(slope_one, *terms)],
        "error_step",
        scratch=[pltpu.VMEM((rows, width), bf16), pltpu.VMEM((rows, width), f32)],
    )

    sum_two, grad_three, sent = None, {}, []
    for g in reversed(range(len(groups))):
        ks = groups[g]
        home = [deltas[g]] + [swap(deltas[g], "dp", 2 * i) for i in range(1, half)]
        if sent:
            home = after((sum_two, sent), *home)
        home = on_core(join, shaped((kept, deltas[g].shape[1]), bf16), home, "join")
        away = swap(home, "dp", 1)
        carry = [sum_two] if sent else []
        sum_two, *grads = on_core(
            part(three_back, ks=ks, carried=len(carry)),
            [shaped((n_mid, n_rows), f32)]
            + [shaped((n_mid, n_top), bf16 if k else f32) for k in ks],
            [act_two_t, home, away] + [third[k] for k in ks] + carry,
            "three_back",
            scratch=[pltpu.VMEM((n_rows, len(ks) * n_top), bf16)],
        )
        grad_three.update(zip(ks, grads))
        if not sent:
            sent = [swap(grad_three[k], "mp", 1) for k in ks]
    gots_three = summed(grad_three, planes, dict(zip(groups[1], sent)))
    grad_two = {}
    delta_two, *grads = on_core(
        two_back,
        [shaped((n_mid, n_rows), bf16)] + [shaped((hidden, n_mid), bf16 if k else f32) for k in planes],
        [sum_two, slope_two, act_one],
        "two_back",
        flops=LONG,
    )
    grad_two = dict(zip(planes, grads))
    farthest = swap(grad_two[n_mp - 1], "mp", 1)
    grad_two[1] = after(farthest, grad_two[1])[0]
    gots_two = summed(grad_two, planes, {n_mp - 1: farthest})
    shape = (half, 2 * tall, n_mp * wide)
    keep, send = on_core(
        part(one_back, n_mp=n_mp, n_dp=n_dp, places=places),
        [shaped(shape, f32), shaped(shape, bf16)],
        [inputs, delta_two, slope_one, grad_four] + [second[k] for k in planes],
        "one_back",
        flops=LONG,
    )
    step = 1
    while step < half:
        got = swap(send, "dp", step)
        step *= 2
        shape = (shape[0] // 2, *shape[1:])
        keep, send = on_core(
            part(halve, step=step), [shaped(shape, f32), shaped(shape, bf16)], [keep, got], "halve"
        )
    got = swap(send, "dp", step)
    half_mp = n_mp // 2 * wide
    keep, send = on_core(
        last_half,
        [shaped((2 * tall, half_mp), f32), shaped((2 * tall, half_mp), bf16)],
        [keep, got],
        "last_half",
    )
    step = n_mp // 2
    while step:
        got = swap(send, "mp", step)
        step //= 2
        if step:
            got = after((gots_two, gots_three), got)[0]
        if step:
            half_mp = step * wide
            keep, send = on_core(
                last_half_mp,
                [shaped((2 * tall, half_mp), f32), shaped((2 * tall, half_mp), bf16)],
                [keep, got],
                "last_half_mp",
            )
    gots_small = [got]

    like = lambda value: shaped(value.shape, f32)
    flat = (weight_in, weight_out.T, moment_in, moment_out.T)
    new_in, new_out, mom_in, mom_out = on_core(
        update_small, [like(value) for value in flat], [keep, *gots_small, *flat], "update_small"
    )
    new_top, mom_top = on_core(
        update_big, [like(weight_top)] * 2, [weight_top, moment_top, grad_three[0], *gots_three], "update_top",
        flops=2_000_000_000,
    )
    new_mid, mom_mid = on_core(
        update_big, [like(weight_mid)] * 2, [weight_mid, moment_mid, grad_two[0], *gots_two], "update_mid"
    )
    return (new_in, new_mid, new_top, new_out.T, mom_in, mom_mid, mom_top, mom_out.T)


def solution(mesh):
    in_specs = (
        P("dp", None, None),
        P("dp", None, None),
        P("dp"),
        P(None, ("mp", "dp")),
        P("mp", "dp"),
        P("dp", "mp"),
        P(("mp", "dp"), None),
        P(None, ("mp", "dp")),
        P("mp", "dp"),
        P("dp", "mp"),
        P(("mp", "dp"), None),
    )
    out_specs = (
        P(None, ("mp", "dp")),
        P("mp", "dp"),
        P("dp", "mp"),
        P(("mp", "dp"), None),
        P(None, ("mp", "dp")),
        P("mp", "dp"),
        P("dp", "mp"),
        P(("mp", "dp"), None),
    )
    return jax.shard_map(
        on_device, mesh=mesh, in_specs=in_specs, out_specs=out_specs, check_vma=False
    )
```

time: 181 us -> 155 us (0.86); the launches traced: 178 us -> 154 us
  waiting for transfers between devices: 94.8 us -> 65.4 us
  starting transfers between devices: 36 us -> 45.3 us
  Pallas kernels: 28.9 us -> 25.3 us
    ppermute x43 -> x37, waiting for transfers between devices: 94.8 us -> 65.4 us  [swap(): return lax.ppermute(value, axis, [(at, at ^ step) for at in range(count)])]
    all_gather x0 -> x1, blocking collectives: none -> 10.4 us  [on_device(): held = lax.all_gather(packed, 'dp')]
    all_to_all x1 -> x0, blocking collectives: 9.51 us -> none  [on_device(): small = lax.all_to_all(small, 'dp', 0, 0, tiled=True)]
    ppermute x43 -> x37, starting transfers between devices: 36 us -> 45.3 us  [swap(): return lax.ppermute(value, axis, [(at, at ^ step) for at in range(count)])]
    pallas_call x23 -> x27, Pallas kernels: 28.9 us -> 25.3 us  [on_core(): pl.pallas_call(body, out_shape=outs, in_specs=[pl.BlockSpec(memory_space=...]
    unnamed x22 -> x30, local copies, waits for them, and re-layouts: 3.37 us -> 4.09 us
  transfers between devices with their start and end apart: 43 -> 37, of which waited for: 18 -> 20; matrix products, arithmetic and copies ran while one was open for 3% -> 2% of each run, Pallas kernels for 14% -> 12%
where the time goes in v3:
time: 155 us; the launch traced here: 154 us
  waiting for transfers between devices  65.4 us (42%)
  starting transfers between devices  45.3 us (29%)
  Pallas kernels  25.3 us (16%)
  blocking collectives  10.4 us (7%)
  local copies, waits for them, and re-layouts  4.09 us (3%)
  other arithmetic  2.15 us (1%)
  between operations  1.64 us (1%)
    ppermute x37, waiting for transfers between devices, swap(): return lax.ppermute(value, axis, [(at, at ^ step) for at in range(count)])  65.4 us
    ppermute x37, starting transfers between devices, swap(): return lax.ppermute(value, axis, [(at, at ^ step) for at in range(count)])  45.3 us
    pallas_call x27, Pallas kernels, on_core(): pl.pallas_call(body, out_shape=outs, in_specs=[pl.BlockSpec(memory_space=...  25.3 us
    all_gather x1, blocking collectives, on_device(): held = lax.all_gather(packed, 'dp')  10.4 us
    unnamed x30, local copies, waits for them, and re-layouts  4.09 us
  transfers between devices with their start and end apart: 37, of which 20 were waited for; matrix products, arithmetic and copies ran while one was open for 2% of the time, Pallas kernels for 12%

profile of v3, /device:TPU:0, one launch (start us, length us, event | category | flops | bytes accessed | tf_op | source)
XLA Modules:
  0.0 154.2 jit_solution(11970005147253613860)
XLA Ops:
  1.7 4.1 %collective-permute-start.1 = (bf16[512,256]{1,0:T(8,128)(2,1)S(1)}, bf16[512,256]{1,0:T(8,128)(2,1)S(1)}, u32[]{:S(2)}, u32[]{:S(2)}) collective-permute-start(bf16[512,256]{1,0:T(8,128)(2,1)S(1)} %convert_element_type.6.refs_0_), channel_id=1, source_target_pairs={{0,2},{1,3},{2,0},{3,1},{4,6},{5,7},{6,4},{7,5},{8,10},{9,11},{10,... | collective-permute-start | bytes 786440 | tf_op jit(solution)/shard_map/ppermute | solution.py:21
  9.0 1.9 %collective-permute-start.3 = (bf16[64,128]{1,0:T(8,128)(2,1)S(1)}, bf16[64,128]{1,0:T(8,128)(2,1)S(1)}, u32[]{:S(2)}, u32[]{:S(2)}) collective-permute-start(bf16[64,128]{1,0:T(8,128)(2,1)S(1)} %pack_small.1.refs_1_), channel_id=1, source_target_pairs={{0,2},{1,3},{2,0},{3,1},{4,6},{5,7},{6,4},{7,5},{8,10},{9,11},{10,... | collective-permute-start | bytes 49160 | tf_op jit(solution)/shard_map/ppermute | solution.py:21
  10.9 2.5 %collective-permute-start.2 = (bf16[64,128]{1,0:T(8,128)(2,1)S(1)}, bf16[64,128]{1,0:T(8,128)(2,1)S(1)}, u32[]{:S(2)}, u32[]{:S(2)}) collective-permute-start(bf16[64,128]{1,0:T(8,128)(2,1)S(1)} %pack_small.1.refs_1_), channel_id=1, source_target_pairs={{0,1},{1,0},{2,3},{3,2},{4,5},{5,4},{6,7},{7,6},{8,9},{9,8},{10,11... | collective-permute-start | bytes 49160 | tf_op jit(solution)/shard_map/ppermute | solution.py:21
  17.0 2.6 %collective-permute-done.4.refs_4_ = bf16[64,128]{1,0:T(8,128)(2,1)S(1)} collective-permute-done((bf16[64,128]{1,0:T(8,128)(2,1)S(1)}, bf16[64,128]{1,0:T(8,128)(2,1)S(1)}, u32[]{:S(2)}, u32[]{:S(2)}) %collective-permute-start.4) | collective-permute-done | bytes 16416 | tf_op jit(solution)/shard_map/ppermute | solution.py:21
  19.5 2.0 %collective-permute-start.8 = (bf16[256,512]{1,0:T(8,128)(2,1)S(1)}, bf16[256,512]{1,0:T(8,128)(2,1)S(1)}, u32[]{:S(2)}, u32[]{:S(2)}) collective-permute-start(bf16[256,512]{1,0:T(8,128)(2,1)S(1)} %convert_element_type.7.refs_0_), channel_id=1, source_target_pairs={{0,2},{1,3},{2,0},{3,1},{4,6},{5,7},{6,4},{7,5},{8,10},{9,11},{10,... | collective-permute-start | bytes 786440 | tf_op jit(solution)/shard_map/ppermute | solution.py:21
  21.5 1.7 %collective-permute-start.7 = (bf16[256,512]{1,0:T(8,128)(2,1)S(1)}, bf16[256,512]{1,0:T(8,128)(2,1)S(1)}, u32[]{:S(2)}, u32[]{:S(2)}) collective-permute-start(bf16[256,512]{1,0:T(8,128)(2,1)S(1)} %convert_element_type.7.refs_0_), channel_id=1, source_target_pairs={{0,1},{1,0},{2,3},{3,2},{4,5},{5,4},{6,7},{7,6},{8,9},{9,8},{10,11... | collective-permute-start | bytes 786440 | tf_op jit(solution)/shard_map/ppermute | solution.py:21
  23.6 10.4 %all-gather = bf16[3072,128]{1,0:T(8,128)(2,1)S(1)} all-gather(bf16[384,128]{1,0:T(8,128)(2,1)S(1)} %pack_all.1), channel_id=2, replica_groups=mesh['dp'=8,'mp'=4] {'dp'}, dimensions={0}, use_global_device_ids=true | all-gather | bytes 884736 | tf_op jit(solution)/shard_map/all_gather | solution.py:427
  34.2 4.7 %one_forward.1.act_one = bf16[2048,1024]{1,0:T(8,128)(2,1)S(1)} custom-call(bf16[64,1024]{1,0:T(8,128)(2,1)S(1)} %get-tuple-element.86.inputs, bf16[64,2048]{1,0:T(8,128)(2,1)S(1)} %get-tuple-element.87.first), custom_call_target="tpu_custom_call" | custom-call | tf_op jit(solution)/shard_map/one_forward/pallas_call | solution.py:57
  39.0 1.7 %two_forward.1 = (bf16[1024,256]{1,0:T(8,128)(2,1)S(1)}, bf16[256,1024]{1,0:T(8,128)(2,1)S(1)}, f32[256,1024]{1,0:T(8,128)S(1)}) custom-call(bf16[2048,1024]{1,0:T(8,128)(2,1)S(1)} %one_forward.1.act_one, bf16[512,256]{1,0:T(8,128)(2,1)S(1)} %convert_element_type.6.refs_0_, bf16[512,256]{1,0:T(8,128)(2,1)S(1)} %collective-permute-done.refs_1_, ...), custom_call_target="tpu_custom_call" | custom-call | tf_op jit(solution)/shard_map/two_forward/pallas_call | solution.py:57
  41.5 1.7 %collective-permute-start.13 = (bf16[256,512]{1,0:T(8,128)(2,1)S(1)}, bf16[256,512]{1,0:T(8,128)(2,1)S(1)}, u32[]{:S(2)}, u32[]{:S(2)}) collective-permute-start(bf16[256,512]{1,0:T(8,128)(2,1)S(1)} %collective-permute-done.8.refs_1_), channel_id=1, source_target_pairs={{0,1},{1,0},{2,3},{3,2},{4,5},{5,4},{6,7},{7,6},{8,9},{9,8},{10,11... | collective-permute-start | bytes 786440 | tf_op jit(solution)/shard_map/ppermute | solution.py:21
  47.9 2.1 %collective-permute-done.13.refs_1_ = bf16[256,512]{1,0:T(8,128)(2,1)S(1)} collective-permute-done((bf16[256,512]{1,0:T(8,128)(2,1)S(1)}, bf16[256,512]{1,0:T(8,128)(2,1)S(1)}, u32[]{:S(2)}, u32[]{:S(2)}) %collective-permute-start.13) | collective-permute-done | bytes 262176 | tf_op jit(solution)/shard_map/ppermute | solution.py:21
  49.9 3.6 %collective-permute-done.10.refs_1_ = bf16[128,1024]{1,0:T(8,128)(2,1)S(1)} collective-permute-done((bf16[128,1024]{1,0:T(8,128)(2,1)S(1)}, bf16[128,1024]{1,0:T(8,128)(2,1)S(1)}, u32[]{:S(2)}, u32[]{:S(2)}) %collective-permute-start.10) | collective-permute-done | bytes 262176 | tf_op jit(solution)/shard_map/ppermute | solution.py:21
  53.5 6.2 %collective-permute-done.11.refs_2_ = bf16[128,1024]{1,0:T(8,128)(2,1)S(1)} collective-permute-done((bf16[128,1024]{1,0:T(8,128)(2,1)S(1)}, bf16[128,1024]{1,0:T(8,128)(2,1)S(1)}, u32[]{:S(2)}, u32[]{:S(2)}) %collective-permute-start.11) | collective-permute-done | bytes 262176 | tf_op jit(solution)/shard_map/ppermute | solution.py:21
  66.9 6.2 %one_slope.1.slope = bf16[2048,1024]{1,0:T(8,128)(2,1)S(1)} custom-call(bf16[64,1024]{1,0:T(8,128)(2,1)S(1)} %get-tuple-element.86.inputs, bf16[64,2048]{1,0:T(8,128)(2,1)S(1)} %get-tuple-element.87.first), custom_call_target="tpu_custom_call" | custom-call | flops 12000000000 | tf_op jit(solution)/shard_map/one_slope/pallas_call | solution.py:57
  73.1 3.5 %collective-permute-done.16.refs_6_ = bf16[128,1024]{1,0:T(8,128)(2,1)S(1)} collective-permute-done((bf16[128,1024]{1,0:T(8,128)(2,1)S(1)}, bf16[128,1024]{1,0:T(8,128)(2,1)S(1)}, u32[]{:S(2)}, u32[]{:S(2)}) %collective-permute-start.16) | collective-permute-done | bytes 262176 | tf_op jit(solution)/shard_map/ppermute | solution.py:21
  79.2 1.8 %collective-permute-start.20 = (bf16[128,1024]{1,0:T(8,128)(2,1)S(1)}, bf16[128,1024]{1,0:T(8,128)(2,1)S(1)}, u32[]{:S(2)}, u32[]{:S(2)}) collective-permute-start(bf16[128,1024]{1,0:T(8,128)(2,1)S(1)} %get-tuple-element.115.refs_0_), channel_id=1, source_target_pairs={{0,24},{4,28},{8,16},{12,20},{16,8},{20,12},{24,0},{28,4},{1,25},{... | collective-permute-start | bytes 786440 | tf_op jit(solution)/shard_map/ppermute | solution.py:21
  82.8 6.7 %collective-permute-done.20.refs_3_ = bf16[128,1024]{1,0:T(8,128)(2,1)S(1)} collective-permute-done((bf16[128,1024]{1,0:T(8,128)(2,1)S(1)}, bf16[128,1024]{1,0:T(8,128)(2,1)S(1)}, u32[]{:S(2)}, u32[]{:S(2)}) %collective-permute-start.20) | collective-permute-done | bytes 262176 | tf_op jit(solution)/shard_map/ppermute | solution.py:21
  89.5 3.9 %collective-permute-done.19.refs_2_ = bf16[128,1024]{1,0:T(8,128)(2,1)S(1)} collective-permute-done((bf16[128,1024]{1,0:T(8,128)(2,1)S(1)}, bf16[128,1024]{1,0:T(8,128)(2,1)S(1)}, u32[]{:S(2)}, u32[]{:S(2)}) %collective-permute-start.19) | collective-permute-done | bytes 262176 | tf_op jit(solution)/shard_map/ppermute | solution.py:21
  98.3 1.7 %collective-permute-start.22 = (bf16[256,512]{1,0:T(8,128)(2,1)S(1)}, bf16[256,512]{1,0:T(8,128)(2,1)S(1)}, u32[]{:S(2)}, u32[]{:S(2)}) collective-permute-start(bf16[256,512]{1,0:T(8,128)(2,1)S(1)} %get-tuple-element.117), channel_id=1, source_target_pairs={{0,1},{1,0},{2,3},{3,2},{4,5},{5,4},{6,7},{7,6},{8,9},{9,8},{10,11... | collective-permute-start | bytes 786440 | tf_op jit(solution)/shard_map/ppermute | solution.py:21
  100.4 3.9 %collective-permute-done.26.refs_3_ = bf16[144,1024]{1,0:T(8,128)(2,1)S(1)} collective-permute-done((bf16[144,1024]{1,0:T(8,128)(2,1)S(1)}, bf16[144,1024]{1,0:T(8,128)(2,1)S(1)}, u32[]{:S(2)}, u32[]{:S(2)}) %collective-permute-start.26) | collective-permute-done | bytes 294944 | tf_op jit(solution)/shard_map/ppermute | solution.py:21
  104.3 5.8 %collective-permute-done.25.refs_2_ = bf16[144,1024]{1,0:T(8,128)(2,1)S(1)} collective-permute-done((bf16[144,1024]{1,0:T(8,128)(2,1)S(1)}, bf16[144,1024]{1,0:T(8,128)(2,1)S(1)}, u32[]{:S(2)}, u32[]{:S(2)}) %collective-permute-start.25) | collective-permute-done | bytes 294944 | tf_op jit(solution)/shard_map/ppermute | solution.py:21
  111.9 2.6 %collective-permute-done.27.away = bf16[512,1024]{1,0:T(8,128)(2,1)S(1)} collective-permute-done((bf16[512,1024]{1,0:T(8,128)(2,1)S(1)}, bf16[512,1024]{1,0:T(8,128)(2,1)S(1)}, u32[]{:S(2)}, u32[]{:S(2)}) %collective-permute-start.27) | collective-permute-done | bytes 1048608 | tf_op jit(solution)/shard_map/ppermute | solution.py:21
  117.2 1.7 %collective-permute-start.31 = (bf16[512,256]{1,0:T(8,128)(2,1)S(1)}, bf16[512,256]{1,0:T(8,128)(2,1)S(1)}, u32[]{:S(2)}, u32[]{:S(2)}) collective-permute-start(bf16[512,256]{1,0:T(8,128)(2,1)S(1)} %get-tuple-element.135), channel_id=1, source_target_pairs={{0,1},{1,0},{2,3},{3,2},{4,5},{5,4},{6,7},{7,6},{8,9},{9,8},{10,11... | collective-permute-start | bytes 786440 | tf_op jit(solution)/shard_map/ppermute | solution.py:21
  118.9 2.5 %one_back.1 = (f32[4,128,256]{2,1,0:T(8,128)S(1)}, bf16[4,128,256]{2,1,0:T(8,128)(2,1)S(1)}) custom-call(bf16[64,1024]{1,0:T(8,128)(2,1)S(1)} %get-tuple-element.86.inputs, bf16[256,1024]{1,0:T(8,128)(2,1)S(1)} %get-tuple-element.126.delta, bf16[2048,1024]{1,0:T(8,128)(2,1)S(1)} %one_slope.1.slope, f32[64,2048]{1,0:T(8,128)S(1)} %get-tuple-element.127.grad_four, ...), custom_call_target="tpu_custom_call" | custom-call | flops 99999997952 | tf_op jit(solution)/shard_map/one_back/pallas_call | solution.py:57
  121.5 2.2 %collective-permute-start.34 = (bf16[256,512]{1,0:T(8,128)(2,1)S(1)}, bf16[256,512]{1,0:T(8,128)(2,1)S(1)}, u32[]{:S(2)}, u32[]{:S(2)}) collective-permute-start(bf16[256,512]{1,0:T(8,128)(2,1)S(1)} %add_up.3), channel_id=1, source_target_pairs={{0,2},{1,3},{2,0},{3,1},{4,6},{5,7},{6,4},{7,5},{8,10},{9,11},{10,... | collective-permute-start | bytes 786440 | tf_op jit(solution)/shard_map/ppermute | solution.py:21
  123.7 1.9 %collective-permute-done.31.got = bf16[512,256]{1,0:T(8,128)(2,1)S(1)} collective-permute-done((bf16[512,256]{1,0:T(8,128)(2,1)S(1)}, bf16[512,256]{1,0:T(8,128)(2,1)S(1)}, u32[]{:S(2)}, u32[]{:S(2)}) %collective-permute-start.31) | collective-permute-done | bytes 262176 | tf_op jit(solution)/shard_map/ppermute | solution.py:21
  125.6 1.9 %collective-permute-start.32 = (bf16[512,256]{1,0:T(8,128)(2,1)S(1)}, bf16[512,256]{1,0:T(8,128)(2,1)S(1)}, u32[]{:S(2)}, u32[]{:S(2)}) collective-permute-start(bf16[512,256]{1,0:T(8,128)(2,1)S(1)} %get-tuple-element.137), channel_id=1, source_target_pairs={{0,1},{1,0},{2,3},{3,2},{4,5},{5,4},{6,7},{7,6},{8,9},{9,8},{10,11... | collective-permute-start | bytes 786440 | tf_op jit(solution)/shard_map/ppermute | solution.py:21
  127.6 3.5 %collective-permute-start.33 = (bf16[512,256]{1,0:T(8,128)(2,1)S(1)}, bf16[512,256]{1,0:T(8,128)(2,1)S(1)}, u32[]{:S(2)}, u32[]{:S(2)}) collective-permute-start(bf16[512,256]{1,0:T(8,128)(2,1)S(1)} %add_up.2), channel_id=1, source_target_pairs={{0,2},{1,3},{2,0},{3,1},{4,6},{5,7},{6,4},{7,5},{8,10},{9,11},{10,... | collective-permute-start | bytes 786440 | tf_op jit(solution)/shard_map/ppermute | solution.py:21
  132.0 4.2 %collective-permute-done.29.got = bf16[2,128,256]{2,1,0:T(8,128)(2,1)S(1)} collective-permute-done((bf16[2,128,256]{2,1,0:T(8,128)(2,1)S(1)}, bf16[2,128,256]{2,1,0:T(8,128)(2,1)S(1)}, u32[]{:S(2)}, u32[]{:S(2)}) %collective-permute-start.29) | collective-permute-done | bytes 131104 | tf_op jit(solution)/shard_map/ppermute | solution.py:21
  137.1 3.5 %collective-permute-done.30.got = bf16[1,128,256]{2,1,0:T(8,128)(2,1)S(1)} collective-permute-done((bf16[1,128,256]{2,1,0:T(8,128)(2,1)S(1)}, bf16[1,128,256]{2,1,0:T(8,128)(2,1)S(1)}, u32[]{:S(2)}, u32[]{:S(2)}) %collective-permute-start.30) | collective-permute-done | bytes 65568 | tf_op jit(solution)/shard_map/ppermute | solution.py:21
  140.7 8.8 %collective-permute-done.35.got = bf16[128,128]{1,0:T(8,128)(2,1)S(1)} collective-permute-done((bf16[128,128]{1,0:T(8,128)(2,1)S(1)}, bf16[128,128]{1,0:T(8,128)(2,1)S(1)}, u32[]{:S(2)}, u32[]{:S(2)}) %collective-permute-start.35) | collective-permute-done | bytes 32800 | tf_op jit(solution)/shard_map/ppermute | solution.py:21
  151.9 1.7 %collective-permute-done.36.refs_0_ = bf16[128,64]{1,0:T(8,128)(2,1)S(1)} collective-permute-done((bf16[128,64]{1,0:T(8,128)(2,1)S(1)}, bf16[128,64]{1,0:T(8,128)(2,1)S(1)}, u32[]{:S(2)}, u32[]{:S(2)}) %collective-permute-start.36) | collective-permute-done | bytes 16416 | tf_op jit(solution)/shard_map/ppermute | solution.py:21
  (102 shorter events, 39.6 us)
Async XLA Ops:
  1.7 21.5 %collective-permute-start.1 = (bf16[512,256]{1,0:T(8,128)(2,1)S(1)}, bf16[512,256]{1,0:T(8,128)(2,1)S(1)}, u32[]{:S(2)}, u32[]{:S(2)}) collective-permute-start(bf16[512,256]{1,0:T(8,128)(2,1)S(1)} %convert_element_type.6.refs_0_), channel_id=1, source_target_pairs={{0,2},{1,3},{2,0},{3,1},{4,6},{5,7},{6,4},{7,5},{8,10},{9,11},{10,... | collective-permute-start | bytes 786440 | tf_op jit(solution)/shard_map/ppermute | solution.py:21
  5.8 17.8 %collective-permute-start = (bf16[512,256]{1,0:T(8,128)(2,1)S(1)}, bf16[512,256]{1,0:T(8,128)(2,1)S(1)}, u32[]{:S(2)}, u32[]{:S(2)}) collective-permute-start(bf16[512,256]{1,0:T(8,128)(2,1)S(1)} %convert_element_type.6.refs_0_), channel_id=1, source_target_pairs={{0,1},{1,0},{2,3},{3,2},{4,5},{5,4},{6,7},{7,6},{8,9},{9,8},{10,11... | collective-permute-start | bytes 786440 | tf_op jit(solution)/shard_map/ppermute | solution.py:21
  9.0 10.6 %collective-permute-start.4 = (bf16[64,128]{1,0:T(8,128)(2,1)S(1)}, bf16[64,128]{1,0:T(8,128)(2,1)S(1)}, u32[]{:S(2)}, u32[]{:S(2)}) collective-permute-start(bf16[64,128]{1,0:T(8,128)(2,1)S(1)} %pack_small.1.refs_1_), channel_id=1, source_target_pairs={{0,3},{1,2},{2,1},{3,0},{4,7},{5,6},{6,5},{7,4},{8,11},{9,10},{10,... | collective-permute-start | bytes 49160 | tf_op jit(solution)/shard_map/ppermute | solution.py:21
  9.0 10.6 %collective-permute-start.3 = (bf16[64,128]{1,0:T(8,128)(2,1)S(1)}, bf16[64,128]{1,0:T(8,128)(2,1)S(1)}, u32[]{:S(2)}, u32[]{:S(2)}) collective-permute-start(bf16[64,128]{1,0:T(8,128)(2,1)S(1)} %pack_small.1.refs_1_), channel_id=1, source_target_pairs={{0,2},{1,3},{2,0},{3,1},{4,6},{5,7},{6,4},{7,5},{8,10},{9,11},{10,... | collective-permute-start | bytes 49160 | tf_op jit(solution)/shard_map/ppermute | solution.py:21
  10.9 8.7 %collective-permute-start.2 = (bf16[64,128]{1,0:T(8,128)(2,1)S(1)}, bf16[64,128]{1,0:T(8,128)(2,1)S(1)}, u32[]{:S(2)}, u32[]{:S(2)}) collective-permute-start(bf16[64,128]{1,0:T(8,128)(2,1)S(1)} %pack_small.1.refs_1_), channel_id=1, source_target_pairs={{0,1},{1,0},{2,3},{3,2},{4,5},{5,4},{6,7},{7,6},{8,9},{9,8},{10,11... | collective-permute-start | bytes 49160 | tf_op jit(solution)/shard_map/ppermute | solution.py:21
  19.5 19.3 %collective-permute-start.8 = (bf16[256,512]{1,0:T(8,128)(2,1)S(1)}, bf16[256,512]{1,0:T(8,128)(2,1)S(1)}, u32[]{:S(2)}, u32[]{:S(2)}) collective-permute-start(bf16[256,512]{1,0:T(8,128)(2,1)S(1)} %convert_element_type.7.refs_0_), channel_id=1, source_target_pairs={{0,2},{1,3},{2,0},{3,1},{4,6},{5,7},{6,4},{7,5},{8,10},{9,11},{10,... | collective-permute-start | bytes 786440 | tf_op jit(solution)/shard_map/ppermute | solution.py:21
  21.5 17.4 %collective-permute-start.7 = (bf16[256,512]{1,0:T(8,128)(2,1)S(1)}, bf16[256,512]{1,0:T(8,128)(2,1)S(1)}, u32[]{:S(2)}, u32[]{:S(2)}) collective-permute-start(bf16[256,512]{1,0:T(8,128)(2,1)S(1)} %convert_element_type.7.refs_0_), channel_id=1, source_target_pairs={{0,1},{1,0},{2,3},{3,2},{4,5},{5,4},{6,7},{7,6},{8,9},{9,8},{10,11... | collective-permute-start | bytes 786440 | tf_op jit(solution)/shard_map/ppermute | solution.py:21
  23.2 15.7 %collective-permute-start.5 = (bf16[512,256]{1,0:T(8,128)(2,1)S(1)}, bf16[512,256]{1,0:T(8,128)(2,1)S(1)}, u32[]{:S(2)}, u32[]{:S(2)}) collective-permute-start(bf16[512,256]{1,0:T(8,128)(2,1)S(1)} %collective-permute-done.1.refs_2_), channel_id=1, source_target_pairs={{0,1},{1,0},{2,3},{3,2},{4,5},{5,4},{6,7},{7,6},{8,9},{9,8},{10,11... | collective-permute-start | bytes 786440 | tf_op jit(solution)/shard_map/ppermute | solution.py:21
  41.5 8.5 %collective-permute-start.13 = (bf16[256,512]{1,0:T(8,128)(2,1)S(1)}, bf16[256,512]{1,0:T(8,128)(2,1)S(1)}, u32[]{:S(2)}, u32[]{:S(2)}) collective-permute-start(bf16[256,512]{1,0:T(8,128)(2,1)S(1)} %collective-permute-done.8.refs_1_), channel_id=1, source_target_pairs={{0,1},{1,0},{2,3},{3,2},{4,5},{5,4},{6,7},{7,6},{8,9},{9,8},{10,11... | collective-permute-start | bytes 786440 | tf_op jit(solution)/shard_map/ppermute | solution.py:21
  44.3 9.2 %collective-permute-start.10 = (bf16[128,1024]{1,0:T(8,128)(2,1)S(1)}, bf16[128,1024]{1,0:T(8,128)(2,1)S(1)}, u32[]{:S(2)}, u32[]{:S(2)}) collective-permute-start(bf16[128,1024]{1,0:T(8,128)(2,1)S(1)} %get-tuple-element.97), channel_id=1, source_target_pairs={{0,8},{4,12},{8,0},{12,4},{16,24},{20,28},{24,16},{28,20},{1,9},{5... | collective-permute-start | bytes 786440 | tf_op jit(solution)/shard_map/ppermute | solution.py:21
  45.9 13.8 %collective-permute-start.11 = (bf16[128,1024]{1,0:T(8,128)(2,1)S(1)}, bf16[128,1024]{1,0:T(8,128)(2,1)S(1)}, u32[]{:S(2)}, u32[]{:S(2)}) collective-permute-start(bf16[128,1024]{1,0:T(8,128)(2,1)S(1)} %get-tuple-element.98), channel_id=1, source_target_pairs={{0,16},{4,20},{8,24},{12,28},{16,0},{20,4},{24,8},{28,12},{1,17},{... | collective-permute-start | bytes 786440 | tf_op jit(solution)/shard_map/ppermute | solution.py:21
  47.4 12.3 %collective-permute-start.12 = (bf16[128,1024]{1,0:T(8,128)(2,1)S(1)}, bf16[128,1024]{1,0:T(8,128)(2,1)S(1)}, u32[]{:S(2)}, u32[]{:S(2)}) collective-permute-start(bf16[128,1024]{1,0:T(8,128)(2,1)S(1)} %get-tuple-element.99), channel_id=1, source_target_pairs={{0,24},{4,28},{8,16},{12,20},{16,8},{20,12},{24,0},{28,4},{1,25},{... | collective-permute-start | bytes 786440 | tf_op jit(solution)/shard_map/ppermute | solution.py:21
  60.2 18.0 %collective-permute-start.6 = (bf16[2,64,128]{2,1,0:T(8,128)(2,1)S(1)}, bf16[2,64,128]{2,1,0:T(8,128)(2,1)S(1)}, u32[]{:S(2)}, u32[]{:S(2)}) collective-permute-start(bf16[2,64,128]{2,1,0:T(8,128)(2,1)S(1)} %get-tuple-element.90.wanted), channel_id=1, source_target_pairs={{0,16},{4,20},{8,24},{12,28},{16,0},{20,4},{24,8},{28,12},{1,17},{... | collective-permute-start | bytes 98312 | tf_op jit(solution)/shard_map/ppermute | solution.py:21
  63.3 9.8 %collective-permute-start.15 = (bf16[128,1024]{1,0:T(8,128)(2,1)S(1)}, bf16[128,1024]{1,0:T(8,128)(2,1)S(1)}, u32[]{:S(2)}, u32[]{:S(2)}) collective-permute-start(bf16[128,1024]{1,0:T(8,128)(2,1)S(1)} %get-tuple-element.104), channel_id=1, source_target_pairs={{0,8},{4,12},{8,0},{12,4},{16,24},{20,28},{24,16},{28,20},{1,9},{5... | collective-permute-start | bytes 786440 | tf_op jit(solution)/shard_map/ppermute | solution.py:21
  64.5 12.2 %collective-permute-start.16 = (bf16[128,1024]{1,0:T(8,128)(2,1)S(1)}, bf16[128,1024]{1,0:T(8,128)(2,1)S(1)}, u32[]{:S(2)}, u32[]{:S(2)}) collective-permute-start(bf16[128,1024]{1,0:T(8,128)(2,1)S(1)} %get-tuple-element.105), channel_id=1, source_target_pairs={{0,16},{4,20},{8,24},{12,28},{16,0},{20,4},{24,8},{28,12},{1,17},{... | collective-permute-start | bytes 786440 | tf_op jit(solution)/shard_map/ppermute | solution.py:21
  65.4 12.8 %collective-permute-start.17 = (bf16[128,1024]{1,0:T(8,128)(2,1)S(1)}, bf16[128,1024]{1,0:T(8,128)(2,1)S(1)}, u32[]{:S(2)}, u32[]{:S(2)}) collective-permute-start(bf16[128,1024]{1,0:T(8,128)(2,1)S(1)} %get-tuple-element.106), channel_id=1, source_target_pairs={{0,24},{4,28},{8,16},{12,20},{16,8},{20,12},{24,0},{28,4},{1,25},{... | collective-permute-start | bytes 786440 | tf_op jit(solution)/shard_map/ppermute | solution.py:21
  79.2 10.2 %collective-permute-start.20 = (bf16[128,1024]{1,0:T(8,128)(2,1)S(1)}, bf16[128,1024]{1,0:T(8,128)(2,1)S(1)}, u32[]{:S(2)}, u32[]{:S(2)}) collective-permute-start(bf16[128,1024]{1,0:T(8,128)(2,1)S(1)} %get-tuple-element.115.refs_0_), channel_id=1, source_target_pairs={{0,24},{4,28},{8,16},{12,20},{16,8},{20,12},{24,0},{28,4},{1,25},{... | collective-permute-start | bytes 786440 | tf_op jit(solution)/shard_map/ppermute | solution.py:21
  81.0 12.3 %collective-permute-start.19 = (bf16[128,1024]{1,0:T(8,128)(2,1)S(1)}, bf16[128,1024]{1,0:T(8,128)(2,1)S(1)}, u32[]{:S(2)}, u32[]{:S(2)}) collective-permute-start(bf16[128,1024]{1,0:T(8,128)(2,1)S(1)} %get-tuple-element.115.refs_0_), channel_id=1, source_target_pairs={{0,16},{4,20},{8,24},{12,28},{16,0},{20,4},{24,8},{28,12},{1,17},{... | collective-permute-start | bytes 786440 | tf_op jit(solution)/shard_map/ppermute | solution.py:21
  81.7 11.7 %collective-permute-start.18 = (bf16[128,1024]{1,0:T(8,128)(2,1)S(1)}, bf16[128,1024]{1,0:T(8,128)(2,1)S(1)}, u32[]{:S(2)}, u32[]{:S(2)}) collective-permute-start(bf16[128,1024]{1,0:T(8,128)(2,1)S(1)} %get-tuple-element.115.refs_0_), channel_id=1, source_target_pairs={{0,8},{4,12},{8,0},{12,4},{16,24},{20,28},{24,16},{28,20},{1,9},{5... | collective-permute-start | bytes 786440 | tf_op jit(solution)/shard_map/ppermute | solution.py:21
  93.5 10.8 %collective-permute-start.26 = (bf16[144,1024]{1,0:T(8,128)(2,1)S(1)}, bf16[144,1024]{1,0:T(8,128)(2,1)S(1)}, u32[]{:S(2)}, u32[]{:S(2)}) collective-permute-start(bf16[144,1024]{1,0:T(8,128)(2,1)S(1)} %get-tuple-element.120.refs_0_), channel_id=1, source_target_pairs={{0,24},{4,28},{8,16},{12,20},{16,8},{20,12},{24,0},{28,4},{1,25},{... | collective-permute-start | bytes 884744 | tf_op jit(solution)/shard_map/ppermute | solution.py:21
  94.8 15.4 %collective-permute-start.25 = (bf16[144,1024]{1,0:T(8,128)(2,1)S(1)}, bf16[144,1024]{1,0:T(8,128)(2,1)S(1)}, u32[]{:S(2)}, u32[]{:S(2)}) collective-permute-start(bf16[144,1024]{1,0:T(8,128)(2,1)S(1)} %get-tuple-element.120.refs_0_), channel_id=1, source_target_pairs={{0,16},{4,20},{8,24},{12,28},{16,0},{20,4},{24,8},{28,12},{1,17},{... | collective-permute-start | bytes 884744 | tf_op jit(solution)/shard_map/ppermute | solution.py:21
  95.7 14.4 %collective-permute-start.24 = (bf16[144,1024]{1,0:T(8,128)(2,1)S(1)}, bf16[144,1024]{1,0:T(8,128)(2,1)S(1)}, u32[]{:S(2)}, u32[]{:S(2)}) collective-permute-start(bf16[144,1024]{1,0:T(8,128)(2,1)S(1)} %get-tuple-element.120.refs_0_), channel_id=1, source_target_pairs={{0,8},{4,12},{8,0},{12,4},{16,24},{20,28},{24,16},{28,20},{1,9},{5... | collective-permute-start | bytes 884744 | tf_op jit(solution)/shard_map/ppermute | solution.py:21
  98.3 11.8 %collective-permute-start.22 = (bf16[256,512]{1,0:T(8,128)(2,1)S(1)}, bf16[256,512]{1,0:T(8,128)(2,1)S(1)}, u32[]{:S(2)}, u32[]{:S(2)}) collective-permute-start(bf16[256,512]{1,0:T(8,128)(2,1)S(1)} %get-tuple-element.117), channel_id=1, source_target_pairs={{0,1},{1,0},{2,3},{3,2},{4,5},{5,4},{6,7},{7,6},{8,9},{9,8},{10,11... | collective-permute-start | bytes 786440 | tf_op jit(solution)/shard_map/ppermute | solution.py:21
  100.0 11.8 %collective-permute-start.23 = (bf16[256,512]{1,0:T(8,128)(2,1)S(1)}, bf16[256,512]{1,0:T(8,128)(2,1)S(1)}, u32[]{:S(2)}, u32[]{:S(2)}) collective-permute-start(bf16[256,512]{1,0:T(8,128)(2,1)S(1)} %get-tuple-element.118), channel_id=1, source_target_pairs={{0,1},{1,0},{2,3},{3,2},{4,5},{5,4},{6,7},{7,6},{8,9},{9,8},{10,11... | collective-permute-start | bytes 786440 | tf_op jit(solution)/shard_map/ppermute | solution.py:21
  117.2 8.4 %collective-permute-start.31 = (bf16[512,256]{1,0:T(8,128)(2,1)S(1)}, bf16[512,256]{1,0:T(8,128)(2,1)S(1)}, u32[]{:S(2)}, u32[]{:S(2)}) collective-permute-start(bf16[512,256]{1,0:T(8,128)(2,1)S(1)} %get-tuple-element.135), channel_id=1, source_target_pairs={{0,1},{1,0},{2,3},{3,2},{4,5},{5,4},{6,7},{7,6},{8,9},{9,8},{10,11... | collective-permute-start | bytes 786440 | tf_op jit(solution)/shard_map/ppermute | solution.py:21
  121.4 9.7 %collective-permute-start.28 = (bf16[4,128,256]{2,1,0:T(8,128)(2,1)S(1)}, bf16[4,128,256]{2,1,0:T(8,128)(2,1)S(1)}, u32[]{:S(2)}, u32[]{:S(2)}) collective-permute-start(bf16[4,128,256]{2,1,0:T(8,128)(2,1)S(1)} %get-tuple-element.129), channel_id=1, source_target_pairs={{0,4},{4,0},{8,12},{12,8},{16,20},{20,16},{24,28},{28,24},{1,5},{5... | collective-permute-start | bytes 786440 | tf_op jit(solution)/shard_map/ppermute | solution.py:21
  121.5 19.1 %collective-permute-start.34 = (bf16[256,512]{1,0:T(8,128)(2,1)S(1)}, bf16[256,512]{1,0:T(8,128)(2,1)S(1)}, u32[]{:S(2)}, u32[]{:S(2)}) collective-permute-start(bf16[256,512]{1,0:T(8,128)(2,1)S(1)} %add_up.3), channel_id=1, source_target_pairs={{0,2},{1,3},{2,0},{3,1},{4,6},{5,7},{6,4},{7,5},{8,10},{9,11},{10,... | collective-permute-start | bytes 786440 | tf_op jit(solution)/shard_map/ppermute | solution.py:21
  125.6 23.9 %collective-permute-start.32 = (bf16[512,256]{1,0:T(8,128)(2,1)S(1)}, bf16[512,256]{1,0:T(8,128)(2,1)S(1)}, u32[]{:S(2)}, u32[]{:S(2)}) collective-permute-start(bf16[512,256]{1,0:T(8,128)(2,1)S(1)} %get-tuple-element.137), channel_id=1, source_target_pairs={{0,1},{1,0},{2,3},{3,2},{4,5},{5,4},{6,7},{7,6},{8,9},{9,8},{10,11... | collective-permute-start | bytes 786440 | tf_op jit(solution)/shard_map/ppermute | solution.py:21
  127.6 21.9 %collective-permute-start.33 = (bf16[512,256]{1,0:T(8,128)(2,1)S(1)}, bf16[512,256]{1,0:T(8,128)(2,1)S(1)}, u32[]{:S(2)}, u32[]{:S(2)}) collective-permute-start(bf16[512,256]{1,0:T(8,128)(2,1)S(1)} %add_up.2), channel_id=1, source_target_pairs={{0,2},{1,3},{2,0},{3,1},{4,6},{5,7},{6,4},{7,5},{8,10},{9,11},{10,... | collective-permute-start | bytes 786440 | tf_op jit(solution)/shard_map/ppermute | solution.py:21
  131.1 5.0 %collective-permute-start.29 = (bf16[2,128,256]{2,1,0:T(8,128)(2,1)S(1)}, bf16[2,128,256]{2,1,0:T(8,128)(2,1)S(1)}, u32[]{:S(2)}, u32[]{:S(2)}) collective-permute-start(bf16[2,128,256]{2,1,0:T(8,128)(2,1)S(1)} %get-tuple-element.131), channel_id=1, source_target_pairs={{0,8},{4,12},{8,0},{12,4},{16,24},{20,28},{24,16},{28,20},{1,9},{5... | collective-permute-start | bytes 393224 | tf_op jit(solution)/shard_map/ppermute | solution.py:21
  136.2 4.3 %collective-permute-start.30 = (bf16[1,128,256]{2,1,0:T(8,128)(2,1)S(1)}, bf16[1,128,256]{2,1,0:T(8,128)(2,1)S(1)}, u32[]{:S(2)}, u32[]{:S(2)}) collective-permute-start(bf16[1,128,256]{2,1,0:T(8,128)(2,1)S(1)} %get-tuple-element.133), channel_id=1, source_target_pairs={{0,16},{4,20},{8,24},{12,28},{16,0},{20,4},{24,8},{28,12},{1,17},{... | collective-permute-start | bytes 196616 | tf_op jit(solution)/shard_map/ppermute | solution.py:21
  140.6 8.9 %collective-permute-start.35 = (bf16[128,128]{1,0:T(8,128)(2,1)S(1)}, bf16[128,128]{1,0:T(8,128)(2,1)S(1)}, u32[]{:S(2)}, u32[]{:S(2)}) collective-permute-start(bf16[128,128]{1,0:T(8,128)(2,1)S(1)} %get-tuple-element.140), channel_id=1, source_target_pairs={{0,2},{1,3},{2,0},{3,1},{4,6},{5,7},{6,4},{7,5},{8,10},{9,11},{10,... | collective-permute-start | bytes 98312 | tf_op jit(solution)/shard_map/ppermute | solution.py:21
  (19 other events, 171.9 us)

commit v4 on v3

--- a/solution.py
+++ b/solution.py
@@ -192,31 +192,68 @@
         out[:, k * span : (k + 1) * span] = dot(act[kept:], third[...], 1, 0).astype(bf16)
 
 
-def three_home(act, got, *refs, kept, rows):
-    half = kept // rows
-    thirds, own, sends = refs[:-half], refs[-half], refs[len(refs) - half + 1 :]
+def divided(kept, bit):
+    return [k for k in kept if not k & bit]
+
+
+def three_home(act, got, *refs, n_third, orders, kept):
+    thirds, own, outs = refs[:n_third], refs[n_third], refs[n_third + 1 :]
+    rows = own.shape[0]
     span = thirds[0].shape[1]
-    for k, third in enumerate(thirds):
-        at = slice(k * span, (k + 1) * span)
-        total = dot(act[:kept], third[...], 1, 0) + got[:, at].astype(f32)
-        own[:, at] = total[:rows]
-        for i, send in enumerate(sends):
-            send[:, at] = total[(i + 1) * rows : (i + 2) * rows].astype(bf16)
+    count = len(kept) * rows
+    blocks = {k: slice(i * rows, (i + 1) * rows) for i, k in enumerate(kept)}
+    half = own.shape[1] // 2
+    step = min(span, half)
+    for at in range(0, own.shape[1], step):
+        third = thirds[at // span]
+        total = dot(act[:count], third[:, at % span : at % span + step], 1, 0)
+        total = total + got[:, at : at + step].astype(f32)
+        own[:, at : at + step] = total[blocks[0]]
+        part = at // half
+        keep, send = outs[2 * part], outs[2 * part + 1]
+        put = slice(at - part * half, at - part * half + step)
+        bit = orders[part][0]
+        for i, k in enumerate(divided(kept, bit)):
+            if k:
+                keep[(i - 1) * rows : i * rows, put] = total[blocks[k]]
+            send[i * rows : (i + 1) * rows, put] = total[blocks[k | bit]].astype(bf16)
+
+
+def three_pass(own, *refs, stage, orders, kept):
+    ins, new_own, outs = refs[:4], refs[4], refs[5:]
+    rows = own.shape[0]
+    half = own.shape[1] // 2
+    for part, order in enumerate(orders):
+        here = list(kept)
+        for bit in order[:stage]:
+            here = divided(here, bit)
+        keep, got = ins[2 * part], ins[2 * part + 1]
+        at = slice(part * half, (part + 1) * half)
+        total = {}
+        for i, k in enumerate(here):
+            value = own[:, at] if k == 0 else keep[(i - 1) * rows : i * rows]
+            total[k] = value + got[i * rows : (i + 1) * rows].astype(f32)
+        new_own[:, at] = total[0]
+        bit = order[stage]
+        send = outs[2 * part + 1] if len(outs) == 4 else outs[part]
+        for i, k in enumerate(divided(here, bit)):
+            if k:
+                outs[2 * part][(i - 1) * rows : i * rows] = total[k]
+            send[i * rows : (i + 1) * rows] = total[k | bit].astype(bf16)
 
 
 def error_step(inputs, wanted, wanted_too, fourth, *refs, groups, half, per, n_in, n_out):
-    terms = refs[: groups * half]
+    terms = refs[: 3 * groups]
     act, pre = refs[-2:]
-    deltas, grad_four = refs[groups * half : groups * half + groups], refs[-3]
-    width = pre.shape[1] // groups
+    deltas, grad_four = refs[3 * groups : 5 * groups], refs[-3]
+    width = pre.shape[1] // groups // 2
     for g in range(groups):
-        at = slice(g * width, (g + 1) * width)
-        own, others = terms[g * half], terms[g * half + 1 : (g + 1) * half]
-        total = own[...]
-        for other in others:
-            total = total + other[...].astype(f32)
-        pre[:, at] = total
-        act[:, at] = gelu_act(total).astype(bf16)
+        for part in range(2):
+            at = slice((2 * g + part) * width, (2 * g + part + 1) * width)
+            total = terms[3 * g][:, part * width : (part + 1) * width]
+            total = total + terms[3 * g + 1 + part][...].astype(f32)
+            pre[:, at] = total
+            act[:, at] = gelu_act(total).astype(bf16)
     predicted = dot(fourth[...], act[...], 1, 1)
     number = jnp.sum(inputs[n_in : n_in + 1, :].astype(f32), axis=1, keepdims=True) / per
     mine = jnp.where(lax.axis_index("dp") >= half, 1, 0)
@@ -227,29 +264,49 @@
     error = jnp.where(row < n_out, error, jnp.zeros_like(error))
     grad_four[...] = dot(error, act[...], 1, 0)
     turned = error.astype(f32).T.astype(bf16)
-    for g in range(groups):
-        at = slice(g * width, (g + 1) * width)
-        delta = dot(turned, fourth[:, at], 1, 0) * gelu_slope(pre[:, at])
-        deltas[g][: delta.shape[0]] = delta.astype(bf16)
-
-
-def join(*refs):
-    rows = refs[-1].shape[0] // (len(refs) - 1)
-    for i, part in enumerate(refs[:-1]):
-        refs[-1][i * rows : (i + 1) * rows] = part[:rows]
-
-
-def three_back(act_t, home, away, *refs, ks, carried):
+    for i, delta in enumerate(deltas):
+        at = slice(i * width, (i + 1) * width)
+        value = dot(turned, fourth[:, at], 1, 0) * gelu_slope(pre[:, at])
+        delta[...] = value.astype(bf16)
+
+
+def join(own, got, out):
+    rows = own.shape[0]
+    out[:rows] = own[...]
+    filled = rows + got.shape[0]
+    out[rows:filled] = got[...]
+    if filled < out.shape[0]:
+        out[filled:] = jnp.zeros((out.shape[0] - filled, out.shape[1]), out.dtype)
+
+
+def join_all(*refs, held, evens, rows):
+    out = refs[-1]
+    half = out.shape[1] // 2
+    for i, blocks in enumerate(held):
+        for j, k in enumerate(blocks):
+            to = evens.index(k) * rows
+            at = slice(i // 2 * half, (i // 2 + 1) * half)
+            out[to : to + rows, at] = refs[i][j * rows : (j + 1) * rows]
+
+
+def three_first(act_t, home, away, grad, *, column):
+    rows = home.shape[0]
+    at = slice(column, column + grad.shape[1])
+    total = dot(act_t[:, :rows], home[:, at], 1, 0) + dot(act_t[:, rows:], away[:, at], 1, 0)
+    grad[...] = total.astype(grad.dtype)
+
+
+def three_back(act_t, home, away, *refs, ks, carried, ready):
     thirds = refs[: len(ks)]
     refs = refs[len(ks) :]
     before = refs[0] if carried else None
     refs = refs[carried:]
-    sum_two, grads, whole = refs[0], refs[1 : 1 + len(ks)], refs[-1]
+    sum_two, grads, whole = refs[0], refs[1 : 1 + len(ks) - ready], refs[-1]
     rows = home.shape[0]
     span = thirds[0].shape[1]
     whole[:rows] = home[...]
     whole[rows:] = away[...]
-    for i in range(len(ks)):
+    for i in range(len(grads)):
         at = slice(i * span, (i + 1) * span)
         grads[i][...] = dot(act_t[...], whole[:, at], 1, 0).astype(grads[i].dtype)
     total = before[...] if carried else None
@@ -259,12 +316,17 @@
     sum_two[...] = total
 
 
-def two_back(sum_two, slope, act_one, delta, *grads):
+def two_first(sum_two, slope, act_one, delta, grad):
     value = (sum_two[...] * slope[...]).astype(bf16)
     delta[...] = value
-    span = act_one.shape[0] // len(grads)
+    grad[...] = dot(act_one[act_one.shape[0] - grad.shape[0] :], value, 1, 1).astype(grad.dtype)
+
+
+def two_back(delta, act_one, *grads):
+    span = grads[0].shape[0]
     for k, grad in enumerate(grads):
-        grad[...] = dot(act_one[k * span : (k + 1) * span], value, 1, 1).astype(grad.dtype)
+        part = act_one[k * span : (k + 1) * span]
+        grad[...] = dot(part, delta[...], 1, 1).astype(grad.dtype)
 
 
 def split_dp(parts, step, keep, send):
@@ -275,7 +337,7 @@
         send[i] = jnp.where(bit, even, odd).astype(bf16)
 
 
-def one_back(inputs, delta, slope, grad_four, *refs, n_mp, n_dp, places):
+def one_back(inputs, delta, slope, grad_four, *refs, n_mp, n_dp, places, n_in, n_out):
     seconds, (keep, send) = refs[:n_mp], refs[n_mp:]
     span = seconds[0].shape[0]
     wide = span // n_dp
@@ -285,7 +347,11 @@
         value = (value * slope[k * span : (k + 1) * span].astype(f32)).astype(bf16)
         grad_one = dot(inputs[...], value, 1, 1)
         at = places.index(k) * span
-        whole.append(jnp.concatenate([grad_one, grad_four[:, at : at + span]], 0))
+        pieces = [grad_one[:n_in], grad_four[:n_out, at : at + span]]
+        spare = keep.shape[1] - n_in - n_out
+        if spare:
+            pieces.append(jnp.zeros((spare, span), f32))
+        whole.append(jnp.concatenate(pieces, 0))
     parts = [
         jnp.concatenate([value[:, d * wide : (d + 1) * wide] for value in whole], 1)
         for d in range(n_dp)
@@ -318,7 +384,6 @@
 def update_small(own, *refs):
     gots, (w_in, w_out, m_in, m_out), outs = refs[:-8], refs[-8:-4], refs[-4:]
     nw_in, nw_out, nm_in, nm_out = outs
-    tall = own.shape[0] // 2
     total = own[...]
     for got in gots:
         total = total + got[...].astype(f32)
@@ -326,7 +391,7 @@
     mom = momentum_decay * m_in[...] + total[:n_in]
     nm_in[...] = mom
     nw_in[...] = w_in[...] - learn_rate * mom
-    mom = momentum_decay * m_out[...] + total[tall : tall + n_out]
+    mom = momentum_decay * m_out[...] + total[n_in : n_in + n_out]
     nm_out[...] = mom
     nw_out[...] = w_out[...] - learn_rate * mom
 
@@ -357,11 +422,13 @@
         held[k] = swap(after(ready, held[parent(k)])[0], "mp", low_bit(k))
 
 
-def summed(held, ks, sent):
+def summed(held, ks, firsts=None):
     gots = []
     for k in sorted((k for k in ks if k), key=lambda k: (low_bit(k), -k)):
-        got = sent[k] if k in sent else swap(held[k], "mp", low_bit(k))
+        got = swap(held[k], "mp", low_bit(k))
         to = parent(k)
+        if firsts is not None:
+            firsts.append(got)
         if to:
             held[to] = on_core(add_up, shaped(got.shape, bf16), [held[to], got], "add_up")
         else:
@@ -396,35 +463,35 @@
     width = hidden * n_mp
     n_mid, n_top = weight_mid.shape[1], weight_top.shape[1]
     planes = range(n_mp)
-    groups = [list(planes[::2]), list(planes[1::2])]
+    groups = [list(planes[: n_mp // 2]), list(planes[n_mp // 2 :])]
     places = [k for ks in groups for k in ks]
     part = functools.partial
 
     piece = on_core(
         part(pack_small, tall=tall), shaped((tall, lanes), bf16), [weight_in, weight_out.T], "pack_small"
     )
+    pieces = [piece] + [swap(piece, "mp", k) for k in planes[1:]]
     second = gathered(weight_mid.astype(bf16), n_mp)
     picked, wanted = on_core(
         part(pick_rows, tall=tall, rows=rows, per=per),
         [shaped((2 * tall, lanes), bf16), shaped((2, tall, rows), bf16)],
         [samples, targets],
         "pick_rows",
-        scalars=[counts],
-    )
-    pieces = [piece] + [swap(piece, "mp", k) for k in planes[1:]]
+        scalars=after(pieces, counts),
+        flops=LONG,
+    )
     top = after((picked, pieces), weight_top.astype(bf16))[0]
     third = gathered(top, n_mp)
-    passed_on(second, n_mp, (picked, pieces))
-
-    early = [second[k] for k in planes if k and not parent(k)]
+
     packed = on_core(
         pack_all,
         shaped(((2 + n_mp) * tall, lanes), bf16),
-        [picked, *after(early, *pieces)],
+        [picked, *pieces],
         "pack_all",
     )
     wanted = [wanted, swap(wanted, "dp", half)]
     held = lax.all_gather(packed, "dp")
+    passed_on(second, n_mp, held)
     inputs, first, fourth = on_core(
         part(place_small, tall=tall, rows=rows, wide=wide, places=places),
         [shaped((tall, n_rows), bf16), shaped((tall, width), bf16), shaped((tall, width), bf16)],
@@ -442,71 +509,142 @@
         "two_forward",
     )
     passed_on(third, n_mp, act_one)
+    evens = list(range(0, n_dp, 2))
+    bits = [1 << i for i in range(1, n_dp.bit_length() - 1)]
+    orders = [bits, bits[::-1]]
     kept = half * rows
+    slope_one = on_core(
+        part(one_slope, tile=128), shaped((width, n_rows), bf16), [inputs, first], "one_slope",
+        flops=12_000_000_000,
+    )
     terms = []
-    ahead = [third[k] for k in planes if k and not parent(k)]
+    ahead = [wanted[1]] + [third[k] for k in planes if k and not parent(k)]
     for ks in groups:
         cols = len(ks) * n_top
         weights = after(ahead, *[third[k] for k in ks])
         away = on_core(
             part(three_away, kept=kept), shaped((kept, cols), bf16), [act_two, *weights], "three_away"
         )
-        own, *sends = on_core(
-            part(three_home, kept=kept, rows=rows),
-            [shaped((rows, cols), f32)] + [shaped((rows, cols), bf16)] * (half - 1),
+        left = half // 2
+        kinds = [shaped(((left - 1) * rows, cols // 2), f32), shaped((left * rows, cols // 2), bf16)]
+        own, *halves = on_core(
+            part(three_home, n_third=len(ks), orders=orders, kept=evens),
+            [shaped((rows, cols), f32)] + kinds * 2,
             [act_two, swap(away, "dp", 1), *weights],
             "three_home",
         )
-        ahead = [swap(send, "dp", 2 * (i + 1)) for i, send in enumerate(sends)]
-        terms += [own, *ahead]
-    slope_one = on_core(
-        part(one_slope, tile=128), shaped((width, n_rows), bf16), [inputs, first], "one_slope",
-        flops=12_000_000_000,
-    )
+        ahead = []
+        for stage in range(len(bits)):
+            sends = halves[1::2] if len(halves) == 4 else halves
+            gots = [swap(send, "dp", order[stage]) for send, order in zip(sends, orders)]
+            ahead = ahead or [slope_one, *gots]
+            if stage + 1 == len(bits):
+                break
+            keeps, left = halves[::2], left // 2
+            kinds = [shaped((left * rows, cols // 2), bf16)]
+            if left > 1:
+                kinds = [shaped(((left - 1) * rows, cols // 2), f32)] + kinds
+            own, *halves = on_core(
+                part(three_pass, stage=stage + 1, orders=orders, kept=evens),
+                [shaped((rows, cols), f32)] + kinds * 2,
+                [own, keeps[0], gots[0], keeps[1], gots[1]],
+                "three_pass",
+            )
+        terms += [own, *gots]
     *deltas, grad_four = on_core(
         part(error_step, groups=len(groups), half=half, per=per, n_in=n_in, n_out=n_out),
-        [shaped((rows + 16 * (g == 0), len(ks) * n_top), bf16) for g, ks in enumerate(groups)] + [shaped((tall, width), f32)],
-        [inputs, *wanted, fourth, *after(slope_one, *terms)],
+        [shaped((rows, len(ks) * n_top // 2), bf16) for ks in groups for _ in range(2)]
+        + [shaped((tall, width), f32)],
+        [inputs, *wanted, fourth, *terms],
         "error_step",
         scratch=[pltpu.VMEM((rows, width), bf16), pltpu.VMEM((rows, width), f32)],
     )
 
-    sum_two, grad_three, sent = None, {}, []
+    sum_two, grad_three = None, {}
+    gathers = {}
     for g in reversed(range(len(groups))):
-        ks = groups[g]
-        home = [deltas[g]] + [swap(deltas[g], "dp", 2 * i) for i in range(1, half)]
-        if sent:
-            home = after((sum_two, sent), *home)
-        home = on_core(join, shaped((kept, deltas[g].shape[1]), bf16), home, "join")
+        held, kinds = [[0], [0]], []
+        arrays = list(deltas[2 * g : 2 * g + 2])
+        cols = arrays[0].shape[1]
+        for stage in range(len(bits)):
+            last = stage + 1 == len(bits)
+            gots = [swap(value, "dp", order[stage]) for value, order in zip(arrays, orders)]
+            more = [[k | order[stage] for k in blocks] for blocks, order in zip(held, orders)]
+            if last:
+                break
+            held = [a + b for a, b in zip(held, more)]
+            spare = 16 * (g == 0 and stage + 2 == len(bits))
+            arrays = [
+                on_core(join, shaped((len(blocks) * rows + spare, cols), bf16), [own, got], "join")
+                for blocks, own, got in zip(held, arrays, gots)
+            ]
+            gathers[g, stage] = gots
+        gathers[g] = (arrays, gots, [held[0], more[0], held[1], more[1]])
+    for g in reversed(range(len(groups))):
+        ks, carried = groups[g], sum_two is not None
+        arrays, gots, blocks = gathers[g]
+        if carried:
+            gots = after((sum_two, firsts[0]), *gots)
+        elif (0, 0) in gathers:
+            gots = after(gathers[0, 0], *gots)
+        home = on_core(
+            part(join_all, held=blocks, evens=evens, rows=rows),
+            shaped((kept, len(ks) * n_top), bf16),
+            [arrays[0], gots[0], arrays[1], gots[1]],
+            "join_all",
+        )
         away = swap(home, "dp", 1)
-        carry = [sum_two] if sent else []
+        carry = [sum_two] if carried else []
+        if not carried:
+            grad_three[ks[-1]] = on_core(
+                part(three_first, column=(len(ks) - 1) * n_top),
+                shaped((n_mid, n_top), bf16),
+                [act_two_t, home, away],
+                "three_first",
+            )
+        made = ks if carried else ks[:-1]
         sum_two, *grads = on_core(
-            part(three_back, ks=ks, carried=len(carry)),
+            part(three_back, ks=ks, carried=len(carry), ready=len(ks) - len(made)),
             [shaped((n_mid, n_rows), f32)]
-            + [shaped((n_mid, n_top), bf16 if k else f32) for k in ks],
+            + [shaped((n_mid, n_top), bf16 if k else f32) for k in made],
             [act_two_t, home, away] + [third[k] for k in ks] + carry,
             "three_back",
             scratch=[pltpu.VMEM((n_rows, len(ks) * n_top), bf16)],
         )
-        grad_three.update(zip(ks, grads))
-        if not sent:
-            sent = [swap(grad_three[k], "mp", 1) for k in ks]
-    gots_three = summed(grad_three, planes, dict(zip(groups[1], sent)))
-    grad_two = {}
-    delta_two, *grads = on_core(
+        grad_three.update(zip(made, grads))
+        if not carried:
+            firsts = []
+            gots_three = summed(grad_three, ks, firsts)
+    delta_two, farthest = on_core(
+        two_first,
+        [shaped((n_mid, n_rows), bf16), shaped((hidden, n_mid), bf16)],
+        [sum_two, slope_two, act_one],
+        "two_first",
+        flops=LONG,
+    )
+    grads = on_core(
         two_back,
-        [shaped((n_mid, n_rows), bf16)] + [shaped((hidden, n_mid), bf16 if k else f32) for k in planes],
-        [sum_two, slope_two, act_one],
+        [shaped((hidden, n_mid), bf16 if k else f32) for k in planes[:-1]],
+        [delta_two, act_one],
         "two_back",
-        flops=LONG,
-    )
-    grad_two = dict(zip(planes, grads))
-    farthest = swap(grad_two[n_mp - 1], "mp", 1)
-    grad_two[1] = after(farthest, grad_two[1])[0]
-    gots_two = summed(grad_two, planes, {n_mp - 1: farthest})
-    shape = (half, 2 * tall, n_mp * wide)
+    )
+    grad_two = dict(zip(planes, [*grads, farthest]))
+    far = n_mp - 1
+    got = swap(grad_two[far], "mp", 1)
+    grad_two[far - 1] = on_core(add_up, shaped(got.shape, bf16), [grad_two[far - 1], got], "add_up")
+    grad_two[1], grad_three[1] = after(grad_two[far - 1], grad_two[1], grad_three[1])
+    gots_two = summed(grad_two, planes[: n_mp - 1])
+    early_three = list(gots_three)
+    gots_three += summed(grad_three, groups[0])
+    like = lambda value: shaped(value.shape, f32)
+    new_top, mom_top = on_core(
+        update_big, [like(weight_top)] * 2, [weight_top, moment_top, grad_three[0], *gots_three], "update_top",
+        flops=2_000_000_000,
+    )
+    n_small = up_to(n_in + n_out, 16)
+    shape = (half, n_small, n_mp * wide)
     keep, send = on_core(
-        part(one_back, n_mp=n_mp, n_dp=n_dp, places=places),
+        part(one_back, n_mp=n_mp, n_dp=n_dp, places=places, n_in=n_in, n_out=n_out),
         [shaped(shape, f32), shaped(shape, bf16)],
         [inputs, delta_two, slope_one, grad_four] + [second[k] for k in planes],
         "one_back",
@@ -515,6 +653,8 @@
     step = 1
     while step < half:
         got = swap(send, "dp", step)
+        if step == 1:
+            got = after(early_three, got)[0]
         step *= 2
         shape = (shape[0] // 2, *shape[1:])
         keep, send = on_core(
@@ -524,7 +664,7 @@
     half_mp = n_mp // 2 * wide
     keep, send = on_core(
         last_half,
-        [shaped((2 * tall, half_mp), f32), shaped((2 * tall, half_mp), bf16)],
+        [shaped((n_small, half_mp), f32), shaped((n_small, half_mp), bf16)],
         [keep, got],
         "last_half",
     )
@@ -533,25 +673,20 @@
         got = swap(send, "mp", step)
         step //= 2
         if step:
-            got = after((gots_two, gots_three), got)[0]
+            got = after((gots_two, mom_top), got)[0]
         if step:
             half_mp = step * wide
             keep, send = on_core(
                 last_half_mp,
-                [shaped((2 * tall, half_mp), f32), shaped((2 * tall, half_mp), bf16)],
+                [shaped((n_small, half_mp), f32), shaped((n_small, half_mp), bf16)],
                 [keep, got],
                 "last_half_mp",
             )
     gots_small = [got]
 
-    like = lambda value: shaped(value.shape, f32)
     flat = (weight_in, weight_out.T, moment_in, moment_out.T)
     new_in, new_out, mom_in, mom_out = on_core(
         update_small, [like(value) for value in flat], [keep, *gots_small, *flat], "update_small"
-    )
-    new_top, mom_top = on_core(
-        update_big, [like(weight_top)] * 2, [weight_top, moment_top, grad_three[0], *gots_three], "update_top",
-        flops=2_000_000_000,
     )
     new_mid, mom_mid = on_core(
         update_big, [like(weight_mid)] * 2, [weight_mid, moment_mid, grad_two[0], *gots_two], "update_mid"

time: 155 us -> 146 us (0.942)
  waiting for transfers between devices: 65.4 us -> 47.5 us
  starting transfers between devices: 45.3 us -> 52.8 us
  Pallas kernels: 25.3 us -> 27.7 us
    ppermute x37 -> x41, waiting for transfers between devices: 65.4 us -> 47.5 us  [swap(): return lax.ppermute(value, axis, [(at, at ^ step) for at in range(count)])]
    ppermute x37 -> x41, starting transfers between devices: 45.3 us -> 52.8 us  [swap(): return lax.ppermute(value, axis, [(at, at ^ step) for at in range(count)])]
    pallas_call x27 -> x35, Pallas kernels: 25.3 us -> 27.7 us  [on_core(): pl.pallas_call(body, out_shape=outs, in_specs=[pl.BlockSpec(memory_space=...]
    unnamed x30 -> x24, local copies, waits for them, and re-layouts: 4.09 us -> 4.37 us
  transfers between devices with their start and end apart: 37 -> 41, of which waited for: 20 -> 21; matrix products, arithmetic and copies ran while one was open for 2% -> 2% of each run, Pallas kernels for 12% -> 16%
where the time goes in v4:
time: 146 us
  starting transfers between devices  52.8 us (36%)
  waiting for transfers between devices  47.5 us (33%)
  Pallas kernels  27.7 us (19%)
  blocking collectives  10.6 us (7%)
  local copies, waits for them, and re-layouts  4.37 us (3%)
  between operations  1.72 us (1%)
    ppermute x41, starting transfers between devices, swap(): return lax.ppermute(value, axis, [(at, at ^ step) for at in range(count)])  52.8 us
    ppermute x41, waiting for transfers between devices, swap(): return lax.ppermute(value, axis, [(at, at ^ step) for at in range(count)])  47.5 us
    pallas_call x35, Pallas kernels, on_core(): pl.pallas_call(body, out_shape=outs, in_specs=[pl.BlockSpec(memory_space=...  27.7 us
    all_gather x1, blocking collectives, on_device(): held = lax.all_gather(packed, 'dp')  10.6 us
    unnamed x24, local copies, waits for them, and re-layouts  4.37 us
  transfers between devices with their start and end apart: 41, of which 21 were waited for; matrix products, arithmetic and copies ran while one was open for 2% of the time, Pallas kernels for 16%

profile of v4, /device:TPU:0, one launch (start us, length us, event | category | flops | bytes accessed | tf_op | source)
XLA Modules:
  0.0 145.8 jit_solution(8944430785400034837)
XLA Ops:
  2.2 5.1 %collective-permute-start.2 = (bf16[64,128]{1,0:T(8,128)(2,1)S(1)}, bf16[64,128]{1,0:T(8,128)(2,1)S(1)}, u32[]{:S(2)}, u32[]{:S(2)}) collective-permute-start(bf16[64,128]{1,0:T(8,128)(2,1)S(1)} %pack_small.1.refs_1_), channel_id=1, source_target_pairs={{0,3},{1,2},{2,1},{3,0},{4,7},{5,6},{6,5},{7,4},{8,11},{9,10},{10,... | collective-permute-start | bytes 49160 | tf_op jit(solution)/shard_map/ppermute | solution.py:21
  9.0 2.4 %collective-permute-start.4 = (bf16[512,256]{1,0:T(8,128)(2,1)S(1)}, bf16[512,256]{1,0:T(8,128)(2,1)S(1)}, u32[]{:S(2)}, u32[]{:S(2)}) collective-permute-start(bf16[512,256]{1,0:T(8,128)(2,1)S(1)} %convert_element_type.6.refs_0_), channel_id=1, source_target_pairs={{0,2},{1,3},{2,0},{3,1},{4,6},{5,7},{6,4},{7,5},{8,10},{9,11},{10,... | collective-permute-start | bytes 786440 | tf_op jit(solution)/shard_map/ppermute | solution.py:21
  11.3 2.0 %collective-permute-start.3 = (bf16[512,256]{1,0:T(8,128)(2,1)S(1)}, bf16[512,256]{1,0:T(8,128)(2,1)S(1)}, u32[]{:S(2)}, u32[]{:S(2)}) collective-permute-start(bf16[512,256]{1,0:T(8,128)(2,1)S(1)} %convert_element_type.6.refs_0_), channel_id=1, source_target_pairs={{0,1},{1,0},{2,3},{3,2},{4,5},{5,4},{6,7},{7,6},{8,9},{9,8},{10,11... | collective-permute-start | bytes 786440 | tf_op jit(solution)/shard_map/ppermute | solution.py:21
  17.7 10.6 %all-gather = bf16[3072,128]{1,0:T(8,128)(2,1)S(1)} all-gather(bf16[384,128]{1,0:T(8,128)(2,1)S(1)} %pack_all.1), channel_id=2, replica_groups=mesh['dp'=8,'mp'=4] {'dp'}, dimensions={0}, use_global_device_ids=true | all-gather | bytes 884736 | tf_op jit(solution)/shard_map/all_gather | solution.py:493
  31.3 4.7 %one_forward.1.act_one = bf16[2048,1024]{1,0:T(8,128)(2,1)S(1)} custom-call(bf16[64,1024]{1,0:T(8,128)(2,1)S(1)} %get-tuple-element.83.inputs, bf16[64,2048]{1,0:T(8,128)(2,1)S(1)} %get-tuple-element.84.first), custom_call_target="tpu_custom_call" | custom-call | tf_op jit(solution)/shard_map/one_forward/pallas_call | solution.py:57
  36.0 4.2 %collective-permute-done.5.refs_3_ = bf16[512,256]{1,0:T(8,128)(2,1)S(1)} collective-permute-done((bf16[512,256]{1,0:T(8,128)(2,1)S(1)}, bf16[512,256]{1,0:T(8,128)(2,1)S(1)}, u32[]{:S(2)}, u32[]{:S(2)}) %collective-permute-start.5) | collective-permute-done | bytes 262176 | tf_op jit(solution)/shard_map/ppermute | solution.py:21
  40.2 1.7 %two_forward.1 = (bf16[1024,256]{1,0:T(8,128)(2,1)S(1)}, bf16[256,1024]{1,0:T(8,128)(2,1)S(1)}, f32[256,1024]{1,0:T(8,128)S(1)}) custom-call(bf16[2048,1024]{1,0:T(8,128)(2,1)S(1)} %one_forward.1.act_one, bf16[512,256]{1,0:T(8,128)(2,1)S(1)} %convert_element_type.6.refs_0_, bf16[512,256]{1,0:T(8,128)(2,1)S(1)} %collective-permute-done.3.refs_1_, ...), custom_call_target="tpu_custom_call" | custom-call | tf_op jit(solution)/shard_map/two_forward/pallas_call | solution.py:57
  48.6 6.4 %one_slope.1.slope = bf16[2048,1024]{1,0:T(8,128)(2,1)S(1)} custom-call(bf16[64,1024]{1,0:T(8,128)(2,1)S(1)} %get-tuple-element.83.inputs, bf16[64,2048]{1,0:T(8,128)(2,1)S(1)} %get-tuple-element.84.first), custom_call_target="tpu_custom_call" | custom-call | flops 12000000000 | tf_op jit(solution)/shard_map/one_slope/pallas_call | solution.py:57
  55.6 2.6 %collective-permute-done.15.got = bf16[512,1024]{1,0:T(8,128)(2,1)S(1)} collective-permute-done((bf16[512,1024]{1,0:T(8,128)(2,1)S(1)}, bf16[512,1024]{1,0:T(8,128)(2,1)S(1)}, u32[]{:S(2)}, u32[]{:S(2)}) %collective-permute-start.15) | collective-permute-done | bytes 1048608 | tf_op jit(solution)/shard_map/ppermute | solution.py:21
  63.0 4.9 %collective-permute-done.16.refs_1_ = bf16[256,512]{1,0:T(8,128)(2,1)S(1)} collective-permute-done((bf16[256,512]{1,0:T(8,128)(2,1)S(1)}, bf16[256,512]{1,0:T(8,128)(2,1)S(1)}, u32[]{:S(2)}, u32[]{:S(2)}) %collective-permute-start.16) | collective-permute-done | bytes 262176 | tf_op jit(solution)/shard_map/ppermute | solution.py:21
  68.6 1.6 %collective-permute-start.18 = (bf16[128,512]{1,0:T(8,128)(2,1)S(1)}, bf16[128,512]{1,0:T(8,128)(2,1)S(1)}, u32[]{:S(2)}, u32[]{:S(2)}) collective-permute-start(bf16[128,512]{1,0:T(8,128)(2,1)S(1)} %get-tuple-element.110), channel_id=1, source_target_pairs={{0,16},{4,20},{8,24},{12,28},{16,0},{20,4},{24,8},{28,12},{1,17},{... | collective-permute-start | bytes 393224 | tf_op jit(solution)/shard_map/ppermute | solution.py:21
  71.7 1.9 %collective-permute-done.18.refs_4_ = bf16[128,512]{1,0:T(8,128)(2,1)S(1)} collective-permute-done((bf16[128,512]{1,0:T(8,128)(2,1)S(1)}, bf16[128,512]{1,0:T(8,128)(2,1)S(1)}, u32[]{:S(2)}, u32[]{:S(2)}) %collective-permute-start.18) | collective-permute-done | bytes 131104 | tf_op jit(solution)/shard_map/ppermute | solution.py:21
  78.2 3.7 %collective-permute-done.24.got = bf16[128,512]{1,0:T(8,128)(2,1)S(1)} collective-permute-done((bf16[128,512]{1,0:T(8,128)(2,1)S(1)}, bf16[128,512]{1,0:T(8,128)(2,1)S(1)}, u32[]{:S(2)}, u32[]{:S(2)}) %collective-permute-start.24) | collective-permute-done | bytes 131104 | tf_op jit(solution)/shard_map/ppermute | solution.py:21
  81.9 1.8 %collective-permute-start.25 = (bf16[256,512]{1,0:T(8,128)(2,1)S(1)}, bf16[256,512]{1,0:T(8,128)(2,1)S(1)}, u32[]{:S(2)}, u32[]{:S(2)}) collective-permute-start(bf16[256,512]{1,0:T(8,128)(2,1)S(1)} %join.6.refs_2_), channel_id=1, source_target_pairs={{0,8},{4,12},{8,0},{12,4},{16,24},{20,28},{24,16},{28,20},{1,9},{5... | collective-permute-start | bytes 786440 | tf_op jit(solution)/shard_map/ppermute | solution.py:21
  86.7 3.1 %collective-permute-done.20.got = bf16[128,512]{1,0:T(8,128)(2,1)S(1)} collective-permute-done((bf16[128,512]{1,0:T(8,128)(2,1)S(1)}, bf16[128,512]{1,0:T(8,128)(2,1)S(1)}, u32[]{:S(2)}, u32[]{:S(2)}) %collective-permute-start.20) | collective-permute-done | bytes 131104 | tf_op jit(solution)/shard_map/ppermute | solution.py:21
  89.8 1.8 %collective-permute-done.22.got = bf16[128,512]{1,0:T(8,128)(2,1)S(1)} collective-permute-done((bf16[128,512]{1,0:T(8,128)(2,1)S(1)}, bf16[128,512]{1,0:T(8,128)(2,1)S(1)}, u32[]{:S(2)}, u32[]{:S(2)}) %collective-permute-start.22) | collective-permute-done | bytes 131104 | tf_op jit(solution)/shard_map/ppermute | solution.py:21
  92.8 1.6 %collective-permute-start.29 = (bf16[272,512]{1,0:T(8,128)(2,1)S(1)}, bf16[272,512]{1,0:T(8,128)(2,1)S(1)}, u32[]{:S(2)}, u32[]{:S(2)}) collective-permute-start(bf16[272,512]{1,0:T(8,128)(2,1)S(1)} %join.7.refs_2_), channel_id=1, source_target_pairs={{0,8},{4,12},{8,0},{12,4},{16,24},{20,28},{24,16},{28,20},{1,9},{5... | collective-permute-start | bytes 835592 | tf_op jit(solution)/shard_map/ppermute | solution.py:21
  97.2 3.8 %collective-permute-done.28.refs_1_ = bf16[272,512]{1,0:T(8,128)(2,1)S(1)} collective-permute-done((bf16[272,512]{1,0:T(8,128)(2,1)S(1)}, bf16[272,512]{1,0:T(8,128)(2,1)S(1)}, u32[]{:S(2)}, u32[]{:S(2)}) %collective-permute-start.28) | collective-permute-done | bytes 278560 | tf_op jit(solution)/shard_map/ppermute | solution.py:21
  101.6 1.7 %collective-permute-done.27.got = bf16[256,512]{1,0:T(8,128)(2,1)S(1)} collective-permute-done((bf16[256,512]{1,0:T(8,128)(2,1)S(1)}, bf16[256,512]{1,0:T(8,128)(2,1)S(1)}, u32[]{:S(2)}, u32[]{:S(2)}) %collective-permute-start.27) | collective-permute-done | bytes 262176 | tf_op jit(solution)/shard_map/ppermute | solution.py:21
  104.2 1.8 %collective-permute-start.31 = (bf16[256,512]{1,0:T(8,128)(2,1)}, bf16[256,512]{1,0:T(8,128)(2,1)}, u32[]{:S(2)}, u32[]{:S(2)}) collective-permute-start(bf16[256,512]{1,0:T(8,128)(2,1)} %add_up.2), channel_id=1, source_target_pairs={{0,2},{1,3},{2,0},{3,1},{4,6},{5,7},{6,4},{7,5},{8,10},{9,11},{10,... | collective-permute-start | bytes 786440 | tf_op jit(solution)/shard_map/ppermute | solution.py:21
  107.9 1.7 %collective-permute-start.35 = (bf16[512,256]{1,0:T(8,128)(2,1)S(1)}, bf16[512,256]{1,0:T(8,128)(2,1)S(1)}, u32[]{:S(2)}, u32[]{:S(2)}) collective-permute-start(bf16[512,256]{1,0:T(8,128)(2,1)S(1)} %get-tuple-element.135), channel_id=1, source_target_pairs={{0,1},{1,0},{2,3},{3,2},{4,5},{5,4},{6,7},{7,6},{8,9},{9,8},{10,11... | collective-permute-start | bytes 786440 | tf_op jit(solution)/shard_map/ppermute | solution.py:21
  109.6 2.5 %one_back.1 = (f32[4,112,256]{2,1,0:T(8,128)S(1)}, bf16[4,112,256]{2,1,0:T(8,128)(2,1)S(1)}) custom-call(bf16[64,1024]{1,0:T(8,128)(2,1)S(1)} %get-tuple-element.83.inputs, bf16[256,1024]{1,0:T(8,128)(2,1)S(1)} %get-tuple-element.123.delta, bf16[2048,1024]{1,0:T(8,128)(2,1)S(1)} %one_slope.1.slope, f32[64,2048]{1,0:T(8,128)S(1)} %get-tuple-element.124.grad_four, ...), custom_call_target="tpu_custom_call" | custom-call | flops 99999997952 | tf_op jit(solution)/shard_map/one_back/pallas_call | solution.py:57
  113.2 7.9 %collective-permute-done.35.got = bf16[512,256]{1,0:T(8,128)(2,1)S(1)} collective-permute-done((bf16[512,256]{1,0:T(8,128)(2,1)S(1)}, bf16[512,256]{1,0:T(8,128)(2,1)S(1)}, u32[]{:S(2)}, u32[]{:S(2)}) %collective-permute-start.35) | collective-permute-done | bytes 262176 | tf_op jit(solution)/shard_map/ppermute | solution.py:21
  122.3 2.0 %collective-permute-start.36 = (bf16[512,256]{1,0:T(8,128)(2,1)S(1)}, bf16[512,256]{1,0:T(8,128)(2,1)S(1)}, u32[]{:S(2)}, u32[]{:S(2)}) collective-permute-start(bf16[512,256]{1,0:T(8,128)(2,1)S(1)} %get-tuple-element.138), channel_id=1, source_target_pairs={{0,1},{1,0},{2,3},{3,2},{4,5},{5,4},{6,7},{7,6},{8,9},{9,8},{10,11... | collective-permute-start | bytes 786440 | tf_op jit(solution)/shard_map/ppermute | solution.py:21
  124.3 2.2 %collective-permute-start.37 = (bf16[512,256]{1,0:T(8,128)(2,1)S(1)}, bf16[512,256]{1,0:T(8,128)(2,1)S(1)}, u32[]{:S(2)}, u32[]{:S(2)}) collective-permute-start(bf16[512,256]{1,0:T(8,128)(2,1)S(1)} %add_up.3), channel_id=1, source_target_pairs={{0,2},{1,3},{2,0},{3,1},{4,6},{5,7},{6,4},{7,5},{8,10},{9,11},{10,... | collective-permute-start | bytes 786440 | tf_op jit(solution)/shard_map/ppermute | solution.py:21
  126.5 1.6 %collective-permute-start.34 = (bf16[1,112,256]{2,1,0:T(8,128)(2,1)S(1)}, bf16[1,112,256]{2,1,0:T(8,128)(2,1)S(1)}, u32[]{:S(2)}, u32[]{:S(2)}) collective-permute-start(bf16[1,112,256]{2,1,0:T(8,128)(2,1)S(1)} %get-tuple-element.132), channel_id=1, source_target_pairs={{0,16},{4,20},{8,24},{12,28},{16,0},{20,4},{24,8},{28,12},{1,17},{... | collective-permute-start | bytes 172040 | tf_op jit(solution)/shard_map/ppermute | solution.py:21
  128.1 2.6 %collective-permute-done.34.got = bf16[1,112,256]{2,1,0:T(8,128)(2,1)S(1)} collective-permute-done((bf16[1,112,256]{2,1,0:T(8,128)(2,1)S(1)}, bf16[1,112,256]{2,1,0:T(8,128)(2,1)S(1)}, u32[]{:S(2)}, u32[]{:S(2)}) %collective-permute-start.34) | collective-permute-done | bytes 57376 | tf_op jit(solution)/shard_map/ppermute | solution.py:21
  130.7 4.0 %collective-permute-start.39 = (bf16[112,128]{1,0:T(8,128)(2,1)S(1)}, bf16[112,128]{1,0:T(8,128)(2,1)S(1)}, u32[]{:S(2)}, u32[]{:S(2)}) collective-permute-start(bf16[112,128]{1,0:T(8,128)(2,1)S(1)} %get-tuple-element.142), channel_id=1, source_target_pairs={{0,2},{1,3},{2,0},{3,1},{4,6},{5,7},{6,4},{7,5},{8,10},{9,11},{10,... | collective-permute-start | bytes 86024 | tf_op jit(solution)/shard_map/ppermute | solution.py:21
  134.8 1.8 %collective-permute-done.38.refs_1_ = bf16[256,512]{1,0:T(8,128)(2,1)S(1)} collective-permute-done((bf16[256,512]{1,0:T(8,128)(2,1)S(1)}, bf16[256,512]{1,0:T(8,128)(2,1)S(1)}, u32[]{:S(2)}, u32[]{:S(2)}) %collective-permute-start.38) | collective-permute-done | bytes 262176 | tf_op jit(solution)/shard_map/ppermute | solution.py:21
  136.6 2.1 %update_top.1 = (f32[256,512]{1,0:T(8,128)}, f32[256,512]{1,0:T(8,128)}) custom-call(f32[256,512]{1,0:T(8,128)S(1)} %copy-done.2, f32[256,512]{1,0:T(8,128)S(1)} %copy-done.10, f32[256,512]{1,0:T(8,128)S(1)} %get-tuple-element.139.own, bf16[256,512]{1,0:T(8,128)(2,1)} %collective-permute-done.31.refs_0_, bf16[256,512]{1,0:T(8,128)(2,1)S(1)} %collective-permute-done.38.refs_1_), custom_call_target="tpu_custom_call" | custom-call | flops 2000000000 | tf_op jit(solution)/shard_map/update_top/pallas_call | solution.py:57
  138.7 2.0 %collective-permute-done.36.refs_0_ = bf16[512,256]{1,0:T(8,128)(2,1)S(1)} collective-permute-done((bf16[512,256]{1,0:T(8,128)(2,1)S(1)}, bf16[512,256]{1,0:T(8,128)(2,1)S(1)}, u32[]{:S(2)}, u32[]{:S(2)}) %collective-permute-start.36) | collective-permute-done | bytes 262176 | tf_op jit(solution)/shard_map/ppermute | solution.py:21
  140.7 2.5 %collective-permute-start.40 = (bf16[112,64]{1,0:T(8,128)(2,1)S(1)}, bf16[112,64]{1,0:T(8,128)(2,1)S(1)}, u32[]{:S(2)}, u32[]{:S(2)}) collective-permute-start(bf16[112,64]{1,0:T(8,128)(2,1)S(1)} %get-tuple-element.145), channel_id=1, source_target_pairs={{0,1},{1,0},{2,3},{3,2},{4,5},{5,4},{6,7},{7,6},{8,9},{9,8},{10,11... | collective-permute-start | bytes 43016 | tf_op jit(solution)/shard_map/ppermute | solution.py:21
  (112 shorter events, 43.7 us)
Async XLA Ops:
  2.2 14.7 %collective-permute-start.2 = (bf16[64,128]{1,0:T(8,128)(2,1)S(1)}, bf16[64,128]{1,0:T(8,128)(2,1)S(1)}, u32[]{:S(2)}, u32[]{:S(2)}) collective-permute-start(bf16[64,128]{1,0:T(8,128)(2,1)S(1)} %pack_small.1.refs_1_), channel_id=1, source_target_pairs={{0,3},{1,2},{2,1},{3,0},{4,7},{5,6},{6,5},{7,4},{8,11},{9,10},{10,... | collective-permute-start | bytes 49160 | tf_op jit(solution)/shard_map/ppermute | solution.py:21
  7.3 9.7 %collective-permute-start.1 = (bf16[64,128]{1,0:T(8,128)(2,1)S(1)}, bf16[64,128]{1,0:T(8,128)(2,1)S(1)}, u32[]{:S(2)}, u32[]{:S(2)}) collective-permute-start(bf16[64,128]{1,0:T(8,128)(2,1)S(1)} %pack_small.1.refs_1_), channel_id=1, source_target_pairs={{0,2},{1,3},{2,0},{3,1},{4,6},{5,7},{6,4},{7,5},{8,10},{9,11},{10,... | collective-permute-start | bytes 49160 | tf_op jit(solution)/shard_map/ppermute | solution.py:21
  7.3 9.7 %collective-permute-start = (bf16[64,128]{1,0:T(8,128)(2,1)S(1)}, bf16[64,128]{1,0:T(8,128)(2,1)S(1)}, u32[]{:S(2)}, u32[]{:S(2)}) collective-permute-start(bf16[64,128]{1,0:T(8,128)(2,1)S(1)} %pack_small.1.refs_1_), channel_id=1, source_target_pairs={{0,1},{1,0},{2,3},{3,2},{4,5},{5,4},{6,7},{7,6},{8,9},{9,8},{10,11... | collective-permute-start | bytes 49160 | tf_op jit(solution)/shard_map/ppermute | solution.py:21
  9.0 19.3 %collective-permute-start.4 = (bf16[512,256]{1,0:T(8,128)(2,1)S(1)}, bf16[512,256]{1,0:T(8,128)(2,1)S(1)}, u32[]{:S(2)}, u32[]{:S(2)}) collective-permute-start(bf16[512,256]{1,0:T(8,128)(2,1)S(1)} %convert_element_type.6.refs_0_), channel_id=1, source_target_pairs={{0,2},{1,3},{2,0},{3,1},{4,6},{5,7},{6,4},{7,5},{8,10},{9,11},{10,... | collective-permute-start | bytes 786440 | tf_op jit(solution)/shard_map/ppermute | solution.py:21
  11.3 24.6 %collective-permute-start.3 = (bf16[512,256]{1,0:T(8,128)(2,1)S(1)}, bf16[512,256]{1,0:T(8,128)(2,1)S(1)}, u32[]{:S(2)}, u32[]{:S(2)}) collective-permute-start(bf16[512,256]{1,0:T(8,128)(2,1)S(1)} %convert_element_type.6.refs_0_), channel_id=1, source_target_pairs={{0,1},{1,0},{2,3},{3,2},{4,5},{5,4},{6,7},{7,6},{8,9},{9,8},{10,11... | collective-permute-start | bytes 786440 | tf_op jit(solution)/shard_map/ppermute | solution.py:21
  17.0 19.0 %collective-permute-start.8 = (bf16[256,512]{1,0:T(8,128)(2,1)S(1)}, bf16[256,512]{1,0:T(8,128)(2,1)S(1)}, u32[]{:S(2)}, u32[]{:S(2)}) collective-permute-start(bf16[256,512]{1,0:T(8,128)(2,1)S(1)} %convert_element_type.7.refs_0_), channel_id=1, source_target_pairs={{0,2},{1,3},{2,0},{3,1},{4,6},{5,7},{6,4},{7,5},{8,10},{9,11},{10,... | collective-permute-start | bytes 786440 | tf_op jit(solution)/shard_map/ppermute | solution.py:21
  17.1 18.9 %collective-permute-start.7 = (bf16[256,512]{1,0:T(8,128)(2,1)S(1)}, bf16[256,512]{1,0:T(8,128)(2,1)S(1)}, u32[]{:S(2)}, u32[]{:S(2)}) collective-permute-start(bf16[256,512]{1,0:T(8,128)(2,1)S(1)} %convert_element_type.7.refs_0_), channel_id=1, source_target_pairs={{0,1},{1,0},{2,3},{3,2},{4,5},{5,4},{6,7},{7,6},{8,9},{9,8},{10,11... | collective-permute-start | bytes 786440 | tf_op jit(solution)/shard_map/ppermute | solution.py:21
  28.2 11.9 %collective-permute-start.5 = (bf16[512,256]{1,0:T(8,128)(2,1)S(1)}, bf16[512,256]{1,0:T(8,128)(2,1)S(1)}, u32[]{:S(2)}, u32[]{:S(2)}) collective-permute-start(bf16[512,256]{1,0:T(8,128)(2,1)S(1)} %collective-permute-done.4.refs_2_), channel_id=1, source_target_pairs={{0,1},{1,0},{2,3},{3,2},{4,5},{5,4},{6,7},{7,6},{8,9},{9,8},{10,11... | collective-permute-start | bytes 786440 | tf_op jit(solution)/shard_map/ppermute | solution.py:21
  29.5 6.4 %collective-permute-start.6 = (bf16[2,64,128]{2,1,0:T(8,128)(2,1)S(1)}, bf16[2,64,128]{2,1,0:T(8,128)(2,1)S(1)}, u32[]{:S(2)}, u32[]{:S(2)}) collective-permute-start(bf16[2,64,128]{2,1,0:T(8,128)(2,1)S(1)} %get-tuple-element.87.wanted), channel_id=1, source_target_pairs={{0,16},{4,20},{8,24},{12,28},{16,0},{20,4},{24,8},{28,12},{1,17},{... | collective-permute-start | bytes 98312 | tf_op jit(solution)/shard_map/ppermute | solution.py:21
  42.4 12.6 %collective-permute-start.14 = (bf16[256,512]{1,0:T(8,128)(2,1)S(1)}, bf16[256,512]{1,0:T(8,128)(2,1)S(1)}, u32[]{:S(2)}, u32[]{:S(2)}) collective-permute-start(bf16[256,512]{1,0:T(8,128)(2,1)S(1)} %collective-permute-done.8.refs_0_), channel_id=1, source_target_pairs={{0,1},{1,0},{2,3},{3,2},{4,5},{5,4},{6,7},{7,6},{8,9},{9,8},{10,11... | collective-permute-start | bytes 786440 | tf_op jit(solution)/shard_map/ppermute | solution.py:21
  45.5 9.5 %collective-permute-start.10 = (bf16[256,512]{1,0:T(8,128)(2,1)S(1)}, bf16[256,512]{1,0:T(8,128)(2,1)S(1)}, u32[]{:S(2)}, u32[]{:S(2)}) collective-permute-start(bf16[256,512]{1,0:T(8,128)(2,1)S(1)} %get-tuple-element.95), channel_id=1, source_target_pairs={{0,8},{4,12},{8,0},{12,4},{16,24},{20,28},{24,16},{28,20},{1,9},{5... | collective-permute-start | bytes 786440 | tf_op jit(solution)/shard_map/ppermute | solution.py:21
  47.0 8.1 %collective-permute-start.11 = (bf16[256,512]{1,0:T(8,128)(2,1)S(1)}, bf16[256,512]{1,0:T(8,128)(2,1)S(1)}, u32[]{:S(2)}, u32[]{:S(2)}) collective-permute-start(bf16[256,512]{1,0:T(8,128)(2,1)S(1)} %get-tuple-element.97), channel_id=1, source_target_pairs={{0,16},{4,20},{8,24},{12,28},{16,0},{20,4},{24,8},{28,12},{1,17},{... | collective-permute-start | bytes 786440 | tf_op jit(solution)/shard_map/ppermute | solution.py:21
  58.7 9.2 %collective-permute-start.16 = (bf16[256,512]{1,0:T(8,128)(2,1)S(1)}, bf16[256,512]{1,0:T(8,128)(2,1)S(1)}, u32[]{:S(2)}, u32[]{:S(2)}) collective-permute-start(bf16[256,512]{1,0:T(8,128)(2,1)S(1)} %get-tuple-element.106), channel_id=1, source_target_pairs={{0,8},{4,12},{8,0},{12,4},{16,24},{20,28},{24,16},{28,20},{1,9},{5... | collective-permute-start | bytes 786440 | tf_op jit(solution)/shard_map/ppermute | solution.py:21
  59.3 9.2 %collective-permute-start.17 = (bf16[256,512]{1,0:T(8,128)(2,1)S(1)}, bf16[256,512]{1,0:T(8,128)(2,1)S(1)}, u32[]{:S(2)}, u32[]{:S(2)}) collective-permute-start(bf16[256,512]{1,0:T(8,128)(2,1)S(1)} %get-tuple-element.108), channel_id=1, source_target_pairs={{0,16},{4,20},{8,24},{12,28},{16,0},{20,4},{24,8},{28,12},{1,17},{... | collective-permute-start | bytes 786440 | tf_op jit(solution)/shard_map/ppermute | solution.py:21
  60.9 10.8 %collective-permute-start.12 = (bf16[128,512]{1,0:T(8,128)(2,1)S(1)}, bf16[128,512]{1,0:T(8,128)(2,1)S(1)}, u32[]{:S(2)}, u32[]{:S(2)}) collective-permute-start(bf16[128,512]{1,0:T(8,128)(2,1)S(1)} %get-tuple-element.99), channel_id=1, source_target_pairs={{0,16},{4,20},{8,24},{12,28},{16,0},{20,4},{24,8},{28,12},{1,17},{... | collective-permute-start | bytes 393224 | tf_op jit(solution)/shard_map/ppermute | solution.py:21
  61.5 10.2 %collective-permute-start.13 = (bf16[128,512]{1,0:T(8,128)(2,1)S(1)}, bf16[128,512]{1,0:T(8,128)(2,1)S(1)}, u32[]{:S(2)}, u32[]{:S(2)}) collective-permute-start(bf16[128,512]{1,0:T(8,128)(2,1)S(1)} %get-tuple-element.100), channel_id=1, source_target_pairs={{0,8},{4,12},{8,0},{12,4},{16,24},{20,28},{24,16},{28,20},{1,9},{5... | collective-permute-start | bytes 393224 | tf_op jit(solution)/shard_map/ppermute | solution.py:21
  76.1 5.8 %collective-permute-start.24 = (bf16[128,512]{1,0:T(8,128)(2,1)S(1)}, bf16[128,512]{1,0:T(8,128)(2,1)S(1)}, u32[]{:S(2)}, u32[]{:S(2)}) collective-permute-start(bf16[128,512]{1,0:T(8,128)(2,1)S(1)} %get-tuple-element.115.own), channel_id=1, source_target_pairs={{0,16},{4,20},{8,24},{12,28},{16,0},{20,4},{24,8},{28,12},{1,17},{... | collective-permute-start | bytes 393224 | tf_op jit(solution)/shard_map/ppermute | solution.py:21
  76.7 7.1 %collective-permute-start.21 = (bf16[128,512]{1,0:T(8,128)(2,1)S(1)}, bf16[128,512]{1,0:T(8,128)(2,1)S(1)}, u32[]{:S(2)}, u32[]{:S(2)}) collective-permute-start(bf16[128,512]{1,0:T(8,128)(2,1)S(1)} %get-tuple-element.113.own), channel_id=1, source_target_pairs={{0,8},{4,12},{8,0},{12,4},{16,24},{20,28},{24,16},{28,20},{1,9},{5... | collective-permute-start | bytes 393224 | tf_op jit(solution)/shard_map/ppermute | solution.py:21
  81.9 9.7 %collective-permute-start.25 = (bf16[256,512]{1,0:T(8,128)(2,1)S(1)}, bf16[256,512]{1,0:T(8,128)(2,1)S(1)}, u32[]{:S(2)}, u32[]{:S(2)}) collective-permute-start(bf16[256,512]{1,0:T(8,128)(2,1)S(1)} %join.6.refs_2_), channel_id=1, source_target_pairs={{0,8},{4,12},{8,0},{12,4},{16,24},{20,28},{24,16},{28,20},{1,9},{5... | collective-permute-start | bytes 786440 | tf_op jit(solution)/shard_map/ppermute | solution.py:21
  83.8 7.8 %collective-permute-start.23 = (bf16[256,512]{1,0:T(8,128)(2,1)S(1)}, bf16[256,512]{1,0:T(8,128)(2,1)S(1)}, u32[]{:S(2)}, u32[]{:S(2)}) collective-permute-start(bf16[256,512]{1,0:T(8,128)(2,1)S(1)} %join.5.refs_0_), channel_id=1, source_target_pairs={{0,16},{4,20},{8,24},{12,28},{16,0},{20,4},{24,8},{28,12},{1,17},{... | collective-permute-start | bytes 786440 | tf_op jit(solution)/shard_map/ppermute | solution.py:21
  84.7 5.1 %collective-permute-start.20 = (bf16[128,512]{1,0:T(8,128)(2,1)S(1)}, bf16[128,512]{1,0:T(8,128)(2,1)S(1)}, u32[]{:S(2)}, u32[]{:S(2)}) collective-permute-start(bf16[128,512]{1,0:T(8,128)(2,1)S(1)} %get-tuple-element.112.own), channel_id=1, source_target_pairs={{0,8},{4,12},{8,0},{12,4},{16,24},{20,28},{24,16},{28,20},{1,9},{5... | collective-permute-start | bytes 393224 | tf_op jit(solution)/shard_map/ppermute | solution.py:21
  86.2 5.4 %collective-permute-start.22 = (bf16[128,512]{1,0:T(8,128)(2,1)S(1)}, bf16[128,512]{1,0:T(8,128)(2,1)S(1)}, u32[]{:S(2)}, u32[]{:S(2)}) collective-permute-start(bf16[128,512]{1,0:T(8,128)(2,1)S(1)} %get-tuple-element.114.own), channel_id=1, source_target_pairs={{0,16},{4,20},{8,24},{12,28},{16,0},{20,4},{24,8},{28,12},{1,17},{... | collective-permute-start | bytes 393224 | tf_op jit(solution)/shard_map/ppermute | solution.py:21
  91.8 9.1 %collective-permute-start.28 = (bf16[272,512]{1,0:T(8,128)(2,1)S(1)}, bf16[272,512]{1,0:T(8,128)(2,1)S(1)}, u32[]{:S(2)}, u32[]{:S(2)}) collective-permute-start(bf16[272,512]{1,0:T(8,128)(2,1)S(1)} %join.4.refs_0_), channel_id=1, source_target_pairs={{0,16},{4,20},{8,24},{12,28},{16,0},{20,4},{24,8},{28,12},{1,17},{... | collective-permute-start | bytes 835592 | tf_op jit(solution)/shard_map/ppermute | solution.py:21
  92.8 8.8 %collective-permute-start.29 = (bf16[272,512]{1,0:T(8,128)(2,1)S(1)}, bf16[272,512]{1,0:T(8,128)(2,1)S(1)}, u32[]{:S(2)}, u32[]{:S(2)}) collective-permute-start(bf16[272,512]{1,0:T(8,128)(2,1)S(1)} %join.7.refs_2_), channel_id=1, source_target_pairs={{0,8},{4,12},{8,0},{12,4},{16,24},{20,28},{24,16},{28,20},{1,9},{5... | collective-permute-start | bytes 835592 | tf_op jit(solution)/shard_map/ppermute | solution.py:21
  94.9 8.4 %collective-permute-start.27 = (bf16[256,512]{1,0:T(8,128)(2,1)S(1)}, bf16[256,512]{1,0:T(8,128)(2,1)S(1)}, u32[]{:S(2)}, u32[]{:S(2)}) collective-permute-start(bf16[256,512]{1,0:T(8,128)(2,1)S(1)} %three_first.1), channel_id=1, source_target_pairs={{0,1},{1,0},{2,3},{3,2},{4,5},{5,4},{6,7},{7,6},{8,9},{9,8},{10,11... | collective-permute-start | bytes 786440 | tf_op jit(solution)/shard_map/ppermute | solution.py:21
  104.2 17.1 %collective-permute-start.31 = (bf16[256,512]{1,0:T(8,128)(2,1)}, bf16[256,512]{1,0:T(8,128)(2,1)}, u32[]{:S(2)}, u32[]{:S(2)}) collective-permute-start(bf16[256,512]{1,0:T(8,128)(2,1)} %add_up.2), channel_id=1, source_target_pairs={{0,2},{1,3},{2,0},{3,1},{4,6},{5,7},{6,4},{7,5},{8,10},{9,11},{10,... | collective-permute-start | bytes 786440 | tf_op jit(solution)/shard_map/ppermute | solution.py:21
  107.9 13.3 %collective-permute-start.35 = (bf16[512,256]{1,0:T(8,128)(2,1)S(1)}, bf16[512,256]{1,0:T(8,128)(2,1)S(1)}, u32[]{:S(2)}, u32[]{:S(2)}) collective-permute-start(bf16[512,256]{1,0:T(8,128)(2,1)S(1)} %get-tuple-element.135), channel_id=1, source_target_pairs={{0,1},{1,0},{2,3},{3,2},{4,5},{5,4},{6,7},{7,6},{8,9},{9,8},{10,11... | collective-permute-start | bytes 786440 | tf_op jit(solution)/shard_map/ppermute | solution.py:21
  112.1 9.2 %collective-permute-start.32 = (bf16[4,112,256]{2,1,0:T(8,128)(2,1)S(1)}, bf16[4,112,256]{2,1,0:T(8,128)(2,1)S(1)}, u32[]{:S(2)}, u32[]{:S(2)}) collective-permute-start(bf16[4,112,256]{2,1,0:T(8,128)(2,1)S(1)} %get-tuple-element.127), channel_id=1, source_target_pairs={{0,4},{4,0},{8,12},{12,8},{16,20},{20,16},{24,28},{28,24},{1,5},{5... | collective-permute-start | bytes 688136 | tf_op jit(solution)/shard_map/ppermute | solution.py:21
  121.2 15.4 %collective-permute-start.38 = (bf16[256,512]{1,0:T(8,128)(2,1)S(1)}, bf16[256,512]{1,0:T(8,128)(2,1)S(1)}, u32[]{:S(2)}, u32[]{:S(2)}) collective-permute-start(bf16[256,512]{1,0:T(8,128)(2,1)S(1)} %get-tuple-element.140), channel_id=1, source_target_pairs={{0,1},{1,0},{2,3},{3,2},{4,5},{5,4},{6,7},{7,6},{8,9},{9,8},{10,11... | collective-permute-start | bytes 786440 | tf_op jit(solution)/shard_map/ppermute | solution.py:21
  122.3 18.4 %collective-permute-start.36 = (bf16[512,256]{1,0:T(8,128)(2,1)S(1)}, bf16[512,256]{1,0:T(8,128)(2,1)S(1)}, u32[]{:S(2)}, u32[]{:S(2)}) collective-permute-start(bf16[512,256]{1,0:T(8,128)(2,1)S(1)} %get-tuple-element.138), channel_id=1, source_target_pairs={{0,1},{1,0},{2,3},{3,2},{4,5},{5,4},{6,7},{7,6},{8,9},{9,8},{10,11... | collective-permute-start | bytes 786440 | tf_op jit(solution)/shard_map/ppermute | solution.py:21
  124.3 16.4 %collective-permute-start.37 = (bf16[512,256]{1,0:T(8,128)(2,1)S(1)}, bf16[512,256]{1,0:T(8,128)(2,1)S(1)}, u32[]{:S(2)}, u32[]{:S(2)}) collective-permute-start(bf16[512,256]{1,0:T(8,128)(2,1)S(1)} %add_up.3), channel_id=1, source_target_pairs={{0,2},{1,3},{2,0},{3,1},{4,6},{5,7},{6,4},{7,5},{8,10},{9,11},{10,... | collective-permute-start | bytes 786440 | tf_op jit(solution)/shard_map/ppermute | solution.py:21
  130.7 7.9 %collective-permute-start.39 = (bf16[112,128]{1,0:T(8,128)(2,1)S(1)}, bf16[112,128]{1,0:T(8,128)(2,1)S(1)}, u32[]{:S(2)}, u32[]{:S(2)}) collective-permute-start(bf16[112,128]{1,0:T(8,128)(2,1)S(1)} %get-tuple-element.142), channel_id=1, source_target_pairs={{0,2},{1,3},{2,0},{3,1},{4,6},{5,7},{6,4},{7,5},{8,10},{9,11},{10,... | collective-permute-start | bytes 86024 | tf_op jit(solution)/shard_map/ppermute | solution.py:21
  (20 other events, 164.0 us)

commit v5 on v4

--- a/solution.py
+++ b/solution.py
@@ -117,11 +117,14 @@
         at += part.shape[0]
 
 
-def place_small(held, inputs, first, fourth, *, tall, rows, wide, places):
+def place_small(held, inputs, first, fourth, number, *, n_in, tall, rows, wide, places):
     n_dp, n_mp = lax.axis_size("dp"), lax.axis_size("mp")
     half = n_dp // 2
-    blocks = list(range(0, n_dp, 2)) + list(range(1, n_dp, 2))
-    for place, k in enumerate(blocks):
+    total = held[0, n_in : n_in + 1].astype(f32)
+    for d in range(1, n_dp):
+        total = total + held[d, n_in : n_in + 1].astype(f32)
+    number[...] = total
+    for place, k in enumerate(range(0, n_dp, 2)):
         at = lax.axis_index("dp") ^ k
         high = at >= half
         pair = jnp.where(high, at - half, at)
@@ -168,46 +171,37 @@
     lax.fori_loop(0, first.shape[1] // tile, step, 0)
 
 
-def two_forward(act_one, *refs):
-    seconds, (act, act_t, slope) = refs[:-3], refs[-3:]
+def two_forward(act_one, near, far, near_too, far_too, act, act_t, slope):
     n_rows = act_one.shape[1]
     cut = min(256, n_rows)
-    span = seconds[0].shape[0]
-    turned = [s[...].T for s in seconds]
-    for c in range(0, n_rows, cut):
-        at = slice(c, c + cut)
-        pre = dot(turned[0], act_one[:span, at], 1, 0)
-        for k in range(1, len(seconds)):
-            pre = pre + dot(turned[k], act_one[k * span : (k + 1) * span, at], 1, 0)
-        value = gelu_act(pre)
-        act_t[:, at] = value.astype(bf16)
-        act[at] = value.T.astype(bf16)
-        slope[:, at] = gelu_slope(pre)
-
-
-def three_away(act, *refs, kept):
-    thirds, out = refs[:-1], refs[-1]
-    span = thirds[0].shape[1]
-    for k, third in enumerate(thirds):
-        out[:, k * span : (k + 1) * span] = dot(act[kept:], third[...], 1, 0).astype(bf16)
+    first, cols = near.shape
+    for side, (left, right) in enumerate(((near, far), (near_too, far_too))):
+        to = slice(side * cols, (side + 1) * cols)
+        left, right = left[...].T, right[...].T
+        for c in range(0, n_rows, cut):
+            at = slice(c, c + cut)
+            pre = dot(left, act_one[:first, at], 1, 0) + dot(right, act_one[first:, at], 1, 0)
+            value = gelu_act(pre)
+            act_t[to, at] = value.astype(bf16)
+            act[at, to] = value.T.astype(bf16)
+            slope[to, at] = gelu_slope(pre)
 
 
 def divided(kept, bit):
     return [k for k in kept if not k & bit]
 
 
-def three_home(act, got, *refs, n_third, orders, kept):
+def three_home(act, *refs, n_third, orders, kept):
     thirds, own, outs = refs[:n_third], refs[n_third], refs[n_third + 1 :]
     rows = own.shape[0]
-    span = thirds[0].shape[1]
-    count = len(kept) * rows
+    mid, span = thirds[0].shape
     blocks = {k: slice(i * rows, (i + 1) * rows) for i, k in enumerate(kept)}
     half = own.shape[1] // 2
-    step = min(span, half)
+    step = math.gcd(span, half)
     for at in range(0, own.shape[1], step):
-        third = thirds[at // span]
-        total = dot(act[:count], third[:, at % span : at % span + step], 1, 0)
-        total = total + got[:, at : at + step].astype(f32)
+        left, right = thirds[at // span], thirds[n_third // 2 + at // span]
+        cut = slice(at % span, at % span + step)
+        total = dot(act[:, :mid], left[:, cut], 1, 0) + dot(act[:, mid:], right[:, cut], 1, 0)
         own[:, at : at + step] = total[blocks[0]]
         part = at // half
         keep, send = outs[2 * part], outs[2 * part + 1]
@@ -242,30 +236,32 @@
             send[i * rows : (i + 1) * rows] = total[k | bit].astype(bf16)
 
 
-def error_step(inputs, wanted, wanted_too, fourth, *refs, groups, half, per, n_in, n_out):
+def error_step(number, wanted, wanted_too, fourth, *refs, widths, half, block, n_out):
+    groups = len(widths)
     terms = refs[: 3 * groups]
     act, pre = refs[-2:]
     deltas, grad_four = refs[3 * groups : 5 * groups], refs[-3]
-    width = pre.shape[1] // groups // 2
-    for g in range(groups):
+    start = 0
+    spots = []
+    for g, width in enumerate(widths):
         for part in range(2):
-            at = slice((2 * g + part) * width, (2 * g + part + 1) * width)
+            at = slice(start, start + width)
+            start += width
+            spots.append(at)
             total = terms[3 * g][:, part * width : (part + 1) * width]
             total = total + terms[3 * g + 1 + part][...].astype(f32)
             pre[:, at] = total
             act[:, at] = gelu_act(total).astype(bf16)
     predicted = dot(fourth[...], act[...], 1, 1)
-    number = jnp.sum(inputs[n_in : n_in + 1, :].astype(f32), axis=1, keepdims=True) / per
     mine = jnp.where(lax.axis_index("dp") >= half, 1, 0)
     wanted = wanted[mine] + wanted_too[mine]
     live = wanted[n_out : n_out + 1, :].astype(f32)
-    error = (2.0 / number * (predicted - wanted.astype(f32)) * live).astype(bf16)
+    error = (2.0 / (number[:, :1] * block) * (predicted - wanted.astype(f32)) * live).astype(bf16)
     row = lax.broadcasted_iota(jnp.int32, error.shape, 0)
     error = jnp.where(row < n_out, error, jnp.zeros_like(error))
     grad_four[...] = dot(error, act[...], 1, 0)
     turned = error.astype(f32).T.astype(bf16)
-    for i, delta in enumerate(deltas):
-        at = slice(i * width, (i + 1) * width)
+    for at, delta in zip(spots, deltas):
         value = dot(turned, fourth[:, at], 1, 0) * gelu_slope(pre[:, at])
         delta[...] = value.astype(bf16)
 
@@ -277,6 +273,17 @@
     out[rows:filled] = got[...]
     if filled < out.shape[0]:
         out[filled:] = jnp.zeros((out.shape[0] - filled, out.shape[1]), out.dtype)
+
+
+def lay(*refs, axis):
+    out, at = refs[-1], 0
+    for value in refs[:-1]:
+        to = at + value.shape[axis]
+        if axis:
+            out[:, at:to] = value[...]
+        else:
+            out[at:to] = value[...]
+        at = to
 
 
 def join_all(*refs, held, evens, rows):
@@ -289,44 +296,47 @@
             out[to : to + rows, at] = refs[i][j * rows : (j + 1) * rows]
 
 
-def three_first(act_t, home, away, grad, *, column):
-    rows = home.shape[0]
-    at = slice(column, column + grad.shape[1])
-    total = dot(act_t[:, :rows], home[:, at], 1, 0) + dot(act_t[:, rows:], away[:, at], 1, 0)
-    grad[...] = total.astype(grad.dtype)
-
-
-def three_back(act_t, home, away, *refs, ks, carried, ready):
-    thirds = refs[: len(ks)]
-    refs = refs[len(ks) :]
-    before = refs[0] if carried else None
-    refs = refs[carried:]
-    sum_two, grads, whole = refs[0], refs[1 : 1 + len(ks) - ready], refs[-1]
-    rows = home.shape[0]
-    span = thirds[0].shape[1]
-    whole[:rows] = home[...]
-    whole[rows:] = away[...]
-    for i in range(len(grads)):
+def three_away(act_t, whole, away):
+    mid = act_t.shape[0] // 2
+    away[...] = dot(act_t[mid:], whole[...], 1, 0).astype(bf16)
+
+
+def three_own(act_t, whole, got, *grads):
+    mid = act_t.shape[0] // 2
+    span = grads[0].shape[1]
+    for i, grad in enumerate(grads):
         at = slice(i * span, (i + 1) * span)
-        grads[i][...] = dot(act_t[...], whole[:, at], 1, 0).astype(grads[i].dtype)
-    total = before[...] if carried else None
-    for i, third in enumerate(thirds):
-        term = dot(third[...], whole[:, i * span : (i + 1) * span], 1, 1)
-        total = term if total is None else total + term
-    sum_two[...] = total
-
-
-def two_first(sum_two, slope, act_one, delta, grad):
+        value = dot(act_t[:mid], whole[:, at], 1, 0) + got[:, at].astype(f32)
+        grad[...] = value.astype(grad.dtype)
+
+
+def three_back(whole, *refs, n_third):
+    thirds, before, sum_two = refs[:n_third], refs[n_third:-1], refs[-1]
+    mid, span = thirds[0].shape
+    for side in range(2):
+        to = slice(side * mid, (side + 1) * mid)
+        total = before[0][to] if before else None
+        for i, third in enumerate(thirds[side * n_third // 2 : (side + 1) * n_third // 2]):
+            term = dot(third[...], whole[:, i * span : (i + 1) * span], 1, 1)
+            total = term if total is None else total + term
+        sum_two[to] = total
+
+
+def two_first(sum_two, slope, act_one, delta, away_far, away):
     value = (sum_two[...] * slope[...]).astype(bf16)
     delta[...] = value
-    grad[...] = dot(act_one[act_one.shape[0] - grad.shape[0] :], value, 1, 1).astype(grad.dtype)
-
-
-def two_back(delta, act_one, *grads):
-    span = grads[0].shape[0]
-    for k, grad in enumerate(grads):
-        part = act_one[k * span : (k + 1) * span]
-        grad[...] = dot(part, delta[...], 1, 1).astype(grad.dtype)
+    mid, near = delta.shape[0] // 2, away.shape[0]
+    away_far[...] = dot(act_one[near:], value[mid:], 1, 1).astype(bf16)
+    away[...] = dot(act_one[:near], value[mid:], 1, 1).astype(bf16)
+
+
+def two_own(delta, act_one, got, *grads, start):
+    mid, span = delta.shape[0] // 2, grads[0].shape[0]
+    for i, grad in enumerate(grads):
+        at = slice(i * span, (i + 1) * span)
+        rows = slice(start + i * span, start + (i + 1) * span)
+        value = dot(act_one[rows], delta[:mid], 1, 1) + got[at].astype(f32)
+        grad[...] = value.astype(grad.dtype)
 
 
 def split_dp(parts, step, keep, send):
@@ -337,13 +347,18 @@
         send[i] = jnp.where(bit, even, odd).astype(bf16)
 
 
-def one_back(inputs, delta, slope, grad_four, *refs, n_mp, n_dp, places, n_in, n_out):
-    seconds, (keep, send) = refs[:n_mp], refs[n_mp:]
-    span = seconds[0].shape[0]
+def one_back(
+    inputs, delta, slope, grad_four, near, far, near_too, far_too, keep, send, *, n_dp, places, n_in, n_out
+):
+    span = far.shape[0]
+    n_mp = near.shape[0] // span + 1
     wide = span // n_dp
+    mid = delta.shape[0] // 2
     whole = []
     for k in range(n_mp):
-        value = dot(seconds[k][...], delta[...], 1, 0)
+        at = slice(k * span, (k + 1) * span)
+        left, right = (near[at], near_too[at]) if k + 1 < n_mp else (far[...], far_too[...])
+        value = dot(left, delta[:mid], 1, 0) + dot(right, delta[mid:], 1, 0)
         value = (value * slope[k * span : (k + 1) * span].astype(f32)).astype(bf16)
         grad_one = dot(inputs[...], value, 1, 1)
         at = places.index(k) * span
@@ -410,6 +425,12 @@
     return lax.optimization_barrier((first, *values))[1:]
 
 
+def laid(values, axis):
+    shape = list(values[0].shape)
+    shape[axis] *= len(values)
+    return on_core(functools.partial(lay, axis=axis), shaped(tuple(shape), bf16), values, "lay")
+
+
 def gathered(own, n_mp):
     held = {0: own}
     for k in [k for k in range(1, n_mp) if parent(k) == 0][::-1]:
@@ -422,13 +443,11 @@
         held[k] = swap(after(ready, held[parent(k)])[0], "mp", low_bit(k))
 
 
-def summed(held, ks, firsts=None):
+def summed(held, ks):
     gots = []
     for k in sorted((k for k in ks if k), key=lambda k: (low_bit(k), -k)):
         got = swap(held[k], "mp", low_bit(k))
         to = parent(k)
-        if firsts is not None:
-            firsts.append(got)
         if to:
             held[to] = on_core(add_up, shaped(got.shape, bf16), [held[to], got], "add_up")
         else:
@@ -455,7 +474,7 @@
     half = n_dp // 2
     per = slots // n_mp
     rows = per * block // 2
-    n_rows = n_dp * rows
+    n_rows = half * rows
     wide = weight_in.shape[1]
     lanes = max(rows, 2 * wide)
     tall = up_to(max(n_in, n_out) + 1, 16)
@@ -463,74 +482,82 @@
     width = hidden * n_mp
     n_mid, n_top = weight_mid.shape[1], weight_top.shape[1]
     planes = range(n_mp)
-    groups = [list(planes[: n_mp // 2]), list(planes[n_mp // 2 :])]
+    groups = [list(planes[:-1]), [n_mp - 1]]
     places = [k for ks in groups for k in ks]
     part = functools.partial
 
     piece = on_core(
         part(pack_small, tall=tall), shaped((tall, lanes), bf16), [weight_in, weight_out.T], "pack_small"
     )
-    pieces = [piece] + [swap(piece, "mp", k) for k in planes[1:]]
     second = gathered(weight_mid.astype(bf16), n_mp)
     picked, wanted = on_core(
         part(pick_rows, tall=tall, rows=rows, per=per),
         [shaped((2 * tall, lanes), bf16), shaped((2, tall, rows), bf16)],
         [samples, targets],
         "pick_rows",
-        scalars=after(pieces, counts),
-        flops=LONG,
-    )
+        scalars=[counts],
+    )
+    pieces = [piece] + [swap(piece, "mp", k) for k in planes[1:]]
     top = after((picked, pieces), weight_top.astype(bf16))[0]
     third = gathered(top, n_mp)
+    early = [second[k] for k in planes if k and not parent(k)]
+    passed_on(second, n_mp, (picked, pieces))
 
     packed = on_core(
         pack_all,
         shaped(((2 + n_mp) * tall, lanes), bf16),
-        [picked, *pieces],
+        [picked, *after(early, *pieces)],
         "pack_all",
     )
     wanted = [wanted, swap(wanted, "dp", half)]
     held = lax.all_gather(packed, "dp")
-    passed_on(second, n_mp, held)
-    inputs, first, fourth = on_core(
-        part(place_small, tall=tall, rows=rows, wide=wide, places=places),
-        [shaped((tall, n_rows), bf16), shaped((tall, width), bf16), shaped((tall, width), bf16)],
+    inputs, first, fourth, number = on_core(
+        part(place_small, n_in=n_in, tall=tall, rows=rows, wide=wide, places=places),
+        [
+            shaped((tall, n_rows), bf16),
+            shaped((tall, width), bf16),
+            shaped((tall, width), bf16),
+            shaped((1, lanes), f32),
+        ],
         [held],
         "place_small",
     )
 
     act_one = on_core(
-        part(one_forward, tile=128), shaped((width, n_rows), bf16), [inputs, first], "one_forward"
-    )
+        part(one_forward, tile=256), shaped((width, n_rows), bf16), [inputs, first], "one_forward"
+    )
+    wide_mid = 2 * n_mid
+    near = laid(after((picked, pieces), *[second[k] for k in planes[:-1]]), 0)
+    third_early = [third[k] for k in planes if k and not parent(k)]
+    far = after((act_one, third_early, wanted[1]), second[n_mp - 1])[0]
+    second_all = [near, far, swap(near, "dp", 1), swap(far, "dp", 1)]
     act_two, act_two_t, slope_two = on_core(
         two_forward,
-        [shaped((n_rows, n_mid), bf16), shaped((n_mid, n_rows), bf16), shaped((n_mid, n_rows), f32)],
-        [act_one] + [second[k] for k in planes],
+        [shaped((n_rows, wide_mid), bf16), shaped((wide_mid, n_rows), bf16), shaped((wide_mid, n_rows), f32)],
+        [act_one, *second_all],
         "two_forward",
     )
-    passed_on(third, n_mp, act_one)
+    passed_on(third, n_mp, act_two)
+    third_too = {k: swap(after(act_one, third[k])[0] if k else top, "dp", 1) for k in planes}
+    third_all = [[third[k] for k in ks] + [third_too[k] for k in ks] for ks in groups]
     evens = list(range(0, n_dp, 2))
     bits = [1 << i for i in range(1, n_dp.bit_length() - 1)]
     orders = [bits, bits[::-1]]
-    kept = half * rows
     slope_one = on_core(
-        part(one_slope, tile=128), shaped((width, n_rows), bf16), [inputs, first], "one_slope",
+        part(one_slope, tile=256), shaped((width, n_rows), bf16), [inputs, first], "one_slope",
         flops=12_000_000_000,
     )
     terms = []
-    ahead = [wanted[1]] + [third[k] for k in planes if k and not parent(k)]
-    for ks in groups:
+    ahead = [third[k] for k in planes if k and not parent(k)]
+    for ks, weights in zip(groups, third_all):
         cols = len(ks) * n_top
-        weights = after(ahead, *[third[k] for k in ks])
-        away = on_core(
-            part(three_away, kept=kept), shaped((kept, cols), bf16), [act_two, *weights], "three_away"
-        )
+        weights = after(ahead, *weights)
         left = half // 2
         kinds = [shaped(((left - 1) * rows, cols // 2), f32), shaped((left * rows, cols // 2), bf16)]
         own, *halves = on_core(
-            part(three_home, n_third=len(ks), orders=orders, kept=evens),
+            part(three_home, n_third=len(weights), orders=orders, kept=evens),
             [shaped((rows, cols), f32)] + kinds * 2,
-            [act_two, swap(away, "dp", 1), *weights],
+            [act_two, *weights],
             "three_home",
         )
         ahead = []
@@ -552,10 +579,10 @@
             )
         terms += [own, *gots]
     *deltas, grad_four = on_core(
-        part(error_step, groups=len(groups), half=half, per=per, n_in=n_in, n_out=n_out),
+        part(error_step, widths=[len(ks) * n_top // 2 for ks in groups], half=half, block=block, n_out=n_out),
         [shaped((rows, len(ks) * n_top // 2), bf16) for ks in groups for _ in range(2)]
         + [shaped((tall, width), f32)],
-        [inputs, *wanted, fourth, *terms],
+        [number, *wanted, fourth, *terms],
         "error_step",
         scratch=[pltpu.VMEM((rows, width), bf16), pltpu.VMEM((rows, width), f32)],
     )
@@ -584,58 +611,67 @@
         ks, carried = groups[g], sum_two is not None
         arrays, gots, blocks = gathers[g]
         if carried:
-            gots = after((sum_two, firsts[0]), *gots)
+            gots = after((sum_two, got_far), *gots)
         elif (0, 0) in gathers:
             gots = after(gathers[0, 0], *gots)
-        home = on_core(
+        whole = on_core(
             part(join_all, held=blocks, evens=evens, rows=rows),
-            shaped((kept, len(ks) * n_top), bf16),
+            shaped((n_rows, len(ks) * n_top), bf16),
             [arrays[0], gots[0], arrays[1], gots[1]],
             "join_all",
         )
-        away = swap(home, "dp", 1)
-        carry = [sum_two] if carried else []
+        away = on_core(
+            three_away, shaped((n_mid, len(ks) * n_top), bf16), [act_two_t, whole], "three_away"
+        )
+        away = swap(away, "dp", 1)
+        sum_two = on_core(
+            part(three_back, n_third=2 * len(ks)),
+            shaped((wide_mid, n_rows), f32),
+            [whole, *third_all[g]] + ([sum_two] if carried else []),
+            "three_back",
+        )
+        grads = on_core(
+            three_own,
+            [shaped((n_mid, n_top), bf16 if k else f32) for k in ks],
+            [act_two_t, whole, away],
+            "three_own",
+        )
+        grad_three.update(zip(ks, grads))
         if not carried:
-            grad_three[ks[-1]] = on_core(
-                part(three_first, column=(len(ks) - 1) * n_top),
-                shaped((n_mid, n_top), bf16),
-                [act_two_t, home, away],
-                "three_first",
-            )
-        made = ks if carried else ks[:-1]
-        sum_two, *grads = on_core(
-            part(three_back, ks=ks, carried=len(carry), ready=len(ks) - len(made)),
-            [shaped((n_mid, n_rows), f32)]
-            + [shaped((n_mid, n_top), bf16 if k else f32) for k in made],
-            [act_two_t, home, away] + [third[k] for k in ks] + carry,
-            "three_back",
-            scratch=[pltpu.VMEM((n_rows, len(ks) * n_top), bf16)],
-        )
-        grad_three.update(zip(made, grads))
-        if not carried:
-            firsts = []
-            gots_three = summed(grad_three, ks, firsts)
-    delta_two, farthest = on_core(
+            got_far = swap(grads[0], "mp", 1)
+    far = n_mp - 1
+    grad_three[far - 1] = on_core(
+        add_up, shaped(got_far.shape, bf16), [grad_three[far - 1], got_far], "add_up"
+    )
+    delta_two, away_far, away = on_core(
         two_first,
-        [shaped((n_mid, n_rows), bf16), shaped((hidden, n_mid), bf16)],
+        [
+            shaped((wide_mid, n_rows), bf16),
+            shaped((hidden, n_mid), bf16),
+            shaped((far * hidden, n_mid), bf16),
+        ],
         [sum_two, slope_two, act_one],
         "two_first",
         flops=LONG,
     )
+    (farthest,) = on_core(
+        part(two_own, start=far * hidden),
+        [shaped((hidden, n_mid), bf16)],
+        [delta_two, act_one, swap(away_far, "dp", 1)],
+        "two_own",
+    )
     grads = on_core(
-        two_back,
+        part(two_own, start=0),
         [shaped((hidden, n_mid), bf16 if k else f32) for k in planes[:-1]],
-        [delta_two, act_one],
-        "two_back",
+        [delta_two, act_one, swap(away, "dp", 1)],
+        "two_own",
     )
     grad_two = dict(zip(planes, [*grads, farthest]))
-    far = n_mp - 1
     got = swap(grad_two[far], "mp", 1)
     grad_two[far - 1] = on_core(add_up, shaped(got.shape, bf16), [grad_two[far - 1], got], "add_up")
     grad_two[1], grad_three[1] = after(grad_two[far - 1], grad_two[1], grad_three[1])
-    gots_two = summed(grad_two, planes[: n_mp - 1])
-    early_three = list(gots_three)
-    gots_three += summed(grad_three, groups[0])
+    gots_two = summed(grad_two, planes[:far])
+    gots_three = summed(grad_three, planes[:far])[::-1]
     like = lambda value: shaped(value.shape, f32)
     new_top, mom_top = on_core(
         update_big, [like(weight_top)] * 2, [weight_top, moment_top, grad_three[0], *gots_three], "update_top",
@@ -644,9 +680,9 @@
     n_small = up_to(n_in + n_out, 16)
     shape = (half, n_small, n_mp * wide)
     keep, send = on_core(
-        part(one_back, n_mp=n_mp, n_dp=n_dp, places=places, n_in=n_in, n_out=n_out),
+        part(one_back, n_dp=n_dp, places=places, n_in=n_in, n_out=n_out),
         [shaped(shape, f32), shaped(shape, bf16)],
-        [inputs, delta_two, slope_one, grad_four] + [second[k] for k in planes],
+        [inputs, delta_two, slope_one, grad_four, *second_all],
         "one_back",
         flops=LONG,
     )
@@ -654,7 +690,7 @@
     while step < half:
         got = swap(send, "dp", step)
         if step == 1:
-            got = after(early_three, got)[0]
+            got = after(gots_three[0], got)[0]
         step *= 2
         shape = (shape[0] // 2, *shape[1:])
         keep, send = on_core(

time: 146 us -> 141 us (0.966)
  waiting for transfers between devices: 47.5 us -> 57 us
  Pallas kernels: 27.7 us -> 20.5 us
  starting transfers between devices: 52.8 us -> 46.1 us
    ppermute x41 -> x47, waiting for transfers between devices: 47.5 us -> 57 us  [swap(): return lax.ppermute(value, axis, [(at, at ^ step) for at in range(count)])]
    pallas_call x35 -> x38, Pallas kernels: 27.7 us -> 20.5 us  [on_core(): pl.pallas_call(body, out_shape=outs, in_specs=[pl.BlockSpec(memory_space=...]
    ppermute x41 -> x47, starting transfers between devices: 52.8 us -> 46.1 us  [swap(): return lax.ppermute(value, axis, [(at, at ^ step) for at in range(count)])]
  transfers between devices with their start and end apart: 41 -> 47, of which waited for: 21 -> 23; matrix products, arithmetic and copies ran while one was open for 2% -> 1% of each run, Pallas kernels for 16% -> 12%
where the time goes in v5:
time: 141 us; the launch traced here: 140 us
  waiting for transfers between devices  57 us (40%)
  starting transfers between devices  46.1 us (33%)
  Pallas kernels  20.5 us (15%)
  blocking collectives  10.4 us (7%)
  local copies, waits for them, and re-layouts  3.37 us (2%)
  between operations  1.72 us (1%)
    ppermute x47, waiting for transfers between devices, swap(): return lax.ppermute(value, axis, [(at, at ^ step) for at in range(count)])  57 us
    ppermute x47, starting transfers between devices, swap(): return lax.ppermute(value, axis, [(at, at ^ step) for at in range(count)])  46.1 us
    pallas_call x38, Pallas kernels, on_core(): pl.pallas_call(body, out_shape=outs, in_specs=[pl.BlockSpec(memory_space=...  20.5 us
    all_gather x1, blocking collectives, on_device(): held = lax.all_gather(packed, 'dp')  10.4 us
    unnamed x24, local copies, waits for them, and re-layouts  3.37 us
  transfers between devices with their start and end apart: 47, of which 23 were waited for; matrix products, arithmetic and copies ran while one was open for 1% of the time, Pallas kernels for 12%

profile of v5, /device:TPU:0, one launch (start us, length us, event | category | flops | bytes accessed | tf_op | source)
XLA Modules:
  0.0 140.3 jit_solution(4257448733023183720)
XLA Ops:
  1.8 4.1 %collective-permute-start.1 = (bf16[512,256]{1,0:T(8,128)(2,1)S(1)}, bf16[512,256]{1,0:T(8,128)(2,1)S(1)}, u32[]{:S(2)}, u32[]{:S(2)}) collective-permute-start(bf16[512,256]{1,0:T(8,128)(2,1)S(1)} %convert_element_type.6.refs_0_), channel_id=1, source_target_pairs={{0,2},{1,3},{2,0},{3,1},{4,6},{5,7},{6,4},{7,5},{8,10},{9,11},{10,... | collective-permute-start | bytes 786440 | tf_op jit(solution)/shard_map/ppermute | solution.py:21
  5.9 1.6 %collective-permute-start = (bf16[512,256]{1,0:T(8,128)(2,1)S(1)}, bf16[512,256]{1,0:T(8,128)(2,1)S(1)}, u32[]{:S(2)}, u32[]{:S(2)}) collective-permute-start(bf16[512,256]{1,0:T(8,128)(2,1)S(1)} %convert_element_type.6.refs_0_), channel_id=1, source_target_pairs={{0,1},{1,0},{2,3},{3,2},{4,5},{5,4},{6,7},{7,6},{8,9},{9,8},{10,11... | collective-permute-start | bytes 786440 | tf_op jit(solution)/shard_map/ppermute | solution.py:21
  9.0 1.9 %collective-permute-start.3 = (bf16[64,128]{1,0:T(8,128)(2,1)S(1)}, bf16[64,128]{1,0:T(8,128)(2,1)S(1)}, u32[]{:S(2)}, u32[]{:S(2)}) collective-permute-start(bf16[64,128]{1,0:T(8,128)(2,1)S(1)} %pack_small.1.refs_1_), channel_id=1, source_target_pairs={{0,2},{1,3},{2,0},{3,1},{4,6},{5,7},{6,4},{7,5},{8,10},{9,11},{10,... | collective-permute-start | bytes 49160 | tf_op jit(solution)/shard_map/ppermute | solution.py:21
  10.9 2.5 %collective-permute-start.2 = (bf16[64,128]{1,0:T(8,128)(2,1)S(1)}, bf16[64,128]{1,0:T(8,128)(2,1)S(1)}, u32[]{:S(2)}, u32[]{:S(2)}) collective-permute-start(bf16[64,128]{1,0:T(8,128)(2,1)S(1)} %pack_small.1.refs_1_), channel_id=1, source_target_pairs={{0,1},{1,0},{2,3},{3,2},{4,5},{5,4},{6,7},{7,6},{8,9},{9,8},{10,11... | collective-permute-start | bytes 49160 | tf_op jit(solution)/shard_map/ppermute | solution.py:21
  15.9 3.7 %collective-permute-done.4.refs_4_ = bf16[64,128]{1,0:T(8,128)(2,1)S(1)} collective-permute-done((bf16[64,128]{1,0:T(8,128)(2,1)S(1)}, bf16[64,128]{1,0:T(8,128)(2,1)S(1)}, u32[]{:S(2)}, u32[]{:S(2)}) %collective-permute-start.4) | collective-permute-done | bytes 16416 | tf_op jit(solution)/shard_map/ppermute | solution.py:21
  19.8 2.0 %collective-permute-start.7 = (bf16[256,512]{1,0:T(8,128)(2,1)S(1)}, bf16[256,512]{1,0:T(8,128)(2,1)S(1)}, u32[]{:S(2)}, u32[]{:S(2)}) collective-permute-start(bf16[256,512]{1,0:T(8,128)(2,1)S(1)} %convert_element_type.7.refs_0_), channel_id=1, source_target_pairs={{0,2},{1,3},{2,0},{3,1},{4,6},{5,7},{6,4},{7,5},{8,10},{9,11},{10,... | collective-permute-start | bytes 786440 | tf_op jit(solution)/shard_map/ppermute | solution.py:21
  21.9 1.7 %collective-permute-start.6 = (bf16[256,512]{1,0:T(8,128)(2,1)S(1)}, bf16[256,512]{1,0:T(8,128)(2,1)S(1)}, u32[]{:S(2)}, u32[]{:S(2)}) collective-permute-start(bf16[256,512]{1,0:T(8,128)(2,1)S(1)} %convert_element_type.7.refs_0_), channel_id=1, source_target_pairs={{0,1},{1,0},{2,3},{3,2},{4,5},{5,4},{6,7},{7,6},{8,9},{9,8},{10,11... | collective-permute-start | bytes 786440 | tf_op jit(solution)/shard_map/ppermute | solution.py:21
  23.9 1.5 %collective-permute-start.5 = (bf16[2,64,128]{2,1,0:T(8,128)(2,1)S(1)}, bf16[2,64,128]{2,1,0:T(8,128)(2,1)S(1)}, u32[]{:S(2)}, u32[]{:S(2)}) collective-permute-start(bf16[2,64,128]{2,1,0:T(8,128)(2,1)S(1)} %get-tuple-element.102.wanted), channel_id=1, source_target_pairs={{0,16},{4,20},{8,24},{12,28},{16,0},{20,4},{24,8},{28,12},{1,17},{... | collective-permute-start | bytes 98312 | tf_op jit(solution)/shard_map/ppermute | solution.py:21
  25.4 10.4 %all-gather = bf16[3072,128]{1,0:T(8,128)(2,1)S(1)} all-gather(bf16[384,128]{1,0:T(8,128)(2,1)S(1)} %pack_all.1), channel_id=2, replica_groups=mesh['dp'=8,'mp'=4] {'dp'}, dimensions={0}, use_global_device_ids=true | all-gather | bytes 884736 | tf_op jit(solution)/shard_map/all_gather | solution.py:513
  36.0 2.3 %one_forward.1.act_one = bf16[2048,512]{1,0:T(8,128)(2,1)S(1)} custom-call(bf16[64,512]{1,0:T(8,128)(2,1)S(1)} %get-tuple-element.100.inputs, bf16[64,2048]{1,0:T(8,128)(2,1)S(1)} %get-tuple-element.104.first), custom_call_target="tpu_custom_call" | custom-call | tf_op jit(solution)/shard_map/one_forward/pallas_call | solution.py:57
  38.3 2.6 %collective-permute-done.8.far = bf16[512,256]{1,0:T(8,128)(2,1)S(1)} collective-permute-done((bf16[512,256]{1,0:T(8,128)(2,1)S(1)}, bf16[512,256]{1,0:T(8,128)(2,1)S(1)}, u32[]{:S(2)}, u32[]{:S(2)}) %collective-permute-start.8) | collective-permute-done | bytes 262176 | tf_op jit(solution)/shard_map/ppermute | solution.py:21
  42.5 1.7 %two_forward.1 = (bf16[512,512]{1,0:T(8,128)(2,1)S(1)}, bf16[512,512]{1,0:T(8,128)(2,1)S(1)}, f32[512,512]{1,0:T(8,128)S(1)}) custom-call(bf16[2048,512]{1,0:T(8,128)(2,1)S(1)} %one_forward.1.act_one, bf16[1536,256]{1,0:T(8,128)(2,1)S(1)} %lay.1.near, bf16[512,256]{1,0:T(8,128)(2,1)S(1)} %collective-permute-done.8.far, ...), custom_call_target="tpu_custom_call" | custom-call | tf_op jit(solution)/shard_map/two_forward/pallas_call | solution.py:57
  46.1 1.6 %collective-permute-start.14 = (bf16[256,768]{1,0:T(8,128)(2,1)S(1)}, bf16[256,768]{1,0:T(8,128)(2,1)S(1)}, u32[]{:S(2)}, u32[]{:S(2)}) collective-permute-start(bf16[256,768]{1,0:T(8,128)(2,1)S(1)} %get-tuple-element.122), channel_id=1, source_target_pairs={{0,8},{4,12},{8,0},{12,4},{16,24},{20,28},{24,16},{28,20},{1,9},{5... | collective-permute-start | bytes 1179656 | tf_op jit(solution)/shard_map/ppermute | solution.py:21
  47.7 1.5 %collective-permute-start.15 = (bf16[256,768]{1,0:T(8,128)(2,1)S(1)}, bf16[256,768]{1,0:T(8,128)(2,1)S(1)}, u32[]{:S(2)}, u32[]{:S(2)}) collective-permute-start(bf16[256,768]{1,0:T(8,128)(2,1)S(1)} %get-tuple-element.124), channel_id=1, source_target_pairs={{0,16},{4,20},{8,24},{12,28},{16,0},{20,4},{24,8},{28,12},{1,17},{... | collective-permute-start | bytes 1179656 | tf_op jit(solution)/shard_map/ppermute | solution.py:21
  49.2 3.4 %collective-permute-done.18.refs_0_ = bf16[256,512]{1,0:T(8,128)(2,1)S(1)} collective-permute-done((bf16[256,512]{1,0:T(8,128)(2,1)S(1)}, bf16[256,512]{1,0:T(8,128)(2,1)S(1)}, u32[]{:S(2)}, u32[]{:S(2)}) %collective-permute-start.18) | collective-permute-done | bytes 262176 | tf_op jit(solution)/shard_map/ppermute | solution.py:21
  52.5 3.3 %one_slope.1.slope = bf16[2048,512]{1,0:T(8,128)(2,1)S(1)} custom-call(bf16[64,512]{1,0:T(8,128)(2,1)S(1)} %get-tuple-element.100.inputs, bf16[64,2048]{1,0:T(8,128)(2,1)S(1)} %get-tuple-element.104.first), custom_call_target="tpu_custom_call" | custom-call | flops 12000000000 | tf_op jit(solution)/shard_map/one_slope/pallas_call | solution.py:57
  63.0 2.1 %collective-permute-done.20.refs_1_ = bf16[256,256]{1,0:T(8,128)(2,1)S(1)} collective-permute-done((bf16[256,256]{1,0:T(8,128)(2,1)S(1)}, bf16[256,256]{1,0:T(8,128)(2,1)S(1)}, u32[]{:S(2)}, u32[]{:S(2)}) %collective-permute-start.20) | collective-permute-done | bytes 131104 | tf_op jit(solution)/shard_map/ppermute | solution.py:21
  65.7 1.7 %collective-permute-start.22 = (bf16[128,256]{1,0:T(8,128)(2,1)S(1)}, bf16[128,256]{1,0:T(8,128)(2,1)S(1)}, u32[]{:S(2)}, u32[]{:S(2)}) collective-permute-start(bf16[128,256]{1,0:T(8,128)(2,1)S(1)} %get-tuple-element.138), channel_id=1, source_target_pairs={{0,16},{4,20},{8,24},{12,28},{16,0},{20,4},{24,8},{28,12},{1,17},{... | collective-permute-start | bytes 196616 | tf_op jit(solution)/shard_map/ppermute | solution.py:21
  70.0 1.6 %collective-permute-done.23.refs_5_ = bf16[128,256]{1,0:T(8,128)(2,1)S(1)} collective-permute-done((bf16[128,256]{1,0:T(8,128)(2,1)S(1)}, bf16[128,256]{1,0:T(8,128)(2,1)S(1)}, u32[]{:S(2)}, u32[]{:S(2)}) %collective-permute-start.23) | collective-permute-done | bytes 65568 | tf_op jit(solution)/shard_map/ppermute | solution.py:21
  73.1 1.5 %collective-permute-start.25 = (bf16[128,256]{1,0:T(8,128)(2,1)S(1)}, bf16[128,256]{1,0:T(8,128)(2,1)S(1)}, u32[]{:S(2)}, u32[]{:S(2)}) collective-permute-start(bf16[128,256]{1,0:T(8,128)(2,1)S(1)} %get-tuple-element.141.own), channel_id=1, source_target_pairs={{0,8},{4,12},{8,0},{12,4},{16,24},{20,28},{24,16},{28,20},{1,9},{5... | collective-permute-start | bytes 196616 | tf_op jit(solution)/shard_map/ppermute | solution.py:21
  75.1 1.6 %collective-permute-start.26 = (bf16[128,768]{1,0:T(8,128)(2,1)S(1)}, bf16[128,768]{1,0:T(8,128)(2,1)S(1)}, u32[]{:S(2)}, u32[]{:S(2)}) collective-permute-start(bf16[128,768]{1,0:T(8,128)(2,1)S(1)} %get-tuple-element.142.own), channel_id=1, source_target_pairs={{0,16},{4,20},{8,24},{12,28},{16,0},{20,4},{24,8},{28,12},{1,17},{... | collective-permute-start | bytes 589832 | tf_op jit(solution)/shard_map/ppermute | solution.py:21
  79.7 3.1 %collective-permute-done.29.refs_3_ = bf16[256,256]{1,0:T(8,128)(2,1)S(1)} collective-permute-done((bf16[256,256]{1,0:T(8,128)(2,1)S(1)}, bf16[256,256]{1,0:T(8,128)(2,1)S(1)}, u32[]{:S(2)}, u32[]{:S(2)}) %collective-permute-start.29) | collective-permute-done | bytes 131104 | tf_op jit(solution)/shard_map/ppermute | solution.py:21
  86.4 1.6 %collective-permute-start.31 = (bf16[256,512]{1,0:T(8,128)(2,1)S(1)}, bf16[256,512]{1,0:T(8,128)(2,1)S(1)}, u32[]{:S(2)}, u32[]{:S(2)}) collective-permute-start(bf16[256,512]{1,0:T(8,128)(2,1)S(1)} %three_own.2), channel_id=1, source_target_pairs={{0,1},{1,0},{2,3},{3,2},{4,5},{5,4},{6,7},{7,6},{8,9},{9,8},{10,11... | collective-permute-start | bytes 786440 | tf_op jit(solution)/shard_map/ppermute | solution.py:21
  88.5 8.2 %collective-permute-done.32.refs_1_ = bf16[272,768]{1,0:T(8,128)(2,1)S(1)} collective-permute-done((bf16[272,768]{1,0:T(8,128)(2,1)S(1)}, bf16[272,768]{1,0:T(8,128)(2,1)S(1)}, u32[]{:S(2)}, u32[]{:S(2)}) %collective-permute-start.32) | collective-permute-done | bytes 417824 | tf_op jit(solution)/shard_map/ppermute | solution.py:21
  104.5 2.1 %one_back.1 = (f32[4,112,256]{2,1,0:T(8,128)S(1)}, bf16[4,112,256]{2,1,0:T(8,128)(2,1)S(1)}) custom-call(bf16[64,512]{1,0:T(8,128)(2,1)S(1)} %get-tuple-element.100.inputs, bf16[512,512]{1,0:T(8,128)(2,1)S(1)} %get-tuple-element.150.delta, bf16[2048,512]{1,0:T(8,128)(2,1)S(1)} %one_slope.1.slope, f32[64,2048]{1,0:T(8,128)S(1)} %get-tuple-element.151.grad_four, ...), custom_call_target="tpu_custom_call" | custom-call | flops 99999997952 | tf_op jit(solution)/shard_map/one_back/pallas_call | solution.py:57
  107.3 7.6 %collective-permute-done.41.got = bf16[512,256]{1,0:T(8,128)(2,1)S(1)} collective-permute-done((bf16[512,256]{1,0:T(8,128)(2,1)S(1)}, bf16[512,256]{1,0:T(8,128)(2,1)S(1)}, u32[]{:S(2)}, u32[]{:S(2)}) %collective-permute-start.41) | collective-permute-done | bytes 262176 | tf_op jit(solution)/shard_map/ppermute | solution.py:21
  115.1 3.4 %collective-permute-done.35.refs_0_ = bf16[256,512]{1,0:T(8,128)(2,1)S(1)} collective-permute-done((bf16[256,512]{1,0:T(8,128)(2,1)S(1)}, bf16[256,512]{1,0:T(8,128)(2,1)S(1)}, u32[]{:S(2)}, u32[]{:S(2)}) %collective-permute-start.35) | collective-permute-done | bytes 262176 | tf_op jit(solution)/shard_map/ppermute | solution.py:21
  119.9 2.8 %collective-permute-start.43 = (bf16[512,256]{1,0:T(8,128)(2,1)S(1)}, bf16[512,256]{1,0:T(8,128)(2,1)S(1)}, u32[]{:S(2)}, u32[]{:S(2)}) collective-permute-start(bf16[512,256]{1,0:T(8,128)(2,1)S(1)} %add_up.3), channel_id=1, source_target_pairs={{0,2},{1,3},{2,0},{3,1},{4,6},{5,7},{6,4},{7,5},{8,10},{9,11},{10,... | collective-permute-start | bytes 786440 | tf_op jit(solution)/shard_map/ppermute | solution.py:21
  124.9 2.8 %collective-permute-done.38.got = bf16[1,112,256]{2,1,0:T(8,128)(2,1)S(1)} collective-permute-done((bf16[1,112,256]{2,1,0:T(8,128)(2,1)S(1)}, bf16[1,112,256]{2,1,0:T(8,128)(2,1)S(1)}, u32[]{:S(2)}, u32[]{:S(2)}) %collective-permute-start.38) | collective-permute-done | bytes 57376 | tf_op jit(solution)/shard_map/ppermute | solution.py:21
  127.8 2.4 %collective-permute-done.44.refs_1_ = bf16[256,512]{1,0:T(8,128)(2,1)S(1)} collective-permute-done((bf16[256,512]{1,0:T(8,128)(2,1)S(1)}, bf16[256,512]{1,0:T(8,128)(2,1)S(1)}, u32[]{:S(2)}, u32[]{:S(2)}) %collective-permute-start.44) | collective-permute-done | bytes 262176 | tf_op jit(solution)/shard_map/ppermute | solution.py:21
  131.4 4.2 %collective-permute-done.42.refs_0_ = bf16[512,256]{1,0:T(8,128)(2,1)S(1)} collective-permute-done((bf16[512,256]{1,0:T(8,128)(2,1)S(1)}, bf16[512,256]{1,0:T(8,128)(2,1)S(1)}, u32[]{:S(2)}, u32[]{:S(2)}) %collective-permute-start.42) | collective-permute-done | bytes 262176 | tf_op jit(solution)/shard_map/ppermute | solution.py:21
  136.8 2.8 %collective-permute-done.46.refs_0_ = bf16[112,64]{1,0:T(8,128)(2,1)S(1)} collective-permute-done((bf16[112,64]{1,0:T(8,128)(2,1)S(1)}, bf16[112,64]{1,0:T(8,128)(2,1)S(1)}, u32[]{:S(2)}, u32[]{:S(2)}) %collective-permute-start.46) | collective-permute-done | bytes 14368 | tf_op jit(solution)/shard_map/ppermute | solution.py:21
  (127 shorter events, 43.4 us)
Async XLA Ops:
  1.8 17.8 %collective-permute-start.1 = (bf16[512,256]{1,0:T(8,128)(2,1)S(1)}, bf16[512,256]{1,0:T(8,128)(2,1)S(1)}, u32[]{:S(2)}, u32[]{:S(2)}) collective-permute-start(bf16[512,256]{1,0:T(8,128)(2,1)S(1)} %convert_element_type.6.refs_0_), channel_id=1, source_target_pairs={{0,2},{1,3},{2,0},{3,1},{4,6},{5,7},{6,4},{7,5},{8,10},{9,11},{10,... | collective-permute-start | bytes 786440 | tf_op jit(solution)/shard_map/ppermute | solution.py:21
  5.9 13.7 %collective-permute-start = (bf16[512,256]{1,0:T(8,128)(2,1)S(1)}, bf16[512,256]{1,0:T(8,128)(2,1)S(1)}, u32[]{:S(2)}, u32[]{:S(2)}) collective-permute-start(bf16[512,256]{1,0:T(8,128)(2,1)S(1)} %convert_element_type.6.refs_0_), channel_id=1, source_target_pairs={{0,1},{1,0},{2,3},{3,2},{4,5},{5,4},{6,7},{7,6},{8,9},{9,8},{10,11... | collective-permute-start | bytes 786440 | tf_op jit(solution)/shard_map/ppermute | solution.py:21
  9.0 10.6 %collective-permute-start.4 = (bf16[64,128]{1,0:T(8,128)(2,1)S(1)}, bf16[64,128]{1,0:T(8,128)(2,1)S(1)}, u32[]{:S(2)}, u32[]{:S(2)}) collective-permute-start(bf16[64,128]{1,0:T(8,128)(2,1)S(1)} %pack_small.1.refs_1_), channel_id=1, source_target_pairs={{0,3},{1,2},{2,1},{3,0},{4,7},{5,6},{6,5},{7,4},{8,11},{9,10},{10,... | collective-permute-start | bytes 49160 | tf_op jit(solution)/shard_map/ppermute | solution.py:21
  9.0 10.6 %collective-permute-start.3 = (bf16[64,128]{1,0:T(8,128)(2,1)S(1)}, bf16[64,128]{1,0:T(8,128)(2,1)S(1)}, u32[]{:S(2)}, u32[]{:S(2)}) collective-permute-start(bf16[64,128]{1,0:T(8,128)(2,1)S(1)} %pack_small.1.refs_1_), channel_id=1, source_target_pairs={{0,2},{1,3},{2,0},{3,1},{4,6},{5,7},{6,4},{7,5},{8,10},{9,11},{10,... | collective-permute-start | bytes 49160 | tf_op jit(solution)/shard_map/ppermute | solution.py:21
  10.9 8.7 %collective-permute-start.2 = (bf16[64,128]{1,0:T(8,128)(2,1)S(1)}, bf16[64,128]{1,0:T(8,128)(2,1)S(1)}, u32[]{:S(2)}, u32[]{:S(2)}) collective-permute-start(bf16[64,128]{1,0:T(8,128)(2,1)S(1)} %pack_small.1.refs_1_), channel_id=1, source_target_pairs={{0,1},{1,0},{2,3},{3,2},{4,5},{5,4},{6,7},{7,6},{8,9},{9,8},{10,11... | collective-permute-start | bytes 49160 | tf_op jit(solution)/shard_map/ppermute | solution.py:21
  19.7 22.8 %collective-permute-start.9 = (bf16[1536,256]{1,0:T(8,128)(2,1)S(1)}, bf16[1536,256]{1,0:T(8,128)(2,1)S(1)}, u32[]{:S(2)}, u32[]{:S(2)}) collective-permute-start(bf16[1536,256]{1,0:T(8,128)(2,1)S(1)} %lay.1.near), channel_id=1, source_target_pairs={{0,4},{4,0},{8,12},{12,8},{16,20},{20,16},{24,28},{28,24},{1,5},{5... | collective-permute-start | bytes 2359304 | tf_op jit(solution)/shard_map/ppermute | solution.py:21
  19.8 18.5 %collective-permute-start.7 = (bf16[256,512]{1,0:T(8,128)(2,1)S(1)}, bf16[256,512]{1,0:T(8,128)(2,1)S(1)}, u32[]{:S(2)}, u32[]{:S(2)}) collective-permute-start(bf16[256,512]{1,0:T(8,128)(2,1)S(1)} %convert_element_type.7.refs_0_), channel_id=1, source_target_pairs={{0,2},{1,3},{2,0},{3,1},{4,6},{5,7},{6,4},{7,5},{8,10},{9,11},{10,... | collective-permute-start | bytes 786440 | tf_op jit(solution)/shard_map/ppermute | solution.py:21
  21.9 16.5 %collective-permute-start.6 = (bf16[256,512]{1,0:T(8,128)(2,1)S(1)}, bf16[256,512]{1,0:T(8,128)(2,1)S(1)}, u32[]{:S(2)}, u32[]{:S(2)}) collective-permute-start(bf16[256,512]{1,0:T(8,128)(2,1)S(1)} %convert_element_type.7.refs_0_), channel_id=1, source_target_pairs={{0,1},{1,0},{2,3},{3,2},{4,5},{5,4},{6,7},{7,6},{8,9},{9,8},{10,11... | collective-permute-start | bytes 786440 | tf_op jit(solution)/shard_map/ppermute | solution.py:21
  23.6 17.4 %collective-permute-start.8 = (bf16[512,256]{1,0:T(8,128)(2,1)S(1)}, bf16[512,256]{1,0:T(8,128)(2,1)S(1)}, u32[]{:S(2)}, u32[]{:S(2)}) collective-permute-start(bf16[512,256]{1,0:T(8,128)(2,1)S(1)} %collective-permute-done.1.refs_2_), channel_id=1, source_target_pairs={{0,1},{1,0},{2,3},{3,2},{4,5},{5,4},{6,7},{7,6},{8,9},{9,8},{10,11... | collective-permute-start | bytes 786440 | tf_op jit(solution)/shard_map/ppermute | solution.py:21
  23.9 14.4 %collective-permute-start.5 = (bf16[2,64,128]{2,1,0:T(8,128)(2,1)S(1)}, bf16[2,64,128]{2,1,0:T(8,128)(2,1)S(1)}, u32[]{:S(2)}, u32[]{:S(2)}) collective-permute-start(bf16[2,64,128]{2,1,0:T(8,128)(2,1)S(1)} %get-tuple-element.102.wanted), channel_id=1, source_target_pairs={{0,16},{4,20},{8,24},{12,28},{16,0},{20,4},{24,8},{28,12},{1,17},{... | collective-permute-start | bytes 98312 | tf_op jit(solution)/shard_map/ppermute | solution.py:21
  44.1 8.4 %collective-permute-start.18 = (bf16[256,512]{1,0:T(8,128)(2,1)S(1)}, bf16[256,512]{1,0:T(8,128)(2,1)S(1)}, u32[]{:S(2)}, u32[]{:S(2)}) collective-permute-start(bf16[256,512]{1,0:T(8,128)(2,1)S(1)} %collective-permute-done.7.refs_2_), channel_id=1, source_target_pairs={{0,1},{1,0},{2,3},{3,2},{4,5},{5,4},{6,7},{7,6},{8,9},{9,8},{10,11... | collective-permute-start | bytes 786440 | tf_op jit(solution)/shard_map/ppermute | solution.py:21
  46.1 10.9 %collective-permute-start.14 = (bf16[256,768]{1,0:T(8,128)(2,1)S(1)}, bf16[256,768]{1,0:T(8,128)(2,1)S(1)}, u32[]{:S(2)}, u32[]{:S(2)}) collective-permute-start(bf16[256,768]{1,0:T(8,128)(2,1)S(1)} %get-tuple-element.122), channel_id=1, source_target_pairs={{0,8},{4,12},{8,0},{12,4},{16,24},{20,28},{24,16},{28,20},{1,9},{5... | collective-permute-start | bytes 1179656 | tf_op jit(solution)/shard_map/ppermute | solution.py:21
  47.7 10.6 %collective-permute-start.15 = (bf16[256,768]{1,0:T(8,128)(2,1)S(1)}, bf16[256,768]{1,0:T(8,128)(2,1)S(1)}, u32[]{:S(2)}, u32[]{:S(2)}) collective-permute-start(bf16[256,768]{1,0:T(8,128)(2,1)S(1)} %get-tuple-element.124), channel_id=1, source_target_pairs={{0,16},{4,20},{8,24},{12,28},{16,0},{20,4},{24,8},{28,12},{1,17},{... | collective-permute-start | bytes 1179656 | tf_op jit(solution)/shard_map/ppermute | solution.py:21
  52.5 5.7 %collective-permute-start.19 = (bf16[256,512]{1,0:T(8,128)(2,1)S(1)}, bf16[256,512]{1,0:T(8,128)(2,1)S(1)}, u32[]{:S(2)}, u32[]{:S(2)}) collective-permute-start(bf16[256,512]{1,0:T(8,128)(2,1)S(1)} %collective-permute-done.18.refs_0_), channel_id=1, source_target_pairs={{0,4},{4,0},{8,12},{12,8},{16,20},{20,16},{24,28},{28,24},{1,5},{5... | collective-permute-start | bytes 786440 | tf_op jit(solution)/shard_map/ppermute | solution.py:21
  58.7 6.4 %collective-permute-start.20 = (bf16[256,256]{1,0:T(8,128)(2,1)S(1)}, bf16[256,256]{1,0:T(8,128)(2,1)S(1)}, u32[]{:S(2)}, u32[]{:S(2)}) collective-permute-start(bf16[256,256]{1,0:T(8,128)(2,1)S(1)} %get-tuple-element.134), channel_id=1, source_target_pairs={{0,8},{4,12},{8,0},{12,4},{16,24},{20,28},{24,16},{28,20},{1,9},{5... | collective-permute-start | bytes 393224 | tf_op jit(solution)/shard_map/ppermute | solution.py:21
  59.3 6.3 %collective-permute-start.21 = (bf16[256,256]{1,0:T(8,128)(2,1)S(1)}, bf16[256,256]{1,0:T(8,128)(2,1)S(1)}, u32[]{:S(2)}, u32[]{:S(2)}) collective-permute-start(bf16[256,256]{1,0:T(8,128)(2,1)S(1)} %get-tuple-element.136), channel_id=1, source_target_pairs={{0,16},{4,20},{8,24},{12,28},{16,0},{20,4},{24,8},{28,12},{1,17},{... | collective-permute-start | bytes 393224 | tf_op jit(solution)/shard_map/ppermute | solution.py:21
  60.9 7.9 %collective-permute-start.16 = (bf16[128,768]{1,0:T(8,128)(2,1)S(1)}, bf16[128,768]{1,0:T(8,128)(2,1)S(1)}, u32[]{:S(2)}, u32[]{:S(2)}) collective-permute-start(bf16[128,768]{1,0:T(8,128)(2,1)S(1)} %get-tuple-element.126), channel_id=1, source_target_pairs={{0,16},{4,20},{8,24},{12,28},{16,0},{20,4},{24,8},{28,12},{1,17},{... | collective-permute-start | bytes 589832 | tf_op jit(solution)/shard_map/ppermute | solution.py:21
  61.5 7.3 %collective-permute-start.17 = (bf16[128,768]{1,0:T(8,128)(2,1)S(1)}, bf16[128,768]{1,0:T(8,128)(2,1)S(1)}, u32[]{:S(2)}, u32[]{:S(2)}) collective-permute-start(bf16[128,768]{1,0:T(8,128)(2,1)S(1)} %get-tuple-element.127), channel_id=1, source_target_pairs={{0,8},{4,12},{8,0},{12,4},{16,24},{20,28},{24,16},{28,20},{1,9},{5... | collective-permute-start | bytes 589832 | tf_op jit(solution)/shard_map/ppermute | solution.py:21
  73.1 5.9 %collective-permute-start.25 = (bf16[128,256]{1,0:T(8,128)(2,1)S(1)}, bf16[128,256]{1,0:T(8,128)(2,1)S(1)}, u32[]{:S(2)}, u32[]{:S(2)}) collective-permute-start(bf16[128,256]{1,0:T(8,128)(2,1)S(1)} %get-tuple-element.141.own), channel_id=1, source_target_pairs={{0,8},{4,12},{8,0},{12,4},{16,24},{20,28},{24,16},{28,20},{1,9},{5... | collective-permute-start | bytes 196616 | tf_op jit(solution)/shard_map/ppermute | solution.py:21
  74.6 9.4 %collective-permute-start.24 = (bf16[128,768]{1,0:T(8,128)(2,1)S(1)}, bf16[128,768]{1,0:T(8,128)(2,1)S(1)}, u32[]{:S(2)}, u32[]{:S(2)}) collective-permute-start(bf16[128,768]{1,0:T(8,128)(2,1)S(1)} %get-tuple-element.140.own), channel_id=1, source_target_pairs={{0,8},{4,12},{8,0},{12,4},{16,24},{20,28},{24,16},{28,20},{1,9},{5... | collective-permute-start | bytes 589832 | tf_op jit(solution)/shard_map/ppermute | solution.py:21
  75.1 9.0 %collective-permute-start.26 = (bf16[128,768]{1,0:T(8,128)(2,1)S(1)}, bf16[128,768]{1,0:T(8,128)(2,1)S(1)}, u32[]{:S(2)}, u32[]{:S(2)}) collective-permute-start(bf16[128,768]{1,0:T(8,128)(2,1)S(1)} %get-tuple-element.142.own), channel_id=1, source_target_pairs={{0,16},{4,20},{8,24},{12,28},{16,0},{20,4},{24,8},{28,12},{1,17},{... | collective-permute-start | bytes 589832 | tf_op jit(solution)/shard_map/ppermute | solution.py:21
  84.5 12.1 %collective-permute-start.32 = (bf16[272,768]{1,0:T(8,128)(2,1)S(1)}, bf16[272,768]{1,0:T(8,128)(2,1)S(1)}, u32[]{:S(2)}, u32[]{:S(2)}) collective-permute-start(bf16[272,768]{1,0:T(8,128)(2,1)S(1)} %join.4.refs_0_), channel_id=1, source_target_pairs={{0,16},{4,20},{8,24},{12,28},{16,0},{20,4},{24,8},{28,12},{1,17},{... | collective-permute-start | bytes 1253384 | tf_op jit(solution)/shard_map/ppermute | solution.py:21
  85.2 11.8 %collective-permute-start.33 = (bf16[272,768]{1,0:T(8,128)(2,1)S(1)}, bf16[272,768]{1,0:T(8,128)(2,1)S(1)}, u32[]{:S(2)}, u32[]{:S(2)}) collective-permute-start(bf16[272,768]{1,0:T(8,128)(2,1)S(1)} %join.7.refs_2_), channel_id=1, source_target_pairs={{0,8},{4,12},{8,0},{12,4},{16,24},{20,28},{24,16},{28,20},{1,9},{5... | collective-permute-start | bytes 1253384 | tf_op jit(solution)/shard_map/ppermute | solution.py:21
  86.4 10.6 %collective-permute-start.31 = (bf16[256,512]{1,0:T(8,128)(2,1)S(1)}, bf16[256,512]{1,0:T(8,128)(2,1)S(1)}, u32[]{:S(2)}, u32[]{:S(2)}) collective-permute-start(bf16[256,512]{1,0:T(8,128)(2,1)S(1)} %three_own.2), channel_id=1, source_target_pairs={{0,1},{1,0},{2,3},{3,2},{4,5},{5,4},{6,7},{7,6},{8,9},{9,8},{10,11... | collective-permute-start | bytes 786440 | tf_op jit(solution)/shard_map/ppermute | solution.py:21
  100.2 6.5 %collective-permute-start.39 = (bf16[1536,256]{1,0:T(8,128)(2,1)S(1)}, bf16[1536,256]{1,0:T(8,128)(2,1)S(1)}, u32[]{:S(2)}, u32[]{:S(2)}) collective-permute-start(bf16[1536,256]{1,0:T(8,128)(2,1)S(1)} %get-tuple-element.161), channel_id=1, source_target_pairs={{0,4},{4,0},{8,12},{12,8},{16,20},{20,16},{24,28},{28,24},{1,5},{5... | collective-permute-start | bytes 2359304 | tf_op jit(solution)/shard_map/ppermute | solution.py:21
  101.7 13.3 %collective-permute-start.41 = (bf16[512,256]{1,0:T(8,128)(2,1)S(1)}, bf16[512,256]{1,0:T(8,128)(2,1)S(1)}, u32[]{:S(2)}, u32[]{:S(2)}) collective-permute-start(bf16[512,256]{1,0:T(8,128)(2,1)S(1)} %two_own.3), channel_id=1, source_target_pairs={{0,1},{1,0},{2,3},{3,2},{4,5},{5,4},{6,7},{7,6},{8,9},{9,8},{10,11... | collective-permute-start | bytes 786440 | tf_op jit(solution)/shard_map/ppermute | solution.py:21
  103.5 15.0 %collective-permute-start.35 = (bf16[256,512]{1,0:T(8,128)(2,1)S(1)}, bf16[256,512]{1,0:T(8,128)(2,1)S(1)}, u32[]{:S(2)}, u32[]{:S(2)}) collective-permute-start(bf16[256,512]{1,0:T(8,128)(2,1)S(1)} %add_up.2), channel_id=1, source_target_pairs={{0,2},{1,3},{2,0},{3,1},{4,6},{5,7},{6,4},{7,5},{8,10},{9,11},{10,... | collective-permute-start | bytes 786440 | tf_op jit(solution)/shard_map/ppermute | solution.py:21
  106.6 8.5 %collective-permute-start.36 = (bf16[4,112,256]{2,1,0:T(8,128)(2,1)S(1)}, bf16[4,112,256]{2,1,0:T(8,128)(2,1)S(1)}, u32[]{:S(2)}, u32[]{:S(2)}) collective-permute-start(bf16[4,112,256]{2,1,0:T(8,128)(2,1)S(1)} %get-tuple-element.154), channel_id=1, source_target_pairs={{0,4},{4,0},{8,12},{12,8},{16,20},{20,16},{24,28},{28,24},{1,5},{5... | collective-permute-start | bytes 688136 | tf_op jit(solution)/shard_map/ppermute | solution.py:21
  115.0 15.2 %collective-permute-start.44 = (bf16[256,512]{1,0:T(8,128)(2,1)S(1)}, bf16[256,512]{1,0:T(8,128)(2,1)S(1)}, u32[]{:S(2)}, u32[]{:S(2)}) collective-permute-start(bf16[256,512]{1,0:T(8,128)(2,1)S(1)} %get-tuple-element.168), channel_id=1, source_target_pairs={{0,1},{1,0},{2,3},{3,2},{4,5},{5,4},{6,7},{7,6},{8,9},{9,8},{10,11... | collective-permute-start | bytes 786440 | tf_op jit(solution)/shard_map/ppermute | solution.py:21
  119.9 15.6 %collective-permute-start.42 = (bf16[512,256]{1,0:T(8,128)(2,1)S(1)}, bf16[512,256]{1,0:T(8,128)(2,1)S(1)}, u32[]{:S(2)}, u32[]{:S(2)}) collective-permute-start(bf16[512,256]{1,0:T(8,128)(2,1)S(1)} %get-tuple-element.166), channel_id=1, source_target_pairs={{0,1},{1,0},{2,3},{3,2},{4,5},{5,4},{6,7},{7,6},{8,9},{9,8},{10,11... | collective-permute-start | bytes 786440 | tf_op jit(solution)/shard_map/ppermute | solution.py:21
  119.9 15.6 %collective-permute-start.43 = (bf16[512,256]{1,0:T(8,128)(2,1)S(1)}, bf16[512,256]{1,0:T(8,128)(2,1)S(1)}, u32[]{:S(2)}, u32[]{:S(2)}) collective-permute-start(bf16[512,256]{1,0:T(8,128)(2,1)S(1)} %add_up.3), channel_id=1, source_target_pairs={{0,2},{1,3},{2,0},{3,1},{4,6},{5,7},{6,4},{7,5},{8,10},{9,11},{10,... | collective-permute-start | bytes 786440 | tf_op jit(solution)/shard_map/ppermute | solution.py:21
  127.8 7.8 %collective-permute-start.45 = (bf16[112,128]{1,0:T(8,128)(2,1)S(1)}, bf16[112,128]{1,0:T(8,128)(2,1)S(1)}, u32[]{:S(2)}, u32[]{:S(2)}) collective-permute-start(bf16[112,128]{1,0:T(8,128)(2,1)S(1)} %get-tuple-element.170), channel_id=1, source_target_pairs={{0,2},{1,3},{2,0},{3,1},{4,6},{5,7},{6,4},{7,5},{8,10},{9,11},{10,... | collective-permute-start | bytes 86024 | tf_op jit(solution)/shard_map/ppermute | solution.py:21
  (26 other events, 170.2 us)

commit v6 on v5

--- a/solution.py
+++ b/solution.py
@@ -171,7 +171,7 @@
     lax.fori_loop(0, first.shape[1] // tile, step, 0)
 
 
-def two_forward(act_one, near, far, near_too, far_too, act, act_t, slope):
+def two_forward(act_one, near, far, near_too, far_too, act, act_t, pre_two):
     n_rows = act_one.shape[1]
     cut = min(256, n_rows)
     first, cols = near.shape
@@ -184,7 +184,13 @@
             value = gelu_act(pre)
             act_t[to, at] = value.astype(bf16)
             act[at, to] = value.T.astype(bf16)
-            slope[to, at] = gelu_slope(pre)
+            pre_two[to, at] = pre
+
+
+def two_slope(pre, out):
+    cut = min(128, pre.shape[0])
+    for c in range(0, pre.shape[0], cut):
+        out[c : c + cut] = gelu_slope(pre[c : c + cut])
 
 
 def divided(kept, bit):
@@ -439,7 +445,7 @@
 
 
 def passed_on(held, n_mp, ready):
-    for k in sorted((k for k in range(1, n_mp) if parent(k)), key=lambda k: -low_bit(k)):
+    for k in sorted((k for k in range(1, n_mp) if parent(k) and k not in held), key=lambda k: -low_bit(k)):
         held[k] = swap(after(ready, held[parent(k)])[0], "mp", low_bit(k))
 
 
@@ -531,15 +537,14 @@
     third_early = [third[k] for k in planes if k and not parent(k)]
     far = after((act_one, third_early, wanted[1]), second[n_mp - 1])[0]
     second_all = [near, far, swap(near, "dp", 1), swap(far, "dp", 1)]
-    act_two, act_two_t, slope_two = on_core(
+    act_two, act_two_t, pre_two = on_core(
         two_forward,
         [shaped((n_rows, wide_mid), bf16), shaped((wide_mid, n_rows), bf16), shaped((wide_mid, n_rows), f32)],
         [act_one, *second_all],
         "two_forward",
     )
-    passed_on(third, n_mp, act_two)
-    third_too = {k: swap(after(act_one, third[k])[0] if k else top, "dp", 1) for k in planes}
-    third_all = [[third[k] for k in ks] + [third_too[k] for k in ks] for ks in groups]
+    passed_on(third, n_mp - 1, act_two)
+    third_all = []
     evens = list(range(0, n_dp, 2))
     bits = [1 << i for i in range(1, n_dp.bit_length() - 1)]
     orders = [bits, bits[::-1]]
@@ -547,11 +552,14 @@
         part(one_slope, tile=256), shaped((width, n_rows), bf16), [inputs, first], "one_slope",
         flops=12_000_000_000,
     )
+    slope_two = on_core(two_slope, shaped((wide_mid, n_rows), f32), [pre_two], "two_slope")
     terms = []
     ahead = [third[k] for k in planes if k and not parent(k)]
-    for ks, weights in zip(groups, third_all):
+    for ks in groups:
         cols = len(ks) * n_top
-        weights = after(ahead, *weights)
+        third_too = [swap(after(act_one, third[k])[0] if k else top, "dp", 1) for k in ks]
+        third_all.append([third[k] for k in ks] + third_too)
+        weights = after(ahead, *third_all[-1])
         left = half // 2
         kinds = [shaped(((left - 1) * rows, cols // 2), f32), shaped((left * rows, cols // 2), bf16)]
         own, *halves = on_core(
@@ -560,11 +568,12 @@
             [act_two, *weights],
             "three_home",
         )
+        passed_on(third, n_mp, halves)
         ahead = []
         for stage in range(len(bits)):
             sends = halves[1::2] if len(halves) == 4 else halves
             gots = [swap(send, "dp", order[stage]) for send, order in zip(sends, orders)]
-            ahead = ahead or [slope_one, *gots]
+            ahead = ahead or [slope_one, slope_two, *gots]
             if stage + 1 == len(bits):
                 break
             keeps, left = halves[::2], left // 2
@@ -689,7 +698,7 @@
     step = 1
     while step < half:
         got = swap(send, "dp", step)
-        if step == 1:
+        if step == 2:
             got = after(gots_three[0], got)[0]
         step *= 2
         shape = (shape[0] // 2, *shape[1:])

time: 141 us -> 139 us (0.986)
  waiting for transfers between devices: 57 us -> 53.4 us
    ppermute x47, waiting for transfers between devices: 57 us -> 53.4 us  [swap(): return lax.ppermute(value, axis, [(at, at ^ step) for at in range(count)])]
    unnamed x24 -> x28, local copies, waits for them, and re-layouts: 3.37 us -> 3.65 us
    pallas_call x38 -> x39, Pallas kernels: 20.5 us -> 20.7 us  [on_core(): pl.pallas_call(body, out_shape=outs, in_specs=[pl.BlockSpec(memory_space=...]
  transfers between devices with their start and end apart: 47 -> 47, of which waited for: 23 -> 24; matrix products, arithmetic and copies ran while one was open for 1% -> 1% of each run, Pallas kernels for 12% -> 10%
where the time goes in v6:
time: 139 us; the launch traced here: 138 us
  waiting for transfers between devices  53.4 us (38%)
  starting transfers between devices  47.2 us (34%)
  Pallas kernels  20.7 us (15%)
  blocking collectives  10.4 us (7%)
  local copies, waits for them, and re-layouts  3.65 us (3%)
  between operations  1.72 us (1%)
    ppermute x47, waiting for transfers between devices, swap(): return lax.ppermute(value, axis, [(at, at ^ step) for at in range(count)])  53.4 us
    ppermute x47, starting transfers between devices, swap(): return lax.ppermute(value, axis, [(at, at ^ step) for at in range(count)])  47.2 us
    pallas_call x39, Pallas kernels, on_core(): pl.pallas_call(body, out_shape=outs, in_specs=[pl.BlockSpec(memory_space=...  20.7 us
    all_gather x1, blocking collectives, on_device(): held = lax.all_gather(packed, 'dp')  10.4 us
    unnamed x28, local copies, waits for them, and re-layouts  3.65 us
  transfers between devices with their start and end apart: 47, of which 24 were waited for; matrix products, arithmetic and copies ran while one was open for 1% of the time, Pallas kernels for 10%

profile of v6, /device:TPU:0, one launch (start us, length us, event | category | flops | bytes accessed | tf_op | source)
XLA Modules:
  0.0 138.3 jit_solution(16244372997460362827)
XLA Ops:
  1.8 4.1 %collective-permute-start.1 = (bf16[512,256]{1,0:T(8,128)(2,1)S(1)}, bf16[512,256]{1,0:T(8,128)(2,1)S(1)}, u32[]{:S(2)}, u32[]{:S(2)}) collective-permute-start(bf16[512,256]{1,0:T(8,128)(2,1)S(1)} %convert_element_type.6.refs_0_), channel_id=1, source_target_pairs={{0,2},{1,3},{2,0},{3,1},{4,6},{5,7},{6,4},{7,5},{8,10},{9,11},{10,... | collective-permute-start | bytes 786440 | tf_op jit(solution)/shard_map/ppermute | solution.py:21
  5.9 1.6 %collective-permute-start = (bf16[512,256]{1,0:T(8,128)(2,1)S(1)}, bf16[512,256]{1,0:T(8,128)(2,1)S(1)}, u32[]{:S(2)}, u32[]{:S(2)}) collective-permute-start(bf16[512,256]{1,0:T(8,128)(2,1)S(1)} %convert_element_type.6.refs_0_), channel_id=1, source_target_pairs={{0,1},{1,0},{2,3},{3,2},{4,5},{5,4},{6,7},{7,6},{8,9},{9,8},{10,11... | collective-permute-start | bytes 786440 | tf_op jit(solution)/shard_map/ppermute | solution.py:21
  9.0 1.9 %collective-permute-start.3 = (bf16[64,128]{1,0:T(8,128)(2,1)S(1)}, bf16[64,128]{1,0:T(8,128)(2,1)S(1)}, u32[]{:S(2)}, u32[]{:S(2)}) collective-permute-start(bf16[64,128]{1,0:T(8,128)(2,1)S(1)} %pack_small.1.refs_1_), channel_id=1, source_target_pairs={{0,2},{1,3},{2,0},{3,1},{4,6},{5,7},{6,4},{7,5},{8,10},{9,11},{10,... | collective-permute-start | bytes 49160 | tf_op jit(solution)/shard_map/ppermute | solution.py:21
  10.9 2.5 %collective-permute-start.2 = (bf16[64,128]{1,0:T(8,128)(2,1)S(1)}, bf16[64,128]{1,0:T(8,128)(2,1)S(1)}, u32[]{:S(2)}, u32[]{:S(2)}) collective-permute-start(bf16[64,128]{1,0:T(8,128)(2,1)S(1)} %pack_small.1.refs_1_), channel_id=1, source_target_pairs={{0,1},{1,0},{2,3},{3,2},{4,5},{5,4},{6,7},{7,6},{8,9},{9,8},{10,11... | collective-permute-start | bytes 49160 | tf_op jit(solution)/shard_map/ppermute | solution.py:21
  15.9 3.7 %collective-permute-done.4.refs_4_ = bf16[64,128]{1,0:T(8,128)(2,1)S(1)} collective-permute-done((bf16[64,128]{1,0:T(8,128)(2,1)S(1)}, bf16[64,128]{1,0:T(8,128)(2,1)S(1)}, u32[]{:S(2)}, u32[]{:S(2)}) %collective-permute-start.4) | collective-permute-done | bytes 16416 | tf_op jit(solution)/shard_map/ppermute | solution.py:21
  19.8 2.0 %collective-permute-start.7 = (bf16[256,512]{1,0:T(8,128)(2,1)S(1)}, bf16[256,512]{1,0:T(8,128)(2,1)S(1)}, u32[]{:S(2)}, u32[]{:S(2)}) collective-permute-start(bf16[256,512]{1,0:T(8,128)(2,1)S(1)} %convert_element_type.7.refs_0_), channel_id=1, source_target_pairs={{0,2},{1,3},{2,0},{3,1},{4,6},{5,7},{6,4},{7,5},{8,10},{9,11},{10,... | collective-permute-start | bytes 786440 | tf_op jit(solution)/shard_map/ppermute | solution.py:21
  21.9 1.7 %collective-permute-start.6 = (bf16[256,512]{1,0:T(8,128)(2,1)S(1)}, bf16[256,512]{1,0:T(8,128)(2,1)S(1)}, u32[]{:S(2)}, u32[]{:S(2)}) collective-permute-start(bf16[256,512]{1,0:T(8,128)(2,1)S(1)} %convert_element_type.7.refs_0_), channel_id=1, source_target_pairs={{0,1},{1,0},{2,3},{3,2},{4,5},{5,4},{6,7},{7,6},{8,9},{9,8},{10,11... | collective-permute-start | bytes 786440 | tf_op jit(solution)/shard_map/ppermute | solution.py:21
  23.9 1.5 %collective-permute-start.5 = (bf16[2,64,128]{2,1,0:T(8,128)(2,1)S(1)}, bf16[2,64,128]{2,1,0:T(8,128)(2,1)S(1)}, u32[]{:S(2)}, u32[]{:S(2)}) collective-permute-start(bf16[2,64,128]{2,1,0:T(8,128)(2,1)S(1)} %get-tuple-element.102.wanted), channel_id=1, source_target_pairs={{0,16},{4,20},{8,24},{12,28},{16,0},{20,4},{24,8},{28,12},{1,17},{... | collective-permute-start | bytes 98312 | tf_op jit(solution)/shard_map/ppermute | solution.py:21
  25.4 10.4 %all-gather = bf16[3072,128]{1,0:T(8,128)(2,1)S(1)} all-gather(bf16[384,128]{1,0:T(8,128)(2,1)S(1)} %pack_all.1), channel_id=2, replica_groups=mesh['dp'=8,'mp'=4] {'dp'}, dimensions={0}, use_global_device_ids=true | all-gather | bytes 884736 | tf_op jit(solution)/shard_map/all_gather | solution.py:519
  36.0 2.3 %one_forward.1.act_one = bf16[2048,512]{1,0:T(8,128)(2,1)S(1)} custom-call(bf16[64,512]{1,0:T(8,128)(2,1)S(1)} %get-tuple-element.100.inputs, bf16[64,2048]{1,0:T(8,128)(2,1)S(1)} %get-tuple-element.104.first), custom_call_target="tpu_custom_call" | custom-call | tf_op jit(solution)/shard_map/one_forward/pallas_call | solution.py:57
  39.3 1.7 %collective-permute-done.8.far = bf16[512,256]{1,0:T(8,128)(2,1)S(1)} collective-permute-done((bf16[512,256]{1,0:T(8,128)(2,1)S(1)}, bf16[512,256]{1,0:T(8,128)(2,1)S(1)}, u32[]{:S(2)}, u32[]{:S(2)}) %collective-permute-start.8) | collective-permute-done | bytes 262176 | tf_op jit(solution)/shard_map/ppermute | solution.py:21
  47.4 1.5 %collective-permute-start.15 = (bf16[256,768]{1,0:T(8,128)(2,1)S(1)}, bf16[256,768]{1,0:T(8,128)(2,1)S(1)}, u32[]{:S(2)}, u32[]{:S(2)}) collective-permute-start(bf16[256,768]{1,0:T(8,128)(2,1)S(1)} %get-tuple-element.124), channel_id=1, source_target_pairs={{0,16},{4,20},{8,24},{12,28},{16,0},{20,4},{24,8},{28,12},{1,17},{... | collective-permute-start | bytes 1179656 | tf_op jit(solution)/shard_map/ppermute | solution.py:21
  48.9 4.4 %collective-permute-done.18.refs_0_ = bf16[256,512]{1,0:T(8,128)(2,1)S(1)} collective-permute-done((bf16[256,512]{1,0:T(8,128)(2,1)S(1)}, bf16[256,512]{1,0:T(8,128)(2,1)S(1)}, u32[]{:S(2)}, u32[]{:S(2)}) %collective-permute-start.18) | collective-permute-done | bytes 262176 | tf_op jit(solution)/shard_map/ppermute | solution.py:21
  53.3 3.3 %one_slope.1.slope = bf16[2048,512]{1,0:T(8,128)(2,1)S(1)} custom-call(bf16[64,512]{1,0:T(8,128)(2,1)S(1)} %get-tuple-element.100.inputs, bf16[64,2048]{1,0:T(8,128)(2,1)S(1)} %get-tuple-element.104.first), custom_call_target="tpu_custom_call" | custom-call | flops 12000000000 | tf_op jit(solution)/shard_map/one_slope/pallas_call | solution.py:57
  59.0 1.5 %collective-permute-start.21 = (bf16[256,256]{1,0:T(8,128)(2,1)S(1)}, bf16[256,256]{1,0:T(8,128)(2,1)S(1)}, u32[]{:S(2)}, u32[]{:S(2)}) collective-permute-start(bf16[256,256]{1,0:T(8,128)(2,1)S(1)} %get-tuple-element.137), channel_id=1, source_target_pairs={{0,16},{4,20},{8,24},{12,28},{16,0},{20,4},{24,8},{28,12},{1,17},{... | collective-permute-start | bytes 393224 | tf_op jit(solution)/shard_map/ppermute | solution.py:21
  63.5 1.9 %collective-permute-done.21.refs_3_ = bf16[256,256]{1,0:T(8,128)(2,1)S(1)} collective-permute-done((bf16[256,256]{1,0:T(8,128)(2,1)S(1)}, bf16[256,256]{1,0:T(8,128)(2,1)S(1)}, u32[]{:S(2)}, u32[]{:S(2)}) %collective-permute-start.21) | collective-permute-done | bytes 131104 | tf_op jit(solution)/shard_map/ppermute | solution.py:21
  65.4 1.6 %collective-permute-start.22 = (bf16[128,256]{1,0:T(8,128)(2,1)S(1)}, bf16[128,256]{1,0:T(8,128)(2,1)S(1)}, u32[]{:S(2)}, u32[]{:S(2)}) collective-permute-start(bf16[128,256]{1,0:T(8,128)(2,1)S(1)} %get-tuple-element.139), channel_id=1, source_target_pairs={{0,16},{4,20},{8,24},{12,28},{16,0},{20,4},{24,8},{28,12},{1,17},{... | collective-permute-start | bytes 196616 | tf_op jit(solution)/shard_map/ppermute | solution.py:21
  67.0 1.6 %collective-permute-start.23 = (bf16[128,256]{1,0:T(8,128)(2,1)S(1)}, bf16[128,256]{1,0:T(8,128)(2,1)S(1)}, u32[]{:S(2)}, u32[]{:S(2)}) collective-permute-start(bf16[128,256]{1,0:T(8,128)(2,1)S(1)} %get-tuple-element.140), channel_id=1, source_target_pairs={{0,8},{4,12},{8,0},{12,4},{16,24},{20,28},{24,16},{28,20},{1,9},{5... | collective-permute-start | bytes 196616 | tf_op jit(solution)/shard_map/ppermute | solution.py:21
  77.1 1.8 %collective-permute-start.29 = (bf16[256,256]{1,0:T(8,128)(2,1)S(1)}, bf16[256,256]{1,0:T(8,128)(2,1)S(1)}, u32[]{:S(2)}, u32[]{:S(2)}) collective-permute-start(bf16[256,256]{1,0:T(8,128)(2,1)S(1)} %join.6.refs_2_), channel_id=1, source_target_pairs={{0,8},{4,12},{8,0},{12,4},{16,24},{20,28},{24,16},{28,20},{1,9},{5... | collective-permute-start | bytes 393224 | tf_op jit(solution)/shard_map/ppermute | solution.py:21
  79.4 3.6 %collective-permute-done.29.refs_3_ = bf16[256,256]{1,0:T(8,128)(2,1)S(1)} collective-permute-done((bf16[256,256]{1,0:T(8,128)(2,1)S(1)}, bf16[256,256]{1,0:T(8,128)(2,1)S(1)}, u32[]{:S(2)}, u32[]{:S(2)}) %collective-permute-start.29) | collective-permute-done | bytes 131104 | tf_op jit(solution)/shard_map/ppermute | solution.py:21
  85.0 1.6 %collective-permute-start.33 = (bf16[272,768]{1,0:T(8,128)(2,1)S(1)}, bf16[272,768]{1,0:T(8,128)(2,1)S(1)}, u32[]{:S(2)}, u32[]{:S(2)}) collective-permute-start(bf16[272,768]{1,0:T(8,128)(2,1)S(1)} %join.7.refs_2_), channel_id=1, source_target_pairs={{0,8},{4,12},{8,0},{12,4},{16,24},{20,28},{24,16},{28,20},{1,9},{5... | collective-permute-start | bytes 1253384 | tf_op jit(solution)/shard_map/ppermute | solution.py:21
  88.2 8.3 %collective-permute-done.32.refs_1_ = bf16[272,768]{1,0:T(8,128)(2,1)S(1)} collective-permute-done((bf16[272,768]{1,0:T(8,128)(2,1)S(1)}, bf16[272,768]{1,0:T(8,128)(2,1)S(1)}, u32[]{:S(2)}, u32[]{:S(2)}) %collective-permute-start.32) | collective-permute-done | bytes 417824 | tf_op jit(solution)/shard_map/ppermute | solution.py:21
  101.8 2.1 %one_back.1 = (f32[4,112,256]{2,1,0:T(8,128)S(1)}, bf16[4,112,256]{2,1,0:T(8,128)(2,1)S(1)}) custom-call(bf16[64,512]{1,0:T(8,128)(2,1)S(1)} %get-tuple-element.100.inputs, bf16[512,512]{1,0:T(8,128)(2,1)S(1)} %get-tuple-element.150.delta, bf16[2048,512]{1,0:T(8,128)(2,1)S(1)} %one_slope.1.slope, f32[64,2048]{1,0:T(8,128)S(1)} %get-tuple-element.151.grad_four, ...), custom_call_target="tpu_custom_call" | custom-call | flops 99999997952 | tf_op jit(solution)/shard_map/one_back/pallas_call | solution.py:57
  107.0 3.0 %collective-permute-done.41.got = bf16[512,256]{1,0:T(8,128)(2,1)S(1)} collective-permute-done((bf16[512,256]{1,0:T(8,128)(2,1)S(1)}, bf16[512,256]{1,0:T(8,128)(2,1)S(1)}, u32[]{:S(2)}, u32[]{:S(2)}) %collective-permute-start.41) | collective-permute-done | bytes 262176 | tf_op jit(solution)/shard_map/ppermute | solution.py:21
  112.5 1.6 %collective-permute-start.42 = (bf16[512,256]{1,0:T(8,128)(2,1)S(1)}, bf16[512,256]{1,0:T(8,128)(2,1)S(1)}, u32[]{:S(2)}, u32[]{:S(2)}) collective-permute-start(bf16[512,256]{1,0:T(8,128)(2,1)S(1)} %get-tuple-element.166), channel_id=1, source_target_pairs={{0,1},{1,0},{2,3},{3,2},{4,5},{5,4},{6,7},{7,6},{8,9},{9,8},{10,11... | collective-permute-start | bytes 786440 | tf_op jit(solution)/shard_map/ppermute | solution.py:21
  114.2 1.8 %collective-permute-done.37.got = bf16[2,112,256]{2,1,0:T(8,128)(2,1)S(1)} collective-permute-done((bf16[2,112,256]{2,1,0:T(8,128)(2,1)S(1)}, bf16[2,112,256]{2,1,0:T(8,128)(2,1)S(1)}, u32[]{:S(2)}, u32[]{:S(2)}) %collective-permute-start.37) | collective-permute-done | bytes 114720 | tf_op jit(solution)/shard_map/ppermute | solution.py:21
  116.0 4.7 %collective-permute-done.36.refs_0_ = bf16[256,512]{1,0:T(8,128)(2,1)S(1)} collective-permute-done((bf16[256,512]{1,0:T(8,128)(2,1)S(1)}, bf16[256,512]{1,0:T(8,128)(2,1)S(1)}, u32[]{:S(2)}, u32[]{:S(2)}) %collective-permute-start.36) | collective-permute-done | bytes 262176 | tf_op jit(solution)/shard_map/ppermute | solution.py:21
  120.7 1.8 %collective-permute-start.38 = (bf16[1,112,256]{2,1,0:T(8,128)(2,1)S(1)}, bf16[1,112,256]{2,1,0:T(8,128)(2,1)S(1)}, u32[]{:S(2)}, u32[]{:S(2)}) collective-permute-start(bf16[1,112,256]{2,1,0:T(8,128)(2,1)S(1)} %get-tuple-element.159), channel_id=1, source_target_pairs={{0,16},{4,20},{8,24},{12,28},{16,0},{20,4},{24,8},{28,12},{1,17},{... | collective-permute-start | bytes 172040 | tf_op jit(solution)/shard_map/ppermute | solution.py:21
  122.5 2.5 %collective-permute-done.38.got = bf16[1,112,256]{2,1,0:T(8,128)(2,1)S(1)} collective-permute-done((bf16[1,112,256]{2,1,0:T(8,128)(2,1)S(1)}, bf16[1,112,256]{2,1,0:T(8,128)(2,1)S(1)}, u32[]{:S(2)}, u32[]{:S(2)}) %collective-permute-start.38) | collective-permute-done | bytes 57376 | tf_op jit(solution)/shard_map/ppermute | solution.py:21
  125.1 4.4 %collective-permute-done.44.refs_1_ = bf16[256,512]{1,0:T(8,128)(2,1)S(1)} collective-permute-done((bf16[256,512]{1,0:T(8,128)(2,1)S(1)}, bf16[256,512]{1,0:T(8,128)(2,1)S(1)}, u32[]{:S(2)}, u32[]{:S(2)}) %collective-permute-start.44) | collective-permute-done | bytes 262176 | tf_op jit(solution)/shard_map/ppermute | solution.py:21
  130.6 2.0 %collective-permute-done.42.refs_0_ = bf16[512,256]{1,0:T(8,128)(2,1)S(1)} collective-permute-done((bf16[512,256]{1,0:T(8,128)(2,1)S(1)}, bf16[512,256]{1,0:T(8,128)(2,1)S(1)}, u32[]{:S(2)}, u32[]{:S(2)}) %collective-permute-start.42) | collective-permute-done | bytes 262176 | tf_op jit(solution)/shard_map/ppermute | solution.py:21
  135.1 2.4 %collective-permute-done.46.refs_0_ = bf16[112,64]{1,0:T(8,128)(2,1)S(1)} collective-permute-done((bf16[112,64]{1,0:T(8,128)(2,1)S(1)}, bf16[112,64]{1,0:T(8,128)(2,1)S(1)}, u32[]{:S(2)}, u32[]{:S(2)}) %collective-permute-start.46) | collective-permute-done | bytes 14368 | tf_op jit(solution)/shard_map/ppermute | solution.py:21
  (132 shorter events, 45.9 us)
Async XLA Ops:
  1.8 17.8 %collective-permute-start.1 = (bf16[512,256]{1,0:T(8,128)(2,1)S(1)}, bf16[512,256]{1,0:T(8,128)(2,1)S(1)}, u32[]{:S(2)}, u32[]{:S(2)}) collective-permute-start(bf16[512,256]{1,0:T(8,128)(2,1)S(1)} %convert_element_type.6.refs_0_), channel_id=1, source_target_pairs={{0,2},{1,3},{2,0},{3,1},{4,6},{5,7},{6,4},{7,5},{8,10},{9,11},{10,... | collective-permute-start | bytes 786440 | tf_op jit(solution)/shard_map/ppermute | solution.py:21
  5.9 13.7 %collective-permute-start = (bf16[512,256]{1,0:T(8,128)(2,1)S(1)}, bf16[512,256]{1,0:T(8,128)(2,1)S(1)}, u32[]{:S(2)}, u32[]{:S(2)}) collective-permute-start(bf16[512,256]{1,0:T(8,128)(2,1)S(1)} %convert_element_type.6.refs_0_), channel_id=1, source_target_pairs={{0,1},{1,0},{2,3},{3,2},{4,5},{5,4},{6,7},{7,6},{8,9},{9,8},{10,11... | collective-permute-start | bytes 786440 | tf_op jit(solution)/shard_map/ppermute | solution.py:21
  9.0 10.6 %collective-permute-start.4 = (bf16[64,128]{1,0:T(8,128)(2,1)S(1)}, bf16[64,128]{1,0:T(8,128)(2,1)S(1)}, u32[]{:S(2)}, u32[]{:S(2)}) collective-permute-start(bf16[64,128]{1,0:T(8,128)(2,1)S(1)} %pack_small.1.refs_1_), channel_id=1, source_target_pairs={{0,3},{1,2},{2,1},{3,0},{4,7},{5,6},{6,5},{7,4},{8,11},{9,10},{10,... | collective-permute-start | bytes 49160 | tf_op jit(solution)/shard_map/ppermute | solution.py:21
  9.0 10.6 %collective-permute-start.3 = (bf16[64,128]{1,0:T(8,128)(2,1)S(1)}, bf16[64,128]{1,0:T(8,128)(2,1)S(1)}, u32[]{:S(2)}, u32[]{:S(2)}) collective-permute-start(bf16[64,128]{1,0:T(8,128)(2,1)S(1)} %pack_small.1.refs_1_), channel_id=1, source_target_pairs={{0,2},{1,3},{2,0},{3,1},{4,6},{5,7},{6,4},{7,5},{8,10},{9,11},{10,... | collective-permute-start | bytes 49160 | tf_op jit(solution)/shard_map/ppermute | solution.py:21
  10.9 8.7 %collective-permute-start.2 = (bf16[64,128]{1,0:T(8,128)(2,1)S(1)}, bf16[64,128]{1,0:T(8,128)(2,1)S(1)}, u32[]{:S(2)}, u32[]{:S(2)}) collective-permute-start(bf16[64,128]{1,0:T(8,128)(2,1)S(1)} %pack_small.1.refs_1_), channel_id=1, source_target_pairs={{0,1},{1,0},{2,3},{3,2},{4,5},{5,4},{6,7},{7,6},{8,9},{9,8},{10,11... | collective-permute-start | bytes 49160 | tf_op jit(solution)/shard_map/ppermute | solution.py:21
  19.7 22.8 %collective-permute-start.9 = (bf16[1536,256]{1,0:T(8,128)(2,1)S(1)}, bf16[1536,256]{1,0:T(8,128)(2,1)S(1)}, u32[]{:S(2)}, u32[]{:S(2)}) collective-permute-start(bf16[1536,256]{1,0:T(8,128)(2,1)S(1)} %lay.1.near), channel_id=1, source_target_pairs={{0,4},{4,0},{8,12},{12,8},{16,20},{20,16},{24,28},{28,24},{1,5},{5... | collective-permute-start | bytes 2359304 | tf_op jit(solution)/shard_map/ppermute | solution.py:21
  19.8 18.5 %collective-permute-start.7 = (bf16[256,512]{1,0:T(8,128)(2,1)S(1)}, bf16[256,512]{1,0:T(8,128)(2,1)S(1)}, u32[]{:S(2)}, u32[]{:S(2)}) collective-permute-start(bf16[256,512]{1,0:T(8,128)(2,1)S(1)} %convert_element_type.7.refs_0_), channel_id=1, source_target_pairs={{0,2},{1,3},{2,0},{3,1},{4,6},{5,7},{6,4},{7,5},{8,10},{9,11},{10,... | collective-permute-start | bytes 786440 | tf_op jit(solution)/shard_map/ppermute | solution.py:21
  21.9 16.9 %collective-permute-start.6 = (bf16[256,512]{1,0:T(8,128)(2,1)S(1)}, bf16[256,512]{1,0:T(8,128)(2,1)S(1)}, u32[]{:S(2)}, u32[]{:S(2)}) collective-permute-start(bf16[256,512]{1,0:T(8,128)(2,1)S(1)} %convert_element_type.7.refs_0_), channel_id=1, source_target_pairs={{0,1},{1,0},{2,3},{3,2},{4,5},{5,4},{6,7},{7,6},{8,9},{9,8},{10,11... | collective-permute-start | bytes 786440 | tf_op jit(solution)/shard_map/ppermute | solution.py:21
  23.6 17.4 %collective-permute-start.8 = (bf16[512,256]{1,0:T(8,128)(2,1)S(1)}, bf16[512,256]{1,0:T(8,128)(2,1)S(1)}, u32[]{:S(2)}, u32[]{:S(2)}) collective-permute-start(bf16[512,256]{1,0:T(8,128)(2,1)S(1)} %collective-permute-done.1.refs_2_), channel_id=1, source_target_pairs={{0,1},{1,0},{2,3},{3,2},{4,5},{5,4},{6,7},{7,6},{8,9},{9,8},{10,11... | collective-permute-start | bytes 786440 | tf_op jit(solution)/shard_map/ppermute | solution.py:21
  23.9 15.0 %collective-permute-start.5 = (bf16[2,64,128]{2,1,0:T(8,128)(2,1)S(1)}, bf16[2,64,128]{2,1,0:T(8,128)(2,1)S(1)}, u32[]{:S(2)}, u32[]{:S(2)}) collective-permute-start(bf16[2,64,128]{2,1,0:T(8,128)(2,1)S(1)} %get-tuple-element.102.wanted), channel_id=1, source_target_pairs={{0,16},{4,20},{8,24},{12,28},{16,0},{20,4},{24,8},{28,12},{1,17},{... | collective-permute-start | bytes 98312 | tf_op jit(solution)/shard_map/ppermute | solution.py:21
  44.9 8.4 %collective-permute-start.18 = (bf16[256,512]{1,0:T(8,128)(2,1)S(1)}, bf16[256,512]{1,0:T(8,128)(2,1)S(1)}, u32[]{:S(2)}, u32[]{:S(2)}) collective-permute-start(bf16[256,512]{1,0:T(8,128)(2,1)S(1)} %collective-permute-done.7.refs_2_), channel_id=1, source_target_pairs={{0,1},{1,0},{2,3},{3,2},{4,5},{5,4},{6,7},{7,6},{8,9},{9,8},{10,11... | collective-permute-start | bytes 786440 | tf_op jit(solution)/shard_map/ppermute | solution.py:21
  45.9 11.1 %collective-permute-start.14 = (bf16[256,768]{1,0:T(8,128)(2,1)S(1)}, bf16[256,768]{1,0:T(8,128)(2,1)S(1)}, u32[]{:S(2)}, u32[]{:S(2)}) collective-permute-start(bf16[256,768]{1,0:T(8,128)(2,1)S(1)} %get-tuple-element.122), channel_id=1, source_target_pairs={{0,8},{4,12},{8,0},{12,4},{16,24},{20,28},{24,16},{28,20},{1,9},{5... | collective-permute-start | bytes 1179656 | tf_op jit(solution)/shard_map/ppermute | solution.py:21
  47.4 10.6 %collective-permute-start.15 = (bf16[256,768]{1,0:T(8,128)(2,1)S(1)}, bf16[256,768]{1,0:T(8,128)(2,1)S(1)}, u32[]{:S(2)}, u32[]{:S(2)}) collective-permute-start(bf16[256,768]{1,0:T(8,128)(2,1)S(1)} %get-tuple-element.124), channel_id=1, source_target_pairs={{0,16},{4,20},{8,24},{12,28},{16,0},{20,4},{24,8},{28,12},{1,17},{... | collective-permute-start | bytes 1179656 | tf_op jit(solution)/shard_map/ppermute | solution.py:21
  58.4 5.0 %collective-permute-start.20 = (bf16[256,256]{1,0:T(8,128)(2,1)S(1)}, bf16[256,256]{1,0:T(8,128)(2,1)S(1)}, u32[]{:S(2)}, u32[]{:S(2)}) collective-permute-start(bf16[256,256]{1,0:T(8,128)(2,1)S(1)} %get-tuple-element.135), channel_id=1, source_target_pairs={{0,8},{4,12},{8,0},{12,4},{16,24},{20,28},{24,16},{28,20},{1,9},{5... | collective-permute-start | bytes 393224 | tf_op jit(solution)/shard_map/ppermute | solution.py:21
  59.0 6.3 %collective-permute-start.21 = (bf16[256,256]{1,0:T(8,128)(2,1)S(1)}, bf16[256,256]{1,0:T(8,128)(2,1)S(1)}, u32[]{:S(2)}, u32[]{:S(2)}) collective-permute-start(bf16[256,256]{1,0:T(8,128)(2,1)S(1)} %get-tuple-element.137), channel_id=1, source_target_pairs={{0,16},{4,20},{8,24},{12,28},{16,0},{20,4},{24,8},{28,12},{1,17},{... | collective-permute-start | bytes 393224 | tf_op jit(solution)/shard_map/ppermute | solution.py:21
  60.7 8.9 %collective-permute-start.16 = (bf16[128,768]{1,0:T(8,128)(2,1)S(1)}, bf16[128,768]{1,0:T(8,128)(2,1)S(1)}, u32[]{:S(2)}, u32[]{:S(2)}) collective-permute-start(bf16[128,768]{1,0:T(8,128)(2,1)S(1)} %get-tuple-element.126), channel_id=1, source_target_pairs={{0,16},{4,20},{8,24},{12,28},{16,0},{20,4},{24,8},{28,12},{1,17},{... | collective-permute-start | bytes 589832 | tf_op jit(solution)/shard_map/ppermute | solution.py:21
  61.3 8.3 %collective-permute-start.17 = (bf16[128,768]{1,0:T(8,128)(2,1)S(1)}, bf16[128,768]{1,0:T(8,128)(2,1)S(1)}, u32[]{:S(2)}, u32[]{:S(2)}) collective-permute-start(bf16[128,768]{1,0:T(8,128)(2,1)S(1)} %get-tuple-element.127), channel_id=1, source_target_pairs={{0,8},{4,12},{8,0},{12,4},{16,24},{20,28},{24,16},{28,20},{1,9},{5... | collective-permute-start | bytes 589832 | tf_op jit(solution)/shard_map/ppermute | solution.py:21
  72.8 6.1 %collective-permute-start.25 = (bf16[128,256]{1,0:T(8,128)(2,1)S(1)}, bf16[128,256]{1,0:T(8,128)(2,1)S(1)}, u32[]{:S(2)}, u32[]{:S(2)}) collective-permute-start(bf16[128,256]{1,0:T(8,128)(2,1)S(1)} %get-tuple-element.142.own), channel_id=1, source_target_pairs={{0,8},{4,12},{8,0},{12,4},{16,24},{20,28},{24,16},{28,20},{1,9},{5... | collective-permute-start | bytes 196616 | tf_op jit(solution)/shard_map/ppermute | solution.py:21
  74.3 9.7 %collective-permute-start.24 = (bf16[128,768]{1,0:T(8,128)(2,1)S(1)}, bf16[128,768]{1,0:T(8,128)(2,1)S(1)}, u32[]{:S(2)}, u32[]{:S(2)}) collective-permute-start(bf16[128,768]{1,0:T(8,128)(2,1)S(1)} %get-tuple-element.141.own), channel_id=1, source_target_pairs={{0,8},{4,12},{8,0},{12,4},{16,24},{20,28},{24,16},{28,20},{1,9},{5... | collective-permute-start | bytes 589832 | tf_op jit(solution)/shard_map/ppermute | solution.py:21
  74.9 9.1 %collective-permute-start.26 = (bf16[128,768]{1,0:T(8,128)(2,1)S(1)}, bf16[128,768]{1,0:T(8,128)(2,1)S(1)}, u32[]{:S(2)}, u32[]{:S(2)}) collective-permute-start(bf16[128,768]{1,0:T(8,128)(2,1)S(1)} %get-tuple-element.143.own), channel_id=1, source_target_pairs={{0,16},{4,20},{8,24},{12,28},{16,0},{20,4},{24,8},{28,12},{1,17},{... | collective-permute-start | bytes 589832 | tf_op jit(solution)/shard_map/ppermute | solution.py:21
  77.1 5.9 %collective-permute-start.29 = (bf16[256,256]{1,0:T(8,128)(2,1)S(1)}, bf16[256,256]{1,0:T(8,128)(2,1)S(1)}, u32[]{:S(2)}, u32[]{:S(2)}) collective-permute-start(bf16[256,256]{1,0:T(8,128)(2,1)S(1)} %join.6.refs_2_), channel_id=1, source_target_pairs={{0,8},{4,12},{8,0},{12,4},{16,24},{20,28},{24,16},{28,20},{1,9},{5... | collective-permute-start | bytes 393224 | tf_op jit(solution)/shard_map/ppermute | solution.py:21
  84.5 12.1 %collective-permute-start.32 = (bf16[272,768]{1,0:T(8,128)(2,1)S(1)}, bf16[272,768]{1,0:T(8,128)(2,1)S(1)}, u32[]{:S(2)}, u32[]{:S(2)}) collective-permute-start(bf16[272,768]{1,0:T(8,128)(2,1)S(1)} %join.4.refs_0_), channel_id=1, source_target_pairs={{0,16},{4,20},{8,24},{12,28},{16,0},{20,4},{24,8},{28,12},{1,17},{... | collective-permute-start | bytes 1253384 | tf_op jit(solution)/shard_map/ppermute | solution.py:21
  85.0 11.8 %collective-permute-start.33 = (bf16[272,768]{1,0:T(8,128)(2,1)S(1)}, bf16[272,768]{1,0:T(8,128)(2,1)S(1)}, u32[]{:S(2)}, u32[]{:S(2)}) collective-permute-start(bf16[272,768]{1,0:T(8,128)(2,1)S(1)} %join.7.refs_2_), channel_id=1, source_target_pairs={{0,8},{4,12},{8,0},{12,4},{16,24},{20,28},{24,16},{28,20},{1,9},{5... | collective-permute-start | bytes 1253384 | tf_op jit(solution)/shard_map/ppermute | solution.py:21
  86.9 9.9 %collective-permute-start.31 = (bf16[256,512]{1,0:T(8,128)(2,1)S(1)}, bf16[256,512]{1,0:T(8,128)(2,1)S(1)}, u32[]{:S(2)}, u32[]{:S(2)}) collective-permute-start(bf16[256,512]{1,0:T(8,128)(2,1)S(1)} %three_own.2), channel_id=1, source_target_pairs={{0,1},{1,0},{2,3},{3,2},{4,5},{5,4},{6,7},{7,6},{8,9},{9,8},{10,11... | collective-permute-start | bytes 786440 | tf_op jit(solution)/shard_map/ppermute | solution.py:21
  100.0 6.4 %collective-permute-start.39 = (bf16[1536,256]{1,0:T(8,128)(2,1)S(1)}, bf16[1536,256]{1,0:T(8,128)(2,1)S(1)}, u32[]{:S(2)}, u32[]{:S(2)}) collective-permute-start(bf16[1536,256]{1,0:T(8,128)(2,1)S(1)} %get-tuple-element.161), channel_id=1, source_target_pairs={{0,4},{4,0},{8,12},{12,8},{16,20},{20,16},{24,28},{28,24},{1,5},{5... | collective-permute-start | bytes 2359304 | tf_op jit(solution)/shard_map/ppermute | solution.py:21
  100.7 9.3 %collective-permute-start.41 = (bf16[512,256]{1,0:T(8,128)(2,1)S(1)}, bf16[512,256]{1,0:T(8,128)(2,1)S(1)}, u32[]{:S(2)}, u32[]{:S(2)}) collective-permute-start(bf16[512,256]{1,0:T(8,128)(2,1)S(1)} %two_own.3), channel_id=1, source_target_pairs={{0,1},{1,0},{2,3},{3,2},{4,5},{5,4},{6,7},{7,6},{8,9},{9,8},{10,11... | collective-permute-start | bytes 786440 | tf_op jit(solution)/shard_map/ppermute | solution.py:21
  104.0 7.2 %collective-permute-start.34 = (bf16[4,112,256]{2,1,0:T(8,128)(2,1)S(1)}, bf16[4,112,256]{2,1,0:T(8,128)(2,1)S(1)}, u32[]{:S(2)}, u32[]{:S(2)}) collective-permute-start(bf16[4,112,256]{2,1,0:T(8,128)(2,1)S(1)} %get-tuple-element.153), channel_id=1, source_target_pairs={{0,4},{4,0},{8,12},{12,8},{16,20},{20,16},{24,28},{28,24},{1,5},{5... | collective-permute-start | bytes 688136 | tf_op jit(solution)/shard_map/ppermute | solution.py:21
  105.0 15.7 %collective-permute-start.36 = (bf16[256,512]{1,0:T(8,128)(2,1)S(1)}, bf16[256,512]{1,0:T(8,128)(2,1)S(1)}, u32[]{:S(2)}, u32[]{:S(2)}) collective-permute-start(bf16[256,512]{1,0:T(8,128)(2,1)S(1)} %add_up.2), channel_id=1, source_target_pairs={{0,2},{1,3},{2,0},{3,1},{4,6},{5,7},{6,4},{7,5},{8,10},{9,11},{10,... | collective-permute-start | bytes 786440 | tf_op jit(solution)/shard_map/ppermute | solution.py:21
  110.0 19.4 %collective-permute-start.44 = (bf16[256,512]{1,0:T(8,128)(2,1)S(1)}, bf16[256,512]{1,0:T(8,128)(2,1)S(1)}, u32[]{:S(2)}, u32[]{:S(2)}) collective-permute-start(bf16[256,512]{1,0:T(8,128)(2,1)S(1)} %get-tuple-element.168), channel_id=1, source_target_pairs={{0,1},{1,0},{2,3},{3,2},{4,5},{5,4},{6,7},{7,6},{8,9},{9,8},{10,11... | collective-permute-start | bytes 786440 | tf_op jit(solution)/shard_map/ppermute | solution.py:21
  112.5 20.1 %collective-permute-start.42 = (bf16[512,256]{1,0:T(8,128)(2,1)S(1)}, bf16[512,256]{1,0:T(8,128)(2,1)S(1)}, u32[]{:S(2)}, u32[]{:S(2)}) collective-permute-start(bf16[512,256]{1,0:T(8,128)(2,1)S(1)} %get-tuple-element.166), channel_id=1, source_target_pairs={{0,1},{1,0},{2,3},{3,2},{4,5},{5,4},{6,7},{7,6},{8,9},{9,8},{10,11... | collective-permute-start | bytes 786440 | tf_op jit(solution)/shard_map/ppermute | solution.py:21
  114.1 18.5 %collective-permute-start.43 = (bf16[512,256]{1,0:T(8,128)(2,1)S(1)}, bf16[512,256]{1,0:T(8,128)(2,1)S(1)}, u32[]{:S(2)}, u32[]{:S(2)}) collective-permute-start(bf16[512,256]{1,0:T(8,128)(2,1)S(1)} %add_up.3), channel_id=1, source_target_pairs={{0,2},{1,3},{2,0},{3,1},{4,6},{5,7},{6,4},{7,5},{8,10},{9,11},{10,... | collective-permute-start | bytes 786440 | tf_op jit(solution)/shard_map/ppermute | solution.py:21
  125.0 8.6 %collective-permute-start.45 = (bf16[112,128]{1,0:T(8,128)(2,1)S(1)}, bf16[112,128]{1,0:T(8,128)(2,1)S(1)}, u32[]{:S(2)}, u32[]{:S(2)}) collective-permute-start(bf16[112,128]{1,0:T(8,128)(2,1)S(1)} %get-tuple-element.170), channel_id=1, source_target_pairs={{0,2},{1,3},{2,0},{3,1},{4,6},{5,7},{6,4},{7,5},{8,10},{9,11},{10,... | collective-permute-start | bytes 86024 | tf_op jit(solution)/shard_map/ppermute | solution.py:21
  (28 other events, 162.6 us)

commit v7 on v6

--- a/solution.py
+++ b/solution.py
@@ -156,19 +156,19 @@
     lax.fori_loop(0, first.shape[1] // tile, step, 0)
 
 
-def one_slope(inputs, first, out, *, tile):
+def one_slope(inputs, first, out, *, tile, start):
     n_rows = inputs.shape[1]
     cut = min(256, n_rows)
 
     def step(i, _):
         at = pl.ds(pl.multiple_of(i * tile, tile), tile)
-        weights = first[:, at].T
+        weights = first[:, pl.ds(pl.multiple_of(start + i * tile, tile), tile)].T
         for c in range(0, n_rows, cut):
             pre = dot(weights, inputs[:, c : c + cut], 1, 0)
             out[at, c : c + cut] = gelu_slope(pre).astype(bf16)
         return 0
 
-    lax.fori_loop(0, first.shape[1] // tile, step, 0)
+    lax.fori_loop(0, out.shape[0] // tile, step, 0)
 
 
 def two_forward(act_one, near, far, near_too, far_too, act, act_t, pre_two):
@@ -354,7 +354,7 @@
 
 
 def one_back(
-    inputs, delta, slope, grad_four, near, far, near_too, far_too, keep, send, *, n_dp, places, n_in, n_out
+    inputs, delta, slope, slope_more, grad_four, near, far, near_too, far_too, keep, send, *, n_dp, places, n_in, n_out
 ):
     span = far.shape[0]
     n_mp = near.shape[0] // span + 1
@@ -365,7 +365,8 @@
         at = slice(k * span, (k + 1) * span)
         left, right = (near[at], near_too[at]) if k + 1 < n_mp else (far[...], far_too[...])
         value = dot(left, delta[:mid], 1, 0) + dot(right, delta[mid:], 1, 0)
-        value = (value * slope[k * span : (k + 1) * span].astype(f32)).astype(bf16)
+        source, row = (slope, k * span) if 2 * k < n_mp else (slope_more, (k - n_mp // 2) * span)
+        value = (value * source[row : row + span].astype(f32)).astype(bf16)
         grad_one = dot(inputs[...], value, 1, 1)
         at = places.index(k) * span
         pieces = [grad_one[:n_in], grad_four[:n_out, at : at + span]]
@@ -548,16 +549,23 @@
     evens = list(range(0, n_dp, 2))
     bits = [1 << i for i in range(1, n_dp.bit_length() - 1)]
     orders = [bits, bits[::-1]]
-    slope_one = on_core(
-        part(one_slope, tile=256), shaped((width, n_rows), bf16), [inputs, first], "one_slope",
-        flops=12_000_000_000,
-    )
+    slopes = [
+        on_core(
+            part(one_slope, tile=256, start=start),
+            shaped((width // 2, n_rows), bf16),
+            [inputs, first],
+            "one_slope",
+            flops=6_000_000_000,
+        )
+        for start in (0, width // 2)
+    ]
     slope_two = on_core(two_slope, shaped((wide_mid, n_rows), f32), [pre_two], "two_slope")
     terms = []
     ahead = [third[k] for k in planes if k and not parent(k)]
     for ks in groups:
         cols = len(ks) * n_top
-        third_too = [swap(after(act_one, third[k])[0] if k else top, "dp", 1) for k in ks]
+        ready = (act_one, slopes[0]) if n_mp - 1 in ks else act_one
+        third_too = [swap(after(ready, third[k])[0] if k else top, "dp", 1) for k in ks]
         third_all.append([third[k] for k in ks] + third_too)
         weights = after(ahead, *third_all[-1])
         left = half // 2
@@ -573,7 +581,7 @@
         for stage in range(len(bits)):
             sends = halves[1::2] if len(halves) == 4 else halves
             gots = [swap(send, "dp", order[stage]) for send, order in zip(sends, orders)]
-            ahead = ahead or [slope_one, slope_two, *gots]
+            ahead = ahead or [slopes[1], slope_two]
             if stage + 1 == len(bits):
                 break
             keeps, left = halves[::2], left // 2
@@ -691,7 +699,7 @@
     keep, send = on_core(
         part(one_back, n_dp=n_dp, places=places, n_in=n_in, n_out=n_out),
         [shaped(shape, f32), shaped(shape, bf16)],
-        [inputs, delta_two, slope_one, grad_four, *second_all],
+        [inputs, delta_two, *slopes, grad_four, *second_all],
         "one_back",
         flops=LONG,
     )

time: 139 us -> 136 us (0.978)
    pallas_call x39 -> x40, Pallas kernels: 20.7 us -> 20.7 us  [on_core(): pl.pallas_call(body, out_shape=outs, in_specs=[pl.BlockSpec(memory_space=...]
where the time goes in v7:
time: 136 us
  waiting for transfers between devices  52.1 us (38%)
  starting transfers between devices  46.3 us (34%)
  Pallas kernels  20.7 us (15%)
  blocking collectives  10.4 us (8%)
  local copies, waits for them, and re-layouts  3.65 us (3%)
  between operations  1.73 us (1%)
    ppermute x47, waiting for transfers between devices, swap(): return lax.ppermute(value, axis, [(at, at ^ step) for at in range(count)])  52.1 us
    ppermute x47, starting transfers between devices, swap(): return lax.ppermute(value, axis, [(at, at ^ step) for at in range(count)])  46.3 us
    pallas_call x40, Pallas kernels, on_core(): pl.pallas_call(body, out_shape=outs, in_specs=[pl.BlockSpec(memory_space=...  20.7 us
    all_gather x1, blocking collectives, on_device(): held = lax.all_gather(packed, 'dp')  10.4 us
    unnamed x28, local copies, waits for them, and re-layouts  3.65 us
  transfers between devices with their start and end apart: 47, of which 24 were waited for; matrix products, arithmetic and copies ran while one was open for 1% of the time, Pallas kernels for 10%

profile of v7, /device:TPU:0, one launch (start us, length us, event | category | flops | bytes accessed | tf_op | source)
XLA Modules:
  0.0 136.0 jit_solution(17068705531016058238)
XLA Ops:
  1.8 4.1 %collective-permute-start.1 = (bf16[512,256]{1,0:T(8,128)(2,1)S(1)}, bf16[512,256]{1,0:T(8,128)(2,1)S(1)}, u32[]{:S(2)}, u32[]{:S(2)}) collective-permute-start(bf16[512,256]{1,0:T(8,128)(2,1)S(1)} %convert_element_type.6.refs_0_), channel_id=1, source_target_pairs={{0,2},{1,3},{2,0},{3,1},{4,6},{5,7},{6,4},{7,5},{8,10},{9,11},{10,... | collective-permute-start | bytes 786440 | tf_op jit(solution)/shard_map/ppermute | solution.py:21
  5.9 1.6 %collective-permute-start = (bf16[512,256]{1,0:T(8,128)(2,1)S(1)}, bf16[512,256]{1,0:T(8,128)(2,1)S(1)}, u32[]{:S(2)}, u32[]{:S(2)}) collective-permute-start(bf16[512,256]{1,0:T(8,128)(2,1)S(1)} %convert_element_type.6.refs_0_), channel_id=1, source_target_pairs={{0,1},{1,0},{2,3},{3,2},{4,5},{5,4},{6,7},{7,6},{8,9},{9,8},{10,11... | collective-permute-start | bytes 786440 | tf_op jit(solution)/shard_map/ppermute | solution.py:21
  9.0 1.9 %collective-permute-start.3 = (bf16[64,128]{1,0:T(8,128)(2,1)S(1)}, bf16[64,128]{1,0:T(8,128)(2,1)S(1)}, u32[]{:S(2)}, u32[]{:S(2)}) collective-permute-start(bf16[64,128]{1,0:T(8,128)(2,1)S(1)} %pack_small.1.refs_1_), channel_id=1, source_target_pairs={{0,2},{1,3},{2,0},{3,1},{4,6},{5,7},{6,4},{7,5},{8,10},{9,11},{10,... | collective-permute-start | bytes 49160 | tf_op jit(solution)/shard_map/ppermute | solution.py:21
  10.9 2.5 %collective-permute-start.2 = (bf16[64,128]{1,0:T(8,128)(2,1)S(1)}, bf16[64,128]{1,0:T(8,128)(2,1)S(1)}, u32[]{:S(2)}, u32[]{:S(2)}) collective-permute-start(bf16[64,128]{1,0:T(8,128)(2,1)S(1)} %pack_small.1.refs_1_), channel_id=1, source_target_pairs={{0,1},{1,0},{2,3},{3,2},{4,5},{5,4},{6,7},{7,6},{8,9},{9,8},{10,11... | collective-permute-start | bytes 49160 | tf_op jit(solution)/shard_map/ppermute | solution.py:21
  15.9 3.7 %collective-permute-done.4.refs_4_ = bf16[64,128]{1,0:T(8,128)(2,1)S(1)} collective-permute-done((bf16[64,128]{1,0:T(8,128)(2,1)S(1)}, bf16[64,128]{1,0:T(8,128)(2,1)S(1)}, u32[]{:S(2)}, u32[]{:S(2)}) %collective-permute-start.4) | collective-permute-done | bytes 16416 | tf_op jit(solution)/shard_map/ppermute | solution.py:21
  19.8 2.0 %collective-permute-start.7 = (bf16[256,512]{1,0:T(8,128)(2,1)S(1)}, bf16[256,512]{1,0:T(8,128)(2,1)S(1)}, u32[]{:S(2)}, u32[]{:S(2)}) collective-permute-start(bf16[256,512]{1,0:T(8,128)(2,1)S(1)} %convert_element_type.7.refs_0_), channel_id=1, source_target_pairs={{0,2},{1,3},{2,0},{3,1},{4,6},{5,7},{6,4},{7,5},{8,10},{9,11},{10,... | collective-permute-start | bytes 786440 | tf_op jit(solution)/shard_map/ppermute | solution.py:21
  21.9 1.7 %collective-permute-start.6 = (bf16[256,512]{1,0:T(8,128)(2,1)S(1)}, bf16[256,512]{1,0:T(8,128)(2,1)S(1)}, u32[]{:S(2)}, u32[]{:S(2)}) collective-permute-start(bf16[256,512]{1,0:T(8,128)(2,1)S(1)} %convert_element_type.7.refs_0_), channel_id=1, source_target_pairs={{0,1},{1,0},{2,3},{3,2},{4,5},{5,4},{6,7},{7,6},{8,9},{9,8},{10,11... | collective-permute-start | bytes 786440 | tf_op jit(solution)/shard_map/ppermute | solution.py:21
  23.9 1.5 %collective-permute-start.5 = (bf16[2,64,128]{2,1,0:T(8,128)(2,1)S(1)}, bf16[2,64,128]{2,1,0:T(8,128)(2,1)S(1)}, u32[]{:S(2)}, u32[]{:S(2)}) collective-permute-start(bf16[2,64,128]{2,1,0:T(8,128)(2,1)S(1)} %get-tuple-element.102.wanted), channel_id=1, source_target_pairs={{0,16},{4,20},{8,24},{12,28},{16,0},{20,4},{24,8},{28,12},{1,17},{... | collective-permute-start | bytes 98312 | tf_op jit(solution)/shard_map/ppermute | solution.py:21
  25.4 10.4 %all-gather = bf16[3072,128]{1,0:T(8,128)(2,1)S(1)} all-gather(bf16[384,128]{1,0:T(8,128)(2,1)S(1)} %pack_all.1), channel_id=2, replica_groups=mesh['dp'=8,'mp'=4] {'dp'}, dimensions={0}, use_global_device_ids=true | all-gather | bytes 884736 | tf_op jit(solution)/shard_map/all_gather | solution.py:520
  36.0 2.3 %one_forward.1.act_one = bf16[2048,512]{1,0:T(8,128)(2,1)S(1)} custom-call(bf16[64,512]{1,0:T(8,128)(2,1)S(1)} %get-tuple-element.100.inputs, bf16[64,2048]{1,0:T(8,128)(2,1)S(1)} %get-tuple-element.104.first), custom_call_target="tpu_custom_call" | custom-call | tf_op jit(solution)/shard_map/one_forward/pallas_call | solution.py:57
  39.3 1.7 %collective-permute-done.8.far = bf16[512,256]{1,0:T(8,128)(2,1)S(1)} collective-permute-done((bf16[512,256]{1,0:T(8,128)(2,1)S(1)}, bf16[512,256]{1,0:T(8,128)(2,1)S(1)}, u32[]{:S(2)}, u32[]{:S(2)}) %collective-permute-start.8) | collective-permute-done | bytes 262176 | tf_op jit(solution)/shard_map/ppermute | solution.py:21
  45.9 1.5 %one_slope.3.slope = bf16[1024,512]{1,0:T(8,128)(2,1)S(1)} custom-call(bf16[64,512]{1,0:T(8,128)(2,1)S(1)} %get-tuple-element.100.inputs, bf16[64,2048]{1,0:T(8,128)(2,1)S(1)} %get-tuple-element.104.first), custom_call_target="tpu_custom_call" | custom-call | flops 6000000000 | tf_op jit(solution)/shard_map/one_slope/pallas_call | solution.py:57
  47.4 1.6 %collective-permute-start.14 = (bf16[256,768]{1,0:T(8,128)(2,1)S(1)}, bf16[256,768]{1,0:T(8,128)(2,1)S(1)}, u32[]{:S(2)}, u32[]{:S(2)}) collective-permute-start(bf16[256,768]{1,0:T(8,128)(2,1)S(1)} %get-tuple-element.122), channel_id=1, source_target_pairs={{0,8},{4,12},{8,0},{12,4},{16,24},{20,28},{24,16},{28,20},{1,9},{5... | collective-permute-start | bytes 1179656 | tf_op jit(solution)/shard_map/ppermute | solution.py:21
  49.0 1.5 %collective-permute-start.15 = (bf16[256,768]{1,0:T(8,128)(2,1)S(1)}, bf16[256,768]{1,0:T(8,128)(2,1)S(1)}, u32[]{:S(2)}, u32[]{:S(2)}) collective-permute-start(bf16[256,768]{1,0:T(8,128)(2,1)S(1)} %get-tuple-element.124), channel_id=1, source_target_pairs={{0,16},{4,20},{8,24},{12,28},{16,0},{20,4},{24,8},{28,12},{1,17},{... | collective-permute-start | bytes 1179656 | tf_op jit(solution)/shard_map/ppermute | solution.py:21
  50.5 2.8 %collective-permute-done.18.refs_0_ = bf16[256,512]{1,0:T(8,128)(2,1)S(1)} collective-permute-done((bf16[256,512]{1,0:T(8,128)(2,1)S(1)}, bf16[256,512]{1,0:T(8,128)(2,1)S(1)}, u32[]{:S(2)}, u32[]{:S(2)}) %collective-permute-start.18) | collective-permute-done | bytes 262176 | tf_op jit(solution)/shard_map/ppermute | solution.py:21
  53.3 1.7 %one_slope.2.slope_more = bf16[1024,512]{1,0:T(8,128)(2,1)S(1)} custom-call(bf16[64,512]{1,0:T(8,128)(2,1)S(1)} %get-tuple-element.100.inputs, bf16[64,2048]{1,0:T(8,128)(2,1)S(1)} %get-tuple-element.104.first), custom_call_target="tpu_custom_call" | custom-call | flops 6000000000 | tf_op jit(solution)/shard_map/one_slope/pallas_call | solution.py:57
  55.9 1.6 %collective-permute-start.20 = (bf16[256,256]{1,0:T(8,128)(2,1)S(1)}, bf16[256,256]{1,0:T(8,128)(2,1)S(1)}, u32[]{:S(2)}, u32[]{:S(2)}) collective-permute-start(bf16[256,256]{1,0:T(8,128)(2,1)S(1)} %get-tuple-element.135), channel_id=1, source_target_pairs={{0,8},{4,12},{8,0},{12,4},{16,24},{20,28},{24,16},{28,20},{1,9},{5... | collective-permute-start | bytes 393224 | tf_op jit(solution)/shard_map/ppermute | solution.py:21
  59.7 1.6 %collective-permute-start.16 = (bf16[128,768]{1,0:T(8,128)(2,1)S(1)}, bf16[128,768]{1,0:T(8,128)(2,1)S(1)}, u32[]{:S(2)}, u32[]{:S(2)}) collective-permute-start(bf16[128,768]{1,0:T(8,128)(2,1)S(1)} %get-tuple-element.126), channel_id=1, source_target_pairs={{0,16},{4,20},{8,24},{12,28},{16,0},{20,4},{24,8},{28,12},{1,17},{... | collective-permute-start | bytes 589832 | tf_op jit(solution)/shard_map/ppermute | solution.py:21
  61.9 1.9 %collective-permute-done.21.refs_3_ = bf16[256,256]{1,0:T(8,128)(2,1)S(1)} collective-permute-done((bf16[256,256]{1,0:T(8,128)(2,1)S(1)}, bf16[256,256]{1,0:T(8,128)(2,1)S(1)}, u32[]{:S(2)}, u32[]{:S(2)}) %collective-permute-start.21) | collective-permute-done | bytes 131104 | tf_op jit(solution)/shard_map/ppermute | solution.py:21
  63.8 1.6 %collective-permute-start.22 = (bf16[128,256]{1,0:T(8,128)(2,1)S(1)}, bf16[128,256]{1,0:T(8,128)(2,1)S(1)}, u32[]{:S(2)}, u32[]{:S(2)}) collective-permute-start(bf16[128,256]{1,0:T(8,128)(2,1)S(1)} %get-tuple-element.139), channel_id=1, source_target_pairs={{0,16},{4,20},{8,24},{12,28},{16,0},{20,4},{24,8},{28,12},{1,17},{... | collective-permute-start | bytes 196616 | tf_op jit(solution)/shard_map/ppermute | solution.py:21
  66.0 2.0 %collective-permute-done.16.refs_1_ = bf16[128,768]{1,0:T(8,128)(2,1)S(1)} collective-permute-done((bf16[128,768]{1,0:T(8,128)(2,1)S(1)}, bf16[128,768]{1,0:T(8,128)(2,1)S(1)}, u32[]{:S(2)}, u32[]{:S(2)}) %collective-permute-start.16) | collective-permute-done | bytes 196640 | tf_op jit(solution)/shard_map/ppermute | solution.py:21
  77.6 3.8 %collective-permute-done.29.refs_3_ = bf16[256,256]{1,0:T(8,128)(2,1)S(1)} collective-permute-done((bf16[256,256]{1,0:T(8,128)(2,1)S(1)}, bf16[256,256]{1,0:T(8,128)(2,1)S(1)}, u32[]{:S(2)}, u32[]{:S(2)}) %collective-permute-start.29) | collective-permute-done | bytes 131104 | tf_op jit(solution)/shard_map/ppermute | solution.py:21
  85.7 8.8 %collective-permute-done.32.refs_1_ = bf16[272,768]{1,0:T(8,128)(2,1)S(1)} collective-permute-done((bf16[272,768]{1,0:T(8,128)(2,1)S(1)}, bf16[272,768]{1,0:T(8,128)(2,1)S(1)}, u32[]{:S(2)}, u32[]{:S(2)}) %collective-permute-start.32) | collective-permute-done | bytes 417824 | tf_op jit(solution)/shard_map/ppermute | solution.py:21
  99.9 2.1 %one_back.1 = (f32[4,112,256]{2,1,0:T(8,128)S(1)}, bf16[4,112,256]{2,1,0:T(8,128)(2,1)S(1)}) custom-call(bf16[64,512]{1,0:T(8,128)(2,1)S(1)} %get-tuple-element.100.inputs, bf16[512,512]{1,0:T(8,128)(2,1)S(1)} %get-tuple-element.150.delta, bf16[1024,512]{1,0:T(8,128)(2,1)S(1)} %one_slope.3.slope, bf16[1024,512]{1,0:T(8,128)(2,1)S(1)} %one_slope.2.slope_more, ...), custom_call_target="tpu_custom_call" | custom-call | flops 99999997952 | tf_op jit(solution)/shard_map/one_back/pallas_call | solution.py:57
  103.0 1.8 %collective-permute-start.36 = (bf16[256,512]{1,0:T(8,128)(2,1)S(1)}, bf16[256,512]{1,0:T(8,128)(2,1)S(1)}, u32[]{:S(2)}, u32[]{:S(2)}) collective-permute-start(bf16[256,512]{1,0:T(8,128)(2,1)S(1)} %add_up.2), channel_id=1, source_target_pairs={{0,2},{1,3},{2,0},{3,1},{4,6},{5,7},{6,4},{7,5},{8,10},{9,11},{10,... | collective-permute-start | bytes 786440 | tf_op jit(solution)/shard_map/ppermute | solution.py:21
  105.5 3.0 %collective-permute-done.41.got = bf16[512,256]{1,0:T(8,128)(2,1)S(1)} collective-permute-done((bf16[512,256]{1,0:T(8,128)(2,1)S(1)}, bf16[512,256]{1,0:T(8,128)(2,1)S(1)}, u32[]{:S(2)}, u32[]{:S(2)}) %collective-permute-start.41) | collective-permute-done | bytes 262176 | tf_op jit(solution)/shard_map/ppermute | solution.py:21
  109.7 1.7 %collective-permute-start.42 = (bf16[512,256]{1,0:T(8,128)(2,1)S(1)}, bf16[512,256]{1,0:T(8,128)(2,1)S(1)}, u32[]{:S(2)}, u32[]{:S(2)}) collective-permute-start(bf16[512,256]{1,0:T(8,128)(2,1)S(1)} %get-tuple-element.166), channel_id=1, source_target_pairs={{0,1},{1,0},{2,3},{3,2},{4,5},{5,4},{6,7},{7,6},{8,9},{9,8},{10,11... | collective-permute-start | bytes 786440 | tf_op jit(solution)/shard_map/ppermute | solution.py:21
  113.8 5.0 %collective-permute-done.36.refs_0_ = bf16[256,512]{1,0:T(8,128)(2,1)S(1)} collective-permute-done((bf16[256,512]{1,0:T(8,128)(2,1)S(1)}, bf16[256,512]{1,0:T(8,128)(2,1)S(1)}, u32[]{:S(2)}, u32[]{:S(2)}) %collective-permute-start.36) | collective-permute-done | bytes 262176 | tf_op jit(solution)/shard_map/ppermute | solution.py:21
  120.3 2.8 %collective-permute-done.38.got = bf16[1,112,256]{2,1,0:T(8,128)(2,1)S(1)} collective-permute-done((bf16[1,112,256]{2,1,0:T(8,128)(2,1)S(1)}, bf16[1,112,256]{2,1,0:T(8,128)(2,1)S(1)}, u32[]{:S(2)}, u32[]{:S(2)}) %collective-permute-start.38) | collective-permute-done | bytes 57376 | tf_op jit(solution)/shard_map/ppermute | solution.py:21
  123.2 5.0 %collective-permute-done.44.refs_1_ = bf16[256,512]{1,0:T(8,128)(2,1)S(1)} collective-permute-done((bf16[256,512]{1,0:T(8,128)(2,1)S(1)}, bf16[256,512]{1,0:T(8,128)(2,1)S(1)}, u32[]{:S(2)}, u32[]{:S(2)}) %collective-permute-start.44) | collective-permute-done | bytes 262176 | tf_op jit(solution)/shard_map/ppermute | solution.py:21
  129.3 1.7 %collective-permute-done.42.refs_0_ = bf16[512,256]{1,0:T(8,128)(2,1)S(1)} collective-permute-done((bf16[512,256]{1,0:T(8,128)(2,1)S(1)}, bf16[512,256]{1,0:T(8,128)(2,1)S(1)}, u32[]{:S(2)}, u32[]{:S(2)}) %collective-permute-start.42) | collective-permute-done | bytes 262176 | tf_op jit(solution)/shard_map/ppermute | solution.py:21
  132.9 2.4 %collective-permute-done.46.refs_0_ = bf16[112,64]{1,0:T(8,128)(2,1)S(1)} collective-permute-done((bf16[112,64]{1,0:T(8,128)(2,1)S(1)}, bf16[112,64]{1,0:T(8,128)(2,1)S(1)}, u32[]{:S(2)}, u32[]{:S(2)}) %collective-permute-start.46) | collective-permute-done | bytes 14368 | tf_op jit(solution)/shard_map/ppermute | solution.py:21
  (133 shorter events, 44.9 us)
Async XLA Ops:
  1.8 17.8 %collective-permute-start.1 = (bf16[512,256]{1,0:T(8,128)(2,1)S(1)}, bf16[512,256]{1,0:T(8,128)(2,1)S(1)}, u32[]{:S(2)}, u32[]{:S(2)}) collective-permute-start(bf16[512,256]{1,0:T(8,128)(2,1)S(1)} %convert_element_type.6.refs_0_), channel_id=1, source_target_pairs={{0,2},{1,3},{2,0},{3,1},{4,6},{5,7},{6,4},{7,5},{8,10},{9,11},{10,... | collective-permute-start | bytes 786440 | tf_op jit(solution)/shard_map/ppermute | solution.py:21
  5.9 13.7 %collective-permute-start = (bf16[512,256]{1,0:T(8,128)(2,1)S(1)}, bf16[512,256]{1,0:T(8,128)(2,1)S(1)}, u32[]{:S(2)}, u32[]{:S(2)}) collective-permute-start(bf16[512,256]{1,0:T(8,128)(2,1)S(1)} %convert_element_type.6.refs_0_), channel_id=1, source_target_pairs={{0,1},{1,0},{2,3},{3,2},{4,5},{5,4},{6,7},{7,6},{8,9},{9,8},{10,11... | collective-permute-start | bytes 786440 | tf_op jit(solution)/shard_map/ppermute | solution.py:21
  9.0 10.6 %collective-permute-start.4 = (bf16[64,128]{1,0:T(8,128)(2,1)S(1)}, bf16[64,128]{1,0:T(8,128)(2,1)S(1)}, u32[]{:S(2)}, u32[]{:S(2)}) collective-permute-start(bf16[64,128]{1,0:T(8,128)(2,1)S(1)} %pack_small.1.refs_1_), channel_id=1, source_target_pairs={{0,3},{1,2},{2,1},{3,0},{4,7},{5,6},{6,5},{7,4},{8,11},{9,10},{10,... | collective-permute-start | bytes 49160 | tf_op jit(solution)/shard_map/ppermute | solution.py:21
  9.0 10.6 %collective-permute-start.3 = (bf16[64,128]{1,0:T(8,128)(2,1)S(1)}, bf16[64,128]{1,0:T(8,128)(2,1)S(1)}, u32[]{:S(2)}, u32[]{:S(2)}) collective-permute-start(bf16[64,128]{1,0:T(8,128)(2,1)S(1)} %pack_small.1.refs_1_), channel_id=1, source_target_pairs={{0,2},{1,3},{2,0},{3,1},{4,6},{5,7},{6,4},{7,5},{8,10},{9,11},{10,... | collective-permute-start | bytes 49160 | tf_op jit(solution)/shard_map/ppermute | solution.py:21
  10.9 8.7 %collective-permute-start.2 = (bf16[64,128]{1,0:T(8,128)(2,1)S(1)}, bf16[64,128]{1,0:T(8,128)(2,1)S(1)}, u32[]{:S(2)}, u32[]{:S(2)}) collective-permute-start(bf16[64,128]{1,0:T(8,128)(2,1)S(1)} %pack_small.1.refs_1_), channel_id=1, source_target_pairs={{0,1},{1,0},{2,3},{3,2},{4,5},{5,4},{6,7},{7,6},{8,9},{9,8},{10,11... | collective-permute-start | bytes 49160 | tf_op jit(solution)/shard_map/ppermute | solution.py:21
  19.7 22.8 %collective-permute-start.9 = (bf16[1536,256]{1,0:T(8,128)(2,1)S(1)}, bf16[1536,256]{1,0:T(8,128)(2,1)S(1)}, u32[]{:S(2)}, u32[]{:S(2)}) collective-permute-start(bf16[1536,256]{1,0:T(8,128)(2,1)S(1)} %lay.1.near), channel_id=1, source_target_pairs={{0,4},{4,0},{8,12},{12,8},{16,20},{20,16},{24,28},{28,24},{1,5},{5... | collective-permute-start | bytes 2359304 | tf_op jit(solution)/shard_map/ppermute | solution.py:21
  19.8 18.5 %collective-permute-start.7 = (bf16[256,512]{1,0:T(8,128)(2,1)S(1)}, bf16[256,512]{1,0:T(8,128)(2,1)S(1)}, u32[]{:S(2)}, u32[]{:S(2)}) collective-permute-start(bf16[256,512]{1,0:T(8,128)(2,1)S(1)} %convert_element_type.7.refs_0_), channel_id=1, source_target_pairs={{0,2},{1,3},{2,0},{3,1},{4,6},{5,7},{6,4},{7,5},{8,10},{9,11},{10,... | collective-permute-start | bytes 786440 | tf_op jit(solution)/shard_map/ppermute | solution.py:21
  21.9 16.9 %collective-permute-start.6 = (bf16[256,512]{1,0:T(8,128)(2,1)S(1)}, bf16[256,512]{1,0:T(8,128)(2,1)S(1)}, u32[]{:S(2)}, u32[]{:S(2)}) collective-permute-start(bf16[256,512]{1,0:T(8,128)(2,1)S(1)} %convert_element_type.7.refs_0_), channel_id=1, source_target_pairs={{0,1},{1,0},{2,3},{3,2},{4,5},{5,4},{6,7},{7,6},{8,9},{9,8},{10,11... | collective-permute-start | bytes 786440 | tf_op jit(solution)/shard_map/ppermute | solution.py:21
  23.6 17.4 %collective-permute-start.8 = (bf16[512,256]{1,0:T(8,128)(2,1)S(1)}, bf16[512,256]{1,0:T(8,128)(2,1)S(1)}, u32[]{:S(2)}, u32[]{:S(2)}) collective-permute-start(bf16[512,256]{1,0:T(8,128)(2,1)S(1)} %collective-permute-done.1.refs_2_), channel_id=1, source_target_pairs={{0,1},{1,0},{2,3},{3,2},{4,5},{5,4},{6,7},{7,6},{8,9},{9,8},{10,11... | collective-permute-start | bytes 786440 | tf_op jit(solution)/shard_map/ppermute | solution.py:21
  23.9 15.0 %collective-permute-start.5 = (bf16[2,64,128]{2,1,0:T(8,128)(2,1)S(1)}, bf16[2,64,128]{2,1,0:T(8,128)(2,1)S(1)}, u32[]{:S(2)}, u32[]{:S(2)}) collective-permute-start(bf16[2,64,128]{2,1,0:T(8,128)(2,1)S(1)} %get-tuple-element.102.wanted), channel_id=1, source_target_pairs={{0,16},{4,20},{8,24},{12,28},{16,0},{20,4},{24,8},{28,12},{1,17},{... | collective-permute-start | bytes 98312 | tf_op jit(solution)/shard_map/ppermute | solution.py:21
  44.9 8.4 %collective-permute-start.18 = (bf16[256,512]{1,0:T(8,128)(2,1)S(1)}, bf16[256,512]{1,0:T(8,128)(2,1)S(1)}, u32[]{:S(2)}, u32[]{:S(2)}) collective-permute-start(bf16[256,512]{1,0:T(8,128)(2,1)S(1)} %collective-permute-done.7.refs_2_), channel_id=1, source_target_pairs={{0,1},{1,0},{2,3},{3,2},{4,5},{5,4},{6,7},{7,6},{8,9},{9,8},{10,11... | collective-permute-start | bytes 786440 | tf_op jit(solution)/shard_map/ppermute | solution.py:21
  47.4 11.5 %collective-permute-start.14 = (bf16[256,768]{1,0:T(8,128)(2,1)S(1)}, bf16[256,768]{1,0:T(8,128)(2,1)S(1)}, u32[]{:S(2)}, u32[]{:S(2)}) collective-permute-start(bf16[256,768]{1,0:T(8,128)(2,1)S(1)} %get-tuple-element.122), channel_id=1, source_target_pairs={{0,8},{4,12},{8,0},{12,4},{16,24},{20,28},{24,16},{28,20},{1,9},{5... | collective-permute-start | bytes 1179656 | tf_op jit(solution)/shard_map/ppermute | solution.py:21
  49.0 10.6 %collective-permute-start.15 = (bf16[256,768]{1,0:T(8,128)(2,1)S(1)}, bf16[256,768]{1,0:T(8,128)(2,1)S(1)}, u32[]{:S(2)}, u32[]{:S(2)}) collective-permute-start(bf16[256,768]{1,0:T(8,128)(2,1)S(1)} %get-tuple-element.124), channel_id=1, source_target_pairs={{0,16},{4,20},{8,24},{12,28},{16,0},{20,4},{24,8},{28,12},{1,17},{... | collective-permute-start | bytes 1179656 | tf_op jit(solution)/shard_map/ppermute | solution.py:21
  55.9 6.0 %collective-permute-start.20 = (bf16[256,256]{1,0:T(8,128)(2,1)S(1)}, bf16[256,256]{1,0:T(8,128)(2,1)S(1)}, u32[]{:S(2)}, u32[]{:S(2)}) collective-permute-start(bf16[256,256]{1,0:T(8,128)(2,1)S(1)} %get-tuple-element.135), channel_id=1, source_target_pairs={{0,8},{4,12},{8,0},{12,4},{16,24},{20,28},{24,16},{28,20},{1,9},{5... | collective-permute-start | bytes 393224 | tf_op jit(solution)/shard_map/ppermute | solution.py:21
  57.5 6.3 %collective-permute-start.21 = (bf16[256,256]{1,0:T(8,128)(2,1)S(1)}, bf16[256,256]{1,0:T(8,128)(2,1)S(1)}, u32[]{:S(2)}, u32[]{:S(2)}) collective-permute-start(bf16[256,256]{1,0:T(8,128)(2,1)S(1)} %get-tuple-element.137), channel_id=1, source_target_pairs={{0,16},{4,20},{8,24},{12,28},{16,0},{20,4},{24,8},{28,12},{1,17},{... | collective-permute-start | bytes 393224 | tf_op jit(solution)/shard_map/ppermute | solution.py:21
  59.7 8.3 %collective-permute-start.16 = (bf16[128,768]{1,0:T(8,128)(2,1)S(1)}, bf16[128,768]{1,0:T(8,128)(2,1)S(1)}, u32[]{:S(2)}, u32[]{:S(2)}) collective-permute-start(bf16[128,768]{1,0:T(8,128)(2,1)S(1)} %get-tuple-element.126), channel_id=1, source_target_pairs={{0,16},{4,20},{8,24},{12,28},{16,0},{20,4},{24,8},{28,12},{1,17},{... | collective-permute-start | bytes 589832 | tf_op jit(solution)/shard_map/ppermute | solution.py:21
  61.3 6.7 %collective-permute-start.17 = (bf16[128,768]{1,0:T(8,128)(2,1)S(1)}, bf16[128,768]{1,0:T(8,128)(2,1)S(1)}, u32[]{:S(2)}, u32[]{:S(2)}) collective-permute-start(bf16[128,768]{1,0:T(8,128)(2,1)S(1)} %get-tuple-element.127), channel_id=1, source_target_pairs={{0,8},{4,12},{8,0},{12,4},{16,24},{20,28},{24,16},{28,20},{1,9},{5... | collective-permute-start | bytes 589832 | tf_op jit(solution)/shard_map/ppermute | solution.py:21
  71.8 10.2 %collective-permute-start.24 = (bf16[128,768]{1,0:T(8,128)(2,1)S(1)}, bf16[128,768]{1,0:T(8,128)(2,1)S(1)}, u32[]{:S(2)}, u32[]{:S(2)}) collective-permute-start(bf16[128,768]{1,0:T(8,128)(2,1)S(1)} %get-tuple-element.141.own), channel_id=1, source_target_pairs={{0,8},{4,12},{8,0},{12,4},{16,24},{20,28},{24,16},{28,20},{1,9},{5... | collective-permute-start | bytes 589832 | tf_op jit(solution)/shard_map/ppermute | solution.py:21
  73.3 8.7 %collective-permute-start.26 = (bf16[128,768]{1,0:T(8,128)(2,1)S(1)}, bf16[128,768]{1,0:T(8,128)(2,1)S(1)}, u32[]{:S(2)}, u32[]{:S(2)}) collective-permute-start(bf16[128,768]{1,0:T(8,128)(2,1)S(1)} %get-tuple-element.143.own), channel_id=1, source_target_pairs={{0,16},{4,20},{8,24},{12,28},{16,0},{20,4},{24,8},{28,12},{1,17},{... | collective-permute-start | bytes 589832 | tf_op jit(solution)/shard_map/ppermute | solution.py:21
  75.5 5.9 %collective-permute-start.29 = (bf16[256,256]{1,0:T(8,128)(2,1)S(1)}, bf16[256,256]{1,0:T(8,128)(2,1)S(1)}, u32[]{:S(2)}, u32[]{:S(2)}) collective-permute-start(bf16[256,256]{1,0:T(8,128)(2,1)S(1)} %join.6.refs_2_), channel_id=1, source_target_pairs={{0,8},{4,12},{8,0},{12,4},{16,24},{20,28},{24,16},{28,20},{1,9},{5... | collective-permute-start | bytes 393224 | tf_op jit(solution)/shard_map/ppermute | solution.py:21
  76.3 5.7 %collective-permute-start.27 = (bf16[256,256]{1,0:T(8,128)(2,1)S(1)}, bf16[256,256]{1,0:T(8,128)(2,1)S(1)}, u32[]{:S(2)}, u32[]{:S(2)}) collective-permute-start(bf16[256,256]{1,0:T(8,128)(2,1)S(1)} %join.5.refs_0_), channel_id=1, source_target_pairs={{0,16},{4,20},{8,24},{12,28},{16,0},{20,4},{24,8},{28,12},{1,17},{... | collective-permute-start | bytes 393224 | tf_op jit(solution)/shard_map/ppermute | solution.py:21
  82.5 12.1 %collective-permute-start.32 = (bf16[272,768]{1,0:T(8,128)(2,1)S(1)}, bf16[272,768]{1,0:T(8,128)(2,1)S(1)}, u32[]{:S(2)}, u32[]{:S(2)}) collective-permute-start(bf16[272,768]{1,0:T(8,128)(2,1)S(1)} %join.4.refs_0_), channel_id=1, source_target_pairs={{0,16},{4,20},{8,24},{12,28},{16,0},{20,4},{24,8},{28,12},{1,17},{... | collective-permute-start | bytes 1253384 | tf_op jit(solution)/shard_map/ppermute | solution.py:21
  83.2 11.8 %collective-permute-start.33 = (bf16[272,768]{1,0:T(8,128)(2,1)S(1)}, bf16[272,768]{1,0:T(8,128)(2,1)S(1)}, u32[]{:S(2)}, u32[]{:S(2)}) collective-permute-start(bf16[272,768]{1,0:T(8,128)(2,1)S(1)} %join.7.refs_2_), channel_id=1, source_target_pairs={{0,8},{4,12},{8,0},{12,4},{16,24},{20,28},{24,16},{28,20},{1,9},{5... | collective-permute-start | bytes 1253384 | tf_op jit(solution)/shard_map/ppermute | solution.py:21
  84.3 10.7 %collective-permute-start.31 = (bf16[256,512]{1,0:T(8,128)(2,1)S(1)}, bf16[256,512]{1,0:T(8,128)(2,1)S(1)}, u32[]{:S(2)}, u32[]{:S(2)}) collective-permute-start(bf16[256,512]{1,0:T(8,128)(2,1)S(1)} %three_own.2), channel_id=1, source_target_pairs={{0,1},{1,0},{2,3},{3,2},{4,5},{5,4},{6,7},{7,6},{8,9},{9,8},{10,11... | collective-permute-start | bytes 786440 | tf_op jit(solution)/shard_map/ppermute | solution.py:21
  98.2 6.7 %collective-permute-start.39 = (bf16[1536,256]{1,0:T(8,128)(2,1)S(1)}, bf16[1536,256]{1,0:T(8,128)(2,1)S(1)}, u32[]{:S(2)}, u32[]{:S(2)}) collective-permute-start(bf16[1536,256]{1,0:T(8,128)(2,1)S(1)} %get-tuple-element.161), channel_id=1, source_target_pairs={{0,4},{4,0},{8,12},{12,8},{16,20},{20,16},{24,28},{28,24},{1,5},{5... | collective-permute-start | bytes 2359304 | tf_op jit(solution)/shard_map/ppermute | solution.py:21
  98.9 9.6 %collective-permute-start.41 = (bf16[512,256]{1,0:T(8,128)(2,1)S(1)}, bf16[512,256]{1,0:T(8,128)(2,1)S(1)}, u32[]{:S(2)}, u32[]{:S(2)}) collective-permute-start(bf16[512,256]{1,0:T(8,128)(2,1)S(1)} %two_own.3), channel_id=1, source_target_pairs={{0,1},{1,0},{2,3},{3,2},{4,5},{5,4},{6,7},{7,6},{8,9},{9,8},{10,11... | collective-permute-start | bytes 786440 | tf_op jit(solution)/shard_map/ppermute | solution.py:21
  102.0 6.9 %collective-permute-start.34 = (bf16[4,112,256]{2,1,0:T(8,128)(2,1)S(1)}, bf16[4,112,256]{2,1,0:T(8,128)(2,1)S(1)}, u32[]{:S(2)}, u32[]{:S(2)}) collective-permute-start(bf16[4,112,256]{2,1,0:T(8,128)(2,1)S(1)} %get-tuple-element.153), channel_id=1, source_target_pairs={{0,4},{4,0},{8,12},{12,8},{16,20},{20,16},{24,28},{28,24},{1,5},{5... | collective-permute-start | bytes 688136 | tf_op jit(solution)/shard_map/ppermute | solution.py:21
  103.0 15.8 %collective-permute-start.36 = (bf16[256,512]{1,0:T(8,128)(2,1)S(1)}, bf16[256,512]{1,0:T(8,128)(2,1)S(1)}, u32[]{:S(2)}, u32[]{:S(2)}) collective-permute-start(bf16[256,512]{1,0:T(8,128)(2,1)S(1)} %add_up.2), channel_id=1, source_target_pairs={{0,2},{1,3},{2,0},{3,1},{4,6},{5,7},{6,4},{7,5},{8,10},{9,11},{10,... | collective-permute-start | bytes 786440 | tf_op jit(solution)/shard_map/ppermute | solution.py:21
  108.5 19.7 %collective-permute-start.44 = (bf16[256,512]{1,0:T(8,128)(2,1)S(1)}, bf16[256,512]{1,0:T(8,128)(2,1)S(1)}, u32[]{:S(2)}, u32[]{:S(2)}) collective-permute-start(bf16[256,512]{1,0:T(8,128)(2,1)S(1)} %get-tuple-element.168), channel_id=1, source_target_pairs={{0,1},{1,0},{2,3},{3,2},{4,5},{5,4},{6,7},{7,6},{8,9},{9,8},{10,11... | collective-permute-start | bytes 786440 | tf_op jit(solution)/shard_map/ppermute | solution.py:21
  109.7 21.3 %collective-permute-start.42 = (bf16[512,256]{1,0:T(8,128)(2,1)S(1)}, bf16[512,256]{1,0:T(8,128)(2,1)S(1)}, u32[]{:S(2)}, u32[]{:S(2)}) collective-permute-start(bf16[512,256]{1,0:T(8,128)(2,1)S(1)} %get-tuple-element.166), channel_id=1, source_target_pairs={{0,1},{1,0},{2,3},{3,2},{4,5},{5,4},{6,7},{7,6},{8,9},{9,8},{10,11... | collective-permute-start | bytes 786440 | tf_op jit(solution)/shard_map/ppermute | solution.py:21
  111.4 19.7 %collective-permute-start.43 = (bf16[512,256]{1,0:T(8,128)(2,1)S(1)}, bf16[512,256]{1,0:T(8,128)(2,1)S(1)}, u32[]{:S(2)}, u32[]{:S(2)}) collective-permute-start(bf16[512,256]{1,0:T(8,128)(2,1)S(1)} %add_up.3), channel_id=1, source_target_pairs={{0,2},{1,3},{2,0},{3,1},{4,6},{5,7},{6,4},{7,5},{8,10},{9,11},{10,... | collective-permute-start | bytes 786440 | tf_op jit(solution)/shard_map/ppermute | solution.py:21
  123.1 8.2 %collective-permute-start.45 = (bf16[112,128]{1,0:T(8,128)(2,1)S(1)}, bf16[112,128]{1,0:T(8,128)(2,1)S(1)}, u32[]{:S(2)}, u32[]{:S(2)}) collective-permute-start(bf16[112,128]{1,0:T(8,128)(2,1)S(1)} %get-tuple-element.170), channel_id=1, source_target_pairs={{0,2},{1,3},{2,0},{3,1},{4,6},{5,7},{6,4},{7,5},{8,10},{9,11},{10,... | collective-permute-start | bytes 86024 | tf_op jit(solution)/shard_map/ppermute | solution.py:21
  (28 other events, 154.8 us)

commit v8 on v7

--- a/solution.py
+++ b/solution.py
@@ -275,10 +275,7 @@
 def join(own, got, out):
     rows = own.shape[0]
     out[:rows] = own[...]
-    filled = rows + got.shape[0]
-    out[rows:filled] = got[...]
-    if filled < out.shape[0]:
-        out[filled:] = jnp.zeros((out.shape[0] - filled, out.shape[1]), out.dtype)
+    out[rows:] = got[...]
 
 
 def lay(*refs, axis):
@@ -617,9 +614,8 @@
             if last:
                 break
             held = [a + b for a, b in zip(held, more)]
-            spare = 16 * (g == 0 and stage + 2 == len(bits))
             arrays = [
-                on_core(join, shaped((len(blocks) * rows + spare, cols), bf16), [own, got], "join")
+                on_core(join, shaped((len(blocks) * rows, cols), bf16), [own, got], "join")
                 for blocks, own, got in zip(held, arrays, gots)
             ]
             gathers[g, stage] = gots

time: 136 us -> 136 us (level)
    unnamed x28 -> x24, local copies, waits for them, and re-layouts: 3.65 us -> 3.37 us
  transfers between devices with their start and end apart: 47 -> 47, of which waited for: 24 -> 24; matrix products, arithmetic and copies ran while one was open for 1% -> 1% of each run, Pallas kernels for 10% -> 11%
where the time goes in v8:
time: 136 us
  waiting for transfers between devices  52 us (38%)
  starting transfers between devices  46.3 us (34%)
  Pallas kernels  20.7 us (15%)
  blocking collectives  10.4 us (8%)
  local copies, waits for them, and re-layouts  3.37 us (2%)
  between operations  1.72 us (1%)
    ppermute x47, waiting for transfers between devices, swap(): return lax.ppermute(value, axis, [(at, at ^ step) for at in range(count)])  52 us
    ppermute x47, starting transfers between devices, swap(): return lax.ppermute(value, axis, [(at, at ^ step) for at in range(count)])  46.3 us
    pallas_call x40, Pallas kernels, on_core(): pl.pallas_call(body, out_shape=outs, in_specs=[pl.BlockSpec(memory_space=...  20.7 us
    all_gather x1, blocking collectives, on_device(): held = lax.all_gather(packed, 'dp')  10.4 us
    unnamed x24, local copies, waits for them, and re-layouts  3.37 us
  transfers between devices with their start and end apart: 47, of which 24 were waited for; matrix products, arithmetic and copies ran while one was open for 1% of the time, Pallas kernels for 11%

profile of v8, /device:TPU:0, one launch (start us, length us, event | category | flops | bytes accessed | tf_op | source)
XLA Modules:
  0.0 135.6 jit_solution(2429265149347464891)
XLA Ops:
  1.8 4.1 %collective-permute-start.1 = (bf16[512,256]{1,0:T(8,128)(2,1)S(1)}, bf16[512,256]{1,0:T(8,128)(2,1)S(1)}, u32[]{:S(2)}, u32[]{:S(2)}) collective-permute-start(bf16[512,256]{1,0:T(8,128)(2,1)S(1)} %convert_element_type.6.refs_0_), channel_id=1, source_target_pairs={{0,2},{1,3},{2,0},{3,1},{4,6},{5,7},{6,4},{7,5},{8,10},{9,11},{10,... | collective-permute-start | bytes 786440 | tf_op jit(solution)/shard_map/ppermute | solution.py:21
  5.9 1.6 %collective-permute-start = (bf16[512,256]{1,0:T(8,128)(2,1)S(1)}, bf16[512,256]{1,0:T(8,128)(2,1)S(1)}, u32[]{:S(2)}, u32[]{:S(2)}) collective-permute-start(bf16[512,256]{1,0:T(8,128)(2,1)S(1)} %convert_element_type.6.refs_0_), channel_id=1, source_target_pairs={{0,1},{1,0},{2,3},{3,2},{4,5},{5,4},{6,7},{7,6},{8,9},{9,8},{10,11... | collective-permute-start | bytes 786440 | tf_op jit(solution)/shard_map/ppermute | solution.py:21
  9.0 1.9 %collective-permute-start.3 = (bf16[64,128]{1,0:T(8,128)(2,1)S(1)}, bf16[64,128]{1,0:T(8,128)(2,1)S(1)}, u32[]{:S(2)}, u32[]{:S(2)}) collective-permute-start(bf16[64,128]{1,0:T(8,128)(2,1)S(1)} %pack_small.1.refs_1_), channel_id=1, source_target_pairs={{0,2},{1,3},{2,0},{3,1},{4,6},{5,7},{6,4},{7,5},{8,10},{9,11},{10,... | collective-permute-start | bytes 49160 | tf_op jit(solution)/shard_map/ppermute | solution.py:21
  10.9 2.5 %collective-permute-start.2 = (bf16[64,128]{1,0:T(8,128)(2,1)S(1)}, bf16[64,128]{1,0:T(8,128)(2,1)S(1)}, u32[]{:S(2)}, u32[]{:S(2)}) collective-permute-start(bf16[64,128]{1,0:T(8,128)(2,1)S(1)} %pack_small.1.refs_1_), channel_id=1, source_target_pairs={{0,1},{1,0},{2,3},{3,2},{4,5},{5,4},{6,7},{7,6},{8,9},{9,8},{10,11... | collective-permute-start | bytes 49160 | tf_op jit(solution)/shard_map/ppermute | solution.py:21
  15.9 3.7 %collective-permute-done.4.refs_4_ = bf16[64,128]{1,0:T(8,128)(2,1)S(1)} collective-permute-done((bf16[64,128]{1,0:T(8,128)(2,1)S(1)}, bf16[64,128]{1,0:T(8,128)(2,1)S(1)}, u32[]{:S(2)}, u32[]{:S(2)}) %collective-permute-start.4) | collective-permute-done | bytes 16416 | tf_op jit(solution)/shard_map/ppermute | solution.py:21
  19.8 2.0 %collective-permute-start.7 = (bf16[256,512]{1,0:T(8,128)(2,1)S(1)}, bf16[256,512]{1,0:T(8,128)(2,1)S(1)}, u32[]{:S(2)}, u32[]{:S(2)}) collective-permute-start(bf16[256,512]{1,0:T(8,128)(2,1)S(1)} %convert_element_type.7.refs_0_), channel_id=1, source_target_pairs={{0,2},{1,3},{2,0},{3,1},{4,6},{5,7},{6,4},{7,5},{8,10},{9,11},{10,... | collective-permute-start | bytes 786440 | tf_op jit(solution)/shard_map/ppermute | solution.py:21
  21.9 1.7 %collective-permute-start.6 = (bf16[256,512]{1,0:T(8,128)(2,1)S(1)}, bf16[256,512]{1,0:T(8,128)(2,1)S(1)}, u32[]{:S(2)}, u32[]{:S(2)}) collective-permute-start(bf16[256,512]{1,0:T(8,128)(2,1)S(1)} %convert_element_type.7.refs_0_), channel_id=1, source_target_pairs={{0,1},{1,0},{2,3},{3,2},{4,5},{5,4},{6,7},{7,6},{8,9},{9,8},{10,11... | collective-permute-start | bytes 786440 | tf_op jit(solution)/shard_map/ppermute | solution.py:21
  25.4 10.4 %all-gather = bf16[3072,128]{1,0:T(8,128)(2,1)S(1)} all-gather(bf16[384,128]{1,0:T(8,128)(2,1)S(1)} %pack_all.1), channel_id=2, replica_groups=mesh['dp'=8,'mp'=4] {'dp'}, dimensions={0}, use_global_device_ids=true | all-gather | bytes 884736 | tf_op jit(solution)/shard_map/all_gather | solution.py:517
  36.0 2.3 %one_forward.1.act_one = bf16[2048,512]{1,0:T(8,128)(2,1)S(1)} custom-call(bf16[64,512]{1,0:T(8,128)(2,1)S(1)} %get-tuple-element.100.inputs, bf16[64,2048]{1,0:T(8,128)(2,1)S(1)} %get-tuple-element.104.first), custom_call_target="tpu_custom_call" | custom-call | tf_op jit(solution)/shard_map/one_forward/pallas_call | solution.py:57
  39.3 1.7 %collective-permute-done.8.far = bf16[512,256]{1,0:T(8,128)(2,1)S(1)} collective-permute-done((bf16[512,256]{1,0:T(8,128)(2,1)S(1)}, bf16[512,256]{1,0:T(8,128)(2,1)S(1)}, u32[]{:S(2)}, u32[]{:S(2)}) %collective-permute-start.8) | collective-permute-done | bytes 262176 | tf_op jit(solution)/shard_map/ppermute | solution.py:21
  45.9 1.5 %one_slope.3.slope = bf16[1024,512]{1,0:T(8,128)(2,1)S(1)} custom-call(bf16[64,512]{1,0:T(8,128)(2,1)S(1)} %get-tuple-element.100.inputs, bf16[64,2048]{1,0:T(8,128)(2,1)S(1)} %get-tuple-element.104.first), custom_call_target="tpu_custom_call" | custom-call | flops 6000000000 | tf_op jit(solution)/shard_map/one_slope/pallas_call | solution.py:57
  47.4 1.6 %collective-permute-start.14 = (bf16[256,768]{1,0:T(8,128)(2,1)S(1)}, bf16[256,768]{1,0:T(8,128)(2,1)S(1)}, u32[]{:S(2)}, u32[]{:S(2)}) collective-permute-start(bf16[256,768]{1,0:T(8,128)(2,1)S(1)} %get-tuple-element.122), channel_id=1, source_target_pairs={{0,8},{4,12},{8,0},{12,4},{16,24},{20,28},{24,16},{28,20},{1,9},{5... | collective-permute-start | bytes 1179656 | tf_op jit(solution)/shard_map/ppermute | solution.py:21
  49.0 1.5 %collective-permute-start.15 = (bf16[256,768]{1,0:T(8,128)(2,1)S(1)}, bf16[256,768]{1,0:T(8,128)(2,1)S(1)}, u32[]{:S(2)}, u32[]{:S(2)}) collective-permute-start(bf16[256,768]{1,0:T(8,128)(2,1)S(1)} %get-tuple-element.124), channel_id=1, source_target_pairs={{0,16},{4,20},{8,24},{12,28},{16,0},{20,4},{24,8},{28,12},{1,17},{... | collective-permute-start | bytes 1179656 | tf_op jit(solution)/shard_map/ppermute | solution.py:21
  50.5 2.8 %collective-permute-done.18.refs_0_ = bf16[256,512]{1,0:T(8,128)(2,1)S(1)} collective-permute-done((bf16[256,512]{1,0:T(8,128)(2,1)S(1)}, bf16[256,512]{1,0:T(8,128)(2,1)S(1)}, u32[]{:S(2)}, u32[]{:S(2)}) %collective-permute-start.18) | collective-permute-done | bytes 262176 | tf_op jit(solution)/shard_map/ppermute | solution.py:21
  53.3 1.7 %one_slope.2.slope_more = bf16[1024,512]{1,0:T(8,128)(2,1)S(1)} custom-call(bf16[64,512]{1,0:T(8,128)(2,1)S(1)} %get-tuple-element.100.inputs, bf16[64,2048]{1,0:T(8,128)(2,1)S(1)} %get-tuple-element.104.first), custom_call_target="tpu_custom_call" | custom-call | flops 6000000000 | tf_op jit(solution)/shard_map/one_slope/pallas_call | solution.py:57
  55.9 1.6 %collective-permute-start.20 = (bf16[256,256]{1,0:T(8,128)(2,1)S(1)}, bf16[256,256]{1,0:T(8,128)(2,1)S(1)}, u32[]{:S(2)}, u32[]{:S(2)}) collective-permute-start(bf16[256,256]{1,0:T(8,128)(2,1)S(1)} %get-tuple-element.135), channel_id=1, source_target_pairs={{0,8},{4,12},{8,0},{12,4},{16,24},{20,28},{24,16},{28,20},{1,9},{5... | collective-permute-start | bytes 393224 | tf_op jit(solution)/shard_map/ppermute | solution.py:21
  59.7 1.6 %collective-permute-start.16 = (bf16[128,768]{1,0:T(8,128)(2,1)S(1)}, bf16[128,768]{1,0:T(8,128)(2,1)S(1)}, u32[]{:S(2)}, u32[]{:S(2)}) collective-permute-start(bf16[128,768]{1,0:T(8,128)(2,1)S(1)} %get-tuple-element.126), channel_id=1, source_target_pairs={{0,16},{4,20},{8,24},{12,28},{16,0},{20,4},{24,8},{28,12},{1,17},{... | collective-permute-start | bytes 589832 | tf_op jit(solution)/shard_map/ppermute | solution.py:21
  61.9 1.9 %collective-permute-done.21.refs_3_ = bf16[256,256]{1,0:T(8,128)(2,1)S(1)} collective-permute-done((bf16[256,256]{1,0:T(8,128)(2,1)S(1)}, bf16[256,256]{1,0:T(8,128)(2,1)S(1)}, u32[]{:S(2)}, u32[]{:S(2)}) %collective-permute-start.21) | collective-permute-done | bytes 131104 | tf_op jit(solution)/shard_map/ppermute | solution.py:21
  63.8 1.6 %collective-permute-start.22 = (bf16[128,256]{1,0:T(8,128)(2,1)S(1)}, bf16[128,256]{1,0:T(8,128)(2,1)S(1)}, u32[]{:S(2)}, u32[]{:S(2)}) collective-permute-start(bf16[128,256]{1,0:T(8,128)(2,1)S(1)} %get-tuple-element.139), channel_id=1, source_target_pairs={{0,16},{4,20},{8,24},{12,28},{16,0},{20,4},{24,8},{28,12},{1,17},{... | collective-permute-start | bytes 196616 | tf_op jit(solution)/shard_map/ppermute | solution.py:21
  66.0 2.0 %collective-permute-done.16.refs_1_ = bf16[128,768]{1,0:T(8,128)(2,1)S(1)} collective-permute-done((bf16[128,768]{1,0:T(8,128)(2,1)S(1)}, bf16[128,768]{1,0:T(8,128)(2,1)S(1)}, u32[]{:S(2)}, u32[]{:S(2)}) %collective-permute-start.16) | collective-permute-done | bytes 196640 | tf_op jit(solution)/shard_map/ppermute | solution.py:21
  77.6 3.8 %collective-permute-done.29.refs_3_ = bf16[256,256]{1,0:T(8,128)(2,1)S(1)} collective-permute-done((bf16[256,256]{1,0:T(8,128)(2,1)S(1)}, bf16[256,256]{1,0:T(8,128)(2,1)S(1)}, u32[]{:S(2)}, u32[]{:S(2)}) %collective-permute-start.29) | collective-permute-done | bytes 131104 | tf_op jit(solution)/shard_map/ppermute | solution.py:21
  85.7 8.3 %collective-permute-done.33.refs_3_ = bf16[256,768]{1,0:T(8,128)(2,1)S(1)} collective-permute-done((bf16[256,768]{1,0:T(8,128)(2,1)S(1)}, bf16[256,768]{1,0:T(8,128)(2,1)S(1)}, u32[]{:S(2)}, u32[]{:S(2)}) %collective-permute-start.33) | collective-permute-done | bytes 393248 | tf_op jit(solution)/shard_map/ppermute | solution.py:21
  99.4 2.1 %one_back.1 = (f32[4,112,256]{2,1,0:T(8,128)S(1)}, bf16[4,112,256]{2,1,0:T(8,128)(2,1)S(1)}) custom-call(bf16[64,512]{1,0:T(8,128)(2,1)S(1)} %get-tuple-element.100.inputs, bf16[512,512]{1,0:T(8,128)(2,1)S(1)} %get-tuple-element.150.delta, bf16[1024,512]{1,0:T(8,128)(2,1)S(1)} %one_slope.3.slope, bf16[1024,512]{1,0:T(8,128)(2,1)S(1)} %one_slope.2.slope_more, ...), custom_call_target="tpu_custom_call" | custom-call | flops 99999997952 | tf_op jit(solution)/shard_map/one_back/pallas_call | solution.py:57
  102.3 1.8 %collective-permute-start.36 = (bf16[256,512]{1,0:T(8,128)(2,1)S(1)}, bf16[256,512]{1,0:T(8,128)(2,1)S(1)}, u32[]{:S(2)}, u32[]{:S(2)}) collective-permute-start(bf16[256,512]{1,0:T(8,128)(2,1)S(1)} %add_up.2), channel_id=1, source_target_pairs={{0,2},{1,3},{2,0},{3,1},{4,6},{5,7},{6,4},{7,5},{8,10},{9,11},{10,... | collective-permute-start | bytes 786440 | tf_op jit(solution)/shard_map/ppermute | solution.py:21
  104.7 3.3 %collective-permute-done.41.got = bf16[512,256]{1,0:T(8,128)(2,1)S(1)} collective-permute-done((bf16[512,256]{1,0:T(8,128)(2,1)S(1)}, bf16[512,256]{1,0:T(8,128)(2,1)S(1)}, u32[]{:S(2)}, u32[]{:S(2)}) %collective-permute-start.41) | collective-permute-done | bytes 262176 | tf_op jit(solution)/shard_map/ppermute | solution.py:21
  109.9 1.6 %collective-permute-start.42 = (bf16[512,256]{1,0:T(8,128)(2,1)S(1)}, bf16[512,256]{1,0:T(8,128)(2,1)S(1)}, u32[]{:S(2)}, u32[]{:S(2)}) collective-permute-start(bf16[512,256]{1,0:T(8,128)(2,1)S(1)} %get-tuple-element.166), channel_id=1, source_target_pairs={{0,1},{1,0},{2,3},{3,2},{4,5},{5,4},{6,7},{7,6},{8,9},{9,8},{10,11... | collective-permute-start | bytes 786440 | tf_op jit(solution)/shard_map/ppermute | solution.py:21
  111.5 1.6 %collective-permute-start.43 = (bf16[512,256]{1,0:T(8,128)(2,1)S(1)}, bf16[512,256]{1,0:T(8,128)(2,1)S(1)}, u32[]{:S(2)}, u32[]{:S(2)}) collective-permute-start(bf16[512,256]{1,0:T(8,128)(2,1)S(1)} %add_up.3), channel_id=1, source_target_pairs={{0,2},{1,3},{2,0},{3,1},{4,6},{5,7},{6,4},{7,5},{8,10},{9,11},{10,... | collective-permute-start | bytes 786440 | tf_op jit(solution)/shard_map/ppermute | solution.py:21
  113.3 4.7 %collective-permute-done.36.refs_0_ = bf16[256,512]{1,0:T(8,128)(2,1)S(1)} collective-permute-done((bf16[256,512]{1,0:T(8,128)(2,1)S(1)}, bf16[256,512]{1,0:T(8,128)(2,1)S(1)}, u32[]{:S(2)}, u32[]{:S(2)}) %collective-permute-start.36) | collective-permute-done | bytes 262176 | tf_op jit(solution)/shard_map/ppermute | solution.py:21
  118.8 3.5 %collective-permute-done.38.got = bf16[1,112,256]{2,1,0:T(8,128)(2,1)S(1)} collective-permute-done((bf16[1,112,256]{2,1,0:T(8,128)(2,1)S(1)}, bf16[1,112,256]{2,1,0:T(8,128)(2,1)S(1)}, u32[]{:S(2)}, u32[]{:S(2)}) %collective-permute-start.38) | collective-permute-done | bytes 57376 | tf_op jit(solution)/shard_map/ppermute | solution.py:21
  122.4 5.3 %collective-permute-done.44.refs_1_ = bf16[256,512]{1,0:T(8,128)(2,1)S(1)} collective-permute-done((bf16[256,512]{1,0:T(8,128)(2,1)S(1)}, bf16[256,512]{1,0:T(8,128)(2,1)S(1)}, u32[]{:S(2)}, u32[]{:S(2)}) %collective-permute-start.44) | collective-permute-done | bytes 262176 | tf_op jit(solution)/shard_map/ppermute | solution.py:21
  128.8 1.7 %collective-permute-done.42.refs_0_ = bf16[512,256]{1,0:T(8,128)(2,1)S(1)} collective-permute-done((bf16[512,256]{1,0:T(8,128)(2,1)S(1)}, bf16[512,256]{1,0:T(8,128)(2,1)S(1)}, u32[]{:S(2)}, u32[]{:S(2)}) %collective-permute-start.42) | collective-permute-done | bytes 262176 | tf_op jit(solution)/shard_map/ppermute | solution.py:21
  132.4 2.5 %collective-permute-done.46.refs_0_ = bf16[112,64]{1,0:T(8,128)(2,1)S(1)} collective-permute-done((bf16[112,64]{1,0:T(8,128)(2,1)S(1)}, bf16[112,64]{1,0:T(8,128)(2,1)S(1)}, u32[]{:S(2)}, u32[]{:S(2)}) %collective-permute-start.46) | collective-permute-done | bytes 14368 | tf_op jit(solution)/shard_map/ppermute | solution.py:21
  (129 shorter events, 44.1 us)
Async XLA Ops:
  1.8 17.8 %collective-permute-start.1 = (bf16[512,256]{1,0:T(8,128)(2,1)S(1)}, bf16[512,256]{1,0:T(8,128)(2,1)S(1)}, u32[]{:S(2)}, u32[]{:S(2)}) collective-permute-start(bf16[512,256]{1,0:T(8,128)(2,1)S(1)} %convert_element_type.6.refs_0_), channel_id=1, source_target_pairs={{0,2},{1,3},{2,0},{3,1},{4,6},{5,7},{6,4},{7,5},{8,10},{9,11},{10,... | collective-permute-start | bytes 786440 | tf_op jit(solution)/shard_map/ppermute | solution.py:21
  5.9 13.7 %collective-permute-start = (bf16[512,256]{1,0:T(8,128)(2,1)S(1)}, bf16[512,256]{1,0:T(8,128)(2,1)S(1)}, u32[]{:S(2)}, u32[]{:S(2)}) collective-permute-start(bf16[512,256]{1,0:T(8,128)(2,1)S(1)} %convert_element_type.6.refs_0_), channel_id=1, source_target_pairs={{0,1},{1,0},{2,3},{3,2},{4,5},{5,4},{6,7},{7,6},{8,9},{9,8},{10,11... | collective-permute-start | bytes 786440 | tf_op jit(solution)/shard_map/ppermute | solution.py:21
  9.0 10.6 %collective-permute-start.4 = (bf16[64,128]{1,0:T(8,128)(2,1)S(1)}, bf16[64,128]{1,0:T(8,128)(2,1)S(1)}, u32[]{:S(2)}, u32[]{:S(2)}) collective-permute-start(bf16[64,128]{1,0:T(8,128)(2,1)S(1)} %pack_small.1.refs_1_), channel_id=1, source_target_pairs={{0,3},{1,2},{2,1},{3,0},{4,7},{5,6},{6,5},{7,4},{8,11},{9,10},{10,... | collective-permute-start | bytes 49160 | tf_op jit(solution)/shard_map/ppermute | solution.py:21
  9.0 10.6 %collective-permute-start.3 = (bf16[64,128]{1,0:T(8,128)(2,1)S(1)}, bf16[64,128]{1,0:T(8,128)(2,1)S(1)}, u32[]{:S(2)}, u32[]{:S(2)}) collective-permute-start(bf16[64,128]{1,0:T(8,128)(2,1)S(1)} %pack_small.1.refs_1_), channel_id=1, source_target_pairs={{0,2},{1,3},{2,0},{3,1},{4,6},{5,7},{6,4},{7,5},{8,10},{9,11},{10,... | collective-permute-start | bytes 49160 | tf_op jit(solution)/shard_map/ppermute | solution.py:21
  10.9 8.7 %collective-permute-start.2 = (bf16[64,128]{1,0:T(8,128)(2,1)S(1)}, bf16[64,128]{1,0:T(8,128)(2,1)S(1)}, u32[]{:S(2)}, u32[]{:S(2)}) collective-permute-start(bf16[64,128]{1,0:T(8,128)(2,1)S(1)} %pack_small.1.refs_1_), channel_id=1, source_target_pairs={{0,1},{1,0},{2,3},{3,2},{4,5},{5,4},{6,7},{7,6},{8,9},{9,8},{10,11... | collective-permute-start | bytes 49160 | tf_op jit(solution)/shard_map/ppermute | solution.py:21
  19.7 22.8 %collective-permute-start.9 = (bf16[1536,256]{1,0:T(8,128)(2,1)S(1)}, bf16[1536,256]{1,0:T(8,128)(2,1)S(1)}, u32[]{:S(2)}, u32[]{:S(2)}) collective-permute-start(bf16[1536,256]{1,0:T(8,128)(2,1)S(1)} %lay.1.near), channel_id=1, source_target_pairs={{0,4},{4,0},{8,12},{12,8},{16,20},{20,16},{24,28},{28,24},{1,5},{5... | collective-permute-start | bytes 2359304 | tf_op jit(solution)/shard_map/ppermute | solution.py:21
  19.8 18.5 %collective-permute-start.7 = (bf16[256,512]{1,0:T(8,128)(2,1)S(1)}, bf16[256,512]{1,0:T(8,128)(2,1)S(1)}, u32[]{:S(2)}, u32[]{:S(2)}) collective-permute-start(bf16[256,512]{1,0:T(8,128)(2,1)S(1)} %convert_element_type.7.refs_0_), channel_id=1, source_target_pairs={{0,2},{1,3},{2,0},{3,1},{4,6},{5,7},{6,4},{7,5},{8,10},{9,11},{10,... | collective-permute-start | bytes 786440 | tf_op jit(solution)/shard_map/ppermute | solution.py:21
  21.9 16.9 %collective-permute-start.6 = (bf16[256,512]{1,0:T(8,128)(2,1)S(1)}, bf16[256,512]{1,0:T(8,128)(2,1)S(1)}, u32[]{:S(2)}, u32[]{:S(2)}) collective-permute-start(bf16[256,512]{1,0:T(8,128)(2,1)S(1)} %convert_element_type.7.refs_0_), channel_id=1, source_target_pairs={{0,1},{1,0},{2,3},{3,2},{4,5},{5,4},{6,7},{7,6},{8,9},{9,8},{10,11... | collective-permute-start | bytes 786440 | tf_op jit(solution)/shard_map/ppermute | solution.py:21
  23.6 17.4 %collective-permute-start.8 = (bf16[512,256]{1,0:T(8,128)(2,1)S(1)}, bf16[512,256]{1,0:T(8,128)(2,1)S(1)}, u32[]{:S(2)}, u32[]{:S(2)}) collective-permute-start(bf16[512,256]{1,0:T(8,128)(2,1)S(1)} %collective-permute-done.1.refs_2_), channel_id=1, source_target_pairs={{0,1},{1,0},{2,3},{3,2},{4,5},{5,4},{6,7},{7,6},{8,9},{9,8},{10,11... | collective-permute-start | bytes 786440 | tf_op jit(solution)/shard_map/ppermute | solution.py:21
  23.9 15.0 %collective-permute-start.5 = (bf16[2,64,128]{2,1,0:T(8,128)(2,1)S(1)}, bf16[2,64,128]{2,1,0:T(8,128)(2,1)S(1)}, u32[]{:S(2)}, u32[]{:S(2)}) collective-permute-start(bf16[2,64,128]{2,1,0:T(8,128)(2,1)S(1)} %get-tuple-element.102.wanted), channel_id=1, source_target_pairs={{0,16},{4,20},{8,24},{12,28},{16,0},{20,4},{24,8},{28,12},{1,17},{... | collective-permute-start | bytes 98312 | tf_op jit(solution)/shard_map/ppermute | solution.py:21
  44.9 8.4 %collective-permute-start.18 = (bf16[256,512]{1,0:T(8,128)(2,1)S(1)}, bf16[256,512]{1,0:T(8,128)(2,1)S(1)}, u32[]{:S(2)}, u32[]{:S(2)}) collective-permute-start(bf16[256,512]{1,0:T(8,128)(2,1)S(1)} %collective-permute-done.7.refs_2_), channel_id=1, source_target_pairs={{0,1},{1,0},{2,3},{3,2},{4,5},{5,4},{6,7},{7,6},{8,9},{9,8},{10,11... | collective-permute-start | bytes 786440 | tf_op jit(solution)/shard_map/ppermute | solution.py:21
  47.4 11.5 %collective-permute-start.14 = (bf16[256,768]{1,0:T(8,128)(2,1)S(1)}, bf16[256,768]{1,0:T(8,128)(2,1)S(1)}, u32[]{:S(2)}, u32[]{:S(2)}) collective-permute-start(bf16[256,768]{1,0:T(8,128)(2,1)S(1)} %get-tuple-element.122), channel_id=1, source_target_pairs={{0,8},{4,12},{8,0},{12,4},{16,24},{20,28},{24,16},{28,20},{1,9},{5... | collective-permute-start | bytes 1179656 | tf_op jit(solution)/shard_map/ppermute | solution.py:21
  49.0 10.6 %collective-permute-start.15 = (bf16[256,768]{1,0:T(8,128)(2,1)S(1)}, bf16[256,768]{1,0:T(8,128)(2,1)S(1)}, u32[]{:S(2)}, u32[]{:S(2)}) collective-permute-start(bf16[256,768]{1,0:T(8,128)(2,1)S(1)} %get-tuple-element.124), channel_id=1, source_target_pairs={{0,16},{4,20},{8,24},{12,28},{16,0},{20,4},{24,8},{28,12},{1,17},{... | collective-permute-start | bytes 1179656 | tf_op jit(solution)/shard_map/ppermute | solution.py:21
  55.9 6.0 %collective-permute-start.20 = (bf16[256,256]{1,0:T(8,128)(2,1)S(1)}, bf16[256,256]{1,0:T(8,128)(2,1)S(1)}, u32[]{:S(2)}, u32[]{:S(2)}) collective-permute-start(bf16[256,256]{1,0:T(8,128)(2,1)S(1)} %get-tuple-element.135), channel_id=1, source_target_pairs={{0,8},{4,12},{8,0},{12,4},{16,24},{20,28},{24,16},{28,20},{1,9},{5... | collective-permute-start | bytes 393224 | tf_op jit(solution)/shard_map/ppermute | solution.py:21
  57.5 6.3 %collective-permute-start.21 = (bf16[256,256]{1,0:T(8,128)(2,1)S(1)}, bf16[256,256]{1,0:T(8,128)(2,1)S(1)}, u32[]{:S(2)}, u32[]{:S(2)}) collective-permute-start(bf16[256,256]{1,0:T(8,128)(2,1)S(1)} %get-tuple-element.137), channel_id=1, source_target_pairs={{0,16},{4,20},{8,24},{12,28},{16,0},{20,4},{24,8},{28,12},{1,17},{... | collective-permute-start | bytes 393224 | tf_op jit(solution)/shard_map/ppermute | solution.py:21
  59.7 8.3 %collective-permute-start.16 = (bf16[128,768]{1,0:T(8,128)(2,1)S(1)}, bf16[128,768]{1,0:T(8,128)(2,1)S(1)}, u32[]{:S(2)}, u32[]{:S(2)}) collective-permute-start(bf16[128,768]{1,0:T(8,128)(2,1)S(1)} %get-tuple-element.126), channel_id=1, source_target_pairs={{0,16},{4,20},{8,24},{12,28},{16,0},{20,4},{24,8},{28,12},{1,17},{... | collective-permute-start | bytes 589832 | tf_op jit(solution)/shard_map/ppermute | solution.py:21
  61.3 6.7 %collective-permute-start.17 = (bf16[128,768]{1,0:T(8,128)(2,1)S(1)}, bf16[128,768]{1,0:T(8,128)(2,1)S(1)}, u32[]{:S(2)}, u32[]{:S(2)}) collective-permute-start(bf16[128,768]{1,0:T(8,128)(2,1)S(1)} %get-tuple-element.127), channel_id=1, source_target_pairs={{0,8},{4,12},{8,0},{12,4},{16,24},{20,28},{24,16},{28,20},{1,9},{5... | collective-permute-start | bytes 589832 | tf_op jit(solution)/shard_map/ppermute | solution.py:21
  71.8 10.2 %collective-permute-start.24 = (bf16[128,768]{1,0:T(8,128)(2,1)S(1)}, bf16[128,768]{1,0:T(8,128)(2,1)S(1)}, u32[]{:S(2)}, u32[]{:S(2)}) collective-permute-start(bf16[128,768]{1,0:T(8,128)(2,1)S(1)} %get-tuple-element.141.own), channel_id=1, source_target_pairs={{0,8},{4,12},{8,0},{12,4},{16,24},{20,28},{24,16},{28,20},{1,9},{5... | collective-permute-start | bytes 589832 | tf_op jit(solution)/shard_map/ppermute | solution.py:21
  73.3 8.7 %collective-permute-start.26 = (bf16[128,768]{1,0:T(8,128)(2,1)S(1)}, bf16[128,768]{1,0:T(8,128)(2,1)S(1)}, u32[]{:S(2)}, u32[]{:S(2)}) collective-permute-start(bf16[128,768]{1,0:T(8,128)(2,1)S(1)} %get-tuple-element.143.own), channel_id=1, source_target_pairs={{0,16},{4,20},{8,24},{12,28},{16,0},{20,4},{24,8},{28,12},{1,17},{... | collective-permute-start | bytes 589832 | tf_op jit(solution)/shard_map/ppermute | solution.py:21
  75.5 5.9 %collective-permute-start.29 = (bf16[256,256]{1,0:T(8,128)(2,1)S(1)}, bf16[256,256]{1,0:T(8,128)(2,1)S(1)}, u32[]{:S(2)}, u32[]{:S(2)}) collective-permute-start(bf16[256,256]{1,0:T(8,128)(2,1)S(1)} %join.6.refs_2_), channel_id=1, source_target_pairs={{0,8},{4,12},{8,0},{12,4},{16,24},{20,28},{24,16},{28,20},{1,9},{5... | collective-permute-start | bytes 393224 | tf_op jit(solution)/shard_map/ppermute | solution.py:21
  76.3 5.7 %collective-permute-start.27 = (bf16[256,256]{1,0:T(8,128)(2,1)S(1)}, bf16[256,256]{1,0:T(8,128)(2,1)S(1)}, u32[]{:S(2)}, u32[]{:S(2)}) collective-permute-start(bf16[256,256]{1,0:T(8,128)(2,1)S(1)} %join.5.refs_0_), channel_id=1, source_target_pairs={{0,16},{4,20},{8,24},{12,28},{16,0},{20,4},{24,8},{28,12},{1,17},{... | collective-permute-start | bytes 393224 | tf_op jit(solution)/shard_map/ppermute | solution.py:21
  82.5 11.6 %collective-permute-start.33 = (bf16[256,768]{1,0:T(8,128)(2,1)S(1)}, bf16[256,768]{1,0:T(8,128)(2,1)S(1)}, u32[]{:S(2)}, u32[]{:S(2)}) collective-permute-start(bf16[256,768]{1,0:T(8,128)(2,1)S(1)} %join.7.refs_2_), channel_id=1, source_target_pairs={{0,8},{4,12},{8,0},{12,4},{16,24},{20,28},{24,16},{28,20},{1,9},{5... | collective-permute-start | bytes 1179656 | tf_op jit(solution)/shard_map/ppermute | solution.py:21
  83.2 11.3 %collective-permute-start.32 = (bf16[256,768]{1,0:T(8,128)(2,1)S(1)}, bf16[256,768]{1,0:T(8,128)(2,1)S(1)}, u32[]{:S(2)}, u32[]{:S(2)}) collective-permute-start(bf16[256,768]{1,0:T(8,128)(2,1)S(1)} %join.4.refs_0_), channel_id=1, source_target_pairs={{0,16},{4,20},{8,24},{12,28},{16,0},{20,4},{24,8},{28,12},{1,17},{... | collective-permute-start | bytes 1179656 | tf_op jit(solution)/shard_map/ppermute | solution.py:21
  84.3 10.2 %collective-permute-start.31 = (bf16[256,512]{1,0:T(8,128)(2,1)S(1)}, bf16[256,512]{1,0:T(8,128)(2,1)S(1)}, u32[]{:S(2)}, u32[]{:S(2)}) collective-permute-start(bf16[256,512]{1,0:T(8,128)(2,1)S(1)} %three_own.2), channel_id=1, source_target_pairs={{0,1},{1,0},{2,3},{3,2},{4,5},{5,4},{6,7},{7,6},{8,9},{9,8},{10,11... | collective-permute-start | bytes 786440 | tf_op jit(solution)/shard_map/ppermute | solution.py:21
  97.7 6.4 %collective-permute-start.39 = (bf16[1536,256]{1,0:T(8,128)(2,1)S(1)}, bf16[1536,256]{1,0:T(8,128)(2,1)S(1)}, u32[]{:S(2)}, u32[]{:S(2)}) collective-permute-start(bf16[1536,256]{1,0:T(8,128)(2,1)S(1)} %get-tuple-element.161), channel_id=1, source_target_pairs={{0,4},{4,0},{8,12},{12,8},{16,20},{20,16},{24,28},{28,24},{1,5},{5... | collective-permute-start | bytes 2359304 | tf_op jit(solution)/shard_map/ppermute | solution.py:21
  98.4 9.6 %collective-permute-start.41 = (bf16[512,256]{1,0:T(8,128)(2,1)S(1)}, bf16[512,256]{1,0:T(8,128)(2,1)S(1)}, u32[]{:S(2)}, u32[]{:S(2)}) collective-permute-start(bf16[512,256]{1,0:T(8,128)(2,1)S(1)} %two_own.3), channel_id=1, source_target_pairs={{0,1},{1,0},{2,3},{3,2},{4,5},{5,4},{6,7},{7,6},{8,9},{9,8},{10,11... | collective-permute-start | bytes 786440 | tf_op jit(solution)/shard_map/ppermute | solution.py:21
  101.5 6.9 %collective-permute-start.34 = (bf16[4,112,256]{2,1,0:T(8,128)(2,1)S(1)}, bf16[4,112,256]{2,1,0:T(8,128)(2,1)S(1)}, u32[]{:S(2)}, u32[]{:S(2)}) collective-permute-start(bf16[4,112,256]{2,1,0:T(8,128)(2,1)S(1)} %get-tuple-element.153), channel_id=1, source_target_pairs={{0,4},{4,0},{8,12},{12,8},{16,20},{20,16},{24,28},{28,24},{1,5},{5... | collective-permute-start | bytes 688136 | tf_op jit(solution)/shard_map/ppermute | solution.py:21
  102.3 15.8 %collective-permute-start.36 = (bf16[256,512]{1,0:T(8,128)(2,1)S(1)}, bf16[256,512]{1,0:T(8,128)(2,1)S(1)}, u32[]{:S(2)}, u32[]{:S(2)}) collective-permute-start(bf16[256,512]{1,0:T(8,128)(2,1)S(1)} %add_up.2), channel_id=1, source_target_pairs={{0,2},{1,3},{2,0},{3,1},{4,6},{5,7},{6,4},{7,5},{8,10},{9,11},{10,... | collective-permute-start | bytes 786440 | tf_op jit(solution)/shard_map/ppermute | solution.py:21
  108.0 19.7 %collective-permute-start.44 = (bf16[256,512]{1,0:T(8,128)(2,1)S(1)}, bf16[256,512]{1,0:T(8,128)(2,1)S(1)}, u32[]{:S(2)}, u32[]{:S(2)}) collective-permute-start(bf16[256,512]{1,0:T(8,128)(2,1)S(1)} %get-tuple-element.168), channel_id=1, source_target_pairs={{0,1},{1,0},{2,3},{3,2},{4,5},{5,4},{6,7},{7,6},{8,9},{9,8},{10,11... | collective-permute-start | bytes 786440 | tf_op jit(solution)/shard_map/ppermute | solution.py:21
  109.9 20.6 %collective-permute-start.42 = (bf16[512,256]{1,0:T(8,128)(2,1)S(1)}, bf16[512,256]{1,0:T(8,128)(2,1)S(1)}, u32[]{:S(2)}, u32[]{:S(2)}) collective-permute-start(bf16[512,256]{1,0:T(8,128)(2,1)S(1)} %get-tuple-element.166), channel_id=1, source_target_pairs={{0,1},{1,0},{2,3},{3,2},{4,5},{5,4},{6,7},{7,6},{8,9},{9,8},{10,11... | collective-permute-start | bytes 786440 | tf_op jit(solution)/shard_map/ppermute | solution.py:21
  111.5 19.0 %collective-permute-start.43 = (bf16[512,256]{1,0:T(8,128)(2,1)S(1)}, bf16[512,256]{1,0:T(8,128)(2,1)S(1)}, u32[]{:S(2)}, u32[]{:S(2)}) collective-permute-start(bf16[512,256]{1,0:T(8,128)(2,1)S(1)} %add_up.3), channel_id=1, source_target_pairs={{0,2},{1,3},{2,0},{3,1},{4,6},{5,7},{6,4},{7,5},{8,10},{9,11},{10,... | collective-permute-start | bytes 786440 | tf_op jit(solution)/shard_map/ppermute | solution.py:21
  122.3 8.6 %collective-permute-start.45 = (bf16[112,128]{1,0:T(8,128)(2,1)S(1)}, bf16[112,128]{1,0:T(8,128)(2,1)S(1)}, u32[]{:S(2)}, u32[]{:S(2)}) collective-permute-start(bf16[112,128]{1,0:T(8,128)(2,1)S(1)} %get-tuple-element.170), channel_id=1, source_target_pairs={{0,2},{1,3},{2,0},{3,1},{4,6},{5,7},{6,4},{7,5},{8,10},{9,11},{10,... | collective-permute-start | bytes 86024 | tf_op jit(solution)/shard_map/ppermute | solution.py:21
  (26 other events, 153.6 us)

commit v9 on v8

--- a/solution.py
+++ b/solution.py
@@ -325,12 +325,16 @@
         sum_two[to] = total
 
 
-def two_first(sum_two, slope, act_one, delta, away_far, away):
+def two_first(sum_two, slope, act_one, delta, away):
     value = (sum_two[...] * slope[...]).astype(bf16)
     delta[...] = value
-    mid, near = delta.shape[0] // 2, away.shape[0]
-    away_far[...] = dot(act_one[near:], value[mid:], 1, 1).astype(bf16)
-    away[...] = dot(act_one[:near], value[mid:], 1, 1).astype(bf16)
+    mid = delta.shape[0] // 2
+    away[...] = dot(act_one[act_one.shape[0] - away.shape[0] :], value[mid:], 1, 1).astype(bf16)
+
+
+def two_away(delta, act_one, away):
+    mid = delta.shape[0] // 2
+    away[...] = dot(act_one[: away.shape[0]], delta[mid:], 1, 1).astype(bf16)
 
 
 def two_own(delta, act_one, got, *grads, start):
@@ -656,13 +660,9 @@
     grad_three[far - 1] = on_core(
         add_up, shaped(got_far.shape, bf16), [grad_three[far - 1], got_far], "add_up"
     )
-    delta_two, away_far, away = on_core(
+    delta_two, away_far = on_core(
         two_first,
-        [
-            shaped((wide_mid, n_rows), bf16),
-            shaped((hidden, n_mid), bf16),
-            shaped((far * hidden, n_mid), bf16),
-        ],
+        [shaped((wide_mid, n_rows), bf16), shaped((hidden, n_mid), bf16)],
         [sum_two, slope_two, act_one],
         "two_first",
         flops=LONG,
@@ -672,6 +672,12 @@
         [shaped((hidden, n_mid), bf16)],
         [delta_two, act_one, swap(away_far, "dp", 1)],
         "two_own",
+    )
+    away = on_core(
+        two_away,
+        shaped((far * hidden, n_mid), bf16),
+        [after(farthest, delta_two)[0], act_one],
+        "two_away",
     )
     grads = on_core(
         part(two_own, start=0),

time: 136 us -> 136 us (level)
    pallas_call x40 -> x41, Pallas kernels: 20.7 us -> 20.9 us  [on_core(): pl.pallas_call(body, out_shape=outs, in_specs=[pl.BlockSpec(memory_space=...]
where the time goes in v9:
time: 136 us
  waiting for transfers between devices  50.9 us (37%)
  starting transfers between devices  47.2 us (35%)
  Pallas kernels  20.9 us (15%)
  blocking collectives  10.4 us (8%)
  local copies, waits for them, and re-layouts  3.37 us (2%)
  between operations  1.71 us (1%)
    ppermute x47, waiting for transfers between devices, swap(): return lax.ppermute(value, axis, [(at, at ^ step) for at in range(count)])  50.9 us
    ppermute x47, starting transfers between devices, swap(): return lax.ppermute(value, axis, [(at, at ^ step) for at in range(count)])  47.2 us
    pallas_call x41, Pallas kernels, on_core(): pl.pallas_call(body, out_shape=outs, in_specs=[pl.BlockSpec(memory_space=...  20.9 us
    all_gather x1, blocking collectives, on_device(): held = lax.all_gather(packed, 'dp')  10.4 us
    unnamed x24, local copies, waits for them, and re-layouts  3.37 us
  transfers between devices with their start and end apart: 47, of which 24 were waited for; matrix products, arithmetic and copies ran while one was open for 1% of the time, Pallas kernels for 11%

profile of v9, /device:TPU:0, one launch (start us, length us, event | category | flops | bytes accessed | tf_op | source)
XLA Modules:
  0.0 135.6 jit_solution(17015706275531384966)
XLA Ops:
  1.8 4.1 %collective-permute-start.1 = (bf16[512,256]{1,0:T(8,128)(2,1)S(1)}, bf16[512,256]{1,0:T(8,128)(2,1)S(1)}, u32[]{:S(2)}, u32[]{:S(2)}) collective-permute-start(bf16[512,256]{1,0:T(8,128)(2,1)S(1)} %convert_element_type.6.refs_0_), channel_id=1, source_target_pairs={{0,2},{1,3},{2,0},{3,1},{4,6},{5,7},{6,4},{7,5},{8,10},{9,11},{10,... | collective-permute-start | bytes 786440 | tf_op jit(solution)/shard_map/ppermute | solution.py:21
  5.9 1.6 %collective-permute-start = (bf16[512,256]{1,0:T(8,128)(2,1)S(1)}, bf16[512,256]{1,0:T(8,128)(2,1)S(1)}, u32[]{:S(2)}, u32[]{:S(2)}) collective-permute-start(bf16[512,256]{1,0:T(8,128)(2,1)S(1)} %convert_element_type.6.refs_0_), channel_id=1, source_target_pairs={{0,1},{1,0},{2,3},{3,2},{4,5},{5,4},{6,7},{7,6},{8,9},{9,8},{10,11... | collective-permute-start | bytes 786440 | tf_op jit(solution)/shard_map/ppermute | solution.py:21
  9.0 1.9 %collective-permute-start.3 = (bf16[64,128]{1,0:T(8,128)(2,1)S(1)}, bf16[64,128]{1,0:T(8,128)(2,1)S(1)}, u32[]{:S(2)}, u32[]{:S(2)}) collective-permute-start(bf16[64,128]{1,0:T(8,128)(2,1)S(1)} %pack_small.1.refs_1_), channel_id=1, source_target_pairs={{0,2},{1,3},{2,0},{3,1},{4,6},{5,7},{6,4},{7,5},{8,10},{9,11},{10,... | collective-permute-start | bytes 49160 | tf_op jit(solution)/shard_map/ppermute | solution.py:21
  10.9 2.5 %collective-permute-start.2 = (bf16[64,128]{1,0:T(8,128)(2,1)S(1)}, bf16[64,128]{1,0:T(8,128)(2,1)S(1)}, u32[]{:S(2)}, u32[]{:S(2)}) collective-permute-start(bf16[64,128]{1,0:T(8,128)(2,1)S(1)} %pack_small.1.refs_1_), channel_id=1, source_target_pairs={{0,1},{1,0},{2,3},{3,2},{4,5},{5,4},{6,7},{7,6},{8,9},{9,8},{10,11... | collective-permute-start | bytes 49160 | tf_op jit(solution)/shard_map/ppermute | solution.py:21
  15.9 3.7 %collective-permute-done.4.refs_4_ = bf16[64,128]{1,0:T(8,128)(2,1)S(1)} collective-permute-done((bf16[64,128]{1,0:T(8,128)(2,1)S(1)}, bf16[64,128]{1,0:T(8,128)(2,1)S(1)}, u32[]{:S(2)}, u32[]{:S(2)}) %collective-permute-start.4) | collective-permute-done | bytes 16416 | tf_op jit(solution)/shard_map/ppermute | solution.py:21
  19.8 2.0 %collective-permute-start.7 = (bf16[256,512]{1,0:T(8,128)(2,1)S(1)}, bf16[256,512]{1,0:T(8,128)(2,1)S(1)}, u32[]{:S(2)}, u32[]{:S(2)}) collective-permute-start(bf16[256,512]{1,0:T(8,128)(2,1)S(1)} %convert_element_type.7.refs_0_), channel_id=1, source_target_pairs={{0,2},{1,3},{2,0},{3,1},{4,6},{5,7},{6,4},{7,5},{8,10},{9,11},{10,... | collective-permute-start | bytes 786440 | tf_op jit(solution)/shard_map/ppermute | solution.py:21
  21.9 1.7 %collective-permute-start.6 = (bf16[256,512]{1,0:T(8,128)(2,1)S(1)}, bf16[256,512]{1,0:T(8,128)(2,1)S(1)}, u32[]{:S(2)}, u32[]{:S(2)}) collective-permute-start(bf16[256,512]{1,0:T(8,128)(2,1)S(1)} %convert_element_type.7.refs_0_), channel_id=1, source_target_pairs={{0,1},{1,0},{2,3},{3,2},{4,5},{5,4},{6,7},{7,6},{8,9},{9,8},{10,11... | collective-permute-start | bytes 786440 | tf_op jit(solution)/shard_map/ppermute | solution.py:21
  23.9 1.5 %collective-permute-start.5 = (bf16[2,64,128]{2,1,0:T(8,128)(2,1)S(1)}, bf16[2,64,128]{2,1,0:T(8,128)(2,1)S(1)}, u32[]{:S(2)}, u32[]{:S(2)}) collective-permute-start(bf16[2,64,128]{2,1,0:T(8,128)(2,1)S(1)} %get-tuple-element.102.wanted), channel_id=1, source_target_pairs={{0,16},{4,20},{8,24},{12,28},{16,0},{20,4},{24,8},{28,12},{1,17},{... | collective-permute-start | bytes 98312 | tf_op jit(solution)/shard_map/ppermute | solution.py:21
  25.4 10.4 %all-gather = bf16[3072,128]{1,0:T(8,128)(2,1)S(1)} all-gather(bf16[384,128]{1,0:T(8,128)(2,1)S(1)} %pack_all.1), channel_id=2, replica_groups=mesh['dp'=8,'mp'=4] {'dp'}, dimensions={0}, use_global_device_ids=true | all-gather | bytes 884736 | tf_op jit(solution)/shard_map/all_gather | solution.py:521
  36.0 2.3 %one_forward.1.act_one = bf16[2048,512]{1,0:T(8,128)(2,1)S(1)} custom-call(bf16[64,512]{1,0:T(8,128)(2,1)S(1)} %get-tuple-element.100.inputs, bf16[64,2048]{1,0:T(8,128)(2,1)S(1)} %get-tuple-element.104.first), custom_call_target="tpu_custom_call" | custom-call | tf_op jit(solution)/shard_map/one_forward/pallas_call | solution.py:57
  39.3 1.7 %collective-permute-done.8.far = bf16[512,256]{1,0:T(8,128)(2,1)S(1)} collective-permute-done((bf16[512,256]{1,0:T(8,128)(2,1)S(1)}, bf16[512,256]{1,0:T(8,128)(2,1)S(1)}, u32[]{:S(2)}, u32[]{:S(2)}) %collective-permute-start.8) | collective-permute-done | bytes 262176 | tf_op jit(solution)/shard_map/ppermute | solution.py:21
  45.9 1.5 %one_slope.3.slope = bf16[1024,512]{1,0:T(8,128)(2,1)S(1)} custom-call(bf16[64,512]{1,0:T(8,128)(2,1)S(1)} %get-tuple-element.100.inputs, bf16[64,2048]{1,0:T(8,128)(2,1)S(1)} %get-tuple-element.104.first), custom_call_target="tpu_custom_call" | custom-call | flops 6000000000 | tf_op jit(solution)/shard_map/one_slope/pallas_call | solution.py:57
  47.4 1.6 %collective-permute-start.14 = (bf16[256,768]{1,0:T(8,128)(2,1)S(1)}, bf16[256,768]{1,0:T(8,128)(2,1)S(1)}, u32[]{:S(2)}, u32[]{:S(2)}) collective-permute-start(bf16[256,768]{1,0:T(8,128)(2,1)S(1)} %get-tuple-element.122), channel_id=1, source_target_pairs={{0,8},{4,12},{8,0},{12,4},{16,24},{20,28},{24,16},{28,20},{1,9},{5... | collective-permute-start | bytes 1179656 | tf_op jit(solution)/shard_map/ppermute | solution.py:21
  49.0 1.5 %collective-permute-start.15 = (bf16[256,768]{1,0:T(8,128)(2,1)S(1)}, bf16[256,768]{1,0:T(8,128)(2,1)S(1)}, u32[]{:S(2)}, u32[]{:S(2)}) collective-permute-start(bf16[256,768]{1,0:T(8,128)(2,1)S(1)} %get-tuple-element.124), channel_id=1, source_target_pairs={{0,16},{4,20},{8,24},{12,28},{16,0},{20,4},{24,8},{28,12},{1,17},{... | collective-permute-start | bytes 1179656 | tf_op jit(solution)/shard_map/ppermute | solution.py:21
  50.5 2.8 %collective-permute-done.18.refs_0_ = bf16[256,512]{1,0:T(8,128)(2,1)S(1)} collective-permute-done((bf16[256,512]{1,0:T(8,128)(2,1)S(1)}, bf16[256,512]{1,0:T(8,128)(2,1)S(1)}, u32[]{:S(2)}, u32[]{:S(2)}) %collective-permute-start.18) | collective-permute-done | bytes 262176 | tf_op jit(solution)/shard_map/ppermute | solution.py:21
  53.3 1.7 %one_slope.2.slope_more = bf16[1024,512]{1,0:T(8,128)(2,1)S(1)} custom-call(bf16[64,512]{1,0:T(8,128)(2,1)S(1)} %get-tuple-element.100.inputs, bf16[64,2048]{1,0:T(8,128)(2,1)S(1)} %get-tuple-element.104.first), custom_call_target="tpu_custom_call" | custom-call | flops 6000000000 | tf_op jit(solution)/shard_map/one_slope/pallas_call | solution.py:57
  55.9 1.6 %collective-permute-start.20 = (bf16[256,256]{1,0:T(8,128)(2,1)S(1)}, bf16[256,256]{1,0:T(8,128)(2,1)S(1)}, u32[]{:S(2)}, u32[]{:S(2)}) collective-permute-start(bf16[256,256]{1,0:T(8,128)(2,1)S(1)} %get-tuple-element.135), channel_id=1, source_target_pairs={{0,8},{4,12},{8,0},{12,4},{16,24},{20,28},{24,16},{28,20},{1,9},{5... | collective-permute-start | bytes 393224 | tf_op jit(solution)/shard_map/ppermute | solution.py:21
  57.5 1.5 %collective-permute-start.21 = (bf16[256,256]{1,0:T(8,128)(2,1)S(1)}, bf16[256,256]{1,0:T(8,128)(2,1)S(1)}, u32[]{:S(2)}, u32[]{:S(2)}) collective-permute-start(bf16[256,256]{1,0:T(8,128)(2,1)S(1)} %get-tuple-element.137), channel_id=1, source_target_pairs={{0,16},{4,20},{8,24},{12,28},{16,0},{20,4},{24,8},{28,12},{1,17},{... | collective-permute-start | bytes 393224 | tf_op jit(solution)/shard_map/ppermute | solution.py:21
  59.7 1.6 %collective-permute-start.16 = (bf16[128,768]{1,0:T(8,128)(2,1)S(1)}, bf16[128,768]{1,0:T(8,128)(2,1)S(1)}, u32[]{:S(2)}, u32[]{:S(2)}) collective-permute-start(bf16[128,768]{1,0:T(8,128)(2,1)S(1)} %get-tuple-element.126), channel_id=1, source_target_pairs={{0,16},{4,20},{8,24},{12,28},{16,0},{20,4},{24,8},{28,12},{1,17},{... | collective-permute-start | bytes 589832 | tf_op jit(solution)/shard_map/ppermute | solution.py:21
  61.9 1.9 %collective-permute-done.21.refs_3_ = bf16[256,256]{1,0:T(8,128)(2,1)S(1)} collective-permute-done((bf16[256,256]{1,0:T(8,128)(2,1)S(1)}, bf16[256,256]{1,0:T(8,128)(2,1)S(1)}, u32[]{:S(2)}, u32[]{:S(2)}) %collective-permute-start.21) | collective-permute-done | bytes 131104 | tf_op jit(solution)/shard_map/ppermute | solution.py:21
  63.8 1.6 %collective-permute-start.22 = (bf16[128,256]{1,0:T(8,128)(2,1)S(1)}, bf16[128,256]{1,0:T(8,128)(2,1)S(1)}, u32[]{:S(2)}, u32[]{:S(2)}) collective-permute-start(bf16[128,256]{1,0:T(8,128)(2,1)S(1)} %get-tuple-element.139), channel_id=1, source_target_pairs={{0,16},{4,20},{8,24},{12,28},{16,0},{20,4},{24,8},{28,12},{1,17},{... | collective-permute-start | bytes 196616 | tf_op jit(solution)/shard_map/ppermute | solution.py:21
  66.0 2.0 %collective-permute-done.16.refs_1_ = bf16[128,768]{1,0:T(8,128)(2,1)S(1)} collective-permute-done((bf16[128,768]{1,0:T(8,128)(2,1)S(1)}, bf16[128,768]{1,0:T(8,128)(2,1)S(1)}, u32[]{:S(2)}, u32[]{:S(2)}) %collective-permute-start.16) | collective-permute-done | bytes 196640 | tf_op jit(solution)/shard_map/ppermute | solution.py:21
  77.6 3.8 %collective-permute-done.29.refs_3_ = bf16[256,256]{1,0:T(8,128)(2,1)S(1)} collective-permute-done((bf16[256,256]{1,0:T(8,128)(2,1)S(1)}, bf16[256,256]{1,0:T(8,128)(2,1)S(1)}, u32[]{:S(2)}, u32[]{:S(2)}) %collective-permute-start.29) | collective-permute-done | bytes 131104 | tf_op jit(solution)/shard_map/ppermute | solution.py:21
  85.7 8.3 %collective-permute-done.33.refs_3_ = bf16[256,768]{1,0:T(8,128)(2,1)S(1)} collective-permute-done((bf16[256,768]{1,0:T(8,128)(2,1)S(1)}, bf16[256,768]{1,0:T(8,128)(2,1)S(1)}, u32[]{:S(2)}, u32[]{:S(2)}) %collective-permute-start.33) | collective-permute-done | bytes 393248 | tf_op jit(solution)/shard_map/ppermute | solution.py:21
  99.7 2.1 %one_back.1 = (f32[4,112,256]{2,1,0:T(8,128)S(1)}, bf16[4,112,256]{2,1,0:T(8,128)(2,1)S(1)}) custom-call(bf16[64,512]{1,0:T(8,128)(2,1)S(1)} %get-tuple-element.100.inputs, bf16[512,512]{1,0:T(8,128)(2,1)S(1)} %get-tuple-element.162.delta, bf16[1024,512]{1,0:T(8,128)(2,1)S(1)} %one_slope.3.slope, bf16[1024,512]{1,0:T(8,128)(2,1)S(1)} %one_slope.2.slope_more, ...), custom_call_target="tpu_custom_call" | custom-call | flops 99999997952 | tf_op jit(solution)/shard_map/one_back/pallas_call | solution.py:57
  103.0 1.8 %collective-permute-start.36 = (bf16[256,512]{1,0:T(8,128)(2,1)S(1)}, bf16[256,512]{1,0:T(8,128)(2,1)S(1)}, u32[]{:S(2)}, u32[]{:S(2)}) collective-permute-start(bf16[256,512]{1,0:T(8,128)(2,1)S(1)} %add_up.2), channel_id=1, source_target_pairs={{0,2},{1,3},{2,0},{3,1},{4,6},{5,7},{6,4},{7,5},{8,10},{9,11},{10,... | collective-permute-start | bytes 786440 | tf_op jit(solution)/shard_map/ppermute | solution.py:21
  110.1 2.0 %collective-permute-start.43 = (bf16[512,256]{1,0:T(8,128)(2,1)S(1)}, bf16[512,256]{1,0:T(8,128)(2,1)S(1)}, u32[]{:S(2)}, u32[]{:S(2)}) collective-permute-start(bf16[512,256]{1,0:T(8,128)(2,1)S(1)} %add_up.3), channel_id=1, source_target_pairs={{0,2},{1,3},{2,0},{3,1},{4,6},{5,7},{6,4},{7,5},{8,10},{9,11},{10,... | collective-permute-start | bytes 786440 | tf_op jit(solution)/shard_map/ppermute | solution.py:21
  112.4 6.2 %collective-permute-done.36.refs_0_ = bf16[256,512]{1,0:T(8,128)(2,1)S(1)} collective-permute-done((bf16[256,512]{1,0:T(8,128)(2,1)S(1)}, bf16[256,512]{1,0:T(8,128)(2,1)S(1)}, u32[]{:S(2)}, u32[]{:S(2)}) %collective-permute-start.36) | collective-permute-done | bytes 262176 | tf_op jit(solution)/shard_map/ppermute | solution.py:21
  119.4 3.5 %collective-permute-done.38.got = bf16[1,112,256]{2,1,0:T(8,128)(2,1)S(1)} collective-permute-done((bf16[1,112,256]{2,1,0:T(8,128)(2,1)S(1)}, bf16[1,112,256]{2,1,0:T(8,128)(2,1)S(1)}, u32[]{:S(2)}, u32[]{:S(2)}) %collective-permute-start.38) | collective-permute-done | bytes 57376 | tf_op jit(solution)/shard_map/ppermute | solution.py:21
  122.9 3.8 %collective-permute-done.44.refs_1_ = bf16[256,512]{1,0:T(8,128)(2,1)S(1)} collective-permute-done((bf16[256,512]{1,0:T(8,128)(2,1)S(1)}, bf16[256,512]{1,0:T(8,128)(2,1)S(1)}, u32[]{:S(2)}, u32[]{:S(2)}) %collective-permute-start.44) | collective-permute-done | bytes 262176 | tf_op jit(solution)/shard_map/ppermute | solution.py:21
  127.8 2.9 %collective-permute-done.45.got = bf16[112,128]{1,0:T(8,128)(2,1)S(1)} collective-permute-done((bf16[112,128]{1,0:T(8,128)(2,1)S(1)}, bf16[112,128]{1,0:T(8,128)(2,1)S(1)}, u32[]{:S(2)}, u32[]{:S(2)}) %collective-permute-start.45) | collective-permute-done | bytes 28704 | tf_op jit(solution)/shard_map/ppermute | solution.py:21
  132.2 2.7 %collective-permute-done.46.refs_0_ = bf16[112,64]{1,0:T(8,128)(2,1)S(1)} collective-permute-done((bf16[112,64]{1,0:T(8,128)(2,1)S(1)}, bf16[112,64]{1,0:T(8,128)(2,1)S(1)}, u32[]{:S(2)}, u32[]{:S(2)}) %collective-permute-start.46) | collective-permute-done | bytes 14368 | tf_op jit(solution)/shard_map/ppermute | solution.py:21
  (130 shorter events, 44.2 us)
Async XLA Ops:
  1.8 17.8 %collective-permute-start.1 = (bf16[512,256]{1,0:T(8,128)(2,1)S(1)}, bf16[512,256]{1,0:T(8,128)(2,1)S(1)}, u32[]{:S(2)}, u32[]{:S(2)}) collective-permute-start(bf16[512,256]{1,0:T(8,128)(2,1)S(1)} %convert_element_type.6.refs_0_), channel_id=1, source_target_pairs={{0,2},{1,3},{2,0},{3,1},{4,6},{5,7},{6,4},{7,5},{8,10},{9,11},{10,... | collective-permute-start | bytes 786440 | tf_op jit(solution)/shard_map/ppermute | solution.py:21
  5.9 13.7 %collective-permute-start = (bf16[512,256]{1,0:T(8,128)(2,1)S(1)}, bf16[512,256]{1,0:T(8,128)(2,1)S(1)}, u32[]{:S(2)}, u32[]{:S(2)}) collective-permute-start(bf16[512,256]{1,0:T(8,128)(2,1)S(1)} %convert_element_type.6.refs_0_), channel_id=1, source_target_pairs={{0,1},{1,0},{2,3},{3,2},{4,5},{5,4},{6,7},{7,6},{8,9},{9,8},{10,11... | collective-permute-start | bytes 786440 | tf_op jit(solution)/shard_map/ppermute | solution.py:21
  9.0 10.6 %collective-permute-start.4 = (bf16[64,128]{1,0:T(8,128)(2,1)S(1)}, bf16[64,128]{1,0:T(8,128)(2,1)S(1)}, u32[]{:S(2)}, u32[]{:S(2)}) collective-permute-start(bf16[64,128]{1,0:T(8,128)(2,1)S(1)} %pack_small.1.refs_1_), channel_id=1, source_target_pairs={{0,3},{1,2},{2,1},{3,0},{4,7},{5,6},{6,5},{7,4},{8,11},{9,10},{10,... | collective-permute-start | bytes 49160 | tf_op jit(solution)/shard_map/ppermute | solution.py:21
  9.0 10.6 %collective-permute-start.3 = (bf16[64,128]{1,0:T(8,128)(2,1)S(1)}, bf16[64,128]{1,0:T(8,128)(2,1)S(1)}, u32[]{:S(2)}, u32[]{:S(2)}) collective-permute-start(bf16[64,128]{1,0:T(8,128)(2,1)S(1)} %pack_small.1.refs_1_), channel_id=1, source_target_pairs={{0,2},{1,3},{2,0},{3,1},{4,6},{5,7},{6,4},{7,5},{8,10},{9,11},{10,... | collective-permute-start | bytes 49160 | tf_op jit(solution)/shard_map/ppermute | solution.py:21
  10.9 8.7 %collective-permute-start.2 = (bf16[64,128]{1,0:T(8,128)(2,1)S(1)}, bf16[64,128]{1,0:T(8,128)(2,1)S(1)}, u32[]{:S(2)}, u32[]{:S(2)}) collective-permute-start(bf16[64,128]{1,0:T(8,128)(2,1)S(1)} %pack_small.1.refs_1_), channel_id=1, source_target_pairs={{0,1},{1,0},{2,3},{3,2},{4,5},{5,4},{6,7},{7,6},{8,9},{9,8},{10,11... | collective-permute-start | bytes 49160 | tf_op jit(solution)/shard_map/ppermute | solution.py:21
  19.7 22.8 %collective-permute-start.9 = (bf16[1536,256]{1,0:T(8,128)(2,1)S(1)}, bf16[1536,256]{1,0:T(8,128)(2,1)S(1)}, u32[]{:S(2)}, u32[]{:S(2)}) collective-permute-start(bf16[1536,256]{1,0:T(8,128)(2,1)S(1)} %lay.1.near), channel_id=1, source_target_pairs={{0,4},{4,0},{8,12},{12,8},{16,20},{20,16},{24,28},{28,24},{1,5},{5... | collective-permute-start | bytes 2359304 | tf_op jit(solution)/shard_map/ppermute | solution.py:21
  19.8 18.5 %collective-permute-start.7 = (bf16[256,512]{1,0:T(8,128)(2,1)S(1)}, bf16[256,512]{1,0:T(8,128)(2,1)S(1)}, u32[]{:S(2)}, u32[]{:S(2)}) collective-permute-start(bf16[256,512]{1,0:T(8,128)(2,1)S(1)} %convert_element_type.7.refs_0_), channel_id=1, source_target_pairs={{0,2},{1,3},{2,0},{3,1},{4,6},{5,7},{6,4},{7,5},{8,10},{9,11},{10,... | collective-permute-start | bytes 786440 | tf_op jit(solution)/shard_map/ppermute | solution.py:21
  21.9 16.9 %collective-permute-start.6 = (bf16[256,512]{1,0:T(8,128)(2,1)S(1)}, bf16[256,512]{1,0:T(8,128)(2,1)S(1)}, u32[]{:S(2)}, u32[]{:S(2)}) collective-permute-start(bf16[256,512]{1,0:T(8,128)(2,1)S(1)} %convert_element_type.7.refs_0_), channel_id=1, source_target_pairs={{0,1},{1,0},{2,3},{3,2},{4,5},{5,4},{6,7},{7,6},{8,9},{9,8},{10,11... | collective-permute-start | bytes 786440 | tf_op jit(solution)/shard_map/ppermute | solution.py:21
  23.6 17.4 %collective-permute-start.8 = (bf16[512,256]{1,0:T(8,128)(2,1)S(1)}, bf16[512,256]{1,0:T(8,128)(2,1)S(1)}, u32[]{:S(2)}, u32[]{:S(2)}) collective-permute-start(bf16[512,256]{1,0:T(8,128)(2,1)S(1)} %collective-permute-done.1.refs_2_), channel_id=1, source_target_pairs={{0,1},{1,0},{2,3},{3,2},{4,5},{5,4},{6,7},{7,6},{8,9},{9,8},{10,11... | collective-permute-start | bytes 786440 | tf_op jit(solution)/shard_map/ppermute | solution.py:21
  23.9 15.0 %collective-permute-start.5 = (bf16[2,64,128]{2,1,0:T(8,128)(2,1)S(1)}, bf16[2,64,128]{2,1,0:T(8,128)(2,1)S(1)}, u32[]{:S(2)}, u32[]{:S(2)}) collective-permute-start(bf16[2,64,128]{2,1,0:T(8,128)(2,1)S(1)} %get-tuple-element.102.wanted), channel_id=1, source_target_pairs={{0,16},{4,20},{8,24},{12,28},{16,0},{20,4},{24,8},{28,12},{1,17},{... | collective-permute-start | bytes 98312 | tf_op jit(solution)/shard_map/ppermute | solution.py:21
  44.9 8.4 %collective-permute-start.18 = (bf16[256,512]{1,0:T(8,128)(2,1)S(1)}, bf16[256,512]{1,0:T(8,128)(2,1)S(1)}, u32[]{:S(2)}, u32[]{:S(2)}) collective-permute-start(bf16[256,512]{1,0:T(8,128)(2,1)S(1)} %collective-permute-done.7.refs_2_), channel_id=1, source_target_pairs={{0,1},{1,0},{2,3},{3,2},{4,5},{5,4},{6,7},{7,6},{8,9},{9,8},{10,11... | collective-permute-start | bytes 786440 | tf_op jit(solution)/shard_map/ppermute | solution.py:21
  47.4 11.5 %collective-permute-start.14 = (bf16[256,768]{1,0:T(8,128)(2,1)S(1)}, bf16[256,768]{1,0:T(8,128)(2,1)S(1)}, u32[]{:S(2)}, u32[]{:S(2)}) collective-permute-start(bf16[256,768]{1,0:T(8,128)(2,1)S(1)} %get-tuple-element.122), channel_id=1, source_target_pairs={{0,8},{4,12},{8,0},{12,4},{16,24},{20,28},{24,16},{28,20},{1,9},{5... | collective-permute-start | bytes 1179656 | tf_op jit(solution)/shard_map/ppermute | solution.py:21
  49.0 10.6 %collective-permute-start.15 = (bf16[256,768]{1,0:T(8,128)(2,1)S(1)}, bf16[256,768]{1,0:T(8,128)(2,1)S(1)}, u32[]{:S(2)}, u32[]{:S(2)}) collective-permute-start(bf16[256,768]{1,0:T(8,128)(2,1)S(1)} %get-tuple-element.124), channel_id=1, source_target_pairs={{0,16},{4,20},{8,24},{12,28},{16,0},{20,4},{24,8},{28,12},{1,17},{... | collective-permute-start | bytes 1179656 | tf_op jit(solution)/shard_map/ppermute | solution.py:21
  55.9 6.0 %collective-permute-start.20 = (bf16[256,256]{1,0:T(8,128)(2,1)S(1)}, bf16[256,256]{1,0:T(8,128)(2,1)S(1)}, u32[]{:S(2)}, u32[]{:S(2)}) collective-permute-start(bf16[256,256]{1,0:T(8,128)(2,1)S(1)} %get-tuple-element.135), channel_id=1, source_target_pairs={{0,8},{4,12},{8,0},{12,4},{16,24},{20,28},{24,16},{28,20},{1,9},{5... | collective-permute-start | bytes 393224 | tf_op jit(solution)/shard_map/ppermute | solution.py:21
  57.5 6.3 %collective-permute-start.21 = (bf16[256,256]{1,0:T(8,128)(2,1)S(1)}, bf16[256,256]{1,0:T(8,128)(2,1)S(1)}, u32[]{:S(2)}, u32[]{:S(2)}) collective-permute-start(bf16[256,256]{1,0:T(8,128)(2,1)S(1)} %get-tuple-element.137), channel_id=1, source_target_pairs={{0,16},{4,20},{8,24},{12,28},{16,0},{20,4},{24,8},{28,12},{1,17},{... | collective-permute-start | bytes 393224 | tf_op jit(solution)/shard_map/ppermute | solution.py:21
  59.7 8.3 %collective-permute-start.16 = (bf16[128,768]{1,0:T(8,128)(2,1)S(1)}, bf16[128,768]{1,0:T(8,128)(2,1)S(1)}, u32[]{:S(2)}, u32[]{:S(2)}) collective-permute-start(bf16[128,768]{1,0:T(8,128)(2,1)S(1)} %get-tuple-element.126), channel_id=1, source_target_pairs={{0,16},{4,20},{8,24},{12,28},{16,0},{20,4},{24,8},{28,12},{1,17},{... | collective-permute-start | bytes 589832 | tf_op jit(solution)/shard_map/ppermute | solution.py:21
  61.3 6.7 %collective-permute-start.17 = (bf16[128,768]{1,0:T(8,128)(2,1)S(1)}, bf16[128,768]{1,0:T(8,128)(2,1)S(1)}, u32[]{:S(2)}, u32[]{:S(2)}) collective-permute-start(bf16[128,768]{1,0:T(8,128)(2,1)S(1)} %get-tuple-element.127), channel_id=1, source_target_pairs={{0,8},{4,12},{8,0},{12,4},{16,24},{20,28},{24,16},{28,20},{1,9},{5... | collective-permute-start | bytes 589832 | tf_op jit(solution)/shard_map/ppermute | solution.py:21
  71.8 10.2 %collective-permute-start.24 = (bf16[128,768]{1,0:T(8,128)(2,1)S(1)}, bf16[128,768]{1,0:T(8,128)(2,1)S(1)}, u32[]{:S(2)}, u32[]{:S(2)}) collective-permute-start(bf16[128,768]{1,0:T(8,128)(2,1)S(1)} %get-tuple-element.141.own), channel_id=1, source_target_pairs={{0,8},{4,12},{8,0},{12,4},{16,24},{20,28},{24,16},{28,20},{1,9},{5... | collective-permute-start | bytes 589832 | tf_op jit(solution)/shard_map/ppermute | solution.py:21
  73.3 8.7 %collective-permute-start.26 = (bf16[128,768]{1,0:T(8,128)(2,1)S(1)}, bf16[128,768]{1,0:T(8,128)(2,1)S(1)}, u32[]{:S(2)}, u32[]{:S(2)}) collective-permute-start(bf16[128,768]{1,0:T(8,128)(2,1)S(1)} %get-tuple-element.143.own), channel_id=1, source_target_pairs={{0,16},{4,20},{8,24},{12,28},{16,0},{20,4},{24,8},{28,12},{1,17},{... | collective-permute-start | bytes 589832 | tf_op jit(solution)/shard_map/ppermute | solution.py:21
  75.5 5.9 %collective-permute-start.29 = (bf16[256,256]{1,0:T(8,128)(2,1)S(1)}, bf16[256,256]{1,0:T(8,128)(2,1)S(1)}, u32[]{:S(2)}, u32[]{:S(2)}) collective-permute-start(bf16[256,256]{1,0:T(8,128)(2,1)S(1)} %join.6.refs_2_), channel_id=1, source_target_pairs={{0,8},{4,12},{8,0},{12,4},{16,24},{20,28},{24,16},{28,20},{1,9},{5... | collective-permute-start | bytes 393224 | tf_op jit(solution)/shard_map/ppermute | solution.py:21
  76.3 5.7 %collective-permute-start.27 = (bf16[256,256]{1,0:T(8,128)(2,1)S(1)}, bf16[256,256]{1,0:T(8,128)(2,1)S(1)}, u32[]{:S(2)}, u32[]{:S(2)}) collective-permute-start(bf16[256,256]{1,0:T(8,128)(2,1)S(1)} %join.5.refs_0_), channel_id=1, source_target_pairs={{0,16},{4,20},{8,24},{12,28},{16,0},{20,4},{24,8},{28,12},{1,17},{... | collective-permute-start | bytes 393224 | tf_op jit(solution)/shard_map/ppermute | solution.py:21
  82.5 11.6 %collective-permute-start.33 = (bf16[256,768]{1,0:T(8,128)(2,1)S(1)}, bf16[256,768]{1,0:T(8,128)(2,1)S(1)}, u32[]{:S(2)}, u32[]{:S(2)}) collective-permute-start(bf16[256,768]{1,0:T(8,128)(2,1)S(1)} %join.7.refs_2_), channel_id=1, source_target_pairs={{0,8},{4,12},{8,0},{12,4},{16,24},{20,28},{24,16},{28,20},{1,9},{5... | collective-permute-start | bytes 1179656 | tf_op jit(solution)/shard_map/ppermute | solution.py:21
  83.2 11.3 %collective-permute-start.32 = (bf16[256,768]{1,0:T(8,128)(2,1)S(1)}, bf16[256,768]{1,0:T(8,128)(2,1)S(1)}, u32[]{:S(2)}, u32[]{:S(2)}) collective-permute-start(bf16[256,768]{1,0:T(8,128)(2,1)S(1)} %join.4.refs_0_), channel_id=1, source_target_pairs={{0,16},{4,20},{8,24},{12,28},{16,0},{20,4},{24,8},{28,12},{1,17},{... | collective-permute-start | bytes 1179656 | tf_op jit(solution)/shard_map/ppermute | solution.py:21
  84.3 10.2 %collective-permute-start.31 = (bf16[256,512]{1,0:T(8,128)(2,1)S(1)}, bf16[256,512]{1,0:T(8,128)(2,1)S(1)}, u32[]{:S(2)}, u32[]{:S(2)}) collective-permute-start(bf16[256,512]{1,0:T(8,128)(2,1)S(1)} %three_own.2), channel_id=1, source_target_pairs={{0,1},{1,0},{2,3},{3,2},{4,5},{5,4},{6,7},{7,6},{8,9},{9,8},{10,11... | collective-permute-start | bytes 786440 | tf_op jit(solution)/shard_map/ppermute | solution.py:21
  96.7 5.6 %collective-permute-start.35 = (bf16[256,1536]{1,0:T(8,128)(2,1)S(1)}, bf16[256,1536]{1,0:T(8,128)(2,1)S(1)}, u32[]{:S(2)}, u32[]{:S(2)}) collective-permute-start(bf16[256,1536]{1,0:T(8,128)(2,1)S(1)} %three_away.3), channel_id=1, source_target_pairs={{0,4},{4,0},{8,12},{12,8},{16,20},{20,16},{24,28},{28,24},{1,5},{5... | collective-permute-start | bytes 2359304 | tf_op jit(solution)/shard_map/ppermute | solution.py:21
  98.0 8.4 %collective-permute-start.41 = (bf16[512,256]{1,0:T(8,128)(2,1)S(1)}, bf16[512,256]{1,0:T(8,128)(2,1)S(1)}, u32[]{:S(2)}, u32[]{:S(2)}) collective-permute-start(bf16[512,256]{1,0:T(8,128)(2,1)S(1)} %two_own.2), channel_id=1, source_target_pairs={{0,1},{1,0},{2,3},{3,2},{4,5},{5,4},{6,7},{7,6},{8,9},{9,8},{10,11... | collective-permute-start | bytes 786440 | tf_op jit(solution)/shard_map/ppermute | solution.py:21
  101.8 5.7 %collective-permute-start.34 = (bf16[4,112,256]{2,1,0:T(8,128)(2,1)S(1)}, bf16[4,112,256]{2,1,0:T(8,128)(2,1)S(1)}, u32[]{:S(2)}, u32[]{:S(2)}) collective-permute-start(bf16[4,112,256]{2,1,0:T(8,128)(2,1)S(1)} %get-tuple-element.153), channel_id=1, source_target_pairs={{0,4},{4,0},{8,12},{12,8},{16,20},{20,16},{24,28},{28,24},{1,5},{5... | collective-permute-start | bytes 688136 | tf_op jit(solution)/shard_map/ppermute | solution.py:21
  103.0 15.5 %collective-permute-start.36 = (bf16[256,512]{1,0:T(8,128)(2,1)S(1)}, bf16[256,512]{1,0:T(8,128)(2,1)S(1)}, u32[]{:S(2)}, u32[]{:S(2)}) collective-permute-start(bf16[256,512]{1,0:T(8,128)(2,1)S(1)} %add_up.2), channel_id=1, source_target_pairs={{0,2},{1,3},{2,0},{3,1},{4,6},{5,7},{6,4},{7,5},{8,10},{9,11},{10,... | collective-permute-start | bytes 786440 | tf_op jit(solution)/shard_map/ppermute | solution.py:21
  106.5 20.2 %collective-permute-start.44 = (bf16[256,512]{1,0:T(8,128)(2,1)S(1)}, bf16[256,512]{1,0:T(8,128)(2,1)S(1)}, u32[]{:S(2)}, u32[]{:S(2)}) collective-permute-start(bf16[256,512]{1,0:T(8,128)(2,1)S(1)} %get-tuple-element.168), channel_id=1, source_target_pairs={{0,1},{1,0},{2,3},{3,2},{4,5},{5,4},{6,7},{7,6},{8,9},{9,8},{10,11... | collective-permute-start | bytes 786440 | tf_op jit(solution)/shard_map/ppermute | solution.py:21
  108.9 21.9 %collective-permute-start.42 = (bf16[512,256]{1,0:T(8,128)(2,1)S(1)}, bf16[512,256]{1,0:T(8,128)(2,1)S(1)}, u32[]{:S(2)}, u32[]{:S(2)}) collective-permute-start(bf16[512,256]{1,0:T(8,128)(2,1)S(1)} %get-tuple-element.166), channel_id=1, source_target_pairs={{0,1},{1,0},{2,3},{3,2},{4,5},{5,4},{6,7},{7,6},{8,9},{9,8},{10,11... | collective-permute-start | bytes 786440 | tf_op jit(solution)/shard_map/ppermute | solution.py:21
  110.1 20.8 %collective-permute-start.43 = (bf16[512,256]{1,0:T(8,128)(2,1)S(1)}, bf16[512,256]{1,0:T(8,128)(2,1)S(1)}, u32[]{:S(2)}, u32[]{:S(2)}) collective-permute-start(bf16[512,256]{1,0:T(8,128)(2,1)S(1)} %add_up.3), channel_id=1, source_target_pairs={{0,2},{1,3},{2,0},{3,1},{4,6},{5,7},{6,4},{7,5},{8,10},{9,11},{10,... | collective-permute-start | bytes 786440 | tf_op jit(solution)/shard_map/ppermute | solution.py:21
  122.8 7.8 %collective-permute-start.45 = (bf16[112,128]{1,0:T(8,128)(2,1)S(1)}, bf16[112,128]{1,0:T(8,128)(2,1)S(1)}, u32[]{:S(2)}, u32[]{:S(2)}) collective-permute-start(bf16[112,128]{1,0:T(8,128)(2,1)S(1)} %get-tuple-element.170), channel_id=1, source_target_pairs={{0,2},{1,3},{2,0},{3,1},{4,6},{5,7},{6,4},{7,5},{8,10},{9,11},{10,... | collective-permute-start | bytes 86024 | tf_op jit(solution)/shard_map/ppermute | solution.py:21
  (26 other events, 156.3 us)
